TPU v7x, 32 devices: a whole 2x2x4 slice. The times are simulated.
32 devices in a mesh: row: 8 (over y, x, core), col: 4 (over z).
Axes of the slice: x: 2, y: 2, z: 4, core: 2. Of those that a mesh axis runs over, the one named last changes fastest.
Arguments:
- noise: bfloat16 [1024, 16384], P('row', 'col'), as said below
- data: bfloat16 [1024, 16384], P('col', 'row'), may hold values from -5 to 5
Outputs:
- targets: bfloat16 [1024, 16384], P(('row', 'col'))
- noise_potential: float32 [1024], P('row')
- data_potential: float32 [1024], P('col')
Inputs may be any that keep to these rules, and one draw needn't show every extreme that they name: noise latents, real values of order one.
All inputs are finite; a program needn't handle non-finite values.
Results may differ from a plain program's by a relative error of at most 0.022.
Values may be sent and summed in bfloat16 or wider, within the bound.
No kernel may reach another device: no remote copies, remote signals or barrier semaphores. Data moves between devices by JAX's collectives and lax.ppermute only.
A program may use at most 64 MiB of HBM per device.

v0:
```python
import math

import jax
import jax.numpy as jnp
from jax import lax
from jax.sharding import PartitionSpec as P

LATENT = 16384
ITERS = 3


def noise_update(cost_tile, data_pot, epsilon, log_count):
    scores = (data_pot[None, :] - cost_tile) / epsilon
    local_peak = jnp.max(scores, axis=1)
    highest = lax.pmax(local_peak, "col")
    summed = lax.psum(jnp.sum(jnp.exp(scores - highest[:, None]), axis=1), "col")
    return -epsilon * (log_count + highest + jnp.log(summed))


def data_update(cost_tile, noise_pot, epsilon, log_count):
    scores = (noise_pot[:, None] - cost_tile) / epsilon
    local_peak = jnp.max(scores, axis=0)
    highest = lax.pmax(local_peak, "row")
    summed = lax.psum(jnp.sum(jnp.exp(scores - highest[None, :]), axis=0), "row")
    return -epsilon * (log_count + highest + jnp.log(summed))


def per_device(noise, data):
    epsilon = 0.64 / math.sqrt(LATENT)
    contract = (((1,), (1,)), ((), ()))
    noise_full = lax.all_gather(noise, "col", axis=1, tiled=True)
    noise_norm = jnp.sum(jnp.square(noise_full.astype(jnp.float32)), axis=1) / LATENT
    noise_rows = noise.shape[0]
    data_rows = data.shape[0]
    data_full = lax.all_gather(data, "row", axis=1, tiled=True)
    data_norm = jnp.sum(jnp.square(data_full.astype(jnp.float32)), axis=1) / LATENT
    cross = lax.dot_general(noise_full, data_full, contract, preferred_element_type=jnp.float32)
    cost_tile = noise_norm[:, None] + data_norm[None, :] - 2.0 / LATENT * cross
    log_noise = math.log(noise_rows * lax.axis_size("row"))
    log_data = math.log(data_rows * lax.axis_size("col"))
    data_pot = jnp.zeros((data_rows,), jnp.float32)
    for step in range(ITERS):
        noise_pot = noise_update(cost_tile, data_pot, epsilon, log_noise)
        data_pot = data_update(cost_tile, noise_pot, epsilon, log_data)
    noise_pot = noise_update(cost_tile, data_pot, epsilon, log_noise)
    weights = jnp.exp(
        (noise_pot[:, None] + data_pot[None, :] - cost_tile) / epsilon + log_noise
    ).astype(jnp.bfloat16)
    targets = lax.psum_scatter(
        jnp.dot(weights, data_full, preferred_element_type=jnp.float32).astype(jnp.bfloat16),
        "col",
        scatter_dimension=0,
        tiled=True,
    )
    return (targets, noise_pot, data_pot)


def solution(mesh):
    placed = (P("row", "col"), P("col", "row"))
    return jax.shard_map(
        per_device,
        mesh=mesh,
        in_specs=placed,
        out_specs=(P(("row", "col"), None), P("row"), P("col")),
        check_vma=False,
    )
```

profile of v0, /device:TPU:0, one launch (start us, length us, event | category | flops | bytes accessed | tf_op | source)
XLA Modules:
  0.0 396.4 jit_solution(3689586788261267323)
XLA Ops:
  7.2 0.7 all-gather.3.cloned.1.call-update
  7.9 0.7 all-gather.5.cloned.1.call-update
  8.7 84.4 %all-gather.3.cloned.1.call-done = bf16[128,16384]{1,0:T(8,128)(2,1)} async-done(((bf16[128,4096]{1,0:T(8,128)(2,1)}), bf16[128,16384]{1,0:T(8,128)(2,1)}) %all-gather.3.cloned.1.call-update) | async-done | bytes 4194320 | tf_op jit(solution)/shard_map/all_gather | solution.py:31
  93.1 3.1 multiply_reduce_fusion.1
  96.2 51.8 %all-gather.5.cloned.1.call-done = bf16[256,16384]{1,0:T(8,128)(2,1)} async-done(((bf16[256,2048]{1,0:T(8,128)(2,1)}), bf16[256,16384]{1,0:T(8,128)(2,1)}) %all-gather.5.cloned.1.call-update) | async-done | bytes 8388624 | tf_op jit(solution)/shard_map/all_gather | solution.py:35
  147.9 5.3 %multiply_reduce_fusion = f32[256]{0:T(256)S(1)} fusion(bf16[256,16384]{1,0:T(8,128)(2,1)} %all-gather.5.cloned.1.call-done), kind=kLoop, calls=%fused_computation.1 | loop fusion | flops 12582656 | bytes 8389632 | tf_op jit(solution)/shard_map/reduce_sum | solution.py:36
  153.2 0.5 copy-done
  153.7 5.2 %fusion.1 = (f32[128]{0:T(128)S(1)}, f32[128,256]{1,0:T(8,128)S(1)}) fusion(bf16[128,16384]{1,0:T(8,128)(2,1)} %all-gather.3.cloned.1.call-done, bf16[256,16384]{1,0:T(8,128)(2,1)S(1)} %copy-done, f32[256]{0:T(256)S(1)} %broadcast_multiply_fusion, f32[128]{0:T(128)S(1)} %broadcast_multiply_fusion.1), kind=kOutput, calls=%fused_computation.20 | convolution fusion | flops 1073938304 | bytes 12716032 | tf_op jit(solution)/shard_map/dot_general | solution.py:37
  158.9 11.7 %pmax.49 = f32[128]{0:T(128)S(1)} all-reduce(f32[128]{0:T(128)S(1)} %get-tuple-element.3), channel_id=1, replica_groups=mesh['row'=8,'col'=4] {'col'}, use_global_device_ids=true, to_apply=%region_3.0 | all-reduce | flops 128 | bytes 1024 | tf_op jit(solution)/shard_map/pmax | solution.py:15
  170.6 0.2 exponential_reduce_fusion.6
  170.8 8.4 %psum.49 = f32[128]{0:T(128)S(1)} all-reduce(f32[128]{0:T(128)S(1)} %exponential_reduce_fusion.6), channel_id=1, replica_groups=mesh['row'=8,'col'=4] {'col'}, use_global_device_ids=true, to_apply=%region_5.0 | all-reduce | flops 128 | bytes 1024 | tf_op jit(solution)/shard_map/psum | solution.py:16
  179.3 11.8 %pmax.50 = f32[256]{0:T(256)S(1)} all-reduce(f32[256]{0:T(256)S(1)} %fusion.2), channel_id=1, replica_groups=mesh['row'=8,'col'=4] {'row'}, use_global_device_ids=true, to_apply=%region_7.0 | all-reduce | flops 256 | bytes 2048 | tf_op jit(solution)/shard_map/pmax | solution.py:23
  191.1 0.1 exponential_reduce_fusion.5
  191.2 11.8 %psum.50 = f32[256]{0:T(256)S(1)} all-reduce(f32[256]{0:T(256)S(1)} %exponential_reduce_fusion.5), channel_id=1, replica_groups=mesh['row'=8,'col'=4] {'row'}, use_global_device_ids=true, to_apply=%region_9.0 | all-reduce | flops 256 | bytes 2048 | tf_op jit(solution)/shard_map/psum | solution.py:24
  203.0 0.1 fusion.3
  203.2 10.3 %pmax.51 = f32[128]{0:T(128)S(1)} all-reduce(f32[128]{0:T(128)S(1)} %fusion.3), channel_id=1, replica_groups=mesh['row'=8,'col'=4] {'col'}, use_global_device_ids=true, to_apply=%region_11.0 | all-reduce | flops 128 | bytes 1024 | tf_op jit(solution)/shard_map/pmax | solution.py:15
  213.5 0.2 exponential_reduce_fusion.4
  213.7 8.4 %psum.51 = f32[128]{0:T(128)S(1)} all-reduce(f32[128]{0:T(128)S(1)} %exponential_reduce_fusion.4), channel_id=1, replica_groups=mesh['row'=8,'col'=4] {'col'}, use_global_device_ids=true, to_apply=%region_13.0 | all-reduce | flops 128 | bytes 1024 | tf_op jit(solution)/shard_map/psum | solution.py:16
  222.2 11.8 %pmax.52 = f32[256]{0:T(256)S(1)} all-reduce(f32[256]{0:T(256)S(1)} %fusion.4), channel_id=1, replica_groups=mesh['row'=8,'col'=4] {'row'}, use_global_device_ids=true, to_apply=%region_15.0 | all-reduce | flops 256 | bytes 2048 | tf_op jit(solution)/shard_map/pmax | solution.py:23
  234.0 0.1 exponential_reduce_fusion.3
  234.1 11.8 %psum.52 = f32[256]{0:T(256)S(1)} all-reduce(f32[256]{0:T(256)S(1)} %exponential_reduce_fusion.3), channel_id=1, replica_groups=mesh['row'=8,'col'=4] {'row'}, use_global_device_ids=true, to_apply=%region_17.0 | all-reduce | flops 256 | bytes 2048 | tf_op jit(solution)/shard_map/psum | solution.py:24
  246.1 10.3 %pmax.53 = f32[128]{0:T(128)S(1)} all-reduce(f32[128]{0:T(128)S(1)} %fusion.5), channel_id=1, replica_groups=mesh['row'=8,'col'=4] {'col'}, use_global_device_ids=true, to_apply=%region_19.0 | all-reduce | flops 128 | bytes 1024 | tf_op jit(solution)/shard_map/pmax | solution.py:15
  256.4 0.2 exponential_reduce_fusion.2
  256.6 8.4 %psum.53 = f32[128]{0:T(128)S(1)} all-reduce(f32[128]{0:T(128)S(1)} %exponential_reduce_fusion.2), channel_id=1, replica_groups=mesh['row'=8,'col'=4] {'col'}, use_global_device_ids=true, to_apply=%region_21.0 | all-reduce | flops 128 | bytes 1024 | tf_op jit(solution)/shard_map/psum | solution.py:16
  265.1 11.8 %pmax.54 = f32[256]{0:T(256)S(1)} all-reduce(f32[256]{0:T(256)S(1)} %fusion.6), channel_id=1, replica_groups=mesh['row'=8,'col'=4] {'row'}, use_global_device_ids=true, to_apply=%region_23.0 | all-reduce | flops 256 | bytes 2048 | tf_op jit(solution)/shard_map/pmax | solution.py:23
  276.9 0.1 exponential_reduce_fusion.1
  277.0 11.8 %psum.54 = f32[256]{0:T(256)S(1)} all-reduce(f32[256]{0:T(256)S(1)} %exponential_reduce_fusion.1), channel_id=1, replica_groups=mesh['row'=8,'col'=4] {'row'}, use_global_device_ids=true, to_apply=%region_25.0 | all-reduce | flops 256 | bytes 2048 | tf_op jit(solution)/shard_map/psum | solution.py:24
  289.0 10.3 %pmax.55 = f32[128]{0:T(128)S(1)} all-reduce(f32[128]{0:T(128)S(1)} %fusion.7), channel_id=1, replica_groups=mesh['row'=8,'col'=4] {'col'}, use_global_device_ids=true, to_apply=%region_27.0 | all-reduce | flops 128 | bytes 1024 | tf_op jit(solution)/shard_map/pmax | solution.py:15
  299.3 0.2 exponential_reduce_fusion
  299.5 8.4 %psum.55 = f32[128]{0:T(128)S(1)} all-reduce(f32[128]{0:T(128)S(1)} %exponential_reduce_fusion), channel_id=1, replica_groups=mesh['row'=8,'col'=4] {'col'}, use_global_device_ids=true, to_apply=%region_29.0 | all-reduce | flops 128 | bytes 1024 | tf_op jit(solution)/shard_map/psum | solution.py:16
  307.9 6.7 %convolution_convert_fusion = bf16[128,16384]{1,0:T(8,128)(2,1)} fusion(bf16[256,16384]{1,0:T(8,128)(2,1)} %all-gather.5.cloned.1.call-done, f32[128,256]{1,0:T(8,128)S(1)} %get-tuple-element.4, f32[128]{0:T(128)S(1)} %add_multiply_fusion.3, f32[256]{0:T(256)S(1)} %add_multiply_fusion), kind=kOutput, calls=%fused_computation | convolution fusion | flops 1076002816 | bytes 12715520 | tf_op jit(solution)/shard_map/dot_general | solution.py:50
  314.6 75.2 %reduce-scatter.2.cloned.1.call-done = bf16[32,16384]{1,0:T(8,128)(2,1)} async-done(((bf16[128,16384]{1,0:T(8,128)(2,1)}), bf16[32,16384]{1,0:T(8,128)(2,1)}) %reduce-scatter.2.cloned.1.call-update) | async-done | bytes 1048592 | tf_op jit(solution)/shard_map/reduce_scatter | solution.py:49
  (23 shorter events, 0.8 us)
Async XLA Ops:
  7.2 85.9 %all-gather.3.cloned.1.call-start = ((), (), s32[]{:S(2)}) async-start(), calls=%async_computation.1 | async-start | bytes 5242880 | tf_op jit(solution)/shard_map/all_gather | solution.py:31
  7.9 140.0 %all-gather.5.cloned.1.call-start = ((), (), s32[]{:S(2)}) async-start(), calls=%async_computation.2 | async-start | bytes 9437184 | tf_op jit(solution)/shard_map/all_gather | solution.py:35
  8.6 381.2 %reduce-scatter.2.cloned.1.call-start = ((), (), s32[]{:S(2)}) async-start(), calls=%async_computation.3 | async-start | bytes 5242880 | tf_op jit(solution)/shard_map/reduce_scatter | solution.py:49
  147.9 5.8 %copy-start = (bf16[256,16384]{1,0:T(8,128)(2,1)S(1)}, bf16[256,16384]{1,0:T(8,128)(2,1)}, u32[]{:S(2)}) copy-start(bf16[256,16384]{1,0:T(8,128)(2,1)} %all-gather.5.cloned.1.call-done) | copy-start | bytes 25165828
  288.8 25.8 %copy-start.1 = (f32[256]{0:T(256)}, f32[256]{0:T(256)S(1)}, u32[]{:S(2)}) copy-start(f32[256]{0:T(256)S(1)} %add_multiply_fusion) | copy-start | bytes 3076
  307.9 6.7 %copy-start.2 = (f32[128]{0:T(128)}, f32[128]{0:T(128)S(1)}, u32[]{:S(2)}) copy-start(f32[128]{0:T(128)S(1)} %add_multiply_fusion.3) | copy-start | bytes 1540
Sparse Core Ops, SparseCore 0:
  9.6 83.4 all-gather.2
  95.0 52.9 all-gather.4
  314.7 75.0 reduce-scatter.1
where the time goes:
time: 397 us; the launch traced here: 396 us
  waiting for transfers between devices  213 us (54%)
  blocking collectives  147 us (37%)
  between operations  13.8 us (3%)
  matrix products  11.9 us (3%)
  other arithmetic  10.2 us (3%)
    all_gather x1, waiting for transfers between devices, per_device(): noise_full = lax.all_gather(noise, 'col', axis=1, tiled=True)  84.4 us
    reduce_scatter x1, waiting for transfers between devices, per_device(): lax.psum_scatter(jnp.dot(weights, data_full, preferred_element_type=jnp.f...  75.2 us
    all_gather x1, waiting for transfers between devices, per_device(): data_full = lax.all_gather(data, 'row', axis=1, tiled=True)  51.8 us
    pmax x4, blocking collectives, noise_update(): highest = lax.pmax(local_peak, 'col')  42.7 us
    pmax x3, blocking collectives, data_update(): highest = lax.pmax(local_peak, 'row')  35.4 us
    psum x3, blocking collectives, data_update(): lax.psum(jnp.sum(jnp.exp(scores - highest[None, :]), axis=0), 'row')  35.4 us
    psum x4, blocking collectives, noise_update(): lax.psum(jnp.sum(jnp.exp(scores - highest[:, None]), axis=1), 'col')  33.7 us
  transfers between devices with their start and end apart: 3, of which 3 were waited for; matrix products, arithmetic and copies ran while one was open for 1% of the time, Pallas kernels for 0%

commit v1 on v0

--- a/solution.py
+++ b/solution.py
@@ -1,12 +1,20 @@
+import functools
 import math
 
 import jax
 import jax.numpy as jnp
 from jax import lax
+from jax.experimental import pallas as pl
+from jax.experimental.pallas import tpu as pltpu
 from jax.sharding import PartitionSpec as P
 
 LATENT = 16384
 ITERS = 3
+EPSILON = 0.64 / math.sqrt(LATENT)
+LOG2E = math.log2(math.e)
+TO_LOG2 = LOG2E / EPSILON
+CONTRACT = (((1,), (1,)), ((), ()))
+LOCAL_COST_BYTES = 8 * 2**20
 
 
 def noise_update(cost_tile, data_pot, epsilon, log_count):
@@ -25,16 +33,15 @@
     return -epsilon * (log_count + highest + jnp.log(summed))
 
 
-def per_device(noise, data):
-    epsilon = 0.64 / math.sqrt(LATENT)
-    contract = (((1,), (1,)), ((), ()))
+def per_device_tiled(noise, data):
+    epsilon = EPSILON
     noise_full = lax.all_gather(noise, "col", axis=1, tiled=True)
     noise_norm = jnp.sum(jnp.square(noise_full.astype(jnp.float32)), axis=1) / LATENT
     noise_rows = noise.shape[0]
     data_rows = data.shape[0]
     data_full = lax.all_gather(data, "row", axis=1, tiled=True)
     data_norm = jnp.sum(jnp.square(data_full.astype(jnp.float32)), axis=1) / LATENT
-    cross = lax.dot_general(noise_full, data_full, contract, preferred_element_type=jnp.float32)
+    cross = lax.dot_general(noise_full, data_full, CONTRACT, preferred_element_type=jnp.float32)
     cost_tile = noise_norm[:, None] + data_norm[None, :] - 2.0 / LATENT * cross
     log_noise = math.log(noise_rows * lax.axis_size("row"))
     log_data = math.log(data_rows * lax.axis_size("col"))
@@ -55,6 +62,382 @@
     return (targets, noise_pot, data_pot)
 
 
+def swap_row(array, step):
+    count = lax.axis_size("row")
+    return lax.ppermute(array, "row", [(i, i ^ step) for i in range(count)])
+
+
+def swap_col(array, step):
+    count = lax.axis_size("col")
+    return lax.ppermute(array, "col", [(i, i ^ step) for i in range(count)])
+
+
+def plane_gather(pieces):
+    half = len(pieces) // 2
+    along_x = [swap_row(piece, 2) for piece in pieces]
+    along_y = [swap_row(piece, 4) for piece in pieces]
+    across = [swap_row(piece, 4) for piece in along_x[:half]]
+    across += [swap_row(piece, 2) for piece in along_y[half:]]
+    result = []
+    for group in (pieces, along_x, along_y, across):
+        result += [group, [swap_row(piece, 1) for piece in group]]
+    return result
+
+
+def place():
+    return lax.axis_index("row"), lax.axis_index("col")
+
+
+ANY = pl.BlockSpec(memory_space=pl.ANY)
+VMEM = pl.BlockSpec(memory_space=pltpu.VMEM)
+
+
+def run_copies(copies):
+    for copy in copies:
+        copy.start()
+    for copy in copies:
+        copy.wait()
+
+
+def deal_kernel(data_ref, *refs):
+    *outs, sems = refs
+    row, _ = place()
+    count = outs[0].shape[0]
+    copies = []
+    for k, out in enumerate(outs, 1):
+        rows = pl.ds(pl.multiple_of((row ^ k) * count, count), count)
+        copies.append(pltpu.make_async_copy(data_ref.at[rows], out, sems.at[k]))
+    run_copies(copies)
+
+
+def deal(data, n_row):
+    share = data.shape[0] // n_row
+    piece = jax.ShapeDtypeStruct((share, data.shape[1]), data.dtype)
+    return pl.pallas_call(
+        deal_kernel,
+        in_specs=[ANY],
+        out_specs=[ANY] * (n_row - 1),
+        out_shape=[piece] * (n_row - 1),
+        scratch_shapes=[pltpu.SemaphoreType.DMA((n_row,))],
+    )(data)
+
+
+def regroup_kernel(n_row, n_col, *refs):
+    data_ref, noise_ref = refs[:2]
+    received = refs[2 : 1 + n_row]
+    outs = refs[1 + n_row : 1 + n_row + n_col]
+    low_ref, high_ref, sems = refs[1 + n_row + n_col :]
+    row, col = place()
+    share, wide = received[0].shape
+    per_plane = n_row // n_col
+    own = pl.ds(pl.multiple_of(row * share, share), share)
+    half = low_ref.shape[0]
+    halves = [
+        pltpu.make_async_copy(noise_ref.at[pl.ds(0, half)], low_ref, sems.at[n_row]),
+        pltpu.make_async_copy(noise_ref.at[pl.ds(half, half)], high_ref, sems.at[n_row + 1]),
+    ]
+    for k in range(n_row):
+        source = data_ref.at[own] if k == 0 else received[k - 1]
+        origin = row ^ k
+        lanes = pl.ds(pl.multiple_of(lax.rem(origin, per_plane) * wide, wide), wide)
+        step = col ^ (origin // per_plane)
+        for d in range(n_col):
+
+            @pl.when(step == d)
+            def _():
+                pltpu.make_async_copy(source, outs[d].at[:, lanes], sems.at[k]).start()
+
+    for copy in halves:
+        copy.start()
+    for k in range(n_row):
+        source = data_ref.at[own] if k == 0 else received[k - 1]
+        pltpu.make_async_copy(source, outs[0].at[:, pl.ds(0, wide)], sems.at[k]).wait()
+    for copy in halves:
+        copy.wait()
+
+
+def regroup(data, noise, received, n_col):
+    n_row = len(received) + 1
+    share, wide = received[0].shape
+    piece = jax.ShapeDtypeStruct((share, wide * (n_row // n_col)), data.dtype)
+    half = jax.ShapeDtypeStruct((noise.shape[0] // 2, noise.shape[1]), noise.dtype)
+    return pl.pallas_call(
+        functools.partial(regroup_kernel, n_row, n_col),
+        in_specs=[ANY] * (n_row + 1),
+        out_specs=[ANY] * (n_col + 2),
+        out_shape=[piece] * n_col + [half] * 2,
+        scratch_shapes=[pltpu.SemaphoreType.DMA((n_row + 2,))],
+    )(data, noise, *received)
+
+
+def stack_kernel(*refs):
+    *pieces, low_ref, high_ref, sems = refs
+    _, col = place()
+    half = low_ref.shape[0]
+    for d, piece in enumerate(pieces):
+        origin = col ^ d
+        slot = lax.rem(origin, half)
+
+        @pl.when(origin < half)
+        def _():
+            pltpu.make_async_copy(piece, low_ref.at[slot], sems.at[d]).start()
+
+        @pl.when(origin >= half)
+        def _():
+            pltpu.make_async_copy(piece, high_ref.at[slot], sems.at[d]).start()
+
+    for d, piece in enumerate(pieces):
+        pltpu.make_async_copy(piece, low_ref.at[0], sems.at[d]).wait()
+
+
+def stack(pieces):
+    half = jax.ShapeDtypeStruct((len(pieces) // 2,) + pieces[0].shape, pieces[0].dtype)
+    return pl.pallas_call(
+        stack_kernel,
+        in_specs=[ANY] * len(pieces),
+        out_specs=[ANY] * 2,
+        out_shape=[half] * 2,
+        scratch_shapes=[pltpu.SemaphoreType.DMA((len(pieces),))],
+    )(*pieces)
+
+
+def cost_kernel(n_row, n_col, *refs):
+    noise_refs = refs[: 2 * n_row]
+    low_ref, high_ref = refs[2 * n_row : 2 * n_row + 2]
+    parts = refs[2 * n_row + 2 : 2 * n_row + 2 + n_col]
+    noise_all, data_all, noise_sems, data_sems = refs[2 * n_row + 2 + n_col :]
+    row, col = place()
+    per_part = n_row // n_col
+    half = n_col // 2
+    data_copies = [
+        pltpu.make_async_copy(low_ref, data_all.at[pl.ds(0, half)], data_sems.at[0]),
+        pltpu.make_async_copy(high_ref, data_all.at[pl.ds(half, half)], data_sems.at[1]),
+    ]
+    for copy in data_copies:
+        copy.start()
+
+    def noise_copy(k, h, origin):
+        return pltpu.make_async_copy(
+            noise_refs[2 * k + h], noise_all.at[origin, h], noise_sems.at[origin, h]
+        )
+
+    for k in range(n_row):
+        for h in range(2):
+            noise_copy(k, h, row ^ k).start()
+    for copy in data_copies:
+        copy.wait()
+    depth = data_all.shape[-1]
+    columns = data_all.shape[0] * data_all.shape[1]
+    rows_data = data_all[...].reshape(columns, depth)
+    values = rows_data.astype(jnp.float32)
+    norm = jnp.sum(values * values, axis=1, keepdims=True)
+    norm = jnp.broadcast_to(norm, (columns, columns)).T[0:1, :]
+    for d in range(n_col):
+        first = (col ^ d) * per_part
+        for i in range(per_part):
+            for h in range(2):
+                noise_copy(0, h, first + i).wait()
+        rows = noise_all[pl.ds(first, per_part)].reshape(-1, depth)
+        cross = lax.dot_general(rows, rows_data, CONTRACT, preferred_element_type=jnp.float32)
+        values = rows.astype(jnp.float32)
+        part = jnp.sum(values * values, axis=1, keepdims=True)
+        parts[d][...] = (part + norm - 2.0 * cross) * (TO_LOG2 / LATENT)
+
+
+def partial_cost(noise_pieces, data_halves, n_col):
+    n_row = len(noise_pieces)
+    half, depth = noise_pieces[0][0].shape
+    columns = 2 * data_halves[0].shape[0] * data_halves[0].shape[1]
+    rows = 2 * half * n_row
+    return pl.pallas_call(
+        functools.partial(cost_kernel, n_row, n_col),
+        in_specs=[ANY] * (2 * n_row + 2),
+        out_specs=[VMEM] * n_col,
+        out_shape=[jax.ShapeDtypeStruct((rows // n_col, columns), jnp.float32)] * n_col,
+        scratch_shapes=[
+            pltpu.VMEM((n_row, 2, half, depth), jnp.bfloat16),
+            pltpu.VMEM((n_col,) + data_halves[0].shape[1:], jnp.bfloat16),
+            pltpu.SemaphoreType.DMA((n_row, 2)),
+            pltpu.SemaphoreType.DMA((2,)),
+        ],
+        compiler_params=pltpu.CompilerParams(vmem_limit_bytes=40 * 2**20),
+        cost_estimate=pl.CostEstimate(
+            flops=2 * rows * columns * depth, bytes_accessed=2 * rows * depth, transcendentals=0
+        ),
+    )(*[piece for pair in noise_pieces for piece in pair], *data_halves)
+
+
+def sinkhorn_kernel(n_row, n_col, *refs):
+    cost_refs = refs[: n_row * n_col]
+    data_refs = refs[n_row * n_col : n_row * (n_col + 2)]
+    refs = refs[n_row * (n_col + 2) :]
+    target_refs, refs = refs[:n_col], refs[n_col:]
+    noise_pot_ref, data_pot_ref, cost, data_all, f_ref, weights, product, cost_sems, data_sems = refs
+    row, col = place()
+    wide, tall, height, width = cost.shape
+    log_noise = math.log2(tall * height)
+    log_data = math.log2(wide * width)
+    blocks = range(wide)
+    half = n_col // 2
+    cost_copies, data_copies = [], []
+    for k in range(n_row):
+        for d in range(n_col):
+            slot = cost.at[row ^ k, col ^ d]
+            cost_copies.append(
+                pltpu.make_async_copy(cost_refs[k * n_col + d], slot, cost_sems.at[k, d])
+            )
+        for h in range(2):
+            slot = data_all.at[row ^ k, pl.ds(h * half, half)]
+            data_copies.append(pltpu.make_async_copy(data_refs[2 * k + h], slot, data_sems.at[k, h]))
+    for copy in cost_copies + data_copies:
+        copy.start()
+    for copy in cost_copies:
+        copy.wait()
+
+    def row_update(tiles, g):
+        peak = functools.reduce(jnp.maximum, [g[b] - tiles(b) for b in blocks])
+        peak = jnp.max(peak, axis=1, keepdims=True)
+        total = functools.reduce(jnp.add, [jnp.exp2(g[b] - tiles(b) - peak) for b in blocks])
+        total = jnp.sum(total, axis=1, keepdims=True)
+        return -(log_noise + peak + jnp.log2(total))
+
+    def both_updates(chunk, carry, g):
+        high, summed = carry
+        f = row_update(lambda b: cost[b, chunk], g)
+        new_high, new_summed = [], []
+        for b in blocks:
+            scores = f - cost[b, chunk]
+            peak = jnp.max(scores, axis=0, keepdims=True)
+            total = jnp.sum(jnp.exp2(scores - peak), axis=0, keepdims=True)
+            top = jnp.maximum(high[b], peak)
+            new_high.append(top)
+            new_summed.append(summed[b] * jnp.exp2(high[b] - top) + total * jnp.exp2(peak - top))
+        return tuple(new_high), tuple(new_summed)
+
+    def iteration(_, g):
+        first = (
+            tuple(jnp.full((1, width), -jnp.inf, jnp.float32) for b in blocks),
+            tuple(jnp.zeros((1, width), jnp.float32) for b in blocks),
+        )
+        high, summed = lax.fori_loop(0, tall, lambda i, carry: both_updates(i, carry, g), first)
+        return tuple(-(log_data + high[b] + jnp.log2(summed[b])) for b in blocks)
+
+    g = tuple(jnp.zeros((1, width), jnp.float32) for b in blocks)
+    g = lax.fori_loop(0, ITERS, iteration, g)
+    for b in blocks:
+        data_pot_ref[b : b + 1, :] = g[b] * (1.0 / TO_LOG2)
+
+    own = noise_pot_ref.shape[1]
+    per_chunk = height // own
+    chunk = row // per_chunk
+    rows = pl.ds(pl.multiple_of(lax.rem(row, per_chunk) * own, own), own)
+    f = row_update(lambda b: cost[b, chunk, rows, :], g)
+    for b in blocks:
+        scores = (f + g[b] - cost[b, chunk, rows, :]) + log_noise
+        weights[:, b * width : (b + 1) * width] = jnp.exp2(scores).astype(jnp.bfloat16)
+    f_ref[...] = jnp.broadcast_to(f, f_ref.shape)
+    noise_pot_ref[...] = f_ref[...].T[0:1, :] * (1.0 / TO_LOG2)
+
+    for copy in data_copies:
+        copy.wait()
+    depth = data_all.shape[-1]
+    piece = min(depth, 512)
+    share = own // n_col
+
+    def multiply(i, _):
+        lanes = pl.ds(pl.multiple_of(i * piece, piece), piece)
+        latents = data_all[:, :, :, lanes].reshape(wide * width, piece)
+        product[...] = jnp.dot(weights[...], latents, preferred_element_type=jnp.float32)
+        for d in range(n_col):
+            rows = pl.ds(pl.multiple_of((col ^ d) * share, share), share)
+            target_refs[d][:, lanes] = product[rows, :].astype(jnp.bfloat16)
+        return 0
+
+    lax.fori_loop(0, depth // piece, multiply, 0)
+
+
+def sinkhorn(tiles, latents, own):
+    n_row, n_col = len(tiles), len(tiles[0])
+    height, width = tiles[0][0].shape
+    half, share, depth = latents[0][0].shape
+    size = n_row * n_col * height * width
+    return pl.pallas_call(
+        functools.partial(sinkhorn_kernel, n_row, n_col),
+        in_specs=[ANY] * (n_row * (n_col + 2)),
+        out_specs=[VMEM] * (n_col + 2),
+        out_shape=[jax.ShapeDtypeStruct((own // n_col, depth), jnp.bfloat16)] * n_col
+        + [
+            jax.ShapeDtypeStruct((1, own), jnp.float32),
+            jax.ShapeDtypeStruct((n_row, width), jnp.float32),
+        ],
+        scratch_shapes=[
+            pltpu.VMEM((n_row, n_col, height, width), jnp.float32),
+            pltpu.VMEM((n_row, n_col, share, depth), jnp.bfloat16),
+            pltpu.VMEM((own, own), jnp.float32),
+            pltpu.VMEM((own, n_row * width), jnp.bfloat16),
+            pltpu.VMEM((own, min(depth, 512)), jnp.float32),
+            pltpu.SemaphoreType.DMA((n_row, n_col)),
+            pltpu.SemaphoreType.DMA((n_row, 2)),
+        ],
+        compiler_params=pltpu.CompilerParams(vmem_limit_bytes=48 * 2**20),
+        cost_estimate=pl.CostEstimate(
+            flops=60 * size, bytes_accessed=8 * size, transcendentals=8 * size
+        ),
+    )(*[tile for group in tiles for tile in group], *[piece for group in latents for piece in group])
+
+
+def join_kernel(*refs):
+    *pieces, out_ref, sems = refs
+    _, col = place()
+    depth = pieces[0].shape[1]
+    copies = []
+    for d, piece in enumerate(pieces):
+        lanes = pl.ds(pl.multiple_of((col ^ d) * depth, depth), depth)
+        copies.append(pltpu.make_async_copy(piece, out_ref.at[:, lanes], sems.at[d]))
+    run_copies(copies)
+
+
+def join(pieces):
+    share, depth = pieces[0].shape
+    return pl.pallas_call(
+        join_kernel,
+        in_specs=[ANY] * len(pieces),
+        out_specs=ANY,
+        out_shape=jax.ShapeDtypeStruct((share, depth * len(pieces)), pieces[0].dtype),
+        scratch_shapes=[pltpu.SemaphoreType.DMA((len(pieces),))],
+    )(*pieces)
+
+
+def col_exchange(pieces):
+    return [pieces[0]] + [swap_col(piece, d) for d, piece in enumerate(pieces) if d]
+
+
+def per_device_local(noise, data):
+    n_row, n_col = lax.axis_size("row"), lax.axis_size("col")
+    own, own_data = noise.shape[0], data.shape[0]
+    received = [swap_row(piece, k) for k, piece in enumerate(deal(data, n_row), 1)]
+    *spread, low, high = regroup(data, noise, received, n_col)
+    mine = stack(col_exchange(spread))
+    noise_plane = plane_gather([low, high])
+    parts = partial_cost(noise_plane, mine, n_col)
+    data_plane = plane_gather(mine)
+    tile = functools.reduce(jnp.add, col_exchange(parts))
+    tiles = plane_gather([tile] + [swap_col(tile, d) for d in range(1, n_col)])
+    *products, noise_pot, pots = sinkhorn(tiles, data_plane, own)
+    share = own_data // n_row
+    data_pot = lax.dynamic_slice_in_dim(pots, lax.axis_index("col") * share, share, 1)
+    targets = join(col_exchange(products))
+    return (targets, noise_pot.reshape((own,)), data_pot.reshape((own_data,)))
+
+
+def per_device(noise, data):
+    n_row, n_col = lax.axis_size("row"), lax.axis_size("col")
+    whole = 4 * noise.shape[0] * n_row * data.shape[0] * n_col
+    if whole <= LOCAL_COST_BYTES and n_row == 8 and n_col == 4:
+        return per_device_local(noise, data)
+    return per_device_tiled(noise, data)
+
+
 def solution(mesh):
     placed = (P("row", "col"), P("col", "row"))
     return jax.shard_map(

time: 397 us -> 365 us (0.919)
  Pallas kernels: 0 us -> 182 us
  blocking collectives: 147 us -> 0 us
  waiting for transfers between devices: 213 us -> 114 us
  starting transfers between devices: 0.11 us -> 59 us
  between operations: 13.8 us -> 1.16 us
  matrix products: 11.9 us -> 0 us
  other arithmetic: 10.2 us -> 0.03 us
  local copies, waits for them, and re-layouts: 0.48 us -> 6.37 us
    pallas_call x0 -> x6, Pallas kernels: none -> 182 us  [the longest x1 64.7 us: regroup(): pl.pallas_call(functools.partial(regroup_kernel, n_row, n_col), in_specs=...]
    all_gather x2 -> x0, waiting for transfers between devices: 136 us -> none  [the longest x1 84.4 us: per_device(): noise_full = lax.all_gather(noise, 'col', axis=1, tiled=True)]
    ppermute x0 -> x75, waiting for transfers between devices: none -> 114 us  [the longest x63 62.7 us: swap_row(): return lax.ppermute(array, 'row', [(i, i ^ step) for i in range(count)])]
    pmax x7 -> x0, blocking collectives: 78.1 us -> none  [the longest x4 42.7 us: noise_update(): highest = lax.pmax(local_peak, 'col')]
    reduce_scatter x1 -> x0, waiting for transfers between devices: 75.2 us -> none  [per_device(): lax.psum_scatter(jnp.dot(weights, data_full, preferred_element_type=jnp.f...]
    psum x7 -> x0, blocking collectives: 69.1 us -> none  [the longest x3 35.4 us: data_update(): lax.psum(jnp.sum(jnp.exp(scores - highest[None, :]), axis=0), 'row')]
    ppermute x0 -> x75, starting transfers between devices: none -> 59 us  [the longest x63 35.7 us: swap_row(): return lax.ppermute(array, 'row', [(i, i ^ step) for i in range(count)])]
    dot_general x2 -> x0, matrix products: 11.9 us -> none  [the longest x1 6.68 us: per_device(): jnp.dot(weights, data_full, preferred_element_type=jnp.float32)]
  transfers between devices with their start and end apart: 3 -> 75, of which waited for: 3 -> 32; matrix products, arithmetic and copies ran while one was open for 1% -> 0% of each run, Pallas kernels for 0% -> 11%
where the time goes in v1:
time: 365 us; the launch traced here: 362 us
  Pallas kernels  182 us (50%)
  waiting for transfers between devices  114 us (31%)
  starting transfers between devices  59 us (16%)
  local copies, waits for them, and re-layouts  6.37 us (2%)
    pallas_call x1, Pallas kernels, regroup(): pl.pallas_call(functools.partial(regroup_kernel, n_row, n_col), in_specs=...  64.7 us
    ppermute x63, waiting for transfers between devices, swap_row(): return lax.ppermute(array, 'row', [(i, i ^ step) for i in range(count)])  62.7 us
    ppermute x12, waiting for transfers between devices, swap_col(): return lax.ppermute(array, 'col', [(i, i ^ step) for i in range(count)])  51.1 us
    ppermute x63, starting transfers between devices, swap_row(): return lax.ppermute(array, 'row', [(i, i ^ step) for i in range(count)])  35.7 us
    pallas_call x1, Pallas kernels, stack(): pl.pallas_call(stack_kernel, in_specs=[ANY] * len(pieces), out_specs=[ANY...  32.9 us
    pallas_call x1, Pallas kernels, join(): pl.pallas_call(join_kernel, in_specs=[ANY] * len(pieces), out_specs=ANY,...  32.9 us
    pallas_call x1, Pallas kernels, deal(): pl.pallas_call(deal_kernel, in_specs=[ANY], out_specs=[ANY] * (n_row - 1)...  29 us
    ppermute x12, starting transfers between devices, swap_col(): return lax.ppermute(array, 'col', [(i, i ^ step) for i in range(count)])  23.3 us
  transfers between devices with their start and end apart: 75, of which 32 were waited for; matrix products, arithmetic and copies ran while one was open for 0% of the time, Pallas kernels for 11%

profile of v1, /device:TPU:0, one launch (start us, length us, event | category | flops | bytes accessed | tf_op | source)
XLA Modules:
  0.0 362.3 jit_solution(1354633705520397409)
XLA Ops:
  0.6 29.0 %shard_map.49 = (bf16[32,2048]{1,0:T(8,128)(2,1)}, bf16[32,2048]{1,0:T(8,128)(2,1)}, bf16[32,2048]{1,0:T(8,128)(2,1)}, bf16[32,2048]{1,0:T(8,128)(2,1)}, bf16[32...) custom-call(bf16[256,2048]{1,0:T(8,128)(2,1)} %refs_0_.1), custom_call_target="tpu_custom_call" | custom-call | tf_op jit(solution)/shard_map/pallas_call | solution.py:116
  30.1 2.6 collective-permute-start.1
  34.5 2.6 collective-permute-start.5
  39.6 6.9 %collective-permute-done.4.refs_6_ = bf16[32,2048]{1,0:T(8,128)(2,1)S(1)} collective-permute-done((bf16[32,2048]{1,0:T(8,128)(2,1)}, bf16[32,2048]{1,0:T(8,128)(2,1)S(1)}, u32[]{:S(2)}, u32[]{:S(2)}) %collective-permute-start.4) | collective-permute-done | bytes 131104 | tf_op jit(solution)/shard_map/ppermute | solution.py:67
  47.9 64.7 %shard_map.50 = (bf16[32,4096]{1,0:T(8,128)(2,1)}, bf16[32,4096]{1,0:T(8,128)(2,1)}, bf16[32,4096]{1,0:T(8,128)(2,1)}, bf16[32,4096]{1,0:T(8,128)(2,1)}, bf16[64...) custom-call(bf16[256,2048]{1,0:T(8,128)(2,1)} %refs_0_.1, bf16[128,4096]{1,0:T(8,128)(2,1)} %refs_1_.1, ...), custom_call_target="tpu_custom_call" | custom-call | tf_op jit(solution)/shard_map/pallas_call | solution.py:164
  118.1 2.6 collective-permute-start.22
  120.7 3.6 %collective-permute-done.21.refs_1_ = bf16[32,4096]{1,0:T(8,128)(2,1)S(1)} collective-permute-done((bf16[32,4096]{1,0:T(8,128)(2,1)}, bf16[32,4096]{1,0:T(8,128)(2,1)S(1)}, u32[]{:S(2)}, u32[]{:S(2)}) %collective-permute-start.21) | collective-permute-done | bytes 262176 | tf_op jit(solution)/shard_map/ppermute | solution.py:72
  124.3 2.8 collective-permute-start.23
  127.1 12.7 %collective-permute-done.22.refs_2_ = bf16[32,4096]{1,0:T(8,128)(2,1)} collective-permute-done((bf16[32,4096]{1,0:T(8,128)(2,1)}, bf16[32,4096]{1,0:T(8,128)(2,1)}, u32[]{:S(2)}, u32[]{:S(2)}) %collective-permute-start.22) | collective-permute-done | bytes 262176 | tf_op jit(solution)/shard_map/ppermute | solution.py:72
  141.0 32.9 %shard_map.51 = (bf16[2,32,4096]{2,1,0:T(8,128)(2,1)}, bf16[2,32,4096]{2,1,0:T(8,128)(2,1)}) custom-call(bf16[32,4096]{1,0:T(8,128)(2,1)} %get-tuple-element.37.refs_0_, bf16[32,4096]{1,0:T(8,128)(2,1)} %copy-done.6, bf16[32,4096]{1,0:T(8,128)(2,1)} %collective-permute-done.22.refs_2_, bf16[32,4096]{1,0:T(8,128)(2,1)} %copy-done.7), custom_call_target="tpu_custom_call" | custom-call | tf_op jit(solution)/shard_map/pallas_call | solution.py:195
  179.7 9.3 %collective-permute-done.60.refs_36_ = bf16[2,32,4096]{2,1,0:T(8,128)(2,1)S(1)} collective-permute-done((bf16[2,32,4096]{2,1,0:T(8,128)(2,1)}, bf16[2,32,4096]{2,1,0:T(8,128)(2,1)S(1)}, u32[]{:S(2)}, u32[]{:S(2)}) %collective-permute-start.60) | collective-permute-done | bytes 524320 | tf_op jit(solution)/shard_map/ppermute | solution.py:67
  190.5 9.7 %collective-permute-done.61.refs_37_ = bf16[2,32,4096]{2,1,0:T(8,128)(2,1)S(1)} collective-permute-done((bf16[2,32,4096]{2,1,0:T(8,128)(2,1)}, bf16[2,32,4096]{2,1,0:T(8,128)(2,1)S(1)}, u32[]{:S(2)}, u32[]{:S(2)}) %collective-permute-start.61) | collective-permute-done | bytes 524320 | tf_op jit(solution)/shard_map/ppermute | solution.py:67
  201.8 10.5 %collective-permute-done.17.refs_12_ = bf16[64,4096]{1,0:T(8,128)(2,1)S(1)} collective-permute-done((bf16[64,4096]{1,0:T(8,128)(2,1)S(1)}, bf16[64,4096]{1,0:T(8,128)(2,1)S(1)}, u32[]{:S(2)}, u32[]{:S(2)}) %collective-permute-start.17) | collective-permute-done | bytes 524320 | tf_op jit(solution)/shard_map/ppermute | solution.py:67
  219.4 6.3 %shard_map.52 = (f32[256,128]{1,0:T(8,128)S(1)}, f32[256,128]{1,0:T(8,128)S(1)}, f32[256,128]{1,0:T(8,128)S(1)}, f32[256,128]{1,0:T(8,128)S(1)}) custom-call(bf16[64,4096]{1,0:T(8,128)(2,1)S(1)} %copy-done.3, bf16[64,4096]{1,0:T(8,128)(2,1)S(1)} %copy-done.4, bf16[64,4096]{1,0:T(8,128)(2,1)} %collective-permute-done.7.refs_2_, ...), custom_call_target="tpu_custom_call" | custom-call | flops 1073741824 | bytes 8388608 | tf_op jit(solution)/shard_map/pallas_call | solution.py:252
  229.6 3.9 %collective-permute-start.24 = (f32[256,128]{1,0:T(8,128)S(1)}, f32[256,128]{1,0:T(8,128)S(1)}, u32[]{:S(2)}, u32[]{:S(2)}) collective-permute-start(f32[256,128]{1,0:T(8,128)S(1)} %get-tuple-element.44), channel_id=1, source_target_pairs={{0,1},{1,0},{2,3},{3,2},{4,5},{5,4},{6,7},{7,6},{8,9},{9,8},{10,11... | collective-permute-start | bytes 393224 | tf_op jit(solution)/shard_map/ppermute | solution.py:72
  234.6 3.2 collective-permute-done.24
  237.7 2.2 collective-permute-start.26
  239.9 5.6 %collective-permute-done.25 = f32[256,128]{1,0:T(8,128)S(1)} collective-permute-done((f32[256,128]{1,0:T(8,128)S(1)}, f32[256,128]{1,0:T(8,128)S(1)}, u32[]{:S(2)}, u32[]{:S(2)}) %collective-permute-start.25) | collective-permute-done | bytes 131104 | tf_op jit(solution)/shard_map/ppermute | solution.py:72
  250.6 3.8 %collective-permute-done.27.refs_1_ = f32[256,128]{1,0:T(8,128)S(1)} collective-permute-done((f32[256,128]{1,0:T(8,128)S(1)}, f32[256,128]{1,0:T(8,128)S(1)}, u32[]{:S(2)}, u32[]{:S(2)}) %collective-permute-start.27) | collective-permute-done | bytes 131104 | tf_op jit(solution)/shard_map/ppermute | solution.py:72
  254.9 5.9 %collective-permute-done.28.refs_2_ = f32[256,128]{1,0:T(8,128)S(1)} collective-permute-done((f32[256,128]{1,0:T(8,128)S(1)}, f32[256,128]{1,0:T(8,128)S(1)}, u32[]{:S(2)}, u32[]{:S(2)}) %collective-permute-start.28) | collective-permute-done | bytes 131104 | tf_op jit(solution)/shard_map/ppermute | solution.py:72
  262.0 5.0 %collective-permute-done.42.refs_16_ = f32[256,128]{1,0:T(8,128)S(1)} collective-permute-done((f32[256,128]{1,0:T(8,128)S(1)}, f32[256,128]{1,0:T(8,128)S(1)}, u32[]{:S(2)}, u32[]{:S(2)}) %collective-permute-start.42) | collective-permute-done | bytes 131104 | tf_op jit(solution)/shard_map/ppermute | solution.py:67
  267.0 2.0 collective-permute-start.45
  269.0 2.0 collective-permute-start.37
  271.1 2.2 collective-permute-done.44.refs_18_
  281.5 2.7 collective-permute-done.51.refs_25_
  285.3 2.1 collective-permute-done.53.refs_27_
  290.2 16.1 %shard_map.53 = (bf16[32,4096]{1,0:T(8,128)(2,1)S(1)}, bf16[32,4096]{1,0:T(8,128)(2,1)S(1)}, bf16[32,4096]{1,0:T(8,128)(2,1)S(1)}, bf16[32,4096]{1,0:T(8,128)(2,...) custom-call(f32[256,128]{1,0:T(8,128)S(1)} %add_add_fusion.refs_0_, f32[256,128]{1,0:T(8,128)S(1)} %collective-permute-done.27.refs_1_, ...), custom_call_target="tpu_custom_call" | custom-call | flops 62914560 | bytes 8388608 | tf_op jit(solution)/shard_map/pallas_call | solution.py:364
  307.1 2.3 collective-permute-start.73
  309.4 2.0 collective-permute-start.74
  312.2 8.2 %collective-permute-done.72.refs_1_ = bf16[32,4096]{1,0:T(8,128)(2,1)S(1)} collective-permute-done((bf16[32,4096]{1,0:T(8,128)(2,1)S(1)}, bf16[32,4096]{1,0:T(8,128)(2,1)S(1)}, u32[]{:S(2)}, u32[]{:S(2)}) %collective-permute-start.72) | collective-permute-done | bytes 262176 | tf_op jit(solution)/shard_map/ppermute | solution.py:72
  320.3 8.1 %collective-permute-done.73.refs_2_ = bf16[32,4096]{1,0:T(8,128)(2,1)S(1)} collective-permute-done((bf16[32,4096]{1,0:T(8,128)(2,1)S(1)}, bf16[32,4096]{1,0:T(8,128)(2,1)S(1)}, u32[]{:S(2)}, u32[]{:S(2)}) %collective-permute-start.73) | collective-permute-done | bytes 262176 | tf_op jit(solution)/shard_map/ppermute | solution.py:72
  329.2 32.9 %shard_map.54 = bf16[32,16384]{1,0:T(8,128)(2,1)} custom-call(bf16[32,4096]{1,0:T(8,128)(2,1)} %copy-done.5, bf16[32,4096]{1,0:T(8,128)(2,1)} %copy-done.8, bf16[32,4096]{1,0:T(8,128)(2,1)} %copy-done.9, bf16[32,4096]{1,0:T(8,128)(2,1)} %copy-done.10), custom_call_target="tpu_custom_call" | custom-call | tf_op jit(solution)/shard_map/pallas_call | solution.py:402
  (191 shorter events, 54.7 us)
Async XLA Ops:
  34.5 12.0 %collective-permute-start.4 = (bf16[32,2048]{1,0:T(8,128)(2,1)}, bf16[32,2048]{1,0:T(8,128)(2,1)S(1)}, u32[]{:S(2)}, u32[]{:S(2)}) collective-permute-start(bf16[32,2048]{1,0:T(8,128)(2,1)} %get-tuple-element.32), channel_id=1, source_target_pairs={{0,20},{4,16},{8,28},{12,24},{16,4},{20,0},{24,12},{28,8},{1,21},{... | collective-permute-start | bytes 393224 | tf_op jit(solution)/shard_map/ppermute | solution.py:67
  114.5 59.4 %collective-permute-start.9 = (bf16[64,4096]{1,0:T(8,128)(2,1)}, bf16[64,4096]{1,0:T(8,128)(2,1)S(1)}, u32[]{:S(2)}, u32[]{:S(2)}) collective-permute-start(bf16[64,4096]{1,0:T(8,128)(2,1)} %get-tuple-element.35.refs_0_), channel_id=1, source_target_pairs={{0,8},{4,12},{8,0},{12,4},{16,24},{20,28},{24,16},{28,20},{1,9},{5... | collective-permute-start | bytes 1572872 | tf_op jit(solution)/shard_map/ppermute | solution.py:67
  116.0 58.0 %collective-permute-start.14 = (bf16[64,4096]{1,0:T(8,128)(2,1)}, bf16[64,4096]{1,0:T(8,128)(2,1)S(1)}, u32[]{:S(2)}, u32[]{:S(2)}) collective-permute-start(bf16[64,4096]{1,0:T(8,128)(2,1)} %get-tuple-element.36.refs_1_), channel_id=1, source_target_pairs={{0,16},{4,20},{8,24},{12,28},{16,0},{20,4},{24,8},{28,12},{1,17},{... | collective-permute-start | bytes 1572872 | tf_op jit(solution)/shard_map/ppermute | solution.py:67
  117.5 58.0 %collective-permute-start.10 = (bf16[64,4096]{1,0:T(8,128)(2,1)}, bf16[64,4096]{1,0:T(8,128)(2,1)S(1)}, u32[]{:S(2)}, u32[]{:S(2)}) collective-permute-start(bf16[64,4096]{1,0:T(8,128)(2,1)} %get-tuple-element.36.refs_1_), channel_id=1, source_target_pairs={{0,8},{4,12},{8,0},{12,4},{16,24},{20,28},{24,16},{28,20},{1,9},{5... | collective-permute-start | bytes 1572872 | tf_op jit(solution)/shard_map/ppermute | solution.py:67
  118.1 21.7 %collective-permute-start.22 = (bf16[32,4096]{1,0:T(8,128)(2,1)}, bf16[32,4096]{1,0:T(8,128)(2,1)}, u32[]{:S(2)}, u32[]{:S(2)}) collective-permute-start(bf16[32,4096]{1,0:T(8,128)(2,1)} %get-tuple-element.39), channel_id=1, source_target_pairs={{0,2},{1,3},{2,0},{3,1},{4,6},{5,7},{6,4},{7,5},{8,10},{9,11},{10,... | collective-permute-start | bytes 786440 | tf_op jit(solution)/shard_map/ppermute | solution.py:72
  124.3 16.0 %collective-permute-start.23 = (bf16[32,4096]{1,0:T(8,128)(2,1)}, bf16[32,4096]{1,0:T(8,128)(2,1)S(1)}, u32[]{:S(2)}, u32[]{:S(2)}) collective-permute-start(bf16[32,4096]{1,0:T(8,128)(2,1)} %get-tuple-element.40), channel_id=1, source_target_pairs={{0,3},{1,2},{2,1},{3,0},{4,7},{5,6},{6,5},{7,4},{8,11},{9,10},{10,... | collective-permute-start | bytes 786440 | tf_op jit(solution)/shard_map/ppermute | solution.py:72
  139.8 37.3 %collective-permute-start.13 = (bf16[64,4096]{1,0:T(8,128)(2,1)}, bf16[64,4096]{1,0:T(8,128)(2,1)S(1)}, u32[]{:S(2)}, u32[]{:S(2)}) collective-permute-start(bf16[64,4096]{1,0:T(8,128)(2,1)} %get-tuple-element.35.refs_0_), channel_id=1, source_target_pairs={{0,16},{4,20},{8,24},{12,28},{16,0},{20,4},{24,8},{28,12},{1,17},{... | collective-permute-start | bytes 1572872 | tf_op jit(solution)/shard_map/ppermute | solution.py:67
  140.3 37.3 %collective-permute-start.7 = (bf16[64,4096]{1,0:T(8,128)(2,1)}, bf16[64,4096]{1,0:T(8,128)(2,1)}, u32[]{:S(2)}, u32[]{:S(2)}) collective-permute-start(bf16[64,4096]{1,0:T(8,128)(2,1)} %get-tuple-element.35.refs_0_), channel_id=1, source_target_pairs={{0,4},{4,0},{8,12},{12,8},{16,20},{20,16},{24,28},{28,24},{1,5},{5... | collective-permute-start | bytes 1572872 | tf_op jit(solution)/shard_map/ppermute | solution.py:67
  174.0 15.0 %collective-permute-start.60 = (bf16[2,32,4096]{2,1,0:T(8,128)(2,1)}, bf16[2,32,4096]{2,1,0:T(8,128)(2,1)S(1)}, u32[]{:S(2)}, u32[]{:S(2)}) collective-permute-start(bf16[2,32,4096]{2,1,0:T(8,128)(2,1)} %get-tuple-element.41.refs_16_.refs_32_), channel_id=1, source_target_pairs={{0,8},{4,12},{8,0},{12,4},{16,24},{20,28},{24,16},{28,20},{1,9},{5... | collective-permute-start | bytes 1572872 | tf_op jit(solution)/shard_map/ppermute | solution.py:67
  175.6 15.0 %collective-permute-start.65 = (bf16[2,32,4096]{2,1,0:T(8,128)(2,1)}, bf16[2,32,4096]{2,1,0:T(8,128)(2,1)S(1)}, u32[]{:S(2)}, u32[]{:S(2)}) collective-permute-start(bf16[2,32,4096]{2,1,0:T(8,128)(2,1)} %get-tuple-element.42.refs_17_.refs_33_), channel_id=1, source_target_pairs={{0,16},{4,20},{8,24},{12,28},{16,0},{20,4},{24,8},{28,12},{1,17},{... | collective-permute-start | bytes 1572872 | tf_op jit(solution)/shard_map/ppermute | solution.py:67
  177.1 23.2 %collective-permute-start.61 = (bf16[2,32,4096]{2,1,0:T(8,128)(2,1)}, bf16[2,32,4096]{2,1,0:T(8,128)(2,1)S(1)}, u32[]{:S(2)}, u32[]{:S(2)}) collective-permute-start(bf16[2,32,4096]{2,1,0:T(8,128)(2,1)} %get-tuple-element.42.refs_17_.refs_33_), channel_id=1, source_target_pairs={{0,8},{4,12},{8,0},{12,4},{16,24},{20,28},{24,16},{28,20},{1,9},{5... | collective-permute-start | bytes 1572872 | tf_op jit(solution)/shard_map/ppermute | solution.py:67
  177.6 24.1 %collective-permute-start.64 = (bf16[2,32,4096]{2,1,0:T(8,128)(2,1)}, bf16[2,32,4096]{2,1,0:T(8,128)(2,1)S(1)}, u32[]{:S(2)}, u32[]{:S(2)}) collective-permute-start(bf16[2,32,4096]{2,1,0:T(8,128)(2,1)} %get-tuple-element.41.refs_16_.refs_32_), channel_id=1, source_target_pairs={{0,16},{4,20},{8,24},{12,28},{16,0},{20,4},{24,8},{28,12},{1,17},{... | collective-permute-start | bytes 1572872 | tf_op jit(solution)/shard_map/ppermute | solution.py:67
  178.1 34.1 %collective-permute-start.17 = (bf16[64,4096]{1,0:T(8,128)(2,1)S(1)}, bf16[64,4096]{1,0:T(8,128)(2,1)S(1)}, u32[]{:S(2)}, u32[]{:S(2)}) collective-permute-start(bf16[64,4096]{1,0:T(8,128)(2,1)S(1)} %collective-permute-done.9.refs_4_), channel_id=1, source_target_pairs={{0,16},{4,20},{8,24},{12,28},{16,0},{20,4},{24,8},{28,12},{1,17},{... | collective-permute-start | bytes 1572872 | tf_op jit(solution)/shard_map/ppermute | solution.py:67
  189.0 23.2 %collective-permute-start.18 = (bf16[64,4096]{1,0:T(8,128)(2,1)S(1)}, bf16[64,4096]{1,0:T(8,128)(2,1)S(1)}, u32[]{:S(2)}, u32[]{:S(2)}) collective-permute-start(bf16[64,4096]{1,0:T(8,128)(2,1)S(1)} %collective-permute-done.14.refs_9_), channel_id=1, source_target_pairs={{0,8},{4,12},{8,0},{12,4},{16,24},{20,28},{24,16},{28,20},{1,9},{5... | collective-permute-start | bytes 1572872 | tf_op jit(solution)/shard_map/ppermute | solution.py:67
  190.5 22.2 %collective-permute-start.11 = (bf16[64,4096]{1,0:T(8,128)(2,1)S(1)}, bf16[64,4096]{1,0:T(8,128)(2,1)S(1)}, u32[]{:S(2)}, u32[]{:S(2)}) collective-permute-start(bf16[64,4096]{1,0:T(8,128)(2,1)S(1)} %collective-permute-done.9.refs_4_), channel_id=1, source_target_pairs={{0,4},{4,0},{8,12},{12,8},{16,20},{20,16},{24,28},{28,24},{1,5},{5... | collective-permute-start | bytes 1572872 | tf_op jit(solution)/shard_map/ppermute | solution.py:67
  200.2 12.6 %collective-permute-start.16 = (bf16[64,4096]{1,0:T(8,128)(2,1)S(1)}, bf16[64,4096]{1,0:T(8,128)(2,1)S(1)}, u32[]{:S(2)}, u32[]{:S(2)}) collective-permute-start(bf16[64,4096]{1,0:T(8,128)(2,1)S(1)} %collective-permute-done.14.refs_9_), channel_id=1, source_target_pairs={{0,4},{4,0},{8,12},{12,8},{16,20},{20,16},{24,28},{28,24},{1,5},{5... | collective-permute-start | bytes 1572872 | tf_op jit(solution)/shard_map/ppermute | solution.py:67
  212.8 12.9 %collective-permute-start.58 = (bf16[2,32,4096]{2,1,0:T(8,128)(2,1)}, bf16[2,32,4096]{2,1,0:T(8,128)(2,1)S(1)}, u32[]{:S(2)}, u32[]{:S(2)}) collective-permute-start(bf16[2,32,4096]{2,1,0:T(8,128)(2,1)} %get-tuple-element.41.refs_16_.refs_32_), channel_id=1, source_target_pairs={{0,4},{4,0},{8,12},{12,8},{16,20},{20,16},{24,28},{28,24},{1,5},{5... | collective-permute-start | bytes 1572872 | tf_op jit(solution)/shard_map/ppermute | solution.py:67
  213.3 12.9 %collective-permute-start.59 = (bf16[2,32,4096]{2,1,0:T(8,128)(2,1)}, bf16[2,32,4096]{2,1,0:T(8,128)(2,1)S(1)}, u32[]{:S(2)}, u32[]{:S(2)}) collective-permute-start(bf16[2,32,4096]{2,1,0:T(8,128)(2,1)} %get-tuple-element.42.refs_17_.refs_33_), channel_id=1, source_target_pairs={{0,4},{4,0},{8,12},{12,8},{16,20},{20,16},{24,28},{28,24},{1,5},{5... | collective-permute-start | bytes 1572872 | tf_op jit(solution)/shard_map/ppermute | solution.py:67
  214.1 14.0 %collective-permute-start.68 = (bf16[2,32,4096]{2,1,0:T(8,128)(2,1)S(1)}, bf16[2,32,4096]{2,1,0:T(8,128)(2,1)S(1)}, u32[]{:S(2)}, u32[]{:S(2)}) collective-permute-start(bf16[2,32,4096]{2,1,0:T(8,128)(2,1)S(1)} %collective-permute-done.60.refs_36_), channel_id=1, source_target_pairs={{0,16},{4,20},{8,24},{12,28},{16,0},{20,4},{24,8},{28,12},{1,17},{... | collective-permute-start | bytes 1572872 | tf_op jit(solution)/shard_map/ppermute | solution.py:67
  215.7 13.9 %collective-permute-start.69 = (bf16[2,32,4096]{2,1,0:T(8,128)(2,1)S(1)}, bf16[2,32,4096]{2,1,0:T(8,128)(2,1)S(1)}, u32[]{:S(2)}, u32[]{:S(2)}) collective-permute-start(bf16[2,32,4096]{2,1,0:T(8,128)(2,1)S(1)} %collective-permute-done.65.refs_41_), channel_id=1, source_target_pairs={{0,8},{4,12},{8,0},{12,4},{16,24},{20,28},{24,16},{28,20},{1,9},{5... | collective-permute-start | bytes 1572872 | tf_op jit(solution)/shard_map/ppermute | solution.py:67
  217.1 16.4 %collective-permute-start.62 = (bf16[2,32,4096]{2,1,0:T(8,128)(2,1)S(1)}, bf16[2,32,4096]{2,1,0:T(8,128)(2,1)S(1)}, u32[]{:S(2)}, u32[]{:S(2)}) collective-permute-start(bf16[2,32,4096]{2,1,0:T(8,128)(2,1)S(1)} %collective-permute-done.60.refs_36_), channel_id=1, source_target_pairs={{0,4},{4,0},{8,12},{12,8},{16,20},{20,16},{24,28},{28,24},{1,5},{5... | collective-permute-start | bytes 1572872 | tf_op jit(solution)/shard_map/ppermute | solution.py:67
  225.7 20.4 %collective-permute-start.67 = (bf16[2,32,4096]{2,1,0:T(8,128)(2,1)S(1)}, bf16[2,32,4096]{2,1,0:T(8,128)(2,1)S(1)}, u32[]{:S(2)}, u32[]{:S(2)}) collective-permute-start(bf16[2,32,4096]{2,1,0:T(8,128)(2,1)S(1)} %collective-permute-done.65.refs_41_), channel_id=1, source_target_pairs={{0,4},{4,0},{8,12},{12,8},{16,20},{20,16},{24,28},{28,24},{1,5},{5... | collective-permute-start | bytes 1572872 | tf_op jit(solution)/shard_map/ppermute | solution.py:67
  226.2 21.8 %collective-permute-start.63 = (bf16[2,32,4096]{2,1,0:T(8,128)(2,1)S(1)}, bf16[2,32,4096]{2,1,0:T(8,128)(2,1)S(1)}, u32[]{:S(2)}, u32[]{:S(2)}) collective-permute-start(bf16[2,32,4096]{2,1,0:T(8,128)(2,1)S(1)} %collective-permute-done.61.refs_37_), channel_id=1, source_target_pairs={{0,4},{4,0},{8,12},{12,8},{16,20},{20,16},{24,28},{28,24},{1,5},{5... | collective-permute-start | bytes 1572872 | tf_op jit(solution)/shard_map/ppermute | solution.py:67
  228.1 20.9 %collective-permute-start.66 = (bf16[2,32,4096]{2,1,0:T(8,128)(2,1)S(1)}, bf16[2,32,4096]{2,1,0:T(8,128)(2,1)S(1)}, u32[]{:S(2)}, u32[]{:S(2)}) collective-permute-start(bf16[2,32,4096]{2,1,0:T(8,128)(2,1)S(1)} %collective-permute-done.64.refs_40_), channel_id=1, source_target_pairs={{0,4},{4,0},{8,12},{12,8},{16,20},{20,16},{24,28},{28,24},{1,5},{5... | collective-permute-start | bytes 1572872 | tf_op jit(solution)/shard_map/ppermute | solution.py:67
  233.5 12.1 %collective-permute-start.25 = (f32[256,128]{1,0:T(8,128)S(1)}, f32[256,128]{1,0:T(8,128)S(1)}, u32[]{:S(2)}, u32[]{:S(2)}) collective-permute-start(f32[256,128]{1,0:T(8,128)S(1)} %get-tuple-element.45), channel_id=1, source_target_pairs={{0,2},{1,3},{2,0},{3,1},{4,6},{5,7},{6,4},{7,5},{8,10},{9,11},{10,... | collective-permute-start | bytes 393224 | tf_op jit(solution)/shard_map/ppermute | solution.py:72
  245.6 23.4 %collective-permute-start.70 = (bf16[2,32,4096]{2,1,0:T(8,128)(2,1)S(1)}, bf16[2,32,4096]{2,1,0:T(8,128)(2,1)S(1)}, u32[]{:S(2)}, u32[]{:S(2)}) collective-permute-start(bf16[2,32,4096]{2,1,0:T(8,128)(2,1)S(1)} %collective-permute-done.68.refs_44_), channel_id=1, source_target_pairs={{0,4},{4,0},{8,12},{12,8},{16,20},{20,16},{24,28},{28,24},{1,5},{5... | collective-permute-start | bytes 1572872 | tf_op jit(solution)/shard_map/ppermute | solution.py:67
  245.6 23.4 %collective-permute-start.71 = (bf16[2,32,4096]{2,1,0:T(8,128)(2,1)S(1)}, bf16[2,32,4096]{2,1,0:T(8,128)(2,1)S(1)}, u32[]{:S(2)}, u32[]{:S(2)}) collective-permute-start(bf16[2,32,4096]{2,1,0:T(8,128)(2,1)S(1)} %collective-permute-done.69.refs_45_), channel_id=1, source_target_pairs={{0,4},{4,0},{8,12},{12,8},{16,20},{20,16},{24,28},{28,24},{1,5},{5... | collective-permute-start | bytes 1572872 | tf_op jit(solution)/shard_map/ppermute | solution.py:67
  248.0 12.9 %collective-permute-start.28 = (f32[256,128]{1,0:T(8,128)S(1)}, f32[256,128]{1,0:T(8,128)S(1)}, u32[]{:S(2)}, u32[]{:S(2)}) collective-permute-start(f32[256,128]{1,0:T(8,128)S(1)} %add_add_fusion.refs_0_), channel_id=1, source_target_pairs={{0,2},{1,3},{2,0},{3,1},{4,6},{5,7},{6,4},{7,5},{8,10},{9,11},{10,... | collective-permute-start | bytes 393224 | tf_op jit(solution)/shard_map/ppermute | solution.py:72
  249.1 12.3 %collective-permute-start.29 = (f32[256,128]{1,0:T(8,128)S(1)}, f32[256,128]{1,0:T(8,128)S(1)}, u32[]{:S(2)}, u32[]{:S(2)}) collective-permute-start(f32[256,128]{1,0:T(8,128)S(1)} %add_add_fusion.refs_0_), channel_id=1, source_target_pairs={{0,3},{1,2},{2,1},{3,0},{4,7},{5,6},{6,5},{7,4},{8,11},{9,10},{10,... | collective-permute-start | bytes 393224 | tf_op jit(solution)/shard_map/ppermute | solution.py:72
  307.1 13.3 %collective-permute-start.72 = (bf16[32,4096]{1,0:T(8,128)(2,1)S(1)}, bf16[32,4096]{1,0:T(8,128)(2,1)S(1)}, u32[]{:S(2)}, u32[]{:S(2)}) collective-permute-start(bf16[32,4096]{1,0:T(8,128)(2,1)S(1)} %get-tuple-element.48), channel_id=1, source_target_pairs={{0,1},{1,0},{2,3},{3,2},{4,5},{5,4},{6,7},{7,6},{8,9},{9,8},{10,11... | collective-permute-start | bytes 786440 | tf_op jit(solution)/shard_map/ppermute | solution.py:72
  307.1 21.3 %collective-permute-start.73 = (bf16[32,4096]{1,0:T(8,128)(2,1)S(1)}, bf16[32,4096]{1,0:T(8,128)(2,1)S(1)}, u32[]{:S(2)}, u32[]{:S(2)}) collective-permute-start(bf16[32,4096]{1,0:T(8,128)(2,1)S(1)} %get-tuple-element.49), channel_id=1, source_target_pairs={{0,2},{1,3},{2,0},{3,1},{4,6},{5,7},{6,4},{7,5},{8,10},{9,11},{10,... | collective-permute-start | bytes 786440 | tf_op jit(solution)/shard_map/ppermute | solution.py:72
  309.4 19.0 %collective-permute-start.74 = (bf16[32,4096]{1,0:T(8,128)(2,1)S(1)}, bf16[32,4096]{1,0:T(8,128)(2,1)S(1)}, u32[]{:S(2)}, u32[]{:S(2)}) collective-permute-start(bf16[32,4096]{1,0:T(8,128)(2,1)S(1)} %get-tuple-element.50), channel_id=1, source_target_pairs={{0,3},{1,2},{2,1},{3,0},{4,7},{5,6},{6,5},{7,4},{8,11},{9,10},{10,... | collective-permute-start | bytes 786440 | tf_op jit(solution)/shard_map/ppermute | solution.py:72
  (75 other events, 1083.4 us)

commit v2 on v0

--- a/solution.py
+++ b/solution.py
@@ -1,12 +1,20 @@
+import functools
 import math
 
 import jax
 import jax.numpy as jnp
 from jax import lax
+from jax.experimental import pallas as pl
+from jax.experimental.pallas import tpu as pltpu
 from jax.sharding import PartitionSpec as P
 
 LATENT = 16384
 ITERS = 3
+EPSILON = 0.64 / math.sqrt(LATENT)
+LOG2E = math.log2(math.e)
+TO_LOG2 = LOG2E / EPSILON
+CONTRACT = (((1,), (1,)), ((), ()))
+LOCAL_COST_BYTES = 8 * 2**20
 
 
 def noise_update(cost_tile, data_pot, epsilon, log_count):
@@ -25,16 +33,15 @@
     return -epsilon * (log_count + highest + jnp.log(summed))
 
 
-def per_device(noise, data):
-    epsilon = 0.64 / math.sqrt(LATENT)
-    contract = (((1,), (1,)), ((), ()))
+def per_device_tiled(noise, data):
+    epsilon = EPSILON
     noise_full = lax.all_gather(noise, "col", axis=1, tiled=True)
     noise_norm = jnp.sum(jnp.square(noise_full.astype(jnp.float32)), axis=1) / LATENT
     noise_rows = noise.shape[0]
     data_rows = data.shape[0]
     data_full = lax.all_gather(data, "row", axis=1, tiled=True)
     data_norm = jnp.sum(jnp.square(data_full.astype(jnp.float32)), axis=1) / LATENT
-    cross = lax.dot_general(noise_full, data_full, contract, preferred_element_type=jnp.float32)
+    cross = lax.dot_general(noise_full, data_full, CONTRACT, preferred_element_type=jnp.float32)
     cost_tile = noise_norm[:, None] + data_norm[None, :] - 2.0 / LATENT * cross
     log_noise = math.log(noise_rows * lax.axis_size("row"))
     log_data = math.log(data_rows * lax.axis_size("col"))
@@ -55,6 +62,336 @@
     return (targets, noise_pot, data_pot)
 
 
+VMEM = pl.BlockSpec(memory_space=pltpu.VMEM)
+WIDTH = 128
+
+
+def place():
+    return lax.axis_index("row"), lax.axis_index("col")
+
+
+def swap(array, axis, step):
+    count = lax.axis_size(axis)
+    return lax.ppermute(array, axis, [(i, i ^ step) for i in range(count)])
+
+
+def swap_core(array):
+    return swap(array, "row", 1)
+
+
+def swap_x(array):
+    return swap(array, "row", 2)
+
+
+def swap_y(array):
+    return swap(array, "row", 4)
+
+
+def col_exchange(pieces):
+    return [pieces[0]] + [swap(piece, "col", d) for d, piece in enumerate(pieces) if d]
+
+
+def chip_gather(pieces):
+    along_x, along_y, across = [], [], []
+    for i, piece in enumerate(pieces):
+        along_x.append(swap_x(piece))
+        along_y.append(swap_y(piece))
+        across.append(swap_x(along_y[i]) if i % 2 else swap_y(along_x[i]))
+    return [pieces, along_x, along_y, across]
+
+
+def block(index, size):
+    return pl.ds(pl.multiple_of(index * size, size), size)
+
+
+def kernel_call(kernel, outs, scratch, vmem, *operands, flops=0):
+    moved = sum(a.size * a.dtype.itemsize for a in operands)
+    return pl.pallas_call(
+        kernel,
+        in_specs=[VMEM] * len(operands),
+        out_specs=[VMEM] * len(outs),
+        out_shape=[jax.ShapeDtypeStruct(shape, dtype) for shape, dtype in outs],
+        scratch_shapes=scratch,
+        compiler_params=pltpu.CompilerParams(vmem_limit_bytes=vmem * 2**20),
+        cost_estimate=pl.CostEstimate(flops=flops, bytes_accessed=moved, transcendentals=0),
+    )(*operands)
+
+
+def chip_swap(piece, k):
+    return swap(piece, "row", 2 * k) if k else piece
+
+
+def deal_kernel(n_chip, data_ref, noise_ref, *outs):
+    row, _ = place()
+    core, chip = lax.rem(row, 2), row // 2
+    share = data_ref.shape[0] // n_chip
+    for k in range(n_chip):
+        outs[k][...] = data_ref[block(chip ^ k, share), :]
+    half = noise_ref.shape[1] // 2
+    outs[n_chip][...] = noise_ref[:, block(core, half)]
+    outs[n_chip + 1][...] = noise_ref[:, block(1 - core, half)]
+
+
+def deal(data, noise, n_chip):
+    piece = (data.shape[0] // n_chip, data.shape[1])
+    half = (noise.shape[0], noise.shape[1] // 2)
+    return kernel_call(
+        functools.partial(deal_kernel, n_chip),
+        [(piece, data.dtype)] * n_chip + [(half, noise.dtype)] * 2,
+        [],
+        12,
+        data,
+        noise,
+    )
+
+
+def regroup_kernel(n_col, *refs):
+    row, col = place()
+    pieces, outs = refs[:n_col], refs[n_col:]
+    for d in range(n_col):
+        for k in range(n_col):
+
+            @pl.when((row // 2) ^ col ^ d == k)
+            def _():
+                outs[d][...] = pieces[k][...]
+
+
+def regroup(pieces):
+    n_col = len(pieces)
+    out = (pieces[0].shape, pieces[0].dtype)
+    return kernel_call(functools.partial(regroup_kernel, n_col), [out] * n_col, [], 8, *pieces)
+
+
+def cost_kernel(n_col, *refs):
+    noise_refs, latent_refs = refs[:4], refs[4 : 4 + 2 * n_col]
+    own_ref, other_ref, latents, noise = refs[4 + 2 * n_col :]
+    row, col = place()
+    x, y = lax.rem(row // 2, 2), row // 4
+    own, depth = noise_refs[0].shape
+    share = latent_refs[0].shape[0]
+    height = 2 * share
+    for i in range(4):
+        core, far = i % 2, i // 2
+        noise[block(2 * core + (x ^ far), own), :] = noise_refs[i][...]
+    for far in range(2):
+        for d in range(n_col):
+            rows = block((col ^ d) * 2 + (y ^ far), share)
+            latents[rows, :] = latent_refs[far * n_col + d][...]
+    lanes = [slice(i, i + WIDTH) for i in range(0, depth, WIDTH)]
+    squares = jnp.zeros((4 * own, WIDTH), jnp.float32)
+    for part in lanes:
+        values = noise[:, part].astype(jnp.float32)
+        squares += values * values
+    noise_norm = jnp.sum(squares, axis=1, keepdims=True)
+    step = 2 * height
+    for first in range(0, n_col * height, step):
+        rows = slice(first, first + step)
+        cross = lax.dot_general(
+            noise[...], latents[rows, :], CONTRACT, preferred_element_type=jnp.float32
+        )
+        squares = jnp.zeros((step, WIDTH), jnp.float32)
+        for part in lanes:
+            values = latents[rows, part].astype(jnp.float32)
+            squares += values * values
+        norm = jnp.sum(squares, axis=1, keepdims=True)
+        norm = jnp.broadcast_to(norm, (step, WIDTH)).T[0:1, :]
+        cost = (noise_norm + norm - 2.0 * cross) * (TO_LOG2 / LATENT)
+        for i in range(2):
+            own_ref[i, :, rows] = cost[i * own : (i + 1) * own]
+            other_ref[i, :, rows] = cost[(2 + i) * own : (3 + i) * own]
+
+
+def partial_cost(noise_parts, latents):
+    n_col = len(latents) // 2
+    own, depth = noise_parts[0].shape
+    width = 2 * n_col * latents[0].shape[0]
+    return kernel_call(
+        functools.partial(cost_kernel, n_col),
+        [((2, own, width), jnp.float32)] * 2 + [((width, depth), jnp.bfloat16)],
+        [pltpu.VMEM((4 * own, depth), jnp.bfloat16)],
+        24,
+        *noise_parts,
+        *latents,
+        flops=8 * own * width * depth,
+    )
+
+
+def core_sum_kernel(n_col, own_ref, other_ref, *outs):
+    _, col = place()
+    share = own_ref.shape[1] // n_col
+    for d in range(n_col):
+        rows = block(col ^ d, share)
+        outs[d][...] = own_ref[:, rows, :] + other_ref[:, rows, :]
+
+
+def core_sum(own, other, n_col):
+    shape = (2, own.shape[1] // n_col, own.shape[2])
+    return kernel_call(
+        functools.partial(core_sum_kernel, n_col), [(shape, own.dtype)] * n_col, [], 8, own, other
+    )
+
+
+def sinkhorn_kernel(n_col, n_half, *refs):
+    n_cost = 8 * n_half
+    cost_refs, latent_refs, refs = refs[:n_cost], refs[n_cost : n_cost + 2], refs[n_cost + 2 :]
+    target_refs, refs = refs[:n_col], refs[n_col:]
+    noise_pot_ref, data_pot_ref, cost, own_cost, pots, weights = refs
+    row, col = place()
+    x = lax.rem(row // 2, 2)
+    tall, height, wide = cost.shape
+    log_noise = math.log2(tall * height)
+    log_data = math.log2(wide)
+    blocks = range(wide // WIDTH)
+    half_wide = wide // 2
+    pieces, share = cost_refs[0].shape[0], cost_refs[0].shape[2]
+    for i, ref in enumerate(cost_refs):
+        chip, core, half = i // (2 * n_half), i // n_half % 2, i % n_half
+        rows = slice(half * pieces * 2 * share, (half + 1) * pieces * 2 * share)
+        part = slice((chip % 2) * half_wide, (chip % 2 + 1) * half_wide)
+        cost[(chip // 2) * 2 + core, rows, part] = ref[...].reshape(pieces * 2 * share, half_wide)
+
+    def lanes(b):
+        return pl.ds(b * WIDTH, WIDTH)
+
+    def row_update(tile, g):
+        peak = functools.reduce(jnp.maximum, [g[b] - tile(b) for b in blocks])
+        peak = jnp.max(peak, axis=1, keepdims=True)
+        total = functools.reduce(jnp.add, [jnp.exp2(g[b] - tile(b) - peak) for b in blocks])
+        total = jnp.sum(total, axis=1, keepdims=True)
+        return -(log_noise + peak + jnp.log2(total))
+
+    def both_updates(chunk, carry, g):
+        high, summed = carry
+        f = row_update(lambda b: cost[chunk, :, lanes(b)], g)
+        new_high, new_summed = [], []
+        for b in blocks:
+            scores = f - cost[chunk, :, lanes(b)]
+            peak = jnp.max(scores, axis=0, keepdims=True)
+            total = jnp.sum(jnp.exp2(scores - peak), axis=0, keepdims=True)
+            top = jnp.maximum(high[b], peak)
+            new_high.append(top)
+            new_summed.append(summed[b] * jnp.exp2(high[b] - top) + total * jnp.exp2(peak - top))
+        return tuple(new_high), tuple(new_summed)
+
+    def iteration(_, g):
+        first = (
+            tuple(jnp.full((1, WIDTH), -jnp.inf, jnp.float32) for b in blocks),
+            tuple(jnp.zeros((1, WIDTH), jnp.float32) for b in blocks),
+        )
+        high, summed = lax.fori_loop(0, tall, lambda i, carry: both_updates(i, carry, g), first)
+        return tuple(-(log_data + high[b] + jnp.log2(summed[b])) for b in blocks)
+
+    g = tuple(jnp.zeros((1, WIDTH), jnp.float32) for b in blocks)
+    g = lax.fori_loop(0, ITERS, iteration, g)
+    for b in blocks:
+        pots[:, lanes(b)] = g[b] * (1.0 / TO_LOG2)
+    width = half_wide // n_col
+    for far in range(2):
+        data_pot_ref[pl.ds(x ^ far, 1), :] = pots[:, block(far * n_col + col, width)]
+
+    for core in range(2):
+        for d in range(n_col):
+            rows = slice((core * n_col + d) * share, (core * n_col + d + 1) * share)
+            own_cost[rows, :] = cost[core, block(2 * d + x, share), :]
+    f = row_update(lambda b: own_cost[:, lanes(b)], g)
+    for b in blocks:
+        scores = (f + g[b] - own_cost[:, lanes(b)]) + log_noise
+        weights[:, lanes(b)] = jnp.exp2(scores).astype(jnp.bfloat16)
+    own = share * n_col
+    f = jnp.broadcast_to(f[:own], (own, WIDTH)).T[0:1, :] * (1.0 / TO_LOG2)
+    for d in range(n_col):
+        noise_pot_ref[pl.ds(col ^ d, 1), :] = f[:, d * share : (d + 1) * share]
+
+    depth = latent_refs[0].shape[1]
+    step = min(depth, 512)
+    for i in range(0, depth, step):
+        part = slice(i, i + step)
+        product = jnp.dot(
+            weights[:, :half_wide], latent_refs[0][:, part], preferred_element_type=jnp.float32
+        )
+        product += jnp.dot(
+            weights[:, half_wide:], latent_refs[1][:, part], preferred_element_type=jnp.float32
+        )
+        product = product.astype(jnp.bfloat16)
+        for d in range(n_col):
+            target_refs[d][0, :, part] = product[d * share : (d + 1) * share]
+            target_refs[d][1, :, part] = product[own + d * share : own + (d + 1) * share]
+
+
+def sinkhorn(tiles, latents, n_col):
+    n_half = len(tiles[0]) // 2
+    pieces, _, share, half_wide = tiles[0][0].shape
+    height = n_half * pieces * 2 * share
+    wide = 2 * half_wide
+    own = n_col * share
+    return kernel_call(
+        functools.partial(sinkhorn_kernel, n_col, n_half),
+        [((2, share, latents[0].shape[1]), jnp.bfloat16)] * n_col
+        + [((n_col, share), jnp.float32), ((2, half_wide // n_col), jnp.float32)],
+        [
+            pltpu.VMEM((4, height, wide), jnp.float32),
+            pltpu.VMEM((2 * own, wide), jnp.float32),
+            pltpu.VMEM((1, wide), jnp.float32),
+            pltpu.VMEM((2 * own, wide), jnp.bfloat16),
+        ],
+        32,
+        *[tile for group in tiles for tile in group],
+        *latents,
+        flops=240 * height * wide,
+    )
+
+
+def join_kernel(n_col, *refs):
+    *pieces, out_ref = refs
+    row, col = place()
+    depth = pieces[0].shape[2]
+    for d in range(n_col):
+        for other in range(2):
+            lanes = block(2 * (col ^ d) + (lax.rem(row, 2) ^ other), depth)
+            out_ref[:, lanes] = pieces[other * n_col + d][other]
+
+
+def join(pieces, n_col):
+    _, share, depth = pieces[0].shape
+    shape = (share, depth * len(pieces))
+    (out,) = kernel_call(
+        functools.partial(join_kernel, n_col), [(shape, pieces[0].dtype)], [], 12, *pieces
+    )
+    return out
+
+
+def per_device_local(noise, data):
+    n_row, n_col = lax.axis_size("row"), lax.axis_size("col")
+    n_chip = n_row // 2
+    own, own_data = noise.shape[0], data.shape[0]
+    *dealt, own_half, other_half = deal(data, noise, n_chip)
+    spread = regroup([chip_swap(piece, k) for k, piece in enumerate(dealt)])
+    latents = col_exchange(spread)
+    latents = latents + [swap_y(piece) for piece in latents]
+    halves = [own_half, swap_core(other_half)]
+    halves = halves + [swap_x(half) for half in halves]
+    own_part, other_part, near = partial_cost(halves, latents)
+    far = swap_x(near)
+    parts = col_exchange(core_sum(own_part, swap_core(other_part), n_col))
+    tile = functools.reduce(jnp.add, parts)
+    rows = [tile] + [swap(tile, "col", d) for d in range(1, n_col)]
+    halves = [jnp.stack(rows[: n_col // 2]), jnp.stack(rows[n_col // 2 :])]
+    tiles = [group + [swap_core(half) for half in group] for group in chip_gather(halves)]
+    *products, noise_pot, data_pot = sinkhorn(tiles, [near, far], n_col)
+    products = col_exchange(products)
+    targets = join(products + [swap_core(piece) for piece in products], n_col)
+    data_pot = data_pot.reshape((2, 2, own_data // 4)).transpose((1, 0, 2))
+    return (targets, noise_pot.reshape((own,)), data_pot.reshape((own_data,)))
+
+
+def per_device(noise, data):
+    n_row, n_col = lax.axis_size("row"), lax.axis_size("col")
+    whole = 4 * noise.shape[0] * n_row * data.shape[0] * n_col
+    if whole <= LOCAL_COST_BYTES and n_row == 8 and n_col == 4:
+        return per_device_local(noise, data)
+    return per_device_tiled(noise, data)
+
+
 def solution(mesh):
     placed = (P("row", "col"), P("col", "row"))
     return jax.shard_map(

time: 397 us -> 167 us (0.42)
  blocking collectives: 147 us -> 0 us
  waiting for transfers between devices: 213 us -> 105 us
  starting transfers between devices: 0.11 us -> 43.1 us
  between operations: 13.8 us -> 0.75 us
  matrix products: 11.9 us -> 0 us
  Pallas kernels: 0 us -> 11.4 us
  other arithmetic: 10.2 us -> 0.07 us
    all_gather x2 -> x0, waiting for transfers between devices: 136 us -> none  [the longest x1 84.4 us: per_device(): noise_full = lax.all_gather(noise, 'col', axis=1, tiled=True)]
    ppermute x0 -> x42, waiting for transfers between devices: none -> 105 us  [swap(): return lax.ppermute(array, axis, [(i, i ^ step) for i in range(count)])]
    pmax x7 -> x0, blocking collectives: 78.1 us -> none  [the longest x4 42.7 us: noise_update(): highest = lax.pmax(local_peak, 'col')]
    reduce_scatter x1 -> x0, waiting for transfers between devices: 75.2 us -> none  [per_device(): lax.psum_scatter(jnp.dot(weights, data_full, preferred_element_type=jnp.f...]
    psum x7 -> x0, blocking collectives: 69.1 us -> none  [the longest x3 35.4 us: data_update(): lax.psum(jnp.sum(jnp.exp(scores - highest[None, :]), axis=0), 'row')]
    ppermute x0 -> x42, starting transfers between devices: none -> 43.1 us  [swap(): return lax.ppermute(array, axis, [(i, i ^ step) for i in range(count)])]
    dot_general x2 -> x0, matrix products: 11.9 us -> none  [the longest x1 6.68 us: per_device(): jnp.dot(weights, data_full, preferred_element_type=jnp.float32)]
    pallas_call x0 -> x6, Pallas kernels: none -> 11.4 us  [kernel_call(): pl.pallas_call(kernel, in_specs=[VMEM] * len(operands), out_specs=[VMEM]...]
  transfers between devices with their start and end apart: 3 -> 42, of which waited for: 3 -> 21; matrix products, arithmetic and copies ran while one was open for 1% -> 1% of each run, Pallas kernels for 0% -> 0%
where the time goes in v2:
time: 167 us; the launch traced here: 165 us
  waiting for transfers between devices  105 us (63%)
  starting transfers between devices  43.1 us (26%)
  Pallas kernels  11.4 us (7%)
  local copies, waits for them, and re-layouts  3.77 us (2%)
    ppermute x42, waiting for transfers between devices, swap(): return lax.ppermute(array, axis, [(i, i ^ step) for i in range(count)])  105 us
    ppermute x42, starting transfers between devices, swap(): return lax.ppermute(array, axis, [(i, i ^ step) for i in range(count)])  43.1 us
    pallas_call x6, Pallas kernels, kernel_call(): pl.pallas_call(kernel, in_specs=[VMEM] * len(operands), out_specs=[VMEM]...  11.4 us
  transfers between devices with their start and end apart: 42, of which 21 were waited for; matrix products, arithmetic and copies ran while one was open for 1% of the time, Pallas kernels for 0%

profile of v2, /device:TPU:0, one launch (start us, length us, event | category | flops | bytes accessed | tf_op | source)
XLA Modules:
  0.0 164.5 jit_solution(1893352743683392690)
XLA Ops:
  3.2 3.0 %collective-permute-start.3 = (bf16[64,2048]{1,0:T(8,128)(2,1)S(1)}, bf16[64,2048]{1,0:T(8,128)(2,1)S(1)}, u32[]{:S(2)}, u32[]{:S(2)}) collective-permute-start(bf16[64,2048]{1,0:T(8,128)(2,1)S(1)} %get-tuple-element.29), channel_id=1, source_target_pairs={{0,8},{4,12},{8,0},{12,4},{16,24},{20,28},{24,16},{28,20},{1,9},{5... | collective-permute-start | bytes 786440 | tf_op jit(solution)/shard_map/ppermute | solution.py:75
  6.2 1.5 collective-permute-start.4
  7.8 5.6 %collective-permute-done.3.refs_1_ = bf16[64,2048]{1,0:T(8,128)(2,1)S(1)} collective-permute-done((bf16[64,2048]{1,0:T(8,128)(2,1)S(1)}, bf16[64,2048]{1,0:T(8,128)(2,1)S(1)}, u32[]{:S(2)}, u32[]{:S(2)}) %collective-permute-start.3) | collective-permute-done | bytes 262176 | tf_op jit(solution)/shard_map/ppermute | solution.py:75
  13.4 6.2 %collective-permute-done.4.refs_2_ = bf16[64,2048]{1,0:T(8,128)(2,1)S(1)} collective-permute-done((bf16[64,2048]{1,0:T(8,128)(2,1)S(1)}, bf16[64,2048]{1,0:T(8,128)(2,1)S(1)}, u32[]{:S(2)}, u32[]{:S(2)}) %collective-permute-start.4) | collective-permute-done | bytes 262176 | tf_op jit(solution)/shard_map/ppermute | solution.py:75
  19.7 1.6 collective-permute-start.6
  22.6 2.6 %collective-permute-start.7 = (bf16[64,2048]{1,0:T(8,128)(2,1)S(1)}, bf16[64,2048]{1,0:T(8,128)(2,1)S(1)}, u32[]{:S(2)}, u32[]{:S(2)}) collective-permute-start(bf16[64,2048]{1,0:T(8,128)(2,1)S(1)} %get-tuple-element.34), channel_id=1, source_target_pairs={{0,2},{1,3},{2,0},{3,1},{4,6},{5,7},{6,4},{7,5},{8,10},{9,11},{10,... | collective-permute-start | bytes 786440 | tf_op jit(solution)/shard_map/ppermute | solution.py:75
  25.4 4.9 %collective-permute-done.6.refs_5_ = bf16[64,2048]{1,0:T(8,128)(2,1)S(1)} collective-permute-done((bf16[64,2048]{1,0:T(8,128)(2,1)S(1)}, bf16[64,2048]{1,0:T(8,128)(2,1)S(1)}, u32[]{:S(2)}, u32[]{:S(2)}) %collective-permute-start.6) | collective-permute-done | bytes 262176 | tf_op jit(solution)/shard_map/ppermute | solution.py:75
  32.3 11.4 %collective-permute-done.7.refs_6_ = bf16[64,2048]{1,0:T(8,128)(2,1)S(1)} collective-permute-done((bf16[64,2048]{1,0:T(8,128)(2,1)S(1)}, bf16[64,2048]{1,0:T(8,128)(2,1)S(1)}, u32[]{:S(2)}, u32[]{:S(2)}) %collective-permute-start.7) | collective-permute-done | bytes 262176 | tf_op jit(solution)/shard_map/ppermute | solution.py:75
  43.9 1.9 %collective-permute-start.11 = (bf16[64,2048]{1,0:T(8,128)(2,1)S(1)}, bf16[64,2048]{1,0:T(8,128)(2,1)S(1)}, u32[]{:S(2)}, u32[]{:S(2)}) collective-permute-start(bf16[64,2048]{1,0:T(8,128)(2,1)S(1)} %collective-permute-done.7.refs_6_), channel_id=1, source_target_pairs={{0,16},{4,20},{8,24},{12,28},{16,0},{20,4},{24,8},{28,12},{1,17},{... | collective-permute-start | bytes 786440 | tf_op jit(solution)/shard_map/ppermute | solution.py:75
  45.9 4.2 %collective-permute-done.10.refs_9_ = bf16[64,2048]{1,0:T(8,128)(2,1)S(1)} collective-permute-done((bf16[64,2048]{1,0:T(8,128)(2,1)S(1)}, bf16[64,2048]{1,0:T(8,128)(2,1)S(1)}, u32[]{:S(2)}, u32[]{:S(2)}) %collective-permute-start.10) | collective-permute-done | bytes 262176 | tf_op jit(solution)/shard_map/ppermute | solution.py:75
  50.1 2.8 %collective-permute-done.11.refs_10_ = bf16[64,2048]{1,0:T(8,128)(2,1)S(1)} collective-permute-done((bf16[64,2048]{1,0:T(8,128)(2,1)S(1)}, bf16[64,2048]{1,0:T(8,128)(2,1)S(1)}, u32[]{:S(2)}, u32[]{:S(2)}) %collective-permute-start.11) | collective-permute-done | bytes 262176 | tf_op jit(solution)/shard_map/ppermute | solution.py:75
  52.9 2.8 %collective-permute-done.12.refs_11_ = bf16[64,2048]{1,0:T(8,128)(2,1)S(1)} collective-permute-done((bf16[64,2048]{1,0:T(8,128)(2,1)S(1)}, bf16[64,2048]{1,0:T(8,128)(2,1)S(1)}, u32[]{:S(2)}, u32[]{:S(2)}) %collective-permute-start.12) | collective-permute-done | bytes 262176 | tf_op jit(solution)/shard_map/ppermute | solution.py:75
  55.7 2.1 %shard_map.51 = (f32[2,128,512]{2,1,0:T(8,128)S(1)}, f32[2,128,512]{2,1,0:T(8,128)S(1)}, bf16[512,2048]{1,0:T(8,128)(2,1)S(1)}) custom-call(bf16[128,2048]{1,0:T(8,128)(2,1)S(1)} %get-tuple-element.26.refs_0_, bf16[128,2048]{1,0:T(8,128)(2,1)S(1)} %collective-permute-done.refs_1_, bf16[128,2048]{1,0:T(8,128)(2,1)S(1)} %collective-permute-done.1.refs_2_, ...), custom_call_target="tpu_custom_call" | custom-call | flops 1073741824 | bytes 4194304 | tf_op jit(solution)/shard_map/pallas_call | solution.py:109
  59.9 4.9 %collective-permute-start.14 = (f32[2,32,512]{2,1,0:T(8,128)S(1)}, f32[2,32,512]{2,1,0:T(8,128)S(1)}, u32[]{:S(2)}, u32[]{:S(2)}) collective-permute-start(f32[2,32,512]{2,1,0:T(8,128)S(1)} %get-tuple-element.39), channel_id=1, source_target_pairs={{0,1},{1,0},{2,3},{3,2},{4,5},{5,4},{6,7},{7,6},{8,9},{9,8},{10,11... | collective-permute-start | bytes 393224 | tf_op jit(solution)/shard_map/ppermute | solution.py:75
  64.8 1.7 %collective-permute-start.15 = (f32[2,32,512]{2,1,0:T(8,128)S(1)}, f32[2,32,512]{2,1,0:T(8,128)S(1)}, u32[]{:S(2)}, u32[]{:S(2)}) collective-permute-start(f32[2,32,512]{2,1,0:T(8,128)S(1)} %get-tuple-element.40), channel_id=1, source_target_pairs={{0,2},{1,3},{2,0},{3,1},{4,6},{5,7},{6,4},{7,5},{8,10},{9,11},{10,... | collective-permute-start | bytes 393224 | tf_op jit(solution)/shard_map/ppermute | solution.py:75
  67.2 2.9 %collective-permute-done.14 = f32[2,32,512]{2,1,0:T(8,128)S(1)} collective-permute-done((f32[2,32,512]{2,1,0:T(8,128)S(1)}, f32[2,32,512]{2,1,0:T(8,128)S(1)}, u32[]{:S(2)}, u32[]{:S(2)}) %collective-permute-start.14) | collective-permute-done | bytes 131104 | tf_op jit(solution)/shard_map/ppermute | solution.py:75
  70.1 7.6 %collective-permute-done.15 = f32[2,32,512]{2,1,0:T(8,128)S(1)} collective-permute-done((f32[2,32,512]{2,1,0:T(8,128)S(1)}, f32[2,32,512]{2,1,0:T(8,128)S(1)}, u32[]{:S(2)}, u32[]{:S(2)}) %collective-permute-start.15) | collective-permute-done | bytes 131104 | tf_op jit(solution)/shard_map/ppermute | solution.py:75
  77.7 2.4 %collective-permute-start.17 = (f32[2,32,512]{2,1,0:T(8,128)S(1)}, f32[2,32,512]{2,1,0:T(8,128)S(1)}, u32[]{:S(2)}, u32[]{:S(2)}) collective-permute-start(f32[2,32,512]{2,1,0:T(8,128)S(1)} %add_add_fusion), channel_id=1, source_target_pairs={{0,1},{1,0},{2,3},{3,2},{4,5},{5,4},{6,7},{7,6},{8,9},{9,8},{10,11... | collective-permute-start | bytes 393224 | tf_op jit(solution)/shard_map/ppermute | solution.py:75
  80.1 2.9 %collective-permute-done.17 = f32[2,32,512]{2,1,0:T(8,128)S(1)} collective-permute-done((f32[2,32,512]{2,1,0:T(8,128)S(1)}, f32[2,32,512]{2,1,0:T(8,128)S(1)}, u32[]{:S(2)}, u32[]{:S(2)}) %collective-permute-start.17) | collective-permute-done | bytes 131104 | tf_op jit(solution)/shard_map/ppermute | solution.py:75
  85.0 1.6 collective-permute-start.19
  86.5 1.9 %collective-permute-start.18 = (f32[2,32,512]{2,1,0:T(8,128)S(1)}, f32[2,32,512]{2,1,0:T(8,128)S(1)}, u32[]{:S(2)}, u32[]{:S(2)}) collective-permute-start(f32[2,32,512]{2,1,0:T(8,128)S(1)} %add_add_fusion), channel_id=1, source_target_pairs={{0,2},{1,3},{2,0},{3,1},{4,6},{5,7},{6,4},{7,5},{8,10},{9,11},{10,... | collective-permute-start | bytes 393224 | tf_op jit(solution)/shard_map/ppermute | solution.py:75
  88.4 3.3 %collective-permute-done.19 = f32[2,32,512]{2,1,0:T(8,128)S(1)} collective-permute-done((f32[2,32,512]{2,1,0:T(8,128)S(1)}, f32[2,32,512]{2,1,0:T(8,128)S(1)}, u32[]{:S(2)}, u32[]{:S(2)}) %collective-permute-start.19) | collective-permute-done | bytes 131104 | tf_op jit(solution)/shard_map/ppermute | solution.py:75
  91.8 6.2 %collective-permute-done.18 = f32[2,32,512]{2,1,0:T(8,128)S(1)} collective-permute-done((f32[2,32,512]{2,1,0:T(8,128)S(1)}, f32[2,32,512]{2,1,0:T(8,128)S(1)}, u32[]{:S(2)}, u32[]{:S(2)}) %collective-permute-start.18) | collective-permute-done | bytes 131104 | tf_op jit(solution)/shard_map/ppermute | solution.py:75
  100.1 11.9 %collective-permute-done.22.refs_4_ = f32[2,2,32,512]{3,2,1,0:T(8,128)S(1)} collective-permute-done((f32[2,2,32,512]{3,2,1,0:T(8,128)S(1)}, f32[2,2,32,512]{3,2,1,0:T(8,128)S(1)}, u32[]{:S(2)}, u32[]{:S(2)}) %collective-permute-start.22) | collective-permute-done | bytes 262176 | tf_op jit(solution)/shard_map/ppermute | solution.py:75
  112.7 4.5 %collective-permute-done.23.refs_5_ = f32[2,2,32,512]{3,2,1,0:T(8,128)S(1)} collective-permute-done((f32[2,2,32,512]{3,2,1,0:T(8,128)S(1)}, f32[2,2,32,512]{3,2,1,0:T(8,128)S(1)}, u32[]{:S(2)}, u32[]{:S(2)}) %collective-permute-start.23) | collective-permute-done | bytes 262176 | tf_op jit(solution)/shard_map/ppermute | solution.py:75
  118.5 2.3 %collective-permute-done.30.refs_12_ = f32[2,2,32,512]{3,2,1,0:T(8,128)S(1)} collective-permute-done((f32[2,2,32,512]{3,2,1,0:T(8,128)S(1)}, f32[2,2,32,512]{3,2,1,0:T(8,128)S(1)}, u32[]{:S(2)}, u32[]{:S(2)}) %collective-permute-start.30) | collective-permute-done | bytes 262176 | tf_op jit(solution)/shard_map/ppermute | solution.py:75
  121.4 4.6 %collective-permute-done.31.refs_13_ = f32[2,2,32,512]{3,2,1,0:T(8,128)S(1)} collective-permute-done((f32[2,2,32,512]{3,2,1,0:T(8,128)S(1)}, f32[2,2,32,512]{3,2,1,0:T(8,128)S(1)}, u32[]{:S(2)}, u32[]{:S(2)}) %collective-permute-start.31) | collective-permute-done | bytes 262176 | tf_op jit(solution)/shard_map/ppermute | solution.py:75
  127.5 7.9 %shard_map.53 = (bf16[2,32,2048]{2,1,0:T(8,128)(2,1)S(1)}, bf16[2,32,2048]{2,1,0:T(8,128)(2,1)S(1)}, bf16[2,32,2048]{2,1,0:T(8,128)(2,1)S(1)}, bf16[2,32,2048]{2...) custom-call(f32[2,2,32,512]{3,2,1,0:T(8,128)S(1)} %pad_maximum_fusion.refs_0_, ...), custom_call_target="tpu_custom_call" | custom-call | flops 62914560 | bytes 8388608 | tf_op jit(solution)/shard_map/pallas_call | solution.py:109
  135.4 4.9 %collective-permute-start.35 = (bf16[2,32,2048]{2,1,0:T(8,128)(2,1)S(1)}, bf16[2,32,2048]{2,1,0:T(8,128)(2,1)S(1)}, u32[]{:S(2)}, u32[]{:S(2)}) collective-permute-start(bf16[2,32,2048]{2,1,0:T(8,128)(2,1)S(1)} %get-tuple-element.44), channel_id=1, source_target_pairs={{0,1},{1,0},{2,3},{3,2},{4,5},{5,4},{6,7},{7,6},{8,9},{9,8},{10,11... | collective-permute-start | bytes 786440 | tf_op jit(solution)/shard_map/ppermute | solution.py:75
  140.2 1.7 %collective-permute-start.36 = (bf16[2,32,2048]{2,1,0:T(8,128)(2,1)S(1)}, bf16[2,32,2048]{2,1,0:T(8,128)(2,1)S(1)}, u32[]{:S(2)}, u32[]{:S(2)}) collective-permute-start(bf16[2,32,2048]{2,1,0:T(8,128)(2,1)S(1)} %get-tuple-element.45), channel_id=1, source_target_pairs={{0,2},{1,3},{2,0},{3,1},{4,6},{5,7},{6,4},{7,5},{8,10},{9,11},{10,... | collective-permute-start | bytes 786440 | tf_op jit(solution)/shard_map/ppermute | solution.py:75
  142.7 8.9 %collective-permute-done.35.refs_1_ = bf16[2,32,2048]{2,1,0:T(8,128)(2,1)S(1)} collective-permute-done((bf16[2,32,2048]{2,1,0:T(8,128)(2,1)S(1)}, bf16[2,32,2048]{2,1,0:T(8,128)(2,1)S(1)}, u32[]{:S(2)}, u32[]{:S(2)}) %collective-permute-start.35) | collective-permute-done | bytes 262176 | tf_op jit(solution)/shard_map/ppermute | solution.py:75
  151.5 10.0 %collective-permute-done.36.refs_2_ = bf16[2,32,2048]{2,1,0:T(8,128)(2,1)S(1)} collective-permute-done((bf16[2,32,2048]{2,1,0:T(8,128)(2,1)S(1)}, bf16[2,32,2048]{2,1,0:T(8,128)(2,1)S(1)}, u32[]{:S(2)}, u32[]{:S(2)}) %collective-permute-start.36) | collective-permute-done | bytes 262176 | tf_op jit(solution)/shard_map/ppermute | solution.py:75
  (69 shorter events, 21.1 us)
Async XLA Ops:
  3.2 10.1 %collective-permute-start.3 = (bf16[64,2048]{1,0:T(8,128)(2,1)S(1)}, bf16[64,2048]{1,0:T(8,128)(2,1)S(1)}, u32[]{:S(2)}, u32[]{:S(2)}) collective-permute-start(bf16[64,2048]{1,0:T(8,128)(2,1)S(1)} %get-tuple-element.29), channel_id=1, source_target_pairs={{0,8},{4,12},{8,0},{12,4},{16,24},{20,28},{24,16},{28,20},{1,9},{5... | collective-permute-start | bytes 786440 | tf_op jit(solution)/shard_map/ppermute | solution.py:75
  6.2 13.4 %collective-permute-start.4 = (bf16[64,2048]{1,0:T(8,128)(2,1)S(1)}, bf16[64,2048]{1,0:T(8,128)(2,1)S(1)}, u32[]{:S(2)}, u32[]{:S(2)}) collective-permute-start(bf16[64,2048]{1,0:T(8,128)(2,1)S(1)} %get-tuple-element.30), channel_id=1, source_target_pairs={{0,16},{4,20},{8,24},{12,28},{16,0},{20,4},{24,8},{28,12},{1,17},{... | collective-permute-start | bytes 786440 | tf_op jit(solution)/shard_map/ppermute | solution.py:75
  7.7 11.9 %collective-permute-start.5 = (bf16[64,2048]{1,0:T(8,128)(2,1)S(1)}, bf16[64,2048]{1,0:T(8,128)(2,1)S(1)}, u32[]{:S(2)}, u32[]{:S(2)}) collective-permute-start(bf16[64,2048]{1,0:T(8,128)(2,1)S(1)} %get-tuple-element.31), channel_id=1, source_target_pairs={{0,24},{4,28},{8,16},{12,20},{16,8},{20,12},{24,0},{28,4},{1,25},{... | collective-permute-start | bytes 786440 | tf_op jit(solution)/shard_map/ppermute | solution.py:75
  7.8 23.4 %collective-permute-start = (bf16[128,2048]{1,0:T(8,128)(2,1)S(1)}, bf16[128,2048]{1,0:T(8,128)(2,1)S(1)}, u32[]{:S(2)}, u32[]{:S(2)}) collective-permute-start(bf16[128,2048]{1,0:T(8,128)(2,1)S(1)} %get-tuple-element.27), channel_id=1, source_target_pairs={{0,4},{4,0},{8,12},{12,8},{16,20},{20,16},{24,28},{28,24},{1,5},{5... | collective-permute-start | bytes 1572872 | tf_op jit(solution)/shard_map/ppermute | solution.py:75
  19.7 10.6 %collective-permute-start.6 = (bf16[64,2048]{1,0:T(8,128)(2,1)S(1)}, bf16[64,2048]{1,0:T(8,128)(2,1)S(1)}, u32[]{:S(2)}, u32[]{:S(2)}) collective-permute-start(bf16[64,2048]{1,0:T(8,128)(2,1)S(1)} %get-tuple-element.33), channel_id=1, source_target_pairs={{0,1},{1,0},{2,3},{3,2},{4,5},{5,4},{6,7},{7,6},{8,9},{9,8},{10,11... | collective-permute-start | bytes 786440 | tf_op jit(solution)/shard_map/ppermute | solution.py:75
  21.4 24.5 %collective-permute-start.1 = (bf16[128,2048]{1,0:T(8,128)(2,1)S(1)}, bf16[128,2048]{1,0:T(8,128)(2,1)S(1)}, u32[]{:S(2)}, u32[]{:S(2)}) collective-permute-start(bf16[128,2048]{1,0:T(8,128)(2,1)S(1)} %get-tuple-element.26.refs_0_), channel_id=1, source_target_pairs={{0,8},{4,12},{8,0},{12,4},{16,24},{20,28},{24,16},{28,20},{1,9},{5... | collective-permute-start | bytes 1572872 | tf_op jit(solution)/shard_map/ppermute | solution.py:75
  22.6 21.1 %collective-permute-start.7 = (bf16[64,2048]{1,0:T(8,128)(2,1)S(1)}, bf16[64,2048]{1,0:T(8,128)(2,1)S(1)}, u32[]{:S(2)}, u32[]{:S(2)}) collective-permute-start(bf16[64,2048]{1,0:T(8,128)(2,1)S(1)} %get-tuple-element.34), channel_id=1, source_target_pairs={{0,2},{1,3},{2,0},{3,1},{4,6},{5,7},{6,4},{7,5},{8,10},{9,11},{10,... | collective-permute-start | bytes 786440 | tf_op jit(solution)/shard_map/ppermute | solution.py:75
  25.2 18.7 %collective-permute-start.8 = (bf16[64,2048]{1,0:T(8,128)(2,1)S(1)}, bf16[64,2048]{1,0:T(8,128)(2,1)S(1)}, u32[]{:S(2)}, u32[]{:S(2)}) collective-permute-start(bf16[64,2048]{1,0:T(8,128)(2,1)S(1)} %get-tuple-element.35), channel_id=1, source_target_pairs={{0,3},{1,2},{2,1},{3,0},{4,7},{5,6},{6,5},{7,4},{8,11},{9,10},{10,... | collective-permute-start | bytes 786440 | tf_op jit(solution)/shard_map/ppermute | solution.py:75
  30.4 15.4 %collective-permute-start.9 = (bf16[64,2048]{1,0:T(8,128)(2,1)S(1)}, bf16[64,2048]{1,0:T(8,128)(2,1)S(1)}, u32[]{:S(2)}, u32[]{:S(2)}) collective-permute-start(bf16[64,2048]{1,0:T(8,128)(2,1)S(1)} %get-tuple-element.32.refs_4_), channel_id=1, source_target_pairs={{0,16},{4,20},{8,24},{12,28},{16,0},{20,4},{24,8},{28,12},{1,17},{... | collective-permute-start | bytes 786440 | tf_op jit(solution)/shard_map/ppermute | solution.py:75
  31.2 24.5 %collective-permute-start.2 = (bf16[128,2048]{1,0:T(8,128)(2,1)S(1)}, bf16[128,2048]{1,0:T(8,128)(2,1)S(1)}, u32[]{:S(2)}, u32[]{:S(2)}) collective-permute-start(bf16[128,2048]{1,0:T(8,128)(2,1)S(1)} %collective-permute-done.refs_1_), channel_id=1, source_target_pairs={{0,8},{4,12},{8,0},{12,4},{16,24},{20,28},{24,16},{28,20},{1,9},{5... | collective-permute-start | bytes 1572872 | tf_op jit(solution)/shard_map/ppermute | solution.py:75
  43.7 6.4 %collective-permute-start.10 = (bf16[64,2048]{1,0:T(8,128)(2,1)S(1)}, bf16[64,2048]{1,0:T(8,128)(2,1)S(1)}, u32[]{:S(2)}, u32[]{:S(2)}) collective-permute-start(bf16[64,2048]{1,0:T(8,128)(2,1)S(1)} %collective-permute-done.6.refs_5_), channel_id=1, source_target_pairs={{0,16},{4,20},{8,24},{12,28},{16,0},{20,4},{24,8},{28,12},{1,17},{... | collective-permute-start | bytes 786440 | tf_op jit(solution)/shard_map/ppermute | solution.py:75
  43.9 9.0 %collective-permute-start.11 = (bf16[64,2048]{1,0:T(8,128)(2,1)S(1)}, bf16[64,2048]{1,0:T(8,128)(2,1)S(1)}, u32[]{:S(2)}, u32[]{:S(2)}) collective-permute-start(bf16[64,2048]{1,0:T(8,128)(2,1)S(1)} %collective-permute-done.7.refs_6_), channel_id=1, source_target_pairs={{0,16},{4,20},{8,24},{12,28},{16,0},{20,4},{24,8},{28,12},{1,17},{... | collective-permute-start | bytes 786440 | tf_op jit(solution)/shard_map/ppermute | solution.py:75
  45.7 10.0 %collective-permute-start.12 = (bf16[64,2048]{1,0:T(8,128)(2,1)S(1)}, bf16[64,2048]{1,0:T(8,128)(2,1)S(1)}, u32[]{:S(2)}, u32[]{:S(2)}) collective-permute-start(bf16[64,2048]{1,0:T(8,128)(2,1)S(1)} %collective-permute-done.8.refs_7_), channel_id=1, source_target_pairs={{0,16},{4,20},{8,24},{12,28},{16,0},{20,4},{24,8},{28,12},{1,17},{... | collective-permute-start | bytes 786440 | tf_op jit(solution)/shard_map/ppermute | solution.py:75
  57.9 69.5 %collective-permute-start.34 = (bf16[512,2048]{1,0:T(8,128)(2,1)S(1)}, bf16[512,2048]{1,0:T(8,128)(2,1)S(1)}, u32[]{:S(2)}, u32[]{:S(2)}) collective-permute-start(bf16[512,2048]{1,0:T(8,128)(2,1)S(1)} %get-tuple-element.42.refs_16_), channel_id=1, source_target_pairs={{0,8},{4,12},{8,0},{12,4},{16,24},{20,28},{24,16},{28,20},{1,9},{5... | collective-permute-start | bytes 6291464 | tf_op jit(solution)/shard_map/ppermute | solution.py:75
  59.9 10.2 %collective-permute-start.14 = (f32[2,32,512]{2,1,0:T(8,128)S(1)}, f32[2,32,512]{2,1,0:T(8,128)S(1)}, u32[]{:S(2)}, u32[]{:S(2)}) collective-permute-start(f32[2,32,512]{2,1,0:T(8,128)S(1)} %get-tuple-element.39), channel_id=1, source_target_pairs={{0,1},{1,0},{2,3},{3,2},{4,5},{5,4},{6,7},{7,6},{8,9},{9,8},{10,11... | collective-permute-start | bytes 393224 | tf_op jit(solution)/shard_map/ppermute | solution.py:75
  64.8 12.9 %collective-permute-start.15 = (f32[2,32,512]{2,1,0:T(8,128)S(1)}, f32[2,32,512]{2,1,0:T(8,128)S(1)}, u32[]{:S(2)}, u32[]{:S(2)}) collective-permute-start(f32[2,32,512]{2,1,0:T(8,128)S(1)} %get-tuple-element.40), channel_id=1, source_target_pairs={{0,2},{1,3},{2,0},{3,1},{4,6},{5,7},{6,4},{7,5},{8,10},{9,11},{10,... | collective-permute-start | bytes 393224 | tf_op jit(solution)/shard_map/ppermute | solution.py:75
  66.4 11.2 %collective-permute-start.16 = (f32[2,32,512]{2,1,0:T(8,128)S(1)}, f32[2,32,512]{2,1,0:T(8,128)S(1)}, u32[]{:S(2)}, u32[]{:S(2)}) collective-permute-start(f32[2,32,512]{2,1,0:T(8,128)S(1)} %get-tuple-element.41), channel_id=1, source_target_pairs={{0,3},{1,2},{2,1},{3,0},{4,7},{5,6},{6,5},{7,4},{8,11},{9,10},{10,... | collective-permute-start | bytes 393224 | tf_op jit(solution)/shard_map/ppermute | solution.py:75
  83.0 16.2 %collective-permute-start.26 = (f32[2,2,32,512]{3,2,1,0:T(8,128)S(1)}, f32[2,2,32,512]{3,2,1,0:T(8,128)S(1)}, u32[]{:S(2)}, u32[]{:S(2)}) collective-permute-start(f32[2,2,32,512]{3,2,1,0:T(8,128)S(1)} %pad_maximum_fusion.refs_0_), channel_id=1, source_target_pairs={{0,16},{4,20},{8,24},{12,28},{16,0},{20,4},{24,8},{28,12},{1,17},{... | collective-permute-start | bytes 786440 | tf_op jit(solution)/shard_map/ppermute | solution.py:75
  83.7 28.3 %collective-permute-start.22 = (f32[2,2,32,512]{3,2,1,0:T(8,128)S(1)}, f32[2,2,32,512]{3,2,1,0:T(8,128)S(1)}, u32[]{:S(2)}, u32[]{:S(2)}) collective-permute-start(f32[2,2,32,512]{3,2,1,0:T(8,128)S(1)} %pad_maximum_fusion.refs_0_), channel_id=1, source_target_pairs={{0,8},{4,12},{8,0},{12,4},{16,24},{20,28},{24,16},{28,20},{1,9},{5... | collective-permute-start | bytes 786440 | tf_op jit(solution)/shard_map/ppermute | solution.py:75
  85.0 6.8 %collective-permute-start.19 = (f32[2,32,512]{2,1,0:T(8,128)S(1)}, f32[2,32,512]{2,1,0:T(8,128)S(1)}, u32[]{:S(2)}, u32[]{:S(2)}) collective-permute-start(f32[2,32,512]{2,1,0:T(8,128)S(1)} %add_add_fusion), channel_id=1, source_target_pairs={{0,3},{1,2},{2,1},{3,0},{4,7},{5,6},{6,5},{7,4},{8,11},{9,10},{10,... | collective-permute-start | bytes 393224 | tf_op jit(solution)/shard_map/ppermute | solution.py:75
  86.5 11.4 %collective-permute-start.18 = (f32[2,32,512]{2,1,0:T(8,128)S(1)}, f32[2,32,512]{2,1,0:T(8,128)S(1)}, u32[]{:S(2)}, u32[]{:S(2)}) collective-permute-start(f32[2,32,512]{2,1,0:T(8,128)S(1)} %add_add_fusion), channel_id=1, source_target_pairs={{0,2},{1,3},{2,0},{3,1},{4,6},{5,7},{6,4},{7,5},{8,10},{9,11},{10,... | collective-permute-start | bytes 393224 | tf_op jit(solution)/shard_map/ppermute | solution.py:75
  91.8 20.3 %collective-permute-start.20 = (f32[2,2,32,512]{3,2,1,0:T(8,128)S(1)}, f32[2,2,32,512]{3,2,1,0:T(8,128)S(1)}, u32[]{:S(2)}, u32[]{:S(2)}) collective-permute-start(f32[2,2,32,512]{3,2,1,0:T(8,128)S(1)} %pad_maximum_fusion.refs_0_), channel_id=1, source_target_pairs={{0,4},{4,0},{8,12},{12,8},{16,20},{20,16},{24,28},{28,24},{1,5},{5... | collective-permute-start | bytes 786440 | tf_op jit(solution)/shard_map/ppermute | solution.py:75
  98.0 14.6 %collective-permute-start.27 = (f32[2,2,32,512]{3,2,1,0:T(8,128)S(1)}, f32[2,2,32,512]{3,2,1,0:T(8,128)S(1)}, u32[]{:S(2)}, u32[]{:S(2)}) collective-permute-start(f32[2,2,32,512]{3,2,1,0:T(8,128)S(1)} %pad_maximum_fusion.1.refs_1_), channel_id=1, source_target_pairs={{0,16},{4,20},{8,24},{12,28},{16,0},{20,4},{24,8},{28,12},{1,17},{... | collective-permute-start | bytes 786440 | tf_op jit(solution)/shard_map/ppermute | solution.py:75
  99.3 18.0 %collective-permute-start.23 = (f32[2,2,32,512]{3,2,1,0:T(8,128)S(1)}, f32[2,2,32,512]{3,2,1,0:T(8,128)S(1)}, u32[]{:S(2)}, u32[]{:S(2)}) collective-permute-start(f32[2,2,32,512]{3,2,1,0:T(8,128)S(1)} %pad_maximum_fusion.1.refs_1_), channel_id=1, source_target_pairs={{0,8},{4,12},{8,0},{12,4},{16,24},{20,28},{24,16},{28,20},{1,9},{5... | collective-permute-start | bytes 786440 | tf_op jit(solution)/shard_map/ppermute | solution.py:75
  112.6 8.3 %collective-permute-start.30 = (f32[2,2,32,512]{3,2,1,0:T(8,128)S(1)}, f32[2,2,32,512]{3,2,1,0:T(8,128)S(1)}, u32[]{:S(2)}, u32[]{:S(2)}) collective-permute-start(f32[2,2,32,512]{3,2,1,0:T(8,128)S(1)} %collective-permute-done.22.refs_4_), channel_id=1, source_target_pairs={{0,16},{4,20},{8,24},{12,28},{16,0},{20,4},{24,8},{28,12},{1,17},{... | collective-permute-start | bytes 786440 | tf_op jit(solution)/shard_map/ppermute | solution.py:75
  117.2 8.7 %collective-permute-start.31 = (f32[2,2,32,512]{3,2,1,0:T(8,128)S(1)}, f32[2,2,32,512]{3,2,1,0:T(8,128)S(1)}, u32[]{:S(2)}, u32[]{:S(2)}) collective-permute-start(f32[2,2,32,512]{3,2,1,0:T(8,128)S(1)} %collective-permute-done.27.refs_9_), channel_id=1, source_target_pairs={{0,8},{4,12},{8,0},{12,4},{16,24},{20,28},{24,16},{28,20},{1,9},{5... | collective-permute-start | bytes 786440 | tf_op jit(solution)/shard_map/ppermute | solution.py:75
  118.3 7.6 %collective-permute-start.29 = (f32[2,2,32,512]{3,2,1,0:T(8,128)S(1)}, f32[2,2,32,512]{3,2,1,0:T(8,128)S(1)}, u32[]{:S(2)}, u32[]{:S(2)}) collective-permute-start(f32[2,2,32,512]{3,2,1,0:T(8,128)S(1)} %collective-permute-done.27.refs_9_), channel_id=1, source_target_pairs={{0,4},{4,0},{8,12},{12,8},{16,20},{20,16},{24,28},{28,24},{1,5},{5... | collective-permute-start | bytes 786440 | tf_op jit(solution)/shard_map/ppermute | solution.py:75
  135.4 16.2 %collective-permute-start.35 = (bf16[2,32,2048]{2,1,0:T(8,128)(2,1)S(1)}, bf16[2,32,2048]{2,1,0:T(8,128)(2,1)S(1)}, u32[]{:S(2)}, u32[]{:S(2)}) collective-permute-start(bf16[2,32,2048]{2,1,0:T(8,128)(2,1)S(1)} %get-tuple-element.44), channel_id=1, source_target_pairs={{0,1},{1,0},{2,3},{3,2},{4,5},{5,4},{6,7},{7,6},{8,9},{9,8},{10,11... | collective-permute-start | bytes 786440 | tf_op jit(solution)/shard_map/ppermute | solution.py:75
  140.2 21.3 %collective-permute-start.36 = (bf16[2,32,2048]{2,1,0:T(8,128)(2,1)S(1)}, bf16[2,32,2048]{2,1,0:T(8,128)(2,1)S(1)}, u32[]{:S(2)}, u32[]{:S(2)}) collective-permute-start(bf16[2,32,2048]{2,1,0:T(8,128)(2,1)S(1)} %get-tuple-element.45), channel_id=1, source_target_pairs={{0,2},{1,3},{2,0},{3,1},{4,6},{5,7},{6,4},{7,5},{8,10},{9,11},{10,... | collective-permute-start | bytes 786440 | tf_op jit(solution)/shard_map/ppermute | solution.py:75
  141.9 19.7 %collective-permute-start.37 = (bf16[2,32,2048]{2,1,0:T(8,128)(2,1)S(1)}, bf16[2,32,2048]{2,1,0:T(8,128)(2,1)S(1)}, u32[]{:S(2)}, u32[]{:S(2)}) collective-permute-start(bf16[2,32,2048]{2,1,0:T(8,128)(2,1)S(1)} %get-tuple-element.46), channel_id=1, source_target_pairs={{0,3},{1,2},{2,1},{3,0},{4,7},{5,6},{6,5},{7,4},{8,11},{9,10},{10,... | collective-permute-start | bytes 786440 | tf_op jit(solution)/shard_map/ppermute | solution.py:75
  142.7 20.7 %collective-permute-start.38 = (bf16[2,32,2048]{2,1,0:T(8,128)(2,1)S(1)}, bf16[2,32,2048]{2,1,0:T(8,128)(2,1)S(1)}, u32[]{:S(2)}, u32[]{:S(2)}) collective-permute-start(bf16[2,32,2048]{2,1,0:T(8,128)(2,1)S(1)} %get-tuple-element.43.refs_0_), channel_id=1, source_target_pairs={{0,4},{4,0},{8,12},{12,8},{16,20},{20,16},{24,28},{28,24},{1,5},{5... | collective-permute-start | bytes 786440 | tf_op jit(solution)/shard_map/ppermute | solution.py:75
  151.5 11.9 %collective-permute-start.39 = (bf16[2,32,2048]{2,1,0:T(8,128)(2,1)S(1)}, bf16[2,32,2048]{2,1,0:T(8,128)(2,1)S(1)}, u32[]{:S(2)}, u32[]{:S(2)}) collective-permute-start(bf16[2,32,2048]{2,1,0:T(8,128)(2,1)S(1)} %collective-permute-done.35.refs_1_), channel_id=1, source_target_pairs={{0,4},{4,0},{8,12},{12,8},{16,20},{20,16},{24,28},{28,24},{1,5},{5... | collective-permute-start | bytes 786440 | tf_op jit(solution)/shard_map/ppermute | solution.py:75
  (12 other events, 40.3 us)

commit v3 on v0

--- a/solution.py
+++ b/solution.py
@@ -1,12 +1,20 @@
+import functools
 import math
 
 import jax
 import jax.numpy as jnp
 from jax import lax
+from jax.experimental import pallas as pl
+from jax.experimental.pallas import tpu as pltpu
 from jax.sharding import PartitionSpec as P
 
 LATENT = 16384
 ITERS = 3
+EPSILON = 0.64 / math.sqrt(LATENT)
+LOG2E = math.log2(math.e)
+TO_LOG2 = LOG2E / EPSILON
+CONTRACT = (((1,), (1,)), ((), ()))
+LOCAL_COST_BYTES = 8 * 2**20
 
 
 def noise_update(cost_tile, data_pot, epsilon, log_count):
@@ -25,16 +33,15 @@
     return -epsilon * (log_count + highest + jnp.log(summed))
 
 
-def per_device(noise, data):
-    epsilon = 0.64 / math.sqrt(LATENT)
-    contract = (((1,), (1,)), ((), ()))
+def per_device_tiled(noise, data):
+    epsilon = EPSILON
     noise_full = lax.all_gather(noise, "col", axis=1, tiled=True)
     noise_norm = jnp.sum(jnp.square(noise_full.astype(jnp.float32)), axis=1) / LATENT
     noise_rows = noise.shape[0]
     data_rows = data.shape[0]
     data_full = lax.all_gather(data, "row", axis=1, tiled=True)
     data_norm = jnp.sum(jnp.square(data_full.astype(jnp.float32)), axis=1) / LATENT
-    cross = lax.dot_general(noise_full, data_full, contract, preferred_element_type=jnp.float32)
+    cross = lax.dot_general(noise_full, data_full, CONTRACT, preferred_element_type=jnp.float32)
     cost_tile = noise_norm[:, None] + data_norm[None, :] - 2.0 / LATENT * cross
     log_noise = math.log(noise_rows * lax.axis_size("row"))
     log_data = math.log(data_rows * lax.axis_size("col"))
@@ -55,6 +62,331 @@
     return (targets, noise_pot, data_pot)
 
 
+VMEM = pl.BlockSpec(memory_space=pltpu.VMEM)
+WIDTH = 128
+
+
+def place():
+    return lax.axis_index("row"), lax.axis_index("col")
+
+
+def swap(array, axis, step):
+    count = lax.axis_size(axis)
+    return lax.ppermute(array, axis, [(i, i ^ step) for i in range(count)])
+
+
+def swap_core(array):
+    return swap(array, "row", 1)
+
+
+def swap_x(array):
+    return swap(array, "row", 2)
+
+
+def swap_y(array):
+    return swap(array, "row", 4)
+
+
+def after(array, *others):
+    return lax.optimization_barrier((array,) + others)[0]
+
+
+def col_exchange(pieces):
+    return [pieces[0]] + [swap(piece, "col", d) for d, piece in enumerate(pieces) if d]
+
+
+def chip_gather(pieces):
+    along_x, along_y, across = [], [], []
+    for i, piece in enumerate(pieces):
+        along_x.append(swap_x(piece))
+        along_y.append(swap_y(piece))
+        across.append(swap_x(along_y[i]) if i % 2 else swap_y(along_x[i]))
+    return [pieces, along_x, along_y, across]
+
+
+def block(index, size):
+    return pl.ds(pl.multiple_of(index * size, size), size)
+
+
+def kernel_call(kernel, outs, scratch, vmem, *operands, flops=0):
+    moved = sum(a.size * a.dtype.itemsize for a in operands)
+    return pl.pallas_call(
+        kernel,
+        in_specs=[VMEM] * len(operands),
+        out_specs=[VMEM] * len(outs),
+        out_shape=[jax.ShapeDtypeStruct(shape, dtype) for shape, dtype in outs],
+        scratch_shapes=scratch,
+        compiler_params=pltpu.CompilerParams(vmem_limit_bytes=vmem * 2**20),
+        cost_estimate=pl.CostEstimate(flops=flops, bytes_accessed=moved, transcendentals=0),
+    )(*operands)
+
+
+def deal_kernel(n_col, data_ref, noise_ref, *outs):
+    row, col = place()
+    core = lax.rem(row, 2)
+    part = data_ref.shape[1] // n_col
+    for d in range(n_col):
+        outs[d][...] = data_ref[:, block(col ^ d, part)]
+    half = noise_ref.shape[1] // 2
+    outs[n_col][...] = noise_ref[:, block(core, half)]
+    outs[n_col + 1][...] = noise_ref[:, block(1 - core, half)]
+
+
+def deal(data, noise, n_col):
+    piece = (data.shape[0], data.shape[1] // n_col)
+    half = (noise.shape[0], noise.shape[1] // 2)
+    return kernel_call(
+        functools.partial(deal_kernel, n_col),
+        [(piece, data.dtype)] * n_col + [(half, noise.dtype)] * 2,
+        [],
+        12,
+        data,
+        noise,
+    )
+
+
+def deal_noise_kernel(n_col, own_ref, other_ref, *outs):
+    _, col = place()
+    part = own_ref.shape[1] // n_col
+    for d in range(n_col):
+        outs[d][0] = own_ref[:, block(col ^ d, part)]
+        outs[d][1] = other_ref[:, block(col ^ d, part)]
+
+
+def deal_noise(own, other, n_col):
+    shape = (2, own.shape[0], own.shape[1] // n_col)
+    return kernel_call(
+        functools.partial(deal_noise_kernel, n_col), [(shape, own.dtype)] * n_col, [], 8, own, other
+    )
+
+
+def cost_kernel(n_col, n_chip, *refs):
+    noise_refs, latent_refs = refs[:n_col], refs[n_col : n_col + n_chip * n_col]
+    own_ref, other_ref, noise_all = refs[n_col + n_chip * n_col :]
+    row, col = place()
+    _, own, part = noise_refs[0].shape
+    height = latent_refs[0].shape[0]
+    for d in range(n_col):
+        noise_all[(row // 2) ^ col ^ d] = noise_refs[d][...].reshape(2 * own, part)
+    noise_norm = jnp.zeros((2 * own, 1), jnp.float32)
+    for k in range(n_chip):
+        values = noise_all[k].astype(jnp.float32)
+        noise_norm += jnp.sum(values * values, axis=1, keepdims=True)
+    for d in range(n_col):
+        cross = jnp.zeros((2 * own, height), jnp.float32)
+        squares = jnp.zeros((height, part), jnp.float32)
+        for k in range(n_chip):
+            rows = latent_refs[k * n_col + d][...]
+            cross += lax.dot_general(noise_all[k], rows, CONTRACT, preferred_element_type=jnp.float32)
+            values = rows.astype(jnp.float32)
+            squares += values * values
+        norm = jnp.sum(squares, axis=1, keepdims=True)
+        norm = jnp.broadcast_to(norm, (height, WIDTH)).T[0:1, :]
+        cost = (noise_norm + norm - 2.0 * cross) * (TO_LOG2 / LATENT)
+        lanes = block(col ^ d, height)
+        own_ref[:, lanes] = cost[:own]
+        other_ref[:, lanes] = cost[own:]
+
+
+def partial_cost(noise_pieces, latents):
+    n_chip, n_col = len(latents), len(noise_pieces)
+    _, own, part = noise_pieces[0].shape
+    width = n_col * latents[0][0].shape[0]
+    return kernel_call(
+        functools.partial(cost_kernel, n_col, n_chip),
+        [((own, width), jnp.float32)] * 2,
+        [pltpu.VMEM((n_chip, 2 * own, part), jnp.bfloat16)],
+        24,
+        *noise_pieces,
+        *[piece for group in latents for piece in group],
+        flops=4 * own * width * n_chip * part,
+    )
+
+
+def core_sum_kernel(n_col, own_ref, other_ref, *outs):
+    _, col = place()
+    share = own_ref.shape[0] // n_col
+    for d in range(n_col):
+        rows = block(col ^ d, share)
+        outs[d][...] = own_ref[rows, :] + other_ref[rows, :]
+
+
+def core_sum(own, other, n_col):
+    shape = (own.shape[0] // n_col, own.shape[1])
+    return kernel_call(
+        functools.partial(core_sum_kernel, n_col), [(shape, own.dtype)] * n_col, [], 8, own, other
+    )
+
+
+def sinkhorn_kernel(n_col, n_chip, n_half, *refs):
+    n_cost = 2 * n_chip * n_half
+    cost_refs, latent_refs = refs[:n_cost], refs[n_cost : n_cost + n_chip * n_col]
+    refs = refs[n_cost + n_chip * n_col :]
+    target_refs, refs = refs[:n_col], refs[n_col:]
+    noise_pot_ref, data_pot_ref, cost, pots, weights = refs
+    _, col = place()
+    tall, height, wide = cost.shape
+    log_noise = math.log2(tall * height)
+    log_data = math.log2(wide)
+    blocks = range(wide // WIDTH)
+    rows_of_one = height // (2 * n_half)
+    for i, ref in enumerate(cost_refs):
+        k, place_in = divmod(i, 2 * n_half)
+        cost[k, place_in * rows_of_one : (place_in + 1) * rows_of_one, :] = ref[...]
+
+    def lanes(b):
+        return pl.ds(b * WIDTH, WIDTH)
+
+    def row_update(chunk, g):
+        peak = functools.reduce(jnp.maximum, [g[b] - cost[chunk, :, lanes(b)] for b in blocks])
+        peak = jnp.max(peak, axis=1, keepdims=True)
+        total = functools.reduce(
+            jnp.add, [jnp.exp2(g[b] - cost[chunk, :, lanes(b)] - peak) for b in blocks]
+        )
+        total = jnp.sum(total, axis=1, keepdims=True)
+        return -(log_noise + peak + jnp.log2(total))
+
+    def both_updates(chunk, carry, g):
+        high, summed = carry
+        f = row_update(chunk, g)
+        new_high, new_summed = [], []
+        for b in blocks:
+            scores = f - cost[chunk, :, lanes(b)]
+            peak = jnp.max(scores, axis=0, keepdims=True)
+            total = jnp.sum(jnp.exp2(scores - peak), axis=0, keepdims=True)
+            top = jnp.maximum(high[b], peak)
+            new_high.append(top)
+            new_summed.append(summed[b] * jnp.exp2(high[b] - top) + total * jnp.exp2(peak - top))
+        return tuple(new_high), tuple(new_summed)
+
+    def iteration(_, g):
+        first = (
+            tuple(jnp.full((1, WIDTH), -jnp.inf, jnp.float32) for b in blocks),
+            tuple(jnp.zeros((1, WIDTH), jnp.float32) for b in blocks),
+        )
+        high, summed = lax.fori_loop(0, tall, lambda i, carry: both_updates(i, carry, g), first)
+        return tuple(-(log_data + high[b] + jnp.log2(summed[b])) for b in blocks)
+
+    g = tuple(jnp.zeros((1, WIDTH), jnp.float32) for b in blocks)
+    g = lax.fori_loop(0, ITERS, iteration, g)
+    for b in blocks:
+        pots[:, lanes(b)] = g[b] * (1.0 / TO_LOG2)
+    data_pot_ref[...] = pots[:, block(col, wide // n_col)]
+
+    f = row_update(0, g)
+    for b in blocks:
+        scores = (f + g[b] - cost[0, :, lanes(b)]) + log_noise
+        weights[:, lanes(b)] = jnp.exp2(scores).astype(jnp.bfloat16)
+    own = height // 2
+    share = own // n_col
+    f = jnp.broadcast_to(f[:own], (own, WIDTH)).T[0:1, :] * (1.0 / TO_LOG2)
+    for d in range(n_col):
+        noise_pot_ref[pl.ds(col ^ d, 1), :] = f[:, d * share : (d + 1) * share]
+
+    rows_of_one, part = latent_refs[0].shape
+    for k in range(n_chip):
+        product = jnp.zeros((height, part), jnp.float32)
+        for d in range(n_col):
+            product += jnp.dot(
+                weights[:, block(col ^ d, rows_of_one)],
+                latent_refs[k * n_col + d][...],
+                preferred_element_type=jnp.float32,
+            )
+        product = product.astype(jnp.bfloat16)
+        for d in range(n_col):
+            target_refs[d][0, k] = product[d * share : (d + 1) * share]
+            target_refs[d][1, k] = product[own + d * share : own + (d + 1) * share]
+
+
+def sinkhorn(tiles, latents, n_col):
+    n_chip, n_half = len(latents), len(tiles[0]) // 2
+    share_rows, width = tiles[0][0].shape
+    height = 2 * n_half * share_rows
+    part = latents[0][0].shape[1]
+    share = height // (2 * n_col)
+    size = n_chip * height * width
+    piece = ((2, n_chip, share, part), jnp.bfloat16)
+    return kernel_call(
+        functools.partial(sinkhorn_kernel, n_col, n_chip, n_half),
+        [piece] * n_col
+        + [((n_col, share), jnp.float32), ((1, width // n_col), jnp.float32)],
+        [
+            pltpu.VMEM((n_chip, height, width), jnp.float32),
+            pltpu.VMEM((1, width), jnp.float32),
+            pltpu.VMEM((height, width), jnp.bfloat16),
+        ],
+        32,
+        *[tile for group in tiles for tile in group],
+        *[piece for group in latents for piece in group],
+        flops=60 * size,
+    )
+
+
+def join_kernel(n_col, *refs):
+    *pieces, out_ref = refs
+    row, col = place()
+    _, n_chip, _, part = pieces[0].shape
+    for i, piece in enumerate(pieces):
+        other, d = divmod(i, n_col)
+        for k in range(n_chip):
+            out_ref[:, block((row ^ other ^ (2 * k)) * n_col + (col ^ d), part)] = piece[other, k]
+
+
+def join(pieces, n_col):
+    _, n_chip, share, part = pieces[0].shape
+    shape = (share, n_chip * part * len(pieces))
+    (out,) = kernel_call(
+        functools.partial(join_kernel, n_col), [(shape, pieces[0].dtype)], [], 12, *pieces
+    )
+    return out
+
+
+def per_device_local(noise, data):
+    n_col = lax.axis_size("col")
+    own, own_data = noise.shape[0], data.shape[0]
+    *dealt, own_half, other_half = deal(data, noise, n_col)
+    swapped = swap_core(other_half)
+    data_0 = dealt[0]
+    data_1, data_2, data_3 = [swap(dealt[d], "col", d) for d in (1, 2, 3)]
+    x_0, y_0 = swap_x(data_0), swap_y(data_0)
+    across_0 = swap_y(x_0)
+    x_1, y_1 = swap_x(data_1), swap_y(data_1)
+    across_1 = swap_x(y_1)
+    swapped = after(swapped, across_0, x_1, y_1, data_2)
+    noise_pieces = list(deal_noise(own_half, swapped, n_col))
+    noise_pieces[1] = swap(noise_pieces[1], "col", 1)
+    noise_pieces[2] = swap(noise_pieces[2], "col", 2)
+    x_2, y_2 = swap_x(data_2), swap_y(data_2)
+    across_2 = swap_y(x_2)
+    x_3, y_3 = swap_x(data_3), swap_y(data_3)
+    noise_pieces[3] = swap(after(noise_pieces[3], noise_pieces[1], x_2, y_2), "col", 3)
+    across_3 = swap_x(y_3)
+    latents = [
+        [data_0, data_1, data_2, data_3],
+        [x_0, x_1, x_2, x_3],
+        [y_0, y_1, y_2, y_3],
+        [across_0, across_1, across_2, across_3],
+    ]
+    own_part, other_part = partial_cost(noise_pieces, latents)
+    parts = col_exchange(core_sum(own_part, swap_core(other_part), n_col))
+    tile = functools.reduce(jnp.add, parts)
+    rows = [tile] + [swap(tile, "col", d) for d in range(1, n_col)]
+    halves = [jnp.concatenate(rows[: n_col // 2]), jnp.concatenate(rows[n_col // 2 :])]
+    tiles = [group + [swap_core(half) for half in group] for group in chip_gather(halves)]
+    *products, noise_pot, data_pot = sinkhorn(tiles, latents, n_col)
+    products = col_exchange(products)
+    targets = join(products + [swap_core(piece) for piece in products], n_col)
+    return (targets, noise_pot.reshape((own,)), data_pot.reshape((own_data,)))
+
+
+def per_device(noise, data):
+    n_row, n_col = lax.axis_size("row"), lax.axis_size("col")
+    whole = 4 * noise.shape[0] * n_row * data.shape[0] * n_col
+    if whole <= LOCAL_COST_BYTES and n_row == 8 and n_col == 4:
+        return per_device_local(noise, data)
+    return per_device_tiled(noise, data)
+
+
 def solution(mesh):
     placed = (P("row", "col"), P("col", "row"))
     return jax.shard_map(

time: 397 us -> 147 us (0.37)
  blocking collectives: 147 us -> 0 us
  waiting for transfers between devices: 213 us -> 69.6 us
  starting transfers between devices: 0.11 us -> 59.1 us
  between operations: 13.8 us -> 0.78 us
  matrix products: 11.9 us -> 0 us
  Pallas kernels: 0 us -> 11.7 us
  other arithmetic: 10.2 us -> 0.05 us
    all_gather x2 -> x0, waiting for transfers between devices: 136 us -> none  [the longest x1 84.4 us: per_device(): noise_full = lax.all_gather(noise, 'col', axis=1, tiled=True)]
    pmax x7 -> x0, blocking collectives: 78.1 us -> none  [the longest x4 42.7 us: noise_update(): highest = lax.pmax(local_peak, 'col')]
    reduce_scatter x1 -> x0, waiting for transfers between devices: 75.2 us -> none  [per_device(): lax.psum_scatter(jnp.dot(weights, data_full, preferred_element_type=jnp.f...]
    ppermute x0 -> x47, waiting for transfers between devices: none -> 69.6 us  [swap(): return lax.ppermute(array, axis, [(i, i ^ step) for i in range(count)])]
    psum x7 -> x0, blocking collectives: 69.1 us -> none  [the longest x3 35.4 us: data_update(): lax.psum(jnp.sum(jnp.exp(scores - highest[None, :]), axis=0), 'row')]
    ppermute x0 -> x47, starting transfers between devices: none -> 59.1 us  [swap(): return lax.ppermute(array, axis, [(i, i ^ step) for i in range(count)])]
    dot_general x2 -> x0, matrix products: 11.9 us -> none  [the longest x1 6.68 us: per_device(): jnp.dot(weights, data_full, preferred_element_type=jnp.float32)]
    pallas_call x0 -> x6, Pallas kernels: none -> 11.7 us  [kernel_call(): pl.pallas_call(kernel, in_specs=[VMEM] * len(operands), out_specs=[VMEM]...]
  transfers between devices with their start and end apart: 3 -> 47, of which waited for: 3 -> 21; matrix products, arithmetic and copies ran while one was open for 1% -> 0% of each run, Pallas kernels for 0% -> 0%
where the time goes in v3:
time: 147 us; the launch traced here: 144 us
  waiting for transfers between devices  69.6 us (47%)
  starting transfers between devices  59.1 us (40%)
  Pallas kernels  11.7 us (8%)
  local copies, waits for them, and re-layouts  3.06 us (2%)
    ppermute x47, waiting for transfers between devices, swap(): return lax.ppermute(array, axis, [(i, i ^ step) for i in range(count)])  69.6 us
    ppermute x47, starting transfers between devices, swap(): return lax.ppermute(array, axis, [(i, i ^ step) for i in range(count)])  59.1 us
    pallas_call x6, Pallas kernels, kernel_call(): pl.pallas_call(kernel, in_specs=[VMEM] * len(operands), out_specs=[VMEM]...  11.7 us
  transfers between devices with their start and end apart: 47, of which 21 were waited for; matrix products, arithmetic and copies ran while one was open for 0% of the time, Pallas kernels for 0%

profile of v3, /device:TPU:0, one launch (start us, length us, event | category | flops | bytes accessed | tf_op | source)
XLA Modules:
  0.0 144.2 jit_solution(3449514717960948944)
XLA Ops:
  3.2 3.1 %collective-permute-start.3 = (bf16[256,512]{1,0:T(8,128)(2,1)S(1)}, bf16[256,512]{1,0:T(8,128)(2,1)S(1)}, u32[]{:S(2)}, u32[]{:S(2)}) collective-permute-start(bf16[256,512]{1,0:T(8,128)(2,1)S(1)} %get-tuple-element.30), channel_id=1, source_target_pairs={{0,1},{1,0},{2,3},{3,2},{4,5},{5,4},{6,7},{7,6},{8,9},{9,8},{10,11... | collective-permute-start | bytes 786440 | tf_op jit(solution)/shard_map/ppermute | solution.py:75
  7.8 2.6 %collective-permute-start.6 = (bf16[256,512]{1,0:T(8,128)(2,1)S(1)}, bf16[256,512]{1,0:T(8,128)(2,1)S(1)}, u32[]{:S(2)}, u32[]{:S(2)}) collective-permute-start(bf16[256,512]{1,0:T(8,128)(2,1)S(1)} %get-tuple-element.31), channel_id=1, source_target_pairs={{0,2},{1,3},{2,0},{3,1},{4,6},{5,7},{6,4},{7,5},{8,10},{9,11},{10,... | collective-permute-start | bytes 786440 | tf_op jit(solution)/shard_map/ppermute | solution.py:75
  10.4 4.8 %collective-permute-done.3.refs_5_.refs_17_ = bf16[256,512]{1,0:T(8,128)(2,1)S(1)} collective-permute-done((bf16[256,512]{1,0:T(8,128)(2,1)S(1)}, bf16[256,512]{1,0:T(8,128)(2,1)S(1)}, u32[]{:S(2)}, u32[]{:S(2)}) %collective-permute-start.3) | collective-permute-done | bytes 262176 | tf_op jit(solution)/shard_map/ppermute | solution.py:75
  15.2 1.8 %collective-permute-start.5 = (bf16[256,512]{1,0:T(8,128)(2,1)S(1)}, bf16[256,512]{1,0:T(8,128)(2,1)S(1)}, u32[]{:S(2)}, u32[]{:S(2)}) collective-permute-start(bf16[256,512]{1,0:T(8,128)(2,1)S(1)} %collective-permute-done.3.refs_5_.refs_17_), channel_id=1, source_target_pairs={{0,16},{4,20},{8,24},{12,28},{16,0},{20,4},{24,8},{28,12},{1,17},{... | collective-permute-start | bytes 786440 | tf_op jit(solution)/shard_map/ppermute | solution.py:75
  17.0 2.8 %collective-permute-start.4 = (bf16[256,512]{1,0:T(8,128)(2,1)S(1)}, bf16[256,512]{1,0:T(8,128)(2,1)S(1)}, u32[]{:S(2)}, u32[]{:S(2)}) collective-permute-start(bf16[256,512]{1,0:T(8,128)(2,1)S(1)} %collective-permute-done.3.refs_5_.refs_17_), channel_id=1, source_target_pairs={{0,8},{4,12},{8,0},{12,4},{16,24},{20,28},{24,16},{28,20},{1,9},{5... | collective-permute-start | bytes 786440 | tf_op jit(solution)/shard_map/ppermute | solution.py:75
  20.3 2.8 %collective-permute-done.6.refs_6_.refs_18_ = bf16[256,512]{1,0:T(8,128)(2,1)S(1)} collective-permute-done((bf16[256,512]{1,0:T(8,128)(2,1)S(1)}, bf16[256,512]{1,0:T(8,128)(2,1)S(1)}, u32[]{:S(2)}, u32[]{:S(2)}) %collective-permute-start.6) | collective-permute-done | bytes 262176 | tf_op jit(solution)/shard_map/ppermute | solution.py:75
  23.1 2.5 %collective-permute-start.12 = (bf16[256,512]{1,0:T(8,128)(2,1)S(1)}, bf16[256,512]{1,0:T(8,128)(2,1)S(1)}, u32[]{:S(2)}, u32[]{:S(2)}) collective-permute-start(bf16[256,512]{1,0:T(8,128)(2,1)S(1)} %get-tuple-element.38), channel_id=1, source_target_pairs={{0,3},{1,2},{2,1},{3,0},{4,7},{5,6},{6,5},{7,4},{8,11},{9,10},{10,... | collective-permute-start | bytes 786440 | tf_op jit(solution)/shard_map/ppermute | solution.py:75
  27.1 2.0 %collective-permute-start.9 = (bf16[256,512]{1,0:T(8,128)(2,1)S(1)}, bf16[256,512]{1,0:T(8,128)(2,1)S(1)}, u32[]{:S(2)}, u32[]{:S(2)}) collective-permute-start(bf16[256,512]{1,0:T(8,128)(2,1)S(1)} %collective-permute-done.6.refs_6_.refs_18_), channel_id=1, source_target_pairs={{0,8},{4,12},{8,0},{12,4},{16,24},{20,28},{24,16},{28,20},{1,9},{5... | collective-permute-start | bytes 786440 | tf_op jit(solution)/shard_map/ppermute | solution.py:75
  30.7 3.4 %collective-permute-done.12.refs_7_.refs_19_ = bf16[256,512]{1,0:T(8,128)(2,1)S(1)} collective-permute-done((bf16[256,512]{1,0:T(8,128)(2,1)S(1)}, bf16[256,512]{1,0:T(8,128)(2,1)S(1)}, u32[]{:S(2)}, u32[]{:S(2)}) %collective-permute-start.12) | collective-permute-done | bytes 262176 | tf_op jit(solution)/shard_map/ppermute | solution.py:75
  35.7 2.8 %collective-permute-start.13 = (bf16[256,512]{1,0:T(8,128)(2,1)S(1)}, bf16[256,512]{1,0:T(8,128)(2,1)S(1)}, u32[]{:S(2)}, u32[]{:S(2)}) collective-permute-start(bf16[256,512]{1,0:T(8,128)(2,1)S(1)} %collective-permute-done.12.refs_7_.refs_19_), channel_id=1, source_target_pairs={{0,8},{4,12},{8,0},{12,4},{16,24},{20,28},{24,16},{28,20},{1,9},{5... | collective-permute-start | bytes 786440 | tf_op jit(solution)/shard_map/ppermute | solution.py:75
  39.3 1.7 %collective-permute-done.7.refs_1_ = bf16[2,128,512]{2,1,0:T(8,128)(2,1)S(1)} collective-permute-done((bf16[2,128,512]{2,1,0:T(8,128)(2,1)S(1)}, bf16[2,128,512]{2,1,0:T(8,128)(2,1)S(1)}, u32[]{:S(2)}, u32[]{:S(2)}) %collective-permute-start.7) | collective-permute-done | bytes 262176 | tf_op jit(solution)/shard_map/ppermute | solution.py:75
  43.7 2.0 %collective-permute-done.15.refs_15_.refs_27_ = bf16[256,512]{1,0:T(8,128)(2,1)S(1)} collective-permute-done((bf16[256,512]{1,0:T(8,128)(2,1)S(1)}, bf16[256,512]{1,0:T(8,128)(2,1)S(1)}, u32[]{:S(2)}, u32[]{:S(2)}) %collective-permute-start.15) | collective-permute-done | bytes 262176 | tf_op jit(solution)/shard_map/ppermute | solution.py:75
  45.7 4.1 %collective-permute-start.18 = (bf16[256,512]{1,0:T(8,128)(2,1)S(1)}, bf16[256,512]{1,0:T(8,128)(2,1)S(1)}, u32[]{:S(2)}, u32[]{:S(2)}) collective-permute-start(bf16[256,512]{1,0:T(8,128)(2,1)S(1)} %collective-permute-done.15.refs_15_.refs_27_), channel_id=1, source_target_pairs={{0,8},{4,12},{8,0},{12,4},{16,24},{20,28},{24,16},{28,20},{1,9},{5... | collective-permute-start | bytes 786440 | tf_op jit(solution)/shard_map/ppermute | solution.py:75
  49.8 2.7 %collective-permute-start.11 = (bf16[2,128,512]{2,1,0:T(8,128)(2,1)S(1)}, bf16[2,128,512]{2,1,0:T(8,128)(2,1)S(1)}, u32[]{:S(2)}, u32[]{:S(2)}) collective-permute-start(bf16[2,128,512]{2,1,0:T(8,128)(2,1)S(1)} %get-tuple-element.37), channel_id=1, source_target_pairs={{0,3},{1,2},{2,1},{3,0},{4,7},{5,6},{6,5},{7,4},{8,11},{9,10},{10,... | collective-permute-start | bytes 786440 | tf_op jit(solution)/shard_map/ppermute | solution.py:75
  52.5 1.9 %collective-permute-done.18.refs_19_.refs_31_ = bf16[256,512]{1,0:T(8,128)(2,1)S(1)} collective-permute-done((bf16[256,512]{1,0:T(8,128)(2,1)S(1)}, bf16[256,512]{1,0:T(8,128)(2,1)S(1)}, u32[]{:S(2)}, u32[]{:S(2)}) %collective-permute-start.18) | collective-permute-done | bytes 262176 | tf_op jit(solution)/shard_map/ppermute | solution.py:75
  54.4 3.6 %collective-permute-done.11.refs_3_ = bf16[2,128,512]{2,1,0:T(8,128)(2,1)S(1)} collective-permute-done((bf16[2,128,512]{2,1,0:T(8,128)(2,1)S(1)}, bf16[2,128,512]{2,1,0:T(8,128)(2,1)S(1)}, u32[]{:S(2)}, u32[]{:S(2)}) %collective-permute-start.11) | collective-permute-done | bytes 262176 | tf_op jit(solution)/shard_map/ppermute | solution.py:75
  58.0 2.0 %shard_map.51 = (f32[128,1024]{1,0:T(8,128)S(1)}, f32[128,1024]{1,0:T(8,128)S(1)}) custom-call(bf16[2,128,512]{2,1,0:T(8,128)(2,1)S(1)} %get-tuple-element.33.refs_0_, bf16[2,128,512]{2,1,0:T(8,128)(2,1)S(1)} %collective-permute-done.7.refs_1_, bf16[2,128,512]{2,1,0:T(8,128)(2,1)S(1)} %collective-permute-done.8.refs_2_, ...), custom_call_target="tpu_custom_call" | custom-call | flops 1073741824 | bytes 5242880 | tf_op jit(solution)/shard_map/pallas_call | solution.py:113
  60.1 1.9 %collective-permute-done.19.other_ref = f32[128,1024]{1,0:T(8,128)S(1)} collective-permute-done((f32[128,1024]{1,0:T(8,128)S(1)}, f32[128,1024]{1,0:T(8,128)S(1)}, u32[]{:S(2)}, u32[]{:S(2)}) %collective-permute-start.19) | collective-permute-done | bytes 524320 | tf_op jit(solution)/shard_map/ppermute | solution.py:75
  62.1 2.3 %collective-permute-start.20 = (f32[32,1024]{1,0:T(8,128)S(1)}, f32[32,1024]{1,0:T(8,128)S(1)}, u32[]{:S(2)}, u32[]{:S(2)}) collective-permute-start(f32[32,1024]{1,0:T(8,128)S(1)} %get-tuple-element.42), channel_id=1, source_target_pairs={{0,1},{1,0},{2,3},{3,2},{4,5},{5,4},{6,7},{7,6},{8,9},{9,8},{10,11... | collective-permute-start | bytes 393224 | tf_op jit(solution)/shard_map/ppermute | solution.py:75
  64.3 1.7 %collective-permute-start.21 = (f32[32,1024]{1,0:T(8,128)S(1)}, f32[32,1024]{1,0:T(8,128)S(1)}, u32[]{:S(2)}, u32[]{:S(2)}) collective-permute-start(f32[32,1024]{1,0:T(8,128)S(1)} %get-tuple-element.43), channel_id=1, source_target_pairs={{0,2},{1,3},{2,0},{3,1},{4,6},{5,7},{6,4},{7,5},{8,10},{9,11},{10,... | collective-permute-start | bytes 393224 | tf_op jit(solution)/shard_map/ppermute | solution.py:75
  67.4 2.9 %collective-permute-done.20 = f32[32,1024]{1,0:T(8,128)S(1)} collective-permute-done((f32[32,1024]{1,0:T(8,128)S(1)}, f32[32,1024]{1,0:T(8,128)S(1)}, u32[]{:S(2)}, u32[]{:S(2)}) %collective-permute-start.20) | collective-permute-done | bytes 131104 | tf_op jit(solution)/shard_map/ppermute | solution.py:75
  70.3 6.8 %collective-permute-done.21 = f32[32,1024]{1,0:T(8,128)S(1)} collective-permute-done((f32[32,1024]{1,0:T(8,128)S(1)}, f32[32,1024]{1,0:T(8,128)S(1)}, u32[]{:S(2)}, u32[]{:S(2)}) %collective-permute-start.21) | collective-permute-done | bytes 131104 | tf_op jit(solution)/shard_map/ppermute | solution.py:75
  77.1 2.5 %collective-permute-start.23 = (f32[32,1024]{1,0:T(8,128)S(1)}, f32[32,1024]{1,0:T(8,128)S(1)}, u32[]{:S(2)}, u32[]{:S(2)}) collective-permute-start(f32[32,1024]{1,0:T(8,128)S(1)} %add_add_fusion), channel_id=1, source_target_pairs={{0,1},{1,0},{2,3},{3,2},{4,5},{5,4},{6,7},{7,6},{8,9},{9,8},{10,11... | collective-permute-start | bytes 393224 | tf_op jit(solution)/shard_map/ppermute | solution.py:75
  79.6 1.7 %collective-permute-start.24 = (f32[32,1024]{1,0:T(8,128)S(1)}, f32[32,1024]{1,0:T(8,128)S(1)}, u32[]{:S(2)}, u32[]{:S(2)}) collective-permute-start(f32[32,1024]{1,0:T(8,128)S(1)} %add_add_fusion), channel_id=1, source_target_pairs={{0,2},{1,3},{2,0},{3,1},{4,6},{5,7},{6,4},{7,5},{8,10},{9,11},{10,... | collective-permute-start | bytes 393224 | tf_op jit(solution)/shard_map/ppermute | solution.py:75
  85.9 6.5 %collective-permute-done.24 = f32[32,1024]{1,0:T(8,128)S(1)} collective-permute-done((f32[32,1024]{1,0:T(8,128)S(1)}, f32[32,1024]{1,0:T(8,128)S(1)}, u32[]{:S(2)}, u32[]{:S(2)}) %collective-permute-start.24) | collective-permute-done | bytes 131104 | tf_op jit(solution)/shard_map/ppermute | solution.py:75
  96.2 4.1 %collective-permute-done.33.refs_9_ = f32[64,1024]{1,0:T(8,128)S(1)} collective-permute-done((f32[64,1024]{1,0:T(8,128)S(1)}, f32[64,1024]{1,0:T(8,128)S(1)}, u32[]{:S(2)}, u32[]{:S(2)}) %collective-permute-start.33) | collective-permute-done | bytes 262176 | tf_op jit(solution)/shard_map/ppermute | solution.py:75
  102.4 2.0 %collective-permute-done.36.refs_12_ = f32[64,1024]{1,0:T(8,128)S(1)} collective-permute-done((f32[64,1024]{1,0:T(8,128)S(1)}, f32[64,1024]{1,0:T(8,128)S(1)}, u32[]{:S(2)}, u32[]{:S(2)}) %collective-permute-start.36) | collective-permute-done | bytes 262176 | tf_op jit(solution)/shard_map/ppermute | solution.py:75
  104.5 2.2 %collective-permute-done.37.refs_13_ = f32[64,1024]{1,0:T(8,128)S(1)} collective-permute-done((f32[64,1024]{1,0:T(8,128)S(1)}, f32[64,1024]{1,0:T(8,128)S(1)}, u32[]{:S(2)}, u32[]{:S(2)}) %collective-permute-start.37) | collective-permute-done | bytes 262176 | tf_op jit(solution)/shard_map/ppermute | solution.py:75
  108.2 8.4 %shard_map.53 = (bf16[2,4,32,512]{3,2,1,0:T(8,128)(2,1)S(1)}, bf16[2,4,32,512]{3,2,1,0:T(8,128)(2,1)S(1)}, bf16[2,4,32,512]{3,2,1,0:T(8,128)(2,1)S(1)}, bf16[2,4...) custom-call(f32[64,1024]{1,0:T(8,128)S(1)} %pad_maximum_fusion.refs_0_, ...), custom_call_target="tpu_custom_call" | custom-call | flops 62914560 | bytes 8388608 | tf_op jit(solution)/shard_map/pallas_call | solution.py:113
  116.6 3.3 %collective-permute-start.40 = (bf16[2,4,32,512]{3,2,1,0:T(8,128)(2,1)S(1)}, bf16[2,4,32,512]{3,2,1,0:T(8,128)(2,1)S(1)}, u32[]{:S(2)}, u32[]{:S(2)}) collective-permute-start(bf16[2,4,32,512]{3,2,1,0:T(8,128)(2,1)S(1)} %get-tuple-element.46), channel_id=1, source_target_pairs={{0,1},{1,0},{2,3},{3,2},{4,5},{5,4},{6,7},{7,6},{8,9},{9,8},{10,11... | collective-permute-start | bytes 786440 | tf_op jit(solution)/shard_map/ppermute | solution.py:75
  122.7 9.0 %collective-permute-done.40.refs_1_ = bf16[2,4,32,512]{3,2,1,0:T(8,128)(2,1)S(1)} collective-permute-done((bf16[2,4,32,512]{3,2,1,0:T(8,128)(2,1)S(1)}, bf16[2,4,32,512]{3,2,1,0:T(8,128)(2,1)S(1)}, u32[]{:S(2)}, u32[]{:S(2)}) %collective-permute-start.40) | collective-permute-done | bytes 262176 | tf_op jit(solution)/shard_map/ppermute | solution.py:75
  131.7 9.5 %collective-permute-done.41.refs_2_ = bf16[2,4,32,512]{3,2,1,0:T(8,128)(2,1)S(1)} collective-permute-done((bf16[2,4,32,512]{3,2,1,0:T(8,128)(2,1)S(1)}, bf16[2,4,32,512]{3,2,1,0:T(8,128)(2,1)S(1)}, u32[]{:S(2)}, u32[]{:S(2)}) %collective-permute-start.41) | collective-permute-done | bytes 262176 | tf_op jit(solution)/shard_map/ppermute | solution.py:75
  (77 shorter events, 32.1 us)
Async XLA Ops:
  3.2 12.0 %collective-permute-start.3 = (bf16[256,512]{1,0:T(8,128)(2,1)S(1)}, bf16[256,512]{1,0:T(8,128)(2,1)S(1)}, u32[]{:S(2)}, u32[]{:S(2)}) collective-permute-start(bf16[256,512]{1,0:T(8,128)(2,1)S(1)} %get-tuple-element.30), channel_id=1, source_target_pairs={{0,1},{1,0},{2,3},{3,2},{4,5},{5,4},{6,7},{7,6},{8,9},{9,8},{10,11... | collective-permute-start | bytes 786440 | tf_op jit(solution)/shard_map/ppermute | solution.py:75
  6.3 13.5 %collective-permute-start.1 = (bf16[256,512]{1,0:T(8,128)(2,1)S(1)}, bf16[256,512]{1,0:T(8,128)(2,1)S(1)}, u32[]{:S(2)}, u32[]{:S(2)}) collective-permute-start(bf16[256,512]{1,0:T(8,128)(2,1)S(1)} %get-tuple-element.29.refs_4_.refs_16_), channel_id=1, source_target_pairs={{0,8},{4,12},{8,0},{12,4},{16,24},{20,28},{24,16},{28,20},{1,9},{5... | collective-permute-start | bytes 786440 | tf_op jit(solution)/shard_map/ppermute | solution.py:75
  7.8 21.3 %collective-permute-start = (bf16[128,2048]{1,0:T(8,128)(2,1)S(1)}, bf16[128,2048]{1,0:T(8,128)(2,1)S(1)}, u32[]{:S(2)}, u32[]{:S(2)}) collective-permute-start(bf16[128,2048]{1,0:T(8,128)(2,1)S(1)} %get-tuple-element.28), channel_id=1, source_target_pairs={{0,4},{4,0},{8,12},{12,8},{16,20},{20,16},{24,28},{28,24},{1,5},{5... | collective-permute-start | bytes 1572872 | tf_op jit(solution)/shard_map/ppermute | solution.py:75
  7.8 15.3 %collective-permute-start.6 = (bf16[256,512]{1,0:T(8,128)(2,1)S(1)}, bf16[256,512]{1,0:T(8,128)(2,1)S(1)}, u32[]{:S(2)}, u32[]{:S(2)}) collective-permute-start(bf16[256,512]{1,0:T(8,128)(2,1)S(1)} %get-tuple-element.31), channel_id=1, source_target_pairs={{0,2},{1,3},{2,0},{3,1},{4,6},{5,7},{6,4},{7,5},{8,10},{9,11},{10,... | collective-permute-start | bytes 786440 | tf_op jit(solution)/shard_map/ppermute | solution.py:75
  15.2 10.4 %collective-permute-start.5 = (bf16[256,512]{1,0:T(8,128)(2,1)S(1)}, bf16[256,512]{1,0:T(8,128)(2,1)S(1)}, u32[]{:S(2)}, u32[]{:S(2)}) collective-permute-start(bf16[256,512]{1,0:T(8,128)(2,1)S(1)} %collective-permute-done.3.refs_5_.refs_17_), channel_id=1, source_target_pairs={{0,16},{4,20},{8,24},{12,28},{16,0},{20,4},{24,8},{28,12},{1,17},{... | collective-permute-start | bytes 786440 | tf_op jit(solution)/shard_map/ppermute | solution.py:75
  17.0 10.1 %collective-permute-start.4 = (bf16[256,512]{1,0:T(8,128)(2,1)S(1)}, bf16[256,512]{1,0:T(8,128)(2,1)S(1)}, u32[]{:S(2)}, u32[]{:S(2)}) collective-permute-start(bf16[256,512]{1,0:T(8,128)(2,1)S(1)} %collective-permute-done.3.refs_5_.refs_17_), channel_id=1, source_target_pairs={{0,8},{4,12},{8,0},{12,4},{16,24},{20,28},{24,16},{28,20},{1,9},{5... | collective-permute-start | bytes 786440 | tf_op jit(solution)/shard_map/ppermute | solution.py:75
  19.8 9.2 %collective-permute-start.2 = (bf16[256,512]{1,0:T(8,128)(2,1)S(1)}, bf16[256,512]{1,0:T(8,128)(2,1)S(1)}, u32[]{:S(2)}, u32[]{:S(2)}) collective-permute-start(bf16[256,512]{1,0:T(8,128)(2,1)S(1)} %collective-permute-done.1.refs_8_.refs_20_), channel_id=1, source_target_pairs={{0,16},{4,20},{8,24},{12,28},{16,0},{20,4},{24,8},{28,12},{1,17},{... | collective-permute-start | bytes 786440 | tf_op jit(solution)/shard_map/ppermute | solution.py:75
  23.1 11.0 %collective-permute-start.12 = (bf16[256,512]{1,0:T(8,128)(2,1)S(1)}, bf16[256,512]{1,0:T(8,128)(2,1)S(1)}, u32[]{:S(2)}, u32[]{:S(2)}) collective-permute-start(bf16[256,512]{1,0:T(8,128)(2,1)S(1)} %get-tuple-element.38), channel_id=1, source_target_pairs={{0,3},{1,2},{2,1},{3,0},{4,7},{5,6},{6,5},{7,4},{8,11},{9,10},{10,... | collective-permute-start | bytes 786440 | tf_op jit(solution)/shard_map/ppermute | solution.py:75
  25.6 10.1 %collective-permute-start.10 = (bf16[256,512]{1,0:T(8,128)(2,1)S(1)}, bf16[256,512]{1,0:T(8,128)(2,1)S(1)}, u32[]{:S(2)}, u32[]{:S(2)}) collective-permute-start(bf16[256,512]{1,0:T(8,128)(2,1)S(1)} %collective-permute-done.6.refs_6_.refs_18_), channel_id=1, source_target_pairs={{0,16},{4,20},{8,24},{12,28},{16,0},{20,4},{24,8},{28,12},{1,17},{... | collective-permute-start | bytes 786440 | tf_op jit(solution)/shard_map/ppermute | solution.py:75
  27.1 11.4 %collective-permute-start.9 = (bf16[256,512]{1,0:T(8,128)(2,1)S(1)}, bf16[256,512]{1,0:T(8,128)(2,1)S(1)}, u32[]{:S(2)}, u32[]{:S(2)}) collective-permute-start(bf16[256,512]{1,0:T(8,128)(2,1)S(1)} %collective-permute-done.6.refs_6_.refs_18_), channel_id=1, source_target_pairs={{0,8},{4,12},{8,0},{12,4},{16,24},{20,28},{24,16},{28,20},{1,9},{5... | collective-permute-start | bytes 786440 | tf_op jit(solution)/shard_map/ppermute | solution.py:75
  29.1 11.9 %collective-permute-start.7 = (bf16[2,128,512]{2,1,0:T(8,128)(2,1)S(1)}, bf16[2,128,512]{2,1,0:T(8,128)(2,1)S(1)}, u32[]{:S(2)}, u32[]{:S(2)}) collective-permute-start(bf16[2,128,512]{2,1,0:T(8,128)(2,1)S(1)} %get-tuple-element.34), channel_id=1, source_target_pairs={{0,1},{1,0},{2,3},{3,2},{4,5},{5,4},{6,7},{7,6},{8,9},{9,8},{10,11... | collective-permute-start | bytes 786440 | tf_op jit(solution)/shard_map/ppermute | solution.py:75
  29.2 13.0 %collective-permute-start.14 = (bf16[256,512]{1,0:T(8,128)(2,1)S(1)}, bf16[256,512]{1,0:T(8,128)(2,1)S(1)}, u32[]{:S(2)}, u32[]{:S(2)}) collective-permute-start(bf16[256,512]{1,0:T(8,128)(2,1)S(1)} %get-tuple-element.29.refs_4_.refs_16_), channel_id=1, source_target_pairs={{0,16},{4,20},{8,24},{12,28},{16,0},{20,4},{24,8},{28,12},{1,17},{... | collective-permute-start | bytes 786440 | tf_op jit(solution)/shard_map/ppermute | solution.py:75
  34.1 11.6 %collective-permute-start.15 = (bf16[256,512]{1,0:T(8,128)(2,1)S(1)}, bf16[256,512]{1,0:T(8,128)(2,1)S(1)}, u32[]{:S(2)}, u32[]{:S(2)}) collective-permute-start(bf16[256,512]{1,0:T(8,128)(2,1)S(1)} %collective-permute-done.12.refs_7_.refs_19_), channel_id=1, source_target_pairs={{0,16},{4,20},{8,24},{12,28},{16,0},{20,4},{24,8},{28,12},{1,17},{... | collective-permute-start | bytes 786440 | tf_op jit(solution)/shard_map/ppermute | solution.py:75
  35.7 14.1 %collective-permute-start.13 = (bf16[256,512]{1,0:T(8,128)(2,1)S(1)}, bf16[256,512]{1,0:T(8,128)(2,1)S(1)}, u32[]{:S(2)}, u32[]{:S(2)}) collective-permute-start(bf16[256,512]{1,0:T(8,128)(2,1)S(1)} %collective-permute-done.12.refs_7_.refs_19_), channel_id=1, source_target_pairs={{0,8},{4,12},{8,0},{12,4},{16,24},{20,28},{24,16},{28,20},{1,9},{5... | collective-permute-start | bytes 786440 | tf_op jit(solution)/shard_map/ppermute | solution.py:75
  38.5 15.9 %collective-permute-start.8 = (bf16[2,128,512]{2,1,0:T(8,128)(2,1)S(1)}, bf16[2,128,512]{2,1,0:T(8,128)(2,1)S(1)}, u32[]{:S(2)}, u32[]{:S(2)}) collective-permute-start(bf16[2,128,512]{2,1,0:T(8,128)(2,1)S(1)} %get-tuple-element.35), channel_id=1, source_target_pairs={{0,2},{1,3},{2,0},{3,1},{4,6},{5,7},{6,4},{7,5},{8,10},{9,11},{10,... | collective-permute-start | bytes 786440 | tf_op jit(solution)/shard_map/ppermute | solution.py:75
  41.0 11.5 %collective-permute-start.16 = (bf16[256,512]{1,0:T(8,128)(2,1)S(1)}, bf16[256,512]{1,0:T(8,128)(2,1)S(1)}, u32[]{:S(2)}, u32[]{:S(2)}) collective-permute-start(bf16[256,512]{1,0:T(8,128)(2,1)S(1)} %collective-permute-done.5.refs_13_.refs_25_), channel_id=1, source_target_pairs={{0,8},{4,12},{8,0},{12,4},{16,24},{20,28},{24,16},{28,20},{1,9},{5... | collective-permute-start | bytes 786440 | tf_op jit(solution)/shard_map/ppermute | solution.py:75
  42.2 10.3 %collective-permute-start.17 = (bf16[256,512]{1,0:T(8,128)(2,1)S(1)}, bf16[256,512]{1,0:T(8,128)(2,1)S(1)}, u32[]{:S(2)}, u32[]{:S(2)}) collective-permute-start(bf16[256,512]{1,0:T(8,128)(2,1)S(1)} %collective-permute-done.9.refs_10_.refs_22_), channel_id=1, source_target_pairs={{0,16},{4,20},{8,24},{12,28},{16,0},{20,4},{24,8},{28,12},{1,17},{... | collective-permute-start | bytes 786440 | tf_op jit(solution)/shard_map/ppermute | solution.py:75
  45.7 8.7 %collective-permute-start.18 = (bf16[256,512]{1,0:T(8,128)(2,1)S(1)}, bf16[256,512]{1,0:T(8,128)(2,1)S(1)}, u32[]{:S(2)}, u32[]{:S(2)}) collective-permute-start(bf16[256,512]{1,0:T(8,128)(2,1)S(1)} %collective-permute-done.15.refs_15_.refs_27_), channel_id=1, source_target_pairs={{0,8},{4,12},{8,0},{12,4},{16,24},{20,28},{24,16},{28,20},{1,9},{5... | collective-permute-start | bytes 786440 | tf_op jit(solution)/shard_map/ppermute | solution.py:75
  49.8 8.3 %collective-permute-start.11 = (bf16[2,128,512]{2,1,0:T(8,128)(2,1)S(1)}, bf16[2,128,512]{2,1,0:T(8,128)(2,1)S(1)}, u32[]{:S(2)}, u32[]{:S(2)}) collective-permute-start(bf16[2,128,512]{2,1,0:T(8,128)(2,1)S(1)} %get-tuple-element.37), channel_id=1, source_target_pairs={{0,3},{1,2},{2,1},{3,0},{4,7},{5,6},{6,5},{7,4},{8,11},{9,10},{10,... | collective-permute-start | bytes 786440 | tf_op jit(solution)/shard_map/ppermute | solution.py:75
  64.3 12.8 %collective-permute-start.21 = (f32[32,1024]{1,0:T(8,128)S(1)}, f32[32,1024]{1,0:T(8,128)S(1)}, u32[]{:S(2)}, u32[]{:S(2)}) collective-permute-start(f32[32,1024]{1,0:T(8,128)S(1)} %get-tuple-element.43), channel_id=1, source_target_pairs={{0,2},{1,3},{2,0},{3,1},{4,6},{5,7},{6,4},{7,5},{8,10},{9,11},{10,... | collective-permute-start | bytes 393224 | tf_op jit(solution)/shard_map/ppermute | solution.py:75
  66.1 11.0 %collective-permute-start.22 = (f32[32,1024]{1,0:T(8,128)S(1)}, f32[32,1024]{1,0:T(8,128)S(1)}, u32[]{:S(2)}, u32[]{:S(2)}) collective-permute-start(f32[32,1024]{1,0:T(8,128)S(1)} %get-tuple-element.44), channel_id=1, source_target_pairs={{0,3},{1,2},{2,1},{3,0},{4,7},{5,6},{6,5},{7,4},{8,11},{9,10},{10,... | collective-permute-start | bytes 393224 | tf_op jit(solution)/shard_map/ppermute | solution.py:75
  79.6 12.7 %collective-permute-start.24 = (f32[32,1024]{1,0:T(8,128)S(1)}, f32[32,1024]{1,0:T(8,128)S(1)}, u32[]{:S(2)}, u32[]{:S(2)}) collective-permute-start(f32[32,1024]{1,0:T(8,128)S(1)} %add_add_fusion), channel_id=1, source_target_pairs={{0,2},{1,3},{2,0},{3,1},{4,6},{5,7},{6,4},{7,5},{8,10},{9,11},{10,... | collective-permute-start | bytes 393224 | tf_op jit(solution)/shard_map/ppermute | solution.py:75
  81.3 11.1 %collective-permute-start.25 = (f32[32,1024]{1,0:T(8,128)S(1)}, f32[32,1024]{1,0:T(8,128)S(1)}, u32[]{:S(2)}, u32[]{:S(2)}) collective-permute-start(f32[32,1024]{1,0:T(8,128)S(1)} %add_add_fusion), channel_id=1, source_target_pairs={{0,3},{1,2},{2,1},{3,0},{4,7},{5,6},{6,5},{7,4},{8,11},{9,10},{10,... | collective-permute-start | bytes 393224 | tf_op jit(solution)/shard_map/ppermute | solution.py:75
  84.0 10.2 %collective-permute-start.32 = (f32[64,1024]{1,0:T(8,128)S(1)}, f32[64,1024]{1,0:T(8,128)S(1)}, u32[]{:S(2)}, u32[]{:S(2)}) collective-permute-start(f32[64,1024]{1,0:T(8,128)S(1)} %pad_maximum_fusion.refs_0_), channel_id=1, source_target_pairs={{0,16},{4,20},{8,24},{12,28},{16,0},{20,4},{24,8},{28,12},{1,17},{... | collective-permute-start | bytes 786440 | tf_op jit(solution)/shard_map/ppermute | solution.py:75
  85.6 8.6 %collective-permute-start.28 = (f32[64,1024]{1,0:T(8,128)S(1)}, f32[64,1024]{1,0:T(8,128)S(1)}, u32[]{:S(2)}, u32[]{:S(2)}) collective-permute-start(f32[64,1024]{1,0:T(8,128)S(1)} %pad_maximum_fusion.refs_0_), channel_id=1, source_target_pairs={{0,8},{4,12},{8,0},{12,4},{16,24},{20,28},{24,16},{28,20},{1,9},{5... | collective-permute-start | bytes 786440 | tf_op jit(solution)/shard_map/ppermute | solution.py:75
  85.9 8.8 %collective-permute-start.26 = (f32[64,1024]{1,0:T(8,128)S(1)}, f32[64,1024]{1,0:T(8,128)S(1)}, u32[]{:S(2)}, u32[]{:S(2)}) collective-permute-start(f32[64,1024]{1,0:T(8,128)S(1)} %pad_maximum_fusion.refs_0_), channel_id=1, source_target_pairs={{0,4},{4,0},{8,12},{12,8},{16,20},{20,16},{24,28},{28,24},{1,5},{5... | collective-permute-start | bytes 786440 | tf_op jit(solution)/shard_map/ppermute | solution.py:75
  94.7 9.8 %collective-permute-start.36 = (f32[64,1024]{1,0:T(8,128)S(1)}, f32[64,1024]{1,0:T(8,128)S(1)}, u32[]{:S(2)}, u32[]{:S(2)}) collective-permute-start(f32[64,1024]{1,0:T(8,128)S(1)} %collective-permute-done.28.refs_4_), channel_id=1, source_target_pairs={{0,16},{4,20},{8,24},{12,28},{16,0},{20,4},{24,8},{28,12},{1,17},{... | collective-permute-start | bytes 786440 | tf_op jit(solution)/shard_map/ppermute | solution.py:75
  116.6 15.1 %collective-permute-start.40 = (bf16[2,4,32,512]{3,2,1,0:T(8,128)(2,1)S(1)}, bf16[2,4,32,512]{3,2,1,0:T(8,128)(2,1)S(1)}, u32[]{:S(2)}, u32[]{:S(2)}) collective-permute-start(bf16[2,4,32,512]{3,2,1,0:T(8,128)(2,1)S(1)} %get-tuple-element.46), channel_id=1, source_target_pairs={{0,1},{1,0},{2,3},{3,2},{4,5},{5,4},{6,7},{7,6},{8,9},{9,8},{10,11... | collective-permute-start | bytes 786440 | tf_op jit(solution)/shard_map/ppermute | solution.py:75
  119.9 21.3 %collective-permute-start.41 = (bf16[2,4,32,512]{3,2,1,0:T(8,128)(2,1)S(1)}, bf16[2,4,32,512]{3,2,1,0:T(8,128)(2,1)S(1)}, u32[]{:S(2)}, u32[]{:S(2)}) collective-permute-start(bf16[2,4,32,512]{3,2,1,0:T(8,128)(2,1)S(1)} %get-tuple-element.47), channel_id=1, source_target_pairs={{0,2},{1,3},{2,0},{3,1},{4,6},{5,7},{6,4},{7,5},{8,10},{9,11},{10,... | collective-permute-start | bytes 786440 | tf_op jit(solution)/shard_map/ppermute | solution.py:75
  121.3 20.0 %collective-permute-start.42 = (bf16[2,4,32,512]{3,2,1,0:T(8,128)(2,1)S(1)}, bf16[2,4,32,512]{3,2,1,0:T(8,128)(2,1)S(1)}, u32[]{:S(2)}, u32[]{:S(2)}) collective-permute-start(bf16[2,4,32,512]{3,2,1,0:T(8,128)(2,1)S(1)} %get-tuple-element.48), channel_id=1, source_target_pairs={{0,3},{1,2},{2,1},{3,0},{4,7},{5,6},{6,5},{7,4},{8,11},{9,10},{10,... | collective-permute-start | bytes 786440 | tf_op jit(solution)/shard_map/ppermute | solution.py:75
  122.7 19.6 %collective-permute-start.43 = (bf16[2,4,32,512]{3,2,1,0:T(8,128)(2,1)S(1)}, bf16[2,4,32,512]{3,2,1,0:T(8,128)(2,1)S(1)}, u32[]{:S(2)}, u32[]{:S(2)}) collective-permute-start(bf16[2,4,32,512]{3,2,1,0:T(8,128)(2,1)S(1)} %get-tuple-element.45.refs_0_), channel_id=1, source_target_pairs={{0,4},{4,0},{8,12},{12,8},{16,20},{20,16},{24,28},{28,24},{1,5},{5... | collective-permute-start | bytes 786440 | tf_op jit(solution)/shard_map/ppermute | solution.py:75
  131.7 10.6 %collective-permute-start.44 = (bf16[2,4,32,512]{3,2,1,0:T(8,128)(2,1)S(1)}, bf16[2,4,32,512]{3,2,1,0:T(8,128)(2,1)S(1)}, u32[]{:S(2)}, u32[]{:S(2)}) collective-permute-start(bf16[2,4,32,512]{3,2,1,0:T(8,128)(2,1)S(1)} %collective-permute-done.40.refs_1_), channel_id=1, source_target_pairs={{0,4},{4,0},{8,12},{12,8},{16,20},{20,16},{24,28},{28,24},{1,5},{5... | collective-permute-start | bytes 786440 | tf_op jit(solution)/shard_map/ppermute | solution.py:75
  (17 other events, 78.8 us)

commit v4 on v2

--- a/solution.py
+++ b/solution.py
@@ -87,6 +87,10 @@
     return swap(array, "row", 4)
 
 
+def after(array, *others):
+    return lax.optimization_barrier((array,) + others)[0]
+
+
 def col_exchange(pieces):
     return [pieces[0]] + [swap(piece, "col", d) for d, piece in enumerate(pieces) if d]
 
@@ -163,38 +167,40 @@
 
 
 def cost_kernel(n_col, *refs):
-    noise_refs, latent_refs = refs[:4], refs[4 : 4 + 2 * n_col]
-    own_ref, other_ref, latents, noise = refs[4 + 2 * n_col :]
+    noise_refs, latent_refs, refs = refs[:4], refs[4 : 4 + 2 * n_col], refs[4 + 2 * n_col :]
+    own_ref, other_ref, *half_refs, latents, noise = refs
     row, col = place()
     x, y = lax.rem(row // 2, 2), row // 4
     own, depth = noise_refs[0].shape
     share = latent_refs[0].shape[0]
-    height = 2 * share
+    quarter = n_col * share
     for i in range(4):
         core, far = i % 2, i // 2
         noise[block(2 * core + (x ^ far), own), :] = noise_refs[i][...]
     for far in range(2):
         for d in range(n_col):
-            rows = block((col ^ d) * 2 + (y ^ far), share)
+            rows = block((y ^ far) * n_col + (col ^ d), share)
             latents[rows, :] = latent_refs[far * n_col + d][...]
+    for far in range(2):
+        for i in range(2):
+            half_refs[2 * far + i][...] = latents[block(2 * (y ^ far) + i, quarter // 2), :]
     lanes = [slice(i, i + WIDTH) for i in range(0, depth, WIDTH)]
     squares = jnp.zeros((4 * own, WIDTH), jnp.float32)
     for part in lanes:
         values = noise[:, part].astype(jnp.float32)
         squares += values * values
     noise_norm = jnp.sum(squares, axis=1, keepdims=True)
-    step = 2 * height
-    for first in range(0, n_col * height, step):
-        rows = slice(first, first + step)
+    for first in range(0, 2 * quarter, quarter):
+        rows = slice(first, first + quarter)
         cross = lax.dot_general(
             noise[...], latents[rows, :], CONTRACT, preferred_element_type=jnp.float32
         )
-        squares = jnp.zeros((step, WIDTH), jnp.float32)
+        squares = jnp.zeros((quarter, WIDTH), jnp.float32)
         for part in lanes:
             values = latents[rows, part].astype(jnp.float32)
             squares += values * values
         norm = jnp.sum(squares, axis=1, keepdims=True)
-        norm = jnp.broadcast_to(norm, (step, WIDTH)).T[0:1, :]
+        norm = jnp.broadcast_to(norm, (quarter, WIDTH)).T[0:1, :]
         cost = (noise_norm + norm - 2.0 * cross) * (TO_LOG2 / LATENT)
         for i in range(2):
             own_ref[i, :, rows] = cost[i * own : (i + 1) * own]
@@ -204,15 +210,15 @@
 def partial_cost(noise_parts, latents):
     n_col = len(latents) // 2
     own, depth = noise_parts[0].shape
-    width = 2 * n_col * latents[0].shape[0]
+    quarter = n_col * latents[0].shape[0]
     return kernel_call(
         functools.partial(cost_kernel, n_col),
-        [((2, own, width), jnp.float32)] * 2 + [((width, depth), jnp.bfloat16)],
-        [pltpu.VMEM((4 * own, depth), jnp.bfloat16)],
+        [((2, own, 2 * quarter), jnp.float32)] * 2 + [((quarter // 2, depth), jnp.bfloat16)] * 4,
+        [pltpu.VMEM((2 * quarter, depth), jnp.bfloat16), pltpu.VMEM((4 * own, depth), jnp.bfloat16)],
         24,
         *noise_parts,
         *latents,
-        flops=8 * own * width * depth,
+        flops=16 * own * quarter * depth,
     )
 
 
@@ -233,11 +239,11 @@
 
 def sinkhorn_kernel(n_col, n_half, *refs):
     n_cost = 8 * n_half
-    cost_refs, latent_refs, refs = refs[:n_cost], refs[n_cost : n_cost + 2], refs[n_cost + 2 :]
+    cost_refs, latent_refs, refs = refs[:n_cost], refs[n_cost : n_cost + 8], refs[n_cost + 8 :]
     target_refs, refs = refs[:n_col], refs[n_col:]
-    noise_pot_ref, data_pot_ref, cost, own_cost, pots, weights = refs
+    noise_pot_ref, data_pot_ref, cost, own_cost, weights = refs
     row, col = place()
-    x = lax.rem(row // 2, 2)
+    x, y = lax.rem(row // 2, 2), row // 4
     tall, height, wide = cost.shape
     log_noise = math.log2(tall * height)
     log_data = math.log2(wide)
@@ -284,10 +290,8 @@
     g = tuple(jnp.zeros((1, WIDTH), jnp.float32) for b in blocks)
     g = lax.fori_loop(0, ITERS, iteration, g)
     for b in blocks:
-        pots[:, lanes(b)] = g[b] * (1.0 / TO_LOG2)
-    width = half_wide // n_col
-    for far in range(2):
-        data_pot_ref[pl.ds(x ^ far, 1), :] = pots[:, block(far * n_col + col, width)]
+        far, first = divmod(b * WIDTH, half_wide)
+        data_pot_ref[x ^ far, :, first : first + WIDTH] = g[b] * (1.0 / TO_LOG2)
 
     for core in range(2):
         for d in range(n_col):
@@ -306,12 +310,11 @@
     step = min(depth, 512)
     for i in range(0, depth, step):
         part = slice(i, i + step)
-        product = jnp.dot(
-            weights[:, :half_wide], latent_refs[0][:, part], preferred_element_type=jnp.float32
-        )
-        product += jnp.dot(
-            weights[:, half_wide:], latent_refs[1][:, part], preferred_element_type=jnp.float32
-        )
+        product = jnp.zeros((2 * own, step), jnp.float32)
+        for j, ref in enumerate(latent_refs):
+            far_x, far_y, half = j // 4, j // 2 % 2, j % 2
+            columns = block(4 * far_x + 2 * (y ^ far_y) + half, ref.shape[0])
+            product += jnp.dot(weights[:, columns], ref[:, part], preferred_element_type=jnp.float32)
         product = product.astype(jnp.bfloat16)
         for d in range(n_col):
             target_refs[d][0, :, part] = product[d * share : (d + 1) * share]
@@ -327,11 +330,10 @@
     return kernel_call(
         functools.partial(sinkhorn_kernel, n_col, n_half),
         [((2, share, latents[0].shape[1]), jnp.bfloat16)] * n_col
-        + [((n_col, share), jnp.float32), ((2, half_wide // n_col), jnp.float32)],
+        + [((n_col, share), jnp.float32), ((2, 1, half_wide), jnp.float32)],
         [
             pltpu.VMEM((4, height, wide), jnp.float32),
             pltpu.VMEM((2 * own, wide), jnp.float32),
-            pltpu.VMEM((1, wide), jnp.float32),
             pltpu.VMEM((2 * own, wide), jnp.bfloat16),
         ],
         32,
@@ -366,22 +368,27 @@
     own, own_data = noise.shape[0], data.shape[0]
     *dealt, own_half, other_half = deal(data, noise, n_chip)
     spread = regroup([chip_swap(piece, k) for k, piece in enumerate(dealt)])
-    latents = col_exchange(spread)
+    data_0, data_1, data_2 = spread[0], swap(spread[1], "col", 1), swap(spread[2], "col", 2)
+    data_3 = swap(after(spread[3], data_1), "col", 3)
+    latents = [data_0, data_1, data_2, data_3]
     latents = latents + [swap_y(piece) for piece in latents]
     halves = [own_half, swap_core(other_half)]
-    halves = halves + [swap_x(half) for half in halves]
-    own_part, other_part, near = partial_cost(halves, latents)
-    far = swap_x(near)
+    halves = halves + [swap_x(after(halves[0], spread[0])), swap_x(after(halves[1], data_1))]
+    own_part, other_part, *near = partial_cost(halves, latents)
+    over_x = [swap_x(near[0]), swap_x(near[1])]
+    across = [swap_y(over_x[0]), swap_x(near[3])]
     parts = col_exchange(core_sum(own_part, swap_core(other_part), n_col))
     tile = functools.reduce(jnp.add, parts)
-    rows = [tile] + [swap(tile, "col", d) for d in range(1, n_col)]
-    halves = [jnp.stack(rows[: n_col // 2]), jnp.stack(rows[n_col // 2 :])]
+    tile_1, tile_2 = swap(tile, "col", 1), swap(tile, "col", 2)
+    halves = [jnp.stack([tile, tile_1]), jnp.stack([tile_2, swap(tile_2, "col", 1)])]
     tiles = [group + [swap_core(half) for half in group] for group in chip_gather(halves)]
-    *products, noise_pot, data_pot = sinkhorn(tiles, [near, far], n_col)
+    *products, noise_pot, pots = sinkhorn(tiles, list(near) + over_x + across, n_col)
     products = col_exchange(products)
     targets = join(products + [swap_core(piece) for piece in products], n_col)
-    data_pot = data_pot.reshape((2, 2, own_data // 4)).transpose((1, 0, 2))
-    return (targets, noise_pot.reshape((own,)), data_pot.reshape((own_data,)))
+    pots = pots.reshape((2, 2, n_col, own_data // 4))
+    data_pot = lax.dynamic_index_in_dim(pots, lax.axis_index("col"), 2, keepdims=False)
+    data_pot = data_pot.transpose((1, 0, 2)).reshape((own_data,))
+    return (targets, noise_pot.reshape((own,)), data_pot)
 
 
 def per_device(noise, data):

time: 167 us -> 151 us (0.904)
  waiting for transfers between devices: 105 us -> 89.4 us
    ppermute x42 -> x45, waiting for transfers between devices: 105 us -> 89.4 us  [swap(): return lax.ppermute(array, axis, [(i, i ^ step) for i in range(count)])]
    ppermute x42 -> x45, starting transfers between devices: 43.1 us -> 41.9 us  [swap(): return lax.ppermute(array, axis, [(i, i ^ step) for i in range(count)])]
  transfers between devices with their start and end apart: 42 -> 45, of which waited for: 21 -> 19; matrix products, arithmetic and copies ran while one was open for 1% -> 1% of each run, Pallas kernels for 0% -> 0%
where the time goes in v4:
time: 151 us; the launch traced here: 149 us
  waiting for transfers between devices  89.4 us (59%)
  starting transfers between devices  41.9 us (28%)
  Pallas kernels  12.7 us (8%)
  local copies, waits for them, and re-layouts  3.78 us (3%)
    ppermute x45, waiting for transfers between devices, swap(): return lax.ppermute(array, axis, [(i, i ^ step) for i in range(count)])  89.4 us
    ppermute x45, starting transfers between devices, swap(): return lax.ppermute(array, axis, [(i, i ^ step) for i in range(count)])  41.9 us
    pallas_call x6, Pallas kernels, kernel_call(): pl.pallas_call(kernel, in_specs=[VMEM] * len(operands), out_specs=[VMEM]...  12.7 us
  transfers between devices with their start and end apart: 45, of which 19 were waited for; matrix products, arithmetic and copies ran while one was open for 1% of the time, Pallas kernels for 0%

profile of v4, /device:TPU:0, one launch (start us, length us, event | category | flops | bytes accessed | tf_op | source)
XLA Modules:
  0.0 148.7 jit_solution(4941123637843985750)
XLA Ops:
  3.2 3.0 %collective-permute-start.1 = (bf16[64,2048]{1,0:T(8,128)(2,1)S(1)}, bf16[64,2048]{1,0:T(8,128)(2,1)S(1)}, u32[]{:S(2)}, u32[]{:S(2)}) collective-permute-start(bf16[64,2048]{1,0:T(8,128)(2,1)S(1)} %get-tuple-element.35), channel_id=1, source_target_pairs={{0,8},{4,12},{8,0},{12,4},{16,24},{20,28},{24,16},{28,20},{1,9},{5... | collective-permute-start | bytes 786440 | tf_op jit(solution)/shard_map/ppermute | solution.py:75
  7.8 5.6 %collective-permute-done.1.refs_1_ = bf16[64,2048]{1,0:T(8,128)(2,1)S(1)} collective-permute-done((bf16[64,2048]{1,0:T(8,128)(2,1)S(1)}, bf16[64,2048]{1,0:T(8,128)(2,1)S(1)}, u32[]{:S(2)}, u32[]{:S(2)}) %collective-permute-start.1) | collective-permute-done | bytes 262176 | tf_op jit(solution)/shard_map/ppermute | solution.py:75
  13.4 6.2 %collective-permute-done.2.refs_2_ = bf16[64,2048]{1,0:T(8,128)(2,1)S(1)} collective-permute-done((bf16[64,2048]{1,0:T(8,128)(2,1)S(1)}, bf16[64,2048]{1,0:T(8,128)(2,1)S(1)}, u32[]{:S(2)}, u32[]{:S(2)}) %collective-permute-start.2) | collective-permute-done | bytes 262176 | tf_op jit(solution)/shard_map/ppermute | solution.py:75
  19.7 1.6 %collective-permute-start.5 = (bf16[64,2048]{1,0:T(8,128)(2,1)S(1)}, bf16[64,2048]{1,0:T(8,128)(2,1)S(1)}, u32[]{:S(2)}, u32[]{:S(2)}) collective-permute-start(bf16[64,2048]{1,0:T(8,128)(2,1)S(1)} %get-tuple-element.40), channel_id=1, source_target_pairs={{0,1},{1,0},{2,3},{3,2},{4,5},{5,4},{6,7},{7,6},{8,9},{9,8},{10,11... | collective-permute-start | bytes 786440 | tf_op jit(solution)/shard_map/ppermute | solution.py:75
  23.4 2.6 %collective-permute-start.7 = (bf16[64,2048]{1,0:T(8,128)(2,1)S(1)}, bf16[64,2048]{1,0:T(8,128)(2,1)S(1)}, u32[]{:S(2)}, u32[]{:S(2)}) collective-permute-start(bf16[64,2048]{1,0:T(8,128)(2,1)S(1)} %get-tuple-element.42), channel_id=1, source_target_pairs={{0,2},{1,3},{2,0},{3,1},{4,6},{5,7},{6,4},{7,5},{8,10},{9,11},{10,... | collective-permute-start | bytes 786440 | tf_op jit(solution)/shard_map/ppermute | solution.py:75
  26.0 4.1 %collective-permute-done.5.refs_5_ = bf16[64,2048]{1,0:T(8,128)(2,1)S(1)} collective-permute-done((bf16[64,2048]{1,0:T(8,128)(2,1)S(1)}, bf16[64,2048]{1,0:T(8,128)(2,1)S(1)}, u32[]{:S(2)}, u32[]{:S(2)}) %collective-permute-start.5) | collective-permute-done | bytes 262176 | tf_op jit(solution)/shard_map/ppermute | solution.py:75
  30.1 3.2 %collective-permute-start.8 = (bf16[64,2048]{1,0:T(8,128)(2,1)S(1)}, bf16[64,2048]{1,0:T(8,128)(2,1)S(1)}, u32[]{:S(2)}, u32[]{:S(2)}) collective-permute-start(bf16[64,2048]{1,0:T(8,128)(2,1)S(1)} %get-tuple-element.44), channel_id=1, source_target_pairs={{0,3},{1,2},{2,1},{3,0},{4,7},{5,6},{6,5},{7,4},{8,11},{9,10},{10,... | collective-permute-start | bytes 786440 | tf_op jit(solution)/shard_map/ppermute | solution.py:75
  33.3 2.3 %collective-permute-start.6 = (bf16[128,2048]{1,0:T(8,128)(2,1)S(1)}, bf16[128,2048]{1,0:T(8,128)(2,1)S(1)}, u32[]{:S(2)}, u32[]{:S(2)}) collective-permute-start(bf16[128,2048]{1,0:T(8,128)(2,1)S(1)} %collective-permute-done.refs_1_), channel_id=1, source_target_pairs={{0,8},{4,12},{8,0},{12,4},{16,24},{20,28},{24,16},{28,20},{1,9},{5... | collective-permute-start | bytes 1572872 | tf_op jit(solution)/shard_map/ppermute | solution.py:75
  35.6 8.5 %collective-permute-done.7.refs_6_ = bf16[64,2048]{1,0:T(8,128)(2,1)S(1)} collective-permute-done((bf16[64,2048]{1,0:T(8,128)(2,1)S(1)}, bf16[64,2048]{1,0:T(8,128)(2,1)S(1)}, u32[]{:S(2)}, u32[]{:S(2)}) %collective-permute-start.7) | collective-permute-done | bytes 262176 | tf_op jit(solution)/shard_map/ppermute | solution.py:75
  44.5 1.7 %collective-permute-start.12 = (bf16[64,2048]{1,0:T(8,128)(2,1)S(1)}, bf16[64,2048]{1,0:T(8,128)(2,1)S(1)}, u32[]{:S(2)}, u32[]{:S(2)}) collective-permute-start(bf16[64,2048]{1,0:T(8,128)(2,1)S(1)} %collective-permute-done.8.refs_7_), channel_id=1, source_target_pairs={{0,16},{4,20},{8,24},{12,28},{16,0},{20,4},{24,8},{28,12},{1,17},{... | collective-permute-start | bytes 786440 | tf_op jit(solution)/shard_map/ppermute | solution.py:75
  46.2 5.0 %collective-permute-done.11.refs_10_ = bf16[64,2048]{1,0:T(8,128)(2,1)S(1)} collective-permute-done((bf16[64,2048]{1,0:T(8,128)(2,1)S(1)}, bf16[64,2048]{1,0:T(8,128)(2,1)S(1)}, u32[]{:S(2)}, u32[]{:S(2)}) %collective-permute-start.11) | collective-permute-done | bytes 262176 | tf_op jit(solution)/shard_map/ppermute | solution.py:75
  51.1 2.8 %collective-permute-done.12.refs_11_ = bf16[64,2048]{1,0:T(8,128)(2,1)S(1)} collective-permute-done((bf16[64,2048]{1,0:T(8,128)(2,1)S(1)}, bf16[64,2048]{1,0:T(8,128)(2,1)S(1)}, u32[]{:S(2)}, u32[]{:S(2)}) %collective-permute-start.12) | collective-permute-done | bytes 262176 | tf_op jit(solution)/shard_map/ppermute | solution.py:75
  54.0 2.2 %shard_map.51 = (f32[2,128,512]{2,1,0:T(8,128)S(1)}, f32[2,128,512]{2,1,0:T(8,128)S(1)}, bf16[128,2048]{1,0:T(8,128)(2,1)S(1)}, bf16[128,2048]{1,0:T(8,128)(2,1)...) custom-call(bf16[128,2048]{1,0:T(8,128)(2,1)S(1)} %get-tuple-element.39.refs_0_, ...), custom_call_target="tpu_custom_call" | custom-call | flops 1073741824 | bytes 4194304 | tf_op jit(solution)/shard_map/pallas_call | solution.py:113
  56.4 1.8 %collective-permute-done.13.other_ref = f32[2,128,512]{2,1,0:T(8,128)S(1)} collective-permute-done((f32[2,128,512]{2,1,0:T(8,128)S(1)}, f32[2,128,512]{2,1,0:T(8,128)S(1)}, u32[]{:S(2)}, u32[]{:S(2)}) %collective-permute-start.13) | collective-permute-done | bytes 524320 | tf_op jit(solution)/shard_map/ppermute | solution.py:75
  58.3 1.6 %collective-permute-start.14 = (f32[2,32,512]{2,1,0:T(8,128)S(1)}, f32[2,32,512]{2,1,0:T(8,128)S(1)}, u32[]{:S(2)}, u32[]{:S(2)}) collective-permute-start(f32[2,32,512]{2,1,0:T(8,128)S(1)} %get-tuple-element.48), channel_id=1, source_target_pairs={{0,1},{1,0},{2,3},{3,2},{4,5},{5,4},{6,7},{7,6},{8,9},{9,8},{10,11... | collective-permute-start | bytes 393224 | tf_op jit(solution)/shard_map/ppermute | solution.py:75
  60.9 1.8 %collective-permute-start.16 = (f32[2,32,512]{2,1,0:T(8,128)S(1)}, f32[2,32,512]{2,1,0:T(8,128)S(1)}, u32[]{:S(2)}, u32[]{:S(2)}) collective-permute-start(f32[2,32,512]{2,1,0:T(8,128)S(1)} %get-tuple-element.50), channel_id=1, source_target_pairs={{0,3},{1,2},{2,1},{3,0},{4,7},{5,6},{6,5},{7,4},{8,11},{9,10},{10,... | collective-permute-start | bytes 393224 | tf_op jit(solution)/shard_map/ppermute | solution.py:75
  62.9 2.6 %collective-permute-done.14 = f32[2,32,512]{2,1,0:T(8,128)S(1)} collective-permute-done((f32[2,32,512]{2,1,0:T(8,128)S(1)}, f32[2,32,512]{2,1,0:T(8,128)S(1)}, u32[]{:S(2)}, u32[]{:S(2)}) %collective-permute-start.14) | collective-permute-done | bytes 131104 | tf_op jit(solution)/shard_map/ppermute | solution.py:75
  65.5 7.2 %collective-permute-done.15 = f32[2,32,512]{2,1,0:T(8,128)S(1)} collective-permute-done((f32[2,32,512]{2,1,0:T(8,128)S(1)}, f32[2,32,512]{2,1,0:T(8,128)S(1)}, u32[]{:S(2)}, u32[]{:S(2)}) %collective-permute-start.15) | collective-permute-done | bytes 131104 | tf_op jit(solution)/shard_map/ppermute | solution.py:75
  72.7 2.6 %collective-permute-start.18 = (f32[2,32,512]{2,1,0:T(8,128)S(1)}, f32[2,32,512]{2,1,0:T(8,128)S(1)}, u32[]{:S(2)}, u32[]{:S(2)}) collective-permute-start(f32[2,32,512]{2,1,0:T(8,128)S(1)} %add_add_fusion), channel_id=1, source_target_pairs={{0,2},{1,3},{2,0},{3,1},{4,6},{5,7},{6,4},{7,5},{8,10},{9,11},{10,... | collective-permute-start | bytes 393224 | tf_op jit(solution)/shard_map/ppermute | solution.py:75
  76.5 4.3 %collective-permute-done.18 = f32[2,32,512]{2,1,0:T(8,128)S(1)} collective-permute-done((f32[2,32,512]{2,1,0:T(8,128)S(1)}, f32[2,32,512]{2,1,0:T(8,128)S(1)}, u32[]{:S(2)}, u32[]{:S(2)}) %collective-permute-start.18) | collective-permute-done | bytes 131104 | tf_op jit(solution)/shard_map/ppermute | solution.py:75
  85.8 7.8 %collective-permute-done.37.refs_23_ = bf16[128,2048]{1,0:T(8,128)(2,1)S(1)} collective-permute-done((bf16[128,2048]{1,0:T(8,128)(2,1)S(1)}, bf16[128,2048]{1,0:T(8,128)(2,1)S(1)}, u32[]{:S(2)}, u32[]{:S(2)}) %collective-permute-start.37) | collective-permute-done | bytes 524320 | tf_op jit(solution)/shard_map/ppermute | solution.py:75
  93.6 1.7 %collective-permute-start.27 = (f32[2,2,32,512]{3,2,1,0:T(8,128)S(1)}, f32[2,2,32,512]{3,2,1,0:T(8,128)S(1)}, u32[]{:S(2)}, u32[]{:S(2)}) collective-permute-start(f32[2,2,32,512]{3,2,1,0:T(8,128)S(1)} %pad_maximum_fusion.1.refs_1_), channel_id=1, source_target_pairs={{0,16},{4,20},{8,24},{12,28},{16,0},{20,4},{24,8},{28,12},{1,17},{... | collective-permute-start | bytes 786440 | tf_op jit(solution)/shard_map/ppermute | solution.py:75
  95.3 3.4 %collective-permute-done.22.refs_4_ = f32[2,2,32,512]{3,2,1,0:T(8,128)S(1)} collective-permute-done((f32[2,2,32,512]{3,2,1,0:T(8,128)S(1)}, f32[2,2,32,512]{3,2,1,0:T(8,128)S(1)}, u32[]{:S(2)}, u32[]{:S(2)}) %collective-permute-start.22) | collective-permute-done | bytes 262176 | tf_op jit(solution)/shard_map/ppermute | solution.py:75
  99.0 1.8 %collective-permute-start.30 = (f32[2,2,32,512]{3,2,1,0:T(8,128)S(1)}, f32[2,2,32,512]{3,2,1,0:T(8,128)S(1)}, u32[]{:S(2)}, u32[]{:S(2)}) collective-permute-start(f32[2,2,32,512]{3,2,1,0:T(8,128)S(1)} %collective-permute-done.22.refs_4_), channel_id=1, source_target_pairs={{0,16},{4,20},{8,24},{12,28},{16,0},{20,4},{24,8},{28,12},{1,17},{... | collective-permute-start | bytes 786440 | tf_op jit(solution)/shard_map/ppermute | solution.py:75
  101.0 1.8 %collective-permute-start.31 = (f32[2,2,32,512]{3,2,1,0:T(8,128)S(1)}, f32[2,2,32,512]{3,2,1,0:T(8,128)S(1)}, u32[]{:S(2)}, u32[]{:S(2)}) collective-permute-start(f32[2,2,32,512]{3,2,1,0:T(8,128)S(1)} %collective-permute-done.27.refs_9_), channel_id=1, source_target_pairs={{0,8},{4,12},{8,0},{12,4},{16,24},{20,28},{24,16},{28,20},{1,9},{5... | collective-permute-start | bytes 786440 | tf_op jit(solution)/shard_map/ppermute | solution.py:75
  102.7 5.2 %collective-permute-done.23.refs_5_ = f32[2,2,32,512]{3,2,1,0:T(8,128)S(1)} collective-permute-done((f32[2,2,32,512]{3,2,1,0:T(8,128)S(1)}, f32[2,2,32,512]{3,2,1,0:T(8,128)S(1)}, u32[]{:S(2)}, u32[]{:S(2)}) %collective-permute-start.23) | collective-permute-done | bytes 262176 | tf_op jit(solution)/shard_map/ppermute | solution.py:75
  109.0 3.2 %collective-permute-done.31.refs_13_ = f32[2,2,32,512]{3,2,1,0:T(8,128)S(1)} collective-permute-done((f32[2,2,32,512]{3,2,1,0:T(8,128)S(1)}, f32[2,2,32,512]{3,2,1,0:T(8,128)S(1)}, u32[]{:S(2)}, u32[]{:S(2)}) %collective-permute-start.31) | collective-permute-done | bytes 262176 | tf_op jit(solution)/shard_map/ppermute | solution.py:75
  113.8 9.1 %shard_map.53 = (bf16[2,32,2048]{2,1,0:T(8,128)(2,1)S(1)}, bf16[2,32,2048]{2,1,0:T(8,128)(2,1)S(1)}, bf16[2,32,2048]{2,1,0:T(8,128)(2,1)S(1)}, bf16[2,32,2048]{2...) custom-call(f32[2,2,32,512]{3,2,1,0:T(8,128)S(1)} %pad_maximum_fusion.refs_0_, ...), custom_call_target="tpu_custom_call" | custom-call | flops 62914560 | bytes 8388608 | tf_op jit(solution)/shard_map/pallas_call | solution.py:113
  122.8 1.6 %collective-permute-start.38 = (bf16[2,32,2048]{2,1,0:T(8,128)(2,1)S(1)}, bf16[2,32,2048]{2,1,0:T(8,128)(2,1)S(1)}, u32[]{:S(2)}, u32[]{:S(2)}) collective-permute-start(bf16[2,32,2048]{2,1,0:T(8,128)(2,1)S(1)} %get-tuple-element.56), channel_id=1, source_target_pairs={{0,1},{1,0},{2,3},{3,2},{4,5},{5,4},{6,7},{7,6},{8,9},{9,8},{10,11... | collective-permute-start | bytes 786440 | tf_op jit(solution)/shard_map/ppermute | solution.py:75
  125.5 1.8 %collective-permute-start.40 = (bf16[2,32,2048]{2,1,0:T(8,128)(2,1)S(1)}, bf16[2,32,2048]{2,1,0:T(8,128)(2,1)S(1)}, u32[]{:S(2)}, u32[]{:S(2)}) collective-permute-start(bf16[2,32,2048]{2,1,0:T(8,128)(2,1)S(1)} %get-tuple-element.58), channel_id=1, source_target_pairs={{0,3},{1,2},{2,1},{3,0},{4,7},{5,6},{6,5},{7,4},{8,11},{9,10},{10,... | collective-permute-start | bytes 786440 | tf_op jit(solution)/shard_map/ppermute | solution.py:75
  127.3 8.6 %collective-permute-done.38.refs_1_ = bf16[2,32,2048]{2,1,0:T(8,128)(2,1)S(1)} collective-permute-done((bf16[2,32,2048]{2,1,0:T(8,128)(2,1)S(1)}, bf16[2,32,2048]{2,1,0:T(8,128)(2,1)S(1)}, u32[]{:S(2)}, u32[]{:S(2)}) %collective-permute-start.38) | collective-permute-done | bytes 262176 | tf_op jit(solution)/shard_map/ppermute | solution.py:75
  135.9 9.9 %collective-permute-done.39.refs_2_ = bf16[2,32,2048]{2,1,0:T(8,128)(2,1)S(1)} collective-permute-done((bf16[2,32,2048]{2,1,0:T(8,128)(2,1)S(1)}, bf16[2,32,2048]{2,1,0:T(8,128)(2,1)S(1)}, u32[]{:S(2)}, u32[]{:S(2)}) %collective-permute-start.39) | collective-permute-done | bytes 262176 | tf_op jit(solution)/shard_map/ppermute | solution.py:75
  (77 shorter events, 21.4 us)
Async XLA Ops:
  3.2 10.1 %collective-permute-start.1 = (bf16[64,2048]{1,0:T(8,128)(2,1)S(1)}, bf16[64,2048]{1,0:T(8,128)(2,1)S(1)}, u32[]{:S(2)}, u32[]{:S(2)}) collective-permute-start(bf16[64,2048]{1,0:T(8,128)(2,1)S(1)} %get-tuple-element.35), channel_id=1, source_target_pairs={{0,8},{4,12},{8,0},{12,4},{16,24},{20,28},{24,16},{28,20},{1,9},{5... | collective-permute-start | bytes 786440 | tf_op jit(solution)/shard_map/ppermute | solution.py:75
  6.2 13.4 %collective-permute-start.2 = (bf16[64,2048]{1,0:T(8,128)(2,1)S(1)}, bf16[64,2048]{1,0:T(8,128)(2,1)S(1)}, u32[]{:S(2)}, u32[]{:S(2)}) collective-permute-start(bf16[64,2048]{1,0:T(8,128)(2,1)S(1)} %get-tuple-element.36), channel_id=1, source_target_pairs={{0,16},{4,20},{8,24},{12,28},{16,0},{20,4},{24,8},{28,12},{1,17},{... | collective-permute-start | bytes 786440 | tf_op jit(solution)/shard_map/ppermute | solution.py:75
  7.7 11.9 %collective-permute-start.3 = (bf16[64,2048]{1,0:T(8,128)(2,1)S(1)}, bf16[64,2048]{1,0:T(8,128)(2,1)S(1)}, u32[]{:S(2)}, u32[]{:S(2)}) collective-permute-start(bf16[64,2048]{1,0:T(8,128)(2,1)S(1)} %get-tuple-element.37), channel_id=1, source_target_pairs={{0,24},{4,28},{8,16},{12,20},{16,8},{20,12},{24,0},{28,4},{1,25},{... | collective-permute-start | bytes 786440 | tf_op jit(solution)/shard_map/ppermute | solution.py:75
  7.8 25.5 %collective-permute-start = (bf16[128,2048]{1,0:T(8,128)(2,1)S(1)}, bf16[128,2048]{1,0:T(8,128)(2,1)S(1)}, u32[]{:S(2)}, u32[]{:S(2)}) collective-permute-start(bf16[128,2048]{1,0:T(8,128)(2,1)S(1)} %get-tuple-element.33), channel_id=1, source_target_pairs={{0,4},{4,0},{8,12},{12,8},{16,20},{20,16},{24,28},{28,24},{1,5},{5... | collective-permute-start | bytes 1572872 | tf_op jit(solution)/shard_map/ppermute | solution.py:75
  19.7 10.4 %collective-permute-start.5 = (bf16[64,2048]{1,0:T(8,128)(2,1)S(1)}, bf16[64,2048]{1,0:T(8,128)(2,1)S(1)}, u32[]{:S(2)}, u32[]{:S(2)}) collective-permute-start(bf16[64,2048]{1,0:T(8,128)(2,1)S(1)} %get-tuple-element.40), channel_id=1, source_target_pairs={{0,1},{1,0},{2,3},{3,2},{4,5},{5,4},{6,7},{7,6},{8,9},{9,8},{10,11... | collective-permute-start | bytes 786440 | tf_op jit(solution)/shard_map/ppermute | solution.py:75
  21.4 14.2 %collective-permute-start.9 = (bf16[64,2048]{1,0:T(8,128)(2,1)S(1)}, bf16[64,2048]{1,0:T(8,128)(2,1)S(1)}, u32[]{:S(2)}, u32[]{:S(2)}) collective-permute-start(bf16[64,2048]{1,0:T(8,128)(2,1)S(1)} %get-tuple-element.38.refs_4_), channel_id=1, source_target_pairs={{0,16},{4,20},{8,24},{12,28},{16,0},{20,4},{24,8},{28,12},{1,17},{... | collective-permute-start | bytes 786440 | tf_op jit(solution)/shard_map/ppermute | solution.py:75
  22.9 23.3 %collective-permute-start.4 = (bf16[128,2048]{1,0:T(8,128)(2,1)S(1)}, bf16[128,2048]{1,0:T(8,128)(2,1)S(1)}, u32[]{:S(2)}, u32[]{:S(2)}) collective-permute-start(bf16[128,2048]{1,0:T(8,128)(2,1)S(1)} %get-tuple-element.39.refs_0_), channel_id=1, source_target_pairs={{0,8},{4,12},{8,0},{12,4},{16,24},{20,28},{24,16},{28,20},{1,9},{5... | collective-permute-start | bytes 1572872 | tf_op jit(solution)/shard_map/ppermute | solution.py:75
  23.4 20.7 %collective-permute-start.7 = (bf16[64,2048]{1,0:T(8,128)(2,1)S(1)}, bf16[64,2048]{1,0:T(8,128)(2,1)S(1)}, u32[]{:S(2)}, u32[]{:S(2)}) collective-permute-start(bf16[64,2048]{1,0:T(8,128)(2,1)S(1)} %get-tuple-element.42), channel_id=1, source_target_pairs={{0,2},{1,3},{2,0},{3,1},{4,6},{5,7},{6,4},{7,5},{8,10},{9,11},{10,... | collective-permute-start | bytes 786440 | tf_op jit(solution)/shard_map/ppermute | solution.py:75
  30.1 14.4 %collective-permute-start.8 = (bf16[64,2048]{1,0:T(8,128)(2,1)S(1)}, bf16[64,2048]{1,0:T(8,128)(2,1)S(1)}, u32[]{:S(2)}, u32[]{:S(2)}) collective-permute-start(bf16[64,2048]{1,0:T(8,128)(2,1)S(1)} %get-tuple-element.44), channel_id=1, source_target_pairs={{0,3},{1,2},{2,1},{3,0},{4,7},{5,6},{6,5},{7,4},{8,11},{9,10},{10,... | collective-permute-start | bytes 786440 | tf_op jit(solution)/shard_map/ppermute | solution.py:75
  33.3 20.7 %collective-permute-start.6 = (bf16[128,2048]{1,0:T(8,128)(2,1)S(1)}, bf16[128,2048]{1,0:T(8,128)(2,1)S(1)}, u32[]{:S(2)}, u32[]{:S(2)}) collective-permute-start(bf16[128,2048]{1,0:T(8,128)(2,1)S(1)} %collective-permute-done.refs_1_), channel_id=1, source_target_pairs={{0,8},{4,12},{8,0},{12,4},{16,24},{20,28},{24,16},{28,20},{1,9},{5... | collective-permute-start | bytes 1572872 | tf_op jit(solution)/shard_map/ppermute | solution.py:75
  35.6 10.5 %collective-permute-start.10 = (bf16[64,2048]{1,0:T(8,128)(2,1)S(1)}, bf16[64,2048]{1,0:T(8,128)(2,1)S(1)}, u32[]{:S(2)}, u32[]{:S(2)}) collective-permute-start(bf16[64,2048]{1,0:T(8,128)(2,1)S(1)} %collective-permute-done.5.refs_5_), channel_id=1, source_target_pairs={{0,16},{4,20},{8,24},{12,28},{16,0},{20,4},{24,8},{28,12},{1,17},{... | collective-permute-start | bytes 786440 | tf_op jit(solution)/shard_map/ppermute | solution.py:75
  44.5 9.5 %collective-permute-start.12 = (bf16[64,2048]{1,0:T(8,128)(2,1)S(1)}, bf16[64,2048]{1,0:T(8,128)(2,1)S(1)}, u32[]{:S(2)}, u32[]{:S(2)}) collective-permute-start(bf16[64,2048]{1,0:T(8,128)(2,1)S(1)} %collective-permute-done.8.refs_7_), channel_id=1, source_target_pairs={{0,16},{4,20},{8,24},{12,28},{16,0},{20,4},{24,8},{28,12},{1,17},{... | collective-permute-start | bytes 786440 | tf_op jit(solution)/shard_map/ppermute | solution.py:75
  56.3 19.0 %collective-permute-start.34 = (bf16[128,2048]{1,0:T(8,128)(2,1)S(1)}, bf16[128,2048]{1,0:T(8,128)(2,1)S(1)}, u32[]{:S(2)}, u32[]{:S(2)}) collective-permute-start(bf16[128,2048]{1,0:T(8,128)(2,1)S(1)} %get-tuple-element.51.refs_16_), channel_id=1, source_target_pairs={{0,8},{4,12},{8,0},{12,4},{16,24},{20,28},{24,16},{28,20},{1,9},{5... | collective-permute-start | bytes 1572872 | tf_op jit(solution)/shard_map/ppermute | solution.py:75
  59.8 12.9 %collective-permute-start.15 = (f32[2,32,512]{2,1,0:T(8,128)S(1)}, f32[2,32,512]{2,1,0:T(8,128)S(1)}, u32[]{:S(2)}, u32[]{:S(2)}) collective-permute-start(f32[2,32,512]{2,1,0:T(8,128)S(1)} %get-tuple-element.49), channel_id=1, source_target_pairs={{0,2},{1,3},{2,0},{3,1},{4,6},{5,7},{6,4},{7,5},{8,10},{9,11},{10,... | collective-permute-start | bytes 393224 | tf_op jit(solution)/shard_map/ppermute | solution.py:75
  60.9 11.8 %collective-permute-start.16 = (f32[2,32,512]{2,1,0:T(8,128)S(1)}, f32[2,32,512]{2,1,0:T(8,128)S(1)}, u32[]{:S(2)}, u32[]{:S(2)}) collective-permute-start(f32[2,32,512]{2,1,0:T(8,128)S(1)} %get-tuple-element.50), channel_id=1, source_target_pairs={{0,3},{1,2},{2,1},{3,0},{4,7},{5,6},{6,5},{7,4},{8,11},{9,10},{10,... | collective-permute-start | bytes 393224 | tf_op jit(solution)/shard_map/ppermute | solution.py:75
  62.7 20.2 %collective-permute-start.35 = (bf16[128,2048]{1,0:T(8,128)(2,1)S(1)}, bf16[128,2048]{1,0:T(8,128)(2,1)S(1)}, u32[]{:S(2)}, u32[]{:S(2)}) collective-permute-start(bf16[128,2048]{1,0:T(8,128)(2,1)S(1)} %get-tuple-element.52.refs_17_), channel_id=1, source_target_pairs={{0,8},{4,12},{8,0},{12,4},{16,24},{20,28},{24,16},{28,20},{1,9},{5... | collective-permute-start | bytes 1572872 | tf_op jit(solution)/shard_map/ppermute | solution.py:75
  65.5 28.1 %collective-permute-start.37 = (bf16[128,2048]{1,0:T(8,128)(2,1)S(1)}, bf16[128,2048]{1,0:T(8,128)(2,1)S(1)}, u32[]{:S(2)}, u32[]{:S(2)}) collective-permute-start(bf16[128,2048]{1,0:T(8,128)(2,1)S(1)} %get-tuple-element.54.refs_19_), channel_id=1, source_target_pairs={{0,8},{4,12},{8,0},{12,4},{16,24},{20,28},{24,16},{28,20},{1,9},{5... | collective-permute-start | bytes 1572872 | tf_op jit(solution)/shard_map/ppermute | solution.py:75
  72.7 8.1 %collective-permute-start.18 = (f32[2,32,512]{2,1,0:T(8,128)S(1)}, f32[2,32,512]{2,1,0:T(8,128)S(1)}, u32[]{:S(2)}, u32[]{:S(2)}) collective-permute-start(f32[2,32,512]{2,1,0:T(8,128)S(1)} %add_add_fusion), channel_id=1, source_target_pairs={{0,2},{1,3},{2,0},{3,1},{4,6},{5,7},{6,4},{7,5},{8,10},{9,11},{10,... | collective-permute-start | bytes 393224 | tf_op jit(solution)/shard_map/ppermute | solution.py:75
  75.3 25.5 %collective-permute-start.36 = (bf16[128,2048]{1,0:T(8,128)(2,1)S(1)}, bf16[128,2048]{1,0:T(8,128)(2,1)S(1)}, u32[]{:S(2)}, u32[]{:S(2)}) collective-permute-start(bf16[128,2048]{1,0:T(8,128)(2,1)S(1)} %collective-permute-done.34.refs_20_), channel_id=1, source_target_pairs={{0,16},{4,20},{8,24},{12,28},{16,0},{20,4},{24,8},{28,12},{1,17},{... | collective-permute-start | bytes 1572872 | tf_op jit(solution)/shard_map/ppermute | solution.py:75
  82.4 16.4 %collective-permute-start.22 = (f32[2,2,32,512]{3,2,1,0:T(8,128)S(1)}, f32[2,2,32,512]{3,2,1,0:T(8,128)S(1)}, u32[]{:S(2)}, u32[]{:S(2)}) collective-permute-start(f32[2,2,32,512]{3,2,1,0:T(8,128)S(1)} %pad_maximum_fusion.refs_0_), channel_id=1, source_target_pairs={{0,8},{4,12},{8,0},{12,4},{16,24},{20,28},{24,16},{28,20},{1,9},{5... | collective-permute-start | bytes 786440 | tf_op jit(solution)/shard_map/ppermute | solution.py:75
  82.9 16.1 %collective-permute-start.26 = (f32[2,2,32,512]{3,2,1,0:T(8,128)S(1)}, f32[2,2,32,512]{3,2,1,0:T(8,128)S(1)}, u32[]{:S(2)}, u32[]{:S(2)}) collective-permute-start(f32[2,2,32,512]{3,2,1,0:T(8,128)S(1)} %pad_maximum_fusion.refs_0_), channel_id=1, source_target_pairs={{0,16},{4,20},{8,24},{12,28},{16,0},{20,4},{24,8},{28,12},{1,17},{... | collective-permute-start | bytes 786440 | tf_op jit(solution)/shard_map/ppermute | solution.py:75
  85.7 13.3 %collective-permute-start.20 = (f32[2,2,32,512]{3,2,1,0:T(8,128)S(1)}, f32[2,2,32,512]{3,2,1,0:T(8,128)S(1)}, u32[]{:S(2)}, u32[]{:S(2)}) collective-permute-start(f32[2,2,32,512]{3,2,1,0:T(8,128)S(1)} %pad_maximum_fusion.refs_0_), channel_id=1, source_target_pairs={{0,4},{4,0},{8,12},{12,8},{16,20},{20,16},{24,28},{28,24},{1,5},{5... | collective-permute-start | bytes 786440 | tf_op jit(solution)/shard_map/ppermute | solution.py:75
  98.7 9.2 %collective-permute-start.23 = (f32[2,2,32,512]{3,2,1,0:T(8,128)S(1)}, f32[2,2,32,512]{3,2,1,0:T(8,128)S(1)}, u32[]{:S(2)}, u32[]{:S(2)}) collective-permute-start(f32[2,2,32,512]{3,2,1,0:T(8,128)S(1)} %pad_maximum_fusion.1.refs_1_), channel_id=1, source_target_pairs={{0,8},{4,12},{8,0},{12,4},{16,24},{20,28},{24,16},{28,20},{1,9},{5... | collective-permute-start | bytes 786440 | tf_op jit(solution)/shard_map/ppermute | solution.py:75
  99.0 8.9 %collective-permute-start.21 = (f32[2,2,32,512]{3,2,1,0:T(8,128)S(1)}, f32[2,2,32,512]{3,2,1,0:T(8,128)S(1)}, u32[]{:S(2)}, u32[]{:S(2)}) collective-permute-start(f32[2,2,32,512]{3,2,1,0:T(8,128)S(1)} %pad_maximum_fusion.1.refs_1_), channel_id=1, source_target_pairs={{0,4},{4,0},{8,12},{12,8},{16,20},{20,16},{24,28},{28,24},{1,5},{5... | collective-permute-start | bytes 786440 | tf_op jit(solution)/shard_map/ppermute | solution.py:75
  99.0 9.5 %collective-permute-start.30 = (f32[2,2,32,512]{3,2,1,0:T(8,128)S(1)}, f32[2,2,32,512]{3,2,1,0:T(8,128)S(1)}, u32[]{:S(2)}, u32[]{:S(2)}) collective-permute-start(f32[2,2,32,512]{3,2,1,0:T(8,128)S(1)} %collective-permute-done.22.refs_4_), channel_id=1, source_target_pairs={{0,16},{4,20},{8,24},{12,28},{16,0},{20,4},{24,8},{28,12},{1,17},{... | collective-permute-start | bytes 786440 | tf_op jit(solution)/shard_map/ppermute | solution.py:75
  100.8 7.7 %collective-permute-start.24 = (f32[2,2,32,512]{3,2,1,0:T(8,128)S(1)}, f32[2,2,32,512]{3,2,1,0:T(8,128)S(1)}, u32[]{:S(2)}, u32[]{:S(2)}) collective-permute-start(f32[2,2,32,512]{3,2,1,0:T(8,128)S(1)} %collective-permute-done.22.refs_4_), channel_id=1, source_target_pairs={{0,4},{4,0},{8,12},{12,8},{16,20},{20,16},{24,28},{28,24},{1,5},{5... | collective-permute-start | bytes 786440 | tf_op jit(solution)/shard_map/ppermute | solution.py:75
  101.0 11.2 %collective-permute-start.31 = (f32[2,2,32,512]{3,2,1,0:T(8,128)S(1)}, f32[2,2,32,512]{3,2,1,0:T(8,128)S(1)}, u32[]{:S(2)}, u32[]{:S(2)}) collective-permute-start(f32[2,2,32,512]{3,2,1,0:T(8,128)S(1)} %collective-permute-done.27.refs_9_), channel_id=1, source_target_pairs={{0,8},{4,12},{8,0},{12,4},{16,24},{20,28},{24,16},{28,20},{1,9},{5... | collective-permute-start | bytes 786440 | tf_op jit(solution)/shard_map/ppermute | solution.py:75
  122.8 13.0 %collective-permute-start.38 = (bf16[2,32,2048]{2,1,0:T(8,128)(2,1)S(1)}, bf16[2,32,2048]{2,1,0:T(8,128)(2,1)S(1)}, u32[]{:S(2)}, u32[]{:S(2)}) collective-permute-start(bf16[2,32,2048]{2,1,0:T(8,128)(2,1)S(1)} %get-tuple-element.56), channel_id=1, source_target_pairs={{0,1},{1,0},{2,3},{3,2},{4,5},{5,4},{6,7},{7,6},{8,9},{9,8},{10,11... | collective-permute-start | bytes 786440 | tf_op jit(solution)/shard_map/ppermute | solution.py:75
  124.4 21.3 %collective-permute-start.39 = (bf16[2,32,2048]{2,1,0:T(8,128)(2,1)S(1)}, bf16[2,32,2048]{2,1,0:T(8,128)(2,1)S(1)}, u32[]{:S(2)}, u32[]{:S(2)}) collective-permute-start(bf16[2,32,2048]{2,1,0:T(8,128)(2,1)S(1)} %get-tuple-element.57), channel_id=1, source_target_pairs={{0,2},{1,3},{2,0},{3,1},{4,6},{5,7},{6,4},{7,5},{8,10},{9,11},{10,... | collective-permute-start | bytes 786440 | tf_op jit(solution)/shard_map/ppermute | solution.py:75
  125.5 20.2 %collective-permute-start.40 = (bf16[2,32,2048]{2,1,0:T(8,128)(2,1)S(1)}, bf16[2,32,2048]{2,1,0:T(8,128)(2,1)S(1)}, u32[]{:S(2)}, u32[]{:S(2)}) collective-permute-start(bf16[2,32,2048]{2,1,0:T(8,128)(2,1)S(1)} %get-tuple-element.58), channel_id=1, source_target_pairs={{0,3},{1,2},{2,1},{3,0},{4,7},{5,6},{6,5},{7,4},{8,11},{9,10},{10,... | collective-permute-start | bytes 786440 | tf_op jit(solution)/shard_map/ppermute | solution.py:75
  127.3 20.3 %collective-permute-start.41 = (bf16[2,32,2048]{2,1,0:T(8,128)(2,1)S(1)}, bf16[2,32,2048]{2,1,0:T(8,128)(2,1)S(1)}, u32[]{:S(2)}, u32[]{:S(2)}) collective-permute-start(bf16[2,32,2048]{2,1,0:T(8,128)(2,1)S(1)} %get-tuple-element.55.refs_0_), channel_id=1, source_target_pairs={{0,4},{4,0},{8,12},{12,8},{16,20},{20,16},{24,28},{28,24},{1,5},{5... | collective-permute-start | bytes 786440 | tf_op jit(solution)/shard_map/ppermute | solution.py:75
  135.9 11.7 %collective-permute-start.42 = (bf16[2,32,2048]{2,1,0:T(8,128)(2,1)S(1)}, bf16[2,32,2048]{2,1,0:T(8,128)(2,1)S(1)}, u32[]{:S(2)}, u32[]{:S(2)}) collective-permute-start(bf16[2,32,2048]{2,1,0:T(8,128)(2,1)S(1)} %collective-permute-done.38.refs_1_), channel_id=1, source_target_pairs={{0,4},{4,0},{8,12},{12,8},{16,20},{20,16},{24,28},{28,24},{1,5},{5... | collective-permute-start | bytes 786440 | tf_op jit(solution)/shard_map/ppermute | solution.py:75
  (15 other events, 59.5 us)

commit v5 on v3

--- a/solution.py
+++ b/solution.py
@@ -121,28 +121,29 @@
     )(*operands)
 
 
-def deal_kernel(n_col, data_ref, noise_ref, *outs):
-    row, col = place()
+def deal_kernel(n_col, data_ref, *outs):
+    _, col = place()
+    part = data_ref.shape[1] // n_col
+    for d in range(n_col):
+        outs[d][...] = data_ref[:, block(col ^ d, part)]
+
+
+def deal(data, n_col):
+    piece = (data.shape[0], data.shape[1] // n_col)
+    return kernel_call(functools.partial(deal_kernel, n_col), [(piece, data.dtype)] * n_col, [], 8, data)
+
+
+def halve_kernel(noise_ref, own_ref, other_ref):
+    row, _ = place()
     core = lax.rem(row, 2)
-    part = data_ref.shape[1] // n_col
-    for d in range(n_col):
-        outs[d][...] = data_ref[:, block(col ^ d, part)]
-    half = noise_ref.shape[1] // 2
-    outs[n_col][...] = noise_ref[:, block(core, half)]
-    outs[n_col + 1][...] = noise_ref[:, block(1 - core, half)]
-
-
-def deal(data, noise, n_col):
-    piece = (data.shape[0], data.shape[1] // n_col)
+    half = own_ref.shape[1]
+    own_ref[...] = noise_ref[:, block(core, half)]
+    other_ref[...] = noise_ref[:, block(1 - core, half)]
+
+
+def halve(noise):
     half = (noise.shape[0], noise.shape[1] // 2)
-    return kernel_call(
-        functools.partial(deal_kernel, n_col),
-        [(piece, data.dtype)] * n_col + [(half, noise.dtype)] * 2,
-        [],
-        12,
-        data,
-        noise,
-    )
+    return kernel_call(halve_kernel, [(half, noise.dtype)] * 2, [], 8, noise)
 
 
 def deal_noise_kernel(n_col, own_ref, other_ref, *outs):
@@ -218,65 +219,83 @@
     )
 
 
-def sinkhorn_kernel(n_col, n_chip, n_half, *refs):
-    n_cost = 2 * n_chip * n_half
-    cost_refs, latent_refs = refs[:n_cost], refs[n_cost : n_cost + n_chip * n_col]
-    refs = refs[n_cost + n_chip * n_col :]
+def rows_of(refs, b):
+    lanes = slice(b * WIDTH, (b + 1) * WIDTH)
+    parts = []
+    for ref in refs:
+        if len(ref.shape) == 2:
+            parts.append(ref[:, lanes])
+        else:
+            parts += [ref[i, :, lanes] for i in range(ref.shape[0])]
+    return jnp.concatenate(parts)
+
+
+def row_update(refs, g, log_noise):
+    blocks = range(len(g))
+    peak = functools.reduce(jnp.maximum, [g[b] - rows_of(refs, b) for b in blocks])
+    peak = jnp.max(peak, axis=1, keepdims=True)
+    total = functools.reduce(jnp.add, [jnp.exp2(g[b] - rows_of(refs, b) - peak) for b in blocks])
+    total = jnp.sum(total, axis=1, keepdims=True)
+    return -(log_noise + peak + jnp.log2(total))
+
+
+def data_potentials(stats, wide):
+    if not stats:
+        return [jnp.zeros((1, WIDTH), jnp.float32)] * (wide // WIDTH)
+    own, other = stats
+    result = []
+    for first in range(0, wide, WIDTH):
+        lanes = slice(first, first + WIDTH)
+        peak = jnp.maximum(own[0:1, lanes], other[0:1, lanes])
+        total = own[1:2, lanes] * jnp.exp2(own[0:1, lanes] - peak)
+        total += other[1:2, lanes] * jnp.exp2(other[0:1, lanes] - peak)
+        result.append(-(math.log2(wide) + peak + jnp.log2(total)))
+    return result
+
+
+def iteration_kernel(n_groups, log_noise, *refs):
+    *refs, out_ref = refs
+    wide = out_ref.shape[1]
+    chips = [refs[i : i + 3] for i in range(0, 3 * n_groups, 3)]
+    g = data_potentials(refs[3 * n_groups :], wide)
+    potentials = [row_update(chip, g, log_noise) for chip in chips]
+    for b in range(len(g)):
+        scores = [f - rows_of(chip, b) for f, chip in zip(potentials, chips)]
+        peak = functools.reduce(jnp.maximum, [jnp.max(s, axis=0, keepdims=True) for s in scores])
+        total = functools.reduce(jnp.add, [jnp.sum(jnp.exp2(s - peak), axis=0, keepdims=True) for s in scores])
+        out_ref[0:1, b * WIDTH : (b + 1) * WIDTH] = peak
+        out_ref[1:2, b * WIDTH : (b + 1) * WIDTH] = total
+
+
+def iteration(tiles, stats, log_noise):
+    wide = tiles[0][0].shape[1]
+    operands = [piece for group in tiles for piece in group] + list(stats)
+    (own,) = kernel_call(
+        functools.partial(iteration_kernel, len(tiles), log_noise),
+        [((2, wide), jnp.float32)],
+        [],
+        16,
+        *operands,
+        flops=16 * sum(piece.size for piece in operands),
+    )
+    return own, swap_core(own)
+
+
+def target_kernel(n_col, n_chip, log_noise, *refs):
+    tiles, stats, latent_refs = refs[:6], refs[6:8], refs[8 : 8 + n_chip * n_col]
+    refs = refs[8 + n_chip * n_col :]
     target_refs, refs = refs[:n_col], refs[n_col:]
-    noise_pot_ref, data_pot_ref, cost, pots, weights = refs
+    noise_pot_ref, data_pot_ref, pots, weights = refs
     _, col = place()
-    tall, height, wide = cost.shape
-    log_noise = math.log2(tall * height)
-    log_data = math.log2(wide)
-    blocks = range(wide // WIDTH)
-    rows_of_one = height // (2 * n_half)
-    for i, ref in enumerate(cost_refs):
-        k, place_in = divmod(i, 2 * n_half)
-        cost[k, place_in * rows_of_one : (place_in + 1) * rows_of_one, :] = ref[...]
-
-    def lanes(b):
-        return pl.ds(b * WIDTH, WIDTH)
-
-    def row_update(chunk, g):
-        peak = functools.reduce(jnp.maximum, [g[b] - cost[chunk, :, lanes(b)] for b in blocks])
-        peak = jnp.max(peak, axis=1, keepdims=True)
-        total = functools.reduce(
-            jnp.add, [jnp.exp2(g[b] - cost[chunk, :, lanes(b)] - peak) for b in blocks]
-        )
-        total = jnp.sum(total, axis=1, keepdims=True)
-        return -(log_noise + peak + jnp.log2(total))
-
-    def both_updates(chunk, carry, g):
-        high, summed = carry
-        f = row_update(chunk, g)
-        new_high, new_summed = [], []
-        for b in blocks:
-            scores = f - cost[chunk, :, lanes(b)]
-            peak = jnp.max(scores, axis=0, keepdims=True)
-            total = jnp.sum(jnp.exp2(scores - peak), axis=0, keepdims=True)
-            top = jnp.maximum(high[b], peak)
-            new_high.append(top)
-            new_summed.append(summed[b] * jnp.exp2(high[b] - top) + total * jnp.exp2(peak - top))
-        return tuple(new_high), tuple(new_summed)
-
-    def iteration(_, g):
-        first = (
-            tuple(jnp.full((1, WIDTH), -jnp.inf, jnp.float32) for b in blocks),
-            tuple(jnp.zeros((1, WIDTH), jnp.float32) for b in blocks),
-        )
-        high, summed = lax.fori_loop(0, tall, lambda i, carry: both_updates(i, carry, g), first)
-        return tuple(-(log_data + high[b] + jnp.log2(summed[b])) for b in blocks)
-
-    g = tuple(jnp.zeros((1, WIDTH), jnp.float32) for b in blocks)
-    g = lax.fori_loop(0, ITERS, iteration, g)
-    for b in blocks:
-        pots[:, lanes(b)] = g[b] * (1.0 / TO_LOG2)
+    height, wide = weights.shape
+    g = data_potentials(stats, wide)
+    f = row_update(tiles, g, log_noise)
+    for b in range(len(g)):
+        lanes = slice(b * WIDTH, (b + 1) * WIDTH)
+        pots[:, lanes] = g[b] * (1.0 / TO_LOG2)
+        scores = (f + g[b] - rows_of(tiles, b)) + log_noise
+        weights[:, lanes] = jnp.exp2(scores).astype(jnp.bfloat16)
     data_pot_ref[...] = pots[:, block(col, wide // n_col)]
-
-    f = row_update(0, g)
-    for b in blocks:
-        scores = (f + g[b] - cost[0, :, lanes(b)]) + log_noise
-        weights[:, lanes(b)] = jnp.exp2(scores).astype(jnp.bfloat16)
     own = height // 2
     share = own // n_col
     f = jnp.broadcast_to(f[:own], (own, WIDTH)).T[0:1, :] * (1.0 / TO_LOG2)
@@ -298,27 +317,22 @@
             target_refs[d][1, k] = product[own + d * share : own + (d + 1) * share]
 
 
-def sinkhorn(tiles, latents, n_col):
-    n_chip, n_half = len(latents), len(tiles[0]) // 2
-    share_rows, width = tiles[0][0].shape
-    height = 2 * n_half * share_rows
+def make_targets(own_tiles, other_tiles, stats, latents, n_col, log_noise):
+    n_chip = len(latents)
+    share, wide = own_tiles[0].shape
+    own = n_col * share
     part = latents[0][0].shape[1]
-    share = height // (2 * n_col)
-    size = n_chip * height * width
-    piece = ((2, n_chip, share, part), jnp.bfloat16)
     return kernel_call(
-        functools.partial(sinkhorn_kernel, n_col, n_chip, n_half),
-        [piece] * n_col
-        + [((n_col, share), jnp.float32), ((1, width // n_col), jnp.float32)],
-        [
-            pltpu.VMEM((n_chip, height, width), jnp.float32),
-            pltpu.VMEM((1, width), jnp.float32),
-            pltpu.VMEM((height, width), jnp.bfloat16),
-        ],
-        32,
-        *[tile for group in tiles for tile in group],
+        functools.partial(target_kernel, n_col, n_chip, log_noise),
+        [((2, n_chip, share, part), jnp.bfloat16)] * n_col
+        + [((n_col, share), jnp.float32), ((1, wide // n_col), jnp.float32)],
+        [pltpu.VMEM((1, wide), jnp.float32), pltpu.VMEM((2 * own, wide), jnp.bfloat16)],
+        24,
+        *own_tiles,
+        *other_tiles,
+        *stats,
         *[piece for group in latents for piece in group],
-        flops=60 * size,
+        flops=4 * own * wide * n_chip * part,
     )
 
 
@@ -344,23 +358,23 @@
 def per_device_local(noise, data):
     n_col = lax.axis_size("col")
     own, own_data = noise.shape[0], data.shape[0]
-    *dealt, own_half, other_half = deal(data, noise, n_col)
-    swapped = swap_core(other_half)
-    data_0 = dealt[0]
-    data_1, data_2, data_3 = [swap(dealt[d], "col", d) for d in (1, 2, 3)]
+    data_0, *dealt = deal(data, n_col)
+    own_half, other_half = halve(noise)
+    data_1, data_2 = swap(dealt[0], "col", 1), swap(dealt[1], "col", 2)
     x_0, y_0 = swap_x(data_0), swap_y(data_0)
-    across_0 = swap_y(x_0)
-    x_1, y_1 = swap_x(data_1), swap_y(data_1)
+    noise_0, *dealt_noise = deal_noise(own_half, after(swap_core(other_half), x_0, y_0), n_col)
+    data_3 = swap(dealt[2], "col", 3)
+    across_0 = swap_y(after(x_0, noise_0))
+    x_1, y_1 = swap_x(after(data_1, noise_0)), swap_y(after(data_1, noise_0))
+    noise_1 = swap(after(dealt_noise[0], data_2), "col", 1)
     across_1 = swap_x(y_1)
-    swapped = after(swapped, across_0, x_1, y_1, data_2)
-    noise_pieces = list(deal_noise(own_half, swapped, n_col))
-    noise_pieces[1] = swap(noise_pieces[1], "col", 1)
-    noise_pieces[2] = swap(noise_pieces[2], "col", 2)
-    x_2, y_2 = swap_x(data_2), swap_y(data_2)
+    x_2, y_2 = swap_x(after(data_2, x_1)), swap_y(after(data_2, y_1, across_0))
+    noise_2 = swap(after(dealt_noise[1], data_2), "col", 2)
     across_2 = swap_y(x_2)
-    x_3, y_3 = swap_x(data_3), swap_y(data_3)
-    noise_pieces[3] = swap(after(noise_pieces[3], noise_pieces[1], x_2, y_2), "col", 3)
+    x_3, y_3 = swap_x(after(data_3, across_1, x_2, noise_1)), swap_y(after(data_3, y_2, noise_1))
+    noise_3 = swap(after(dealt_noise[2], data_3, noise_1), "col", 3)
     across_3 = swap_x(y_3)
+    noise_pieces = [noise_0, noise_1, noise_2, noise_3]
     latents = [
         [data_0, data_1, data_2, data_3],
         [x_0, x_1, x_2, x_3],
@@ -370,10 +384,24 @@
     own_part, other_part = partial_cost(noise_pieces, latents)
     parts = col_exchange(core_sum(own_part, swap_core(other_part), n_col))
     tile = functools.reduce(jnp.add, parts)
-    rows = [tile] + [swap(tile, "col", d) for d in range(1, n_col)]
-    halves = [jnp.concatenate(rows[: n_col // 2]), jnp.concatenate(rows[n_col // 2 :])]
-    tiles = [group + [swap_core(half) for half in group] for group in chip_gather(halves)]
-    *products, noise_pot, data_pot = sinkhorn(tiles, latents, n_col)
+    tile_1, tile_2 = swap(tile, "col", 1), swap(tile, "col", 2)
+    tile_3 = swap(tile_2, "col", 1)
+    x_tile, y_tile = swap_x(tile), swap_y(tile)
+    pair = jnp.stack([after(tile_1, x_tile, y_tile), tile_2])
+    x_pair, y_pair = swap_x(pair), swap_y(pair)
+    x_last, y_last = swap_x(tile_3), swap_y(tile_3)
+    tiles = [
+        [tile, pair, tile_3],
+        [x_tile, x_pair, x_last],
+        [y_tile, y_pair, y_last],
+        [swap_x(y_tile), swap_y(x_pair), swap_x(y_last)],
+    ]
+    other_tiles = [swap_core(piece) for piece in tiles[0]]
+    log_noise = math.log2(own * lax.axis_size("row"))
+    stats = ()
+    for _ in range(ITERS):
+        stats = iteration(tiles, stats, log_noise)
+    *products, noise_pot, data_pot = make_targets(tiles[0], other_tiles, stats, latents, n_col, log_noise)
     products = col_exchange(products)
     targets = join(products + [swap_core(piece) for piece in products], n_col)
     return (targets, noise_pot.reshape((own,)), data_pot.reshape((own_data,)))

time: 147 us -> 144 us (0.980)
  waiting for transfers between devices: 69.6 us -> 77.3 us
  starting transfers between devices: 59.1 us -> 52.9 us
  Pallas kernels: 11.7 us -> 8.25 us
    ppermute x47 -> x48, waiting for transfers between devices: 69.6 us -> 77.3 us  [swap(): return lax.ppermute(array, axis, [(i, i ^ step) for i in range(count)])]
    ppermute x47 -> x48, starting transfers between devices: 59.1 us -> 52.9 us  [swap(): return lax.ppermute(array, axis, [(i, i ^ step) for i in range(count)])]
    pallas_call x6 -> x10, Pallas kernels: 11.7 us -> 8.25 us  [kernel_call(): pl.pallas_call(kernel, in_specs=[VMEM] * len(operands), out_specs=[VMEM]...]
  transfers between devices with their start and end apart: 47 -> 48, of which waited for: 21 -> 26; matrix products, arithmetic and copies ran while one was open for 0% -> 0% of each run, Pallas kernels for 0% -> 2%
where the time goes in v5:
time: 144 us; the launch traced here: 142 us
  waiting for transfers between devices  77.3 us (54%)
  starting transfers between devices  52.9 us (37%)
  Pallas kernels  8.25 us (6%)
  local copies, waits for them, and re-layouts  2.44 us (2%)
    ppermute x48, waiting for transfers between devices, swap(): return lax.ppermute(array, axis, [(i, i ^ step) for i in range(count)])  77.3 us
    ppermute x48, starting transfers between devices, swap(): return lax.ppermute(array, axis, [(i, i ^ step) for i in range(count)])  52.9 us
    pallas_call x10, Pallas kernels, kernel_call(): pl.pallas_call(kernel, in_specs=[VMEM] * len(operands), out_specs=[VMEM]...  8.25 us
  transfers between devices with their start and end apart: 48, of which 26 were waited for; matrix products, arithmetic and copies ran while one was open for 0% of the time, Pallas kernels for 2%

profile of v5, /device:TPU:0, one launch (start us, length us, event | category | flops | bytes accessed | tf_op | source)
XLA Modules:
  0.0 141.6 jit_solution(12186265059863363357)
XLA Ops:
  3.2 3.0 %collective-permute-start.1 = (bf16[256,512]{1,0:T(8,128)(2,1)S(1)}, bf16[256,512]{1,0:T(8,128)(2,1)S(1)}, u32[]{:S(2)}, u32[]{:S(2)}) collective-permute-start(bf16[256,512]{1,0:T(8,128)(2,1)S(1)} %get-tuple-element.38.refs_4_.refs_8_), channel_id=1, source_target_pairs={{0,8},{4,12},{8,0},{12,4},{16,24},{20,28},{24,16},{28,20},{1,9},{5... | collective-permute-start | bytes 786440 | tf_op jit(solution)/shard_map/ppermute | solution.py:75
  6.2 1.5 %collective-permute-start.2 = (bf16[256,512]{1,0:T(8,128)(2,1)S(1)}, bf16[256,512]{1,0:T(8,128)(2,1)S(1)}, u32[]{:S(2)}, u32[]{:S(2)}) collective-permute-start(bf16[256,512]{1,0:T(8,128)(2,1)S(1)} %get-tuple-element.38.refs_4_.refs_8_), channel_id=1, source_target_pairs={{0,16},{4,20},{8,24},{12,28},{16,0},{20,4},{24,8},{28,12},{1,17},{... | collective-permute-start | bytes 786440 | tf_op jit(solution)/shard_map/ppermute | solution.py:75
  7.7 1.6 %collective-permute-start.8 = (bf16[256,512]{1,0:T(8,128)(2,1)S(1)}, bf16[256,512]{1,0:T(8,128)(2,1)S(1)}, u32[]{:S(2)}, u32[]{:S(2)}) collective-permute-start(bf16[256,512]{1,0:T(8,128)(2,1)S(1)} %get-tuple-element.49), channel_id=1, source_target_pairs={{0,1},{1,0},{2,3},{3,2},{4,5},{5,4},{6,7},{7,6},{8,9},{9,8},{10,11... | collective-permute-start | bytes 786440 | tf_op jit(solution)/shard_map/ppermute | solution.py:75
  9.3 2.6 %collective-permute-start.3 = (bf16[256,512]{1,0:T(8,128)(2,1)S(1)}, bf16[256,512]{1,0:T(8,128)(2,1)S(1)}, u32[]{:S(2)}, u32[]{:S(2)}) collective-permute-start(bf16[256,512]{1,0:T(8,128)(2,1)S(1)} %get-tuple-element.42), channel_id=1, source_target_pairs={{0,2},{1,3},{2,0},{3,1},{4,6},{5,7},{6,4},{7,5},{8,10},{9,11},{10,... | collective-permute-start | bytes 786440 | tf_op jit(solution)/shard_map/ppermute | solution.py:75
  14.0 1.6 %collective-permute-start.14 = (bf16[256,512]{1,0:T(8,128)(2,1)S(1)}, bf16[256,512]{1,0:T(8,128)(2,1)S(1)}, u32[]{:S(2)}, u32[]{:S(2)}) collective-permute-start(bf16[256,512]{1,0:T(8,128)(2,1)S(1)} %collective-permute-done.1.refs_8_.refs_12_), channel_id=1, source_target_pairs={{0,16},{4,20},{8,24},{12,28},{16,0},{20,4},{24,8},{28,12},{1,17},{... | collective-permute-start | bytes 786440 | tf_op jit(solution)/shard_map/ppermute | solution.py:75
  15.6 5.1 %collective-permute-done.8.refs_5_.refs_9_ = bf16[256,512]{1,0:T(8,128)(2,1)S(1)} collective-permute-done((bf16[256,512]{1,0:T(8,128)(2,1)S(1)}, bf16[256,512]{1,0:T(8,128)(2,1)S(1)}, u32[]{:S(2)}, u32[]{:S(2)}) %collective-permute-start.8) | collective-permute-done | bytes 262176 | tf_op jit(solution)/shard_map/ppermute | solution.py:75
  21.2 2.5 %collective-permute-start.6 = (bf16[256,512]{1,0:T(8,128)(2,1)S(1)}, bf16[256,512]{1,0:T(8,128)(2,1)S(1)}, u32[]{:S(2)}, u32[]{:S(2)}) collective-permute-start(bf16[256,512]{1,0:T(8,128)(2,1)S(1)} %get-tuple-element.47), channel_id=1, source_target_pairs={{0,3},{1,2},{2,1},{3,0},{4,7},{5,6},{6,5},{7,4},{8,11},{9,10},{10,... | collective-permute-start | bytes 786440 | tf_op jit(solution)/shard_map/ppermute | solution.py:75
  24.2 3.1 %collective-permute-done.11.refs_13_.refs_17_ = bf16[256,512]{1,0:T(8,128)(2,1)S(1)} collective-permute-done((bf16[256,512]{1,0:T(8,128)(2,1)S(1)}, bf16[256,512]{1,0:T(8,128)(2,1)S(1)}, u32[]{:S(2)}, u32[]{:S(2)}) %collective-permute-start.11) | collective-permute-done | bytes 262176 | tf_op jit(solution)/shard_map/ppermute | solution.py:75
  28.1 2.1 %collective-permute-done.9.refs_9_.refs_13_ = bf16[256,512]{1,0:T(8,128)(2,1)S(1)} collective-permute-done((bf16[256,512]{1,0:T(8,128)(2,1)S(1)}, bf16[256,512]{1,0:T(8,128)(2,1)S(1)}, u32[]{:S(2)}, u32[]{:S(2)}) %collective-permute-start.9) | collective-permute-done | bytes 262176 | tf_op jit(solution)/shard_map/ppermute | solution.py:75
  30.7 1.5 %collective-permute-start.12 = (bf16[256,512]{1,0:T(8,128)(2,1)S(1)}, bf16[256,512]{1,0:T(8,128)(2,1)S(1)}, u32[]{:S(2)}, u32[]{:S(2)}) collective-permute-start(bf16[256,512]{1,0:T(8,128)(2,1)S(1)} %collective-permute-done.11.refs_13_.refs_17_), channel_id=1, source_target_pairs={{0,8},{4,12},{8,0},{12,4},{16,24},{20,28},{24,16},{28,20},{1,9},{5... | collective-permute-start | bytes 786440 | tf_op jit(solution)/shard_map/ppermute | solution.py:75
  32.2 2.5 %collective-permute-done.4.refs_1_ = bf16[2,128,512]{2,1,0:T(8,128)(2,1)S(1)} collective-permute-done((bf16[2,128,512]{2,1,0:T(8,128)(2,1)S(1)}, bf16[2,128,512]{2,1,0:T(8,128)(2,1)S(1)}, u32[]{:S(2)}, u32[]{:S(2)}) %collective-permute-start.4) | collective-permute-done | bytes 262176 | tf_op jit(solution)/shard_map/ppermute | solution.py:75
  34.7 1.5 %collective-permute-start.16 = (bf16[256,512]{1,0:T(8,128)(2,1)S(1)}, bf16[256,512]{1,0:T(8,128)(2,1)S(1)}, u32[]{:S(2)}, u32[]{:S(2)}) collective-permute-start(bf16[256,512]{1,0:T(8,128)(2,1)S(1)} %collective-permute-done.6.refs_7_.refs_11_), channel_id=1, source_target_pairs={{0,16},{4,20},{8,24},{12,28},{16,0},{20,4},{24,8},{28,12},{1,17},{... | collective-permute-start | bytes 786440 | tf_op jit(solution)/shard_map/ppermute | solution.py:75
  37.2 2.8 %collective-permute-start.7 = (bf16[2,128,512]{2,1,0:T(8,128)(2,1)S(1)}, bf16[2,128,512]{2,1,0:T(8,128)(2,1)S(1)}, u32[]{:S(2)}, u32[]{:S(2)}) collective-permute-start(bf16[2,128,512]{2,1,0:T(8,128)(2,1)S(1)} %get-tuple-element.48), channel_id=1, source_target_pairs={{0,3},{1,2},{2,1},{3,0},{4,7},{5,6},{6,5},{7,4},{8,11},{9,10},{10,... | collective-permute-start | bytes 786440 | tf_op jit(solution)/shard_map/ppermute | solution.py:75
  40.0 2.3 %collective-permute-done.12.refs_17_.refs_21_ = bf16[256,512]{1,0:T(8,128)(2,1)S(1)} collective-permute-done((bf16[256,512]{1,0:T(8,128)(2,1)S(1)}, bf16[256,512]{1,0:T(8,128)(2,1)S(1)}, u32[]{:S(2)}, u32[]{:S(2)}) %collective-permute-start.12) | collective-permute-done | bytes 262176 | tf_op jit(solution)/shard_map/ppermute | solution.py:75
  42.6 1.8 %collective-permute-start.17 = (bf16[256,512]{1,0:T(8,128)(2,1)S(1)}, bf16[256,512]{1,0:T(8,128)(2,1)S(1)}, u32[]{:S(2)}, u32[]{:S(2)}) collective-permute-start(bf16[256,512]{1,0:T(8,128)(2,1)S(1)} %collective-permute-done.10.refs_10_.refs_14_), channel_id=1, source_target_pairs={{0,16},{4,20},{8,24},{12,28},{16,0},{20,4},{24,8},{28,12},{1,17},{... | collective-permute-start | bytes 786440 | tf_op jit(solution)/shard_map/ppermute | solution.py:75
  44.3 1.5 %collective-permute-start.18 = (bf16[256,512]{1,0:T(8,128)(2,1)S(1)}, bf16[256,512]{1,0:T(8,128)(2,1)S(1)}, u32[]{:S(2)}, u32[]{:S(2)}) collective-permute-start(bf16[256,512]{1,0:T(8,128)(2,1)S(1)} %collective-permute-done.16.refs_15_.refs_19_), channel_id=1, source_target_pairs={{0,8},{4,12},{8,0},{12,4},{16,24},{20,28},{24,16},{28,20},{1,9},{5... | collective-permute-start | bytes 786440 | tf_op jit(solution)/shard_map/ppermute | solution.py:75
  45.8 9.1 %collective-permute-done.5.refs_2_ = bf16[2,128,512]{2,1,0:T(8,128)(2,1)S(1)} collective-permute-done((bf16[2,128,512]{2,1,0:T(8,128)(2,1)S(1)}, bf16[2,128,512]{2,1,0:T(8,128)(2,1)S(1)}, u32[]{:S(2)}, u32[]{:S(2)}) %collective-permute-start.5) | collective-permute-done | bytes 262176 | tf_op jit(solution)/shard_map/ppermute | solution.py:75
  55.0 2.0 %shard_map.52 = (f32[128,1024]{1,0:T(8,128)S(1)}, f32[128,1024]{1,0:T(8,128)S(1)}) custom-call(bf16[2,128,512]{2,1,0:T(8,128)(2,1)S(1)} %get-tuple-element.40.refs_0_, bf16[2,128,512]{2,1,0:T(8,128)(2,1)S(1)} %collective-permute-done.4.refs_1_, bf16[2,128,512]{2,1,0:T(8,128)(2,1)S(1)} %collective-permute-done.5.refs_2_, ...), custom_call_target="tpu_custom_call" | custom-call | flops 1073741824 | bytes 5242880 | tf_op jit(solution)/shard_map/pallas_call | solution.py:113
  57.1 1.9 %collective-permute-done.19.other_ref = f32[128,1024]{1,0:T(8,128)S(1)} collective-permute-done((f32[128,1024]{1,0:T(8,128)S(1)}, f32[128,1024]{1,0:T(8,128)S(1)}, u32[]{:S(2)}, u32[]{:S(2)}) %collective-permute-start.19) | collective-permute-done | bytes 524320 | tf_op jit(solution)/shard_map/ppermute | solution.py:75
  59.1 6.1 %collective-permute-start.20 = (f32[32,1024]{1,0:T(8,128)S(1)}, f32[32,1024]{1,0:T(8,128)S(1)}, u32[]{:S(2)}, u32[]{:S(2)}) collective-permute-start(f32[32,1024]{1,0:T(8,128)S(1)} %get-tuple-element.59), channel_id=1, source_target_pairs={{0,1},{1,0},{2,3},{3,2},{4,5},{5,4},{6,7},{7,6},{8,9},{9,8},{10,11... | collective-permute-start | bytes 393224 | tf_op jit(solution)/shard_map/ppermute | solution.py:75
  65.6 2.1 %collective-permute-start.22 = (f32[32,1024]{1,0:T(8,128)S(1)}, f32[32,1024]{1,0:T(8,128)S(1)}, u32[]{:S(2)}, u32[]{:S(2)}) collective-permute-start(f32[32,1024]{1,0:T(8,128)S(1)} %get-tuple-element.61), channel_id=1, source_target_pairs={{0,3},{1,2},{2,1},{3,0},{4,7},{5,6},{6,5},{7,4},{8,11},{9,10},{10,... | collective-permute-start | bytes 393224 | tf_op jit(solution)/shard_map/ppermute | solution.py:75
  67.7 2.8 %collective-permute-done.20 = f32[32,1024]{1,0:T(8,128)S(1)} collective-permute-done((f32[32,1024]{1,0:T(8,128)S(1)}, f32[32,1024]{1,0:T(8,128)S(1)}, u32[]{:S(2)}, u32[]{:S(2)}) %collective-permute-start.20) | collective-permute-done | bytes 131104 | tf_op jit(solution)/shard_map/ppermute | solution.py:75
  70.5 7.6 %collective-permute-done.21 = f32[32,1024]{1,0:T(8,128)S(1)} collective-permute-done((f32[32,1024]{1,0:T(8,128)S(1)}, f32[32,1024]{1,0:T(8,128)S(1)}, u32[]{:S(2)}, u32[]{:S(2)}) %collective-permute-start.21) | collective-permute-done | bytes 131104 | tf_op jit(solution)/shard_map/ppermute | solution.py:75
  78.2 2.4 %collective-permute-start.23 = (f32[32,1024]{1,0:T(8,128)S(1)}, f32[32,1024]{1,0:T(8,128)S(1)}, u32[]{:S(2)}, u32[]{:S(2)}) collective-permute-start(f32[32,1024]{1,0:T(8,128)S(1)} %add_add_fusion.refs_0_), channel_id=1, source_target_pairs={{0,1},{1,0},{2,3},{3,2},{4,5},{5,4},{6,7},{7,6},{8,9},{9,8},{10,11... | collective-permute-start | bytes 393224 | tf_op jit(solution)/shard_map/ppermute | solution.py:75
  86.1 3.3 %collective-permute-done.26 = f32[32,1024]{1,0:T(8,128)S(1)} collective-permute-done((f32[32,1024]{1,0:T(8,128)S(1)}, f32[32,1024]{1,0:T(8,128)S(1)}, u32[]{:S(2)}, u32[]{:S(2)}) %collective-permute-start.26) | collective-permute-done | bytes 131104 | tf_op jit(solution)/shard_map/ppermute | solution.py:75
  92.7 3.1 %collective-permute-done.27.refs_2_ = f32[32,1024]{1,0:T(8,128)S(1)} collective-permute-done((f32[32,1024]{1,0:T(8,128)S(1)}, f32[32,1024]{1,0:T(8,128)S(1)}, u32[]{:S(2)}, u32[]{:S(2)}) %collective-permute-start.27) | collective-permute-done | bytes 131104 | tf_op jit(solution)/shard_map/ppermute | solution.py:75
  99.3 3.1 %collective-permute-done.34.refs_8_ = f32[32,1024]{1,0:T(8,128)S(1)} collective-permute-done((f32[32,1024]{1,0:T(8,128)S(1)}, f32[32,1024]{1,0:T(8,128)S(1)}, u32[]{:S(2)}, u32[]{:S(2)}) %collective-permute-start.34) | collective-permute-done | bytes 131104 | tf_op jit(solution)/shard_map/ppermute | solution.py:75
  104.2 3.2 %collective-permute-done.37.refs_11_ = f32[32,1024]{1,0:T(8,128)S(1)} collective-permute-done((f32[32,1024]{1,0:T(8,128)S(1)}, f32[32,1024]{1,0:T(8,128)S(1)}, u32[]{:S(2)}, u32[]{:S(2)}) %collective-permute-start.37) | collective-permute-done | bytes 131104 | tf_op jit(solution)/shard_map/ppermute | solution.py:75
  113.9 2.2 %shard_map.57 = (bf16[2,4,32,512]{3,2,1,0:T(8,128)(2,1)S(1)}, bf16[2,4,32,512]{3,2,1,0:T(8,128)(2,1)S(1)}, bf16[2,4,32,512]{3,2,1,0:T(8,128)(2,1)S(1)}, bf16[2,4...) custom-call(f32[32,1024]{1,0:T(8,128)S(1)} %add_add_fusion.refs_0_, ...), custom_call_target="tpu_custom_call" | custom-call | flops 1073741824 | bytes 5259264 | tf_op jit(solution)/shard_map/pallas_call | solution.py:113
  117.0 3.2 %collective-permute-start.42 = (bf16[2,4,32,512]{3,2,1,0:T(8,128)(2,1)S(1)}, bf16[2,4,32,512]{3,2,1,0:T(8,128)(2,1)S(1)}, u32[]{:S(2)}, u32[]{:S(2)}) collective-permute-start(bf16[2,4,32,512]{3,2,1,0:T(8,128)(2,1)S(1)} %get-tuple-element.65), channel_id=1, source_target_pairs={{0,2},{1,3},{2,0},{3,1},{4,6},{5,7},{6,4},{7,5},{8,10},{9,11},{10,... | collective-permute-start | bytes 786440 | tf_op jit(solution)/shard_map/ppermute | solution.py:75
  120.4 9.3 %collective-permute-done.41.refs_1_ = bf16[2,4,32,512]{3,2,1,0:T(8,128)(2,1)S(1)} collective-permute-done((bf16[2,4,32,512]{3,2,1,0:T(8,128)(2,1)S(1)}, bf16[2,4,32,512]{3,2,1,0:T(8,128)(2,1)S(1)}, u32[]{:S(2)}, u32[]{:S(2)}) %collective-permute-start.41) | collective-permute-done | bytes 262176 | tf_op jit(solution)/shard_map/ppermute | solution.py:75
  129.7 9.0 %collective-permute-done.42.refs_2_ = bf16[2,4,32,512]{3,2,1,0:T(8,128)(2,1)S(1)} collective-permute-done((bf16[2,4,32,512]{3,2,1,0:T(8,128)(2,1)S(1)}, bf16[2,4,32,512]{3,2,1,0:T(8,128)(2,1)S(1)}, u32[]{:S(2)}, u32[]{:S(2)}) %collective-permute-start.42) | collective-permute-done | bytes 262176 | tf_op jit(solution)/shard_map/ppermute | solution.py:75
  (81 shorter events, 33.5 us)
Async XLA Ops:
  1.9 12.0 %collective-permute-start = (bf16[128,2048]{1,0:T(8,128)(2,1)S(1)}, bf16[128,2048]{1,0:T(8,128)(2,1)S(1)}, u32[]{:S(2)}, u32[]{:S(2)}) collective-permute-start(bf16[128,2048]{1,0:T(8,128)(2,1)S(1)} %get-tuple-element.37), channel_id=1, source_target_pairs={{0,4},{4,0},{8,12},{12,8},{16,20},{20,16},{24,28},{28,24},{1,5},{5... | collective-permute-start | bytes 1572872 | tf_op jit(solution)/shard_map/ppermute | solution.py:75
  3.2 9.3 %collective-permute-start.1 = (bf16[256,512]{1,0:T(8,128)(2,1)S(1)}, bf16[256,512]{1,0:T(8,128)(2,1)S(1)}, u32[]{:S(2)}, u32[]{:S(2)}) collective-permute-start(bf16[256,512]{1,0:T(8,128)(2,1)S(1)} %get-tuple-element.38.refs_4_.refs_8_), channel_id=1, source_target_pairs={{0,8},{4,12},{8,0},{12,4},{16,24},{20,28},{24,16},{28,20},{1,9},{5... | collective-permute-start | bytes 786440 | tf_op jit(solution)/shard_map/ppermute | solution.py:75
  6.2 7.8 %collective-permute-start.2 = (bf16[256,512]{1,0:T(8,128)(2,1)S(1)}, bf16[256,512]{1,0:T(8,128)(2,1)S(1)}, u32[]{:S(2)}, u32[]{:S(2)}) collective-permute-start(bf16[256,512]{1,0:T(8,128)(2,1)S(1)} %get-tuple-element.38.refs_4_.refs_8_), channel_id=1, source_target_pairs={{0,16},{4,20},{8,24},{12,28},{16,0},{20,4},{24,8},{28,12},{1,17},{... | collective-permute-start | bytes 786440 | tf_op jit(solution)/shard_map/ppermute | solution.py:75
  7.7 13.0 %collective-permute-start.8 = (bf16[256,512]{1,0:T(8,128)(2,1)S(1)}, bf16[256,512]{1,0:T(8,128)(2,1)S(1)}, u32[]{:S(2)}, u32[]{:S(2)}) collective-permute-start(bf16[256,512]{1,0:T(8,128)(2,1)S(1)} %get-tuple-element.49), channel_id=1, source_target_pairs={{0,1},{1,0},{2,3},{3,2},{4,5},{5,4},{6,7},{7,6},{8,9},{9,8},{10,11... | collective-permute-start | bytes 786440 | tf_op jit(solution)/shard_map/ppermute | solution.py:75
  9.3 14.9 %collective-permute-start.3 = (bf16[256,512]{1,0:T(8,128)(2,1)S(1)}, bf16[256,512]{1,0:T(8,128)(2,1)S(1)}, u32[]{:S(2)}, u32[]{:S(2)}) collective-permute-start(bf16[256,512]{1,0:T(8,128)(2,1)S(1)} %get-tuple-element.42), channel_id=1, source_target_pairs={{0,2},{1,3},{2,0},{3,1},{4,6},{5,7},{6,4},{7,5},{8,10},{9,11},{10,... | collective-permute-start | bytes 786440 | tf_op jit(solution)/shard_map/ppermute | solution.py:75
  14.0 10.2 %collective-permute-start.14 = (bf16[256,512]{1,0:T(8,128)(2,1)S(1)}, bf16[256,512]{1,0:T(8,128)(2,1)S(1)}, u32[]{:S(2)}, u32[]{:S(2)}) collective-permute-start(bf16[256,512]{1,0:T(8,128)(2,1)S(1)} %collective-permute-done.1.refs_8_.refs_12_), channel_id=1, source_target_pairs={{0,16},{4,20},{8,24},{12,28},{16,0},{20,4},{24,8},{28,12},{1,17},{... | collective-permute-start | bytes 786440 | tf_op jit(solution)/shard_map/ppermute | solution.py:75
  21.2 11.0 %collective-permute-start.6 = (bf16[256,512]{1,0:T(8,128)(2,1)S(1)}, bf16[256,512]{1,0:T(8,128)(2,1)S(1)}, u32[]{:S(2)}, u32[]{:S(2)}) collective-permute-start(bf16[256,512]{1,0:T(8,128)(2,1)S(1)} %get-tuple-element.47), channel_id=1, source_target_pairs={{0,3},{1,2},{2,1},{3,0},{4,7},{5,6},{6,5},{7,4},{8,11},{9,10},{10,... | collective-permute-start | bytes 786440 | tf_op jit(solution)/shard_map/ppermute | solution.py:75
  24.2 10.5 %collective-permute-start.4 = (bf16[2,128,512]{2,1,0:T(8,128)(2,1)S(1)}, bf16[2,128,512]{2,1,0:T(8,128)(2,1)S(1)}, u32[]{:S(2)}, u32[]{:S(2)}) collective-permute-start(bf16[2,128,512]{2,1,0:T(8,128)(2,1)S(1)} %get-tuple-element.43), channel_id=1, source_target_pairs={{0,1},{1,0},{2,3},{3,2},{4,5},{5,4},{6,7},{7,6},{8,9},{9,8},{10,11... | collective-permute-start | bytes 786440 | tf_op jit(solution)/shard_map/ppermute | solution.py:75
  27.3 7.4 %collective-permute-start.15 = (bf16[256,512]{1,0:T(8,128)(2,1)S(1)}, bf16[256,512]{1,0:T(8,128)(2,1)S(1)}, u32[]{:S(2)}, u32[]{:S(2)}) collective-permute-start(bf16[256,512]{1,0:T(8,128)(2,1)S(1)} %collective-permute-done.3.refs_6_.refs_10_), channel_id=1, source_target_pairs={{0,16},{4,20},{8,24},{12,28},{16,0},{20,4},{24,8},{28,12},{1,17},{... | collective-permute-start | bytes 786440 | tf_op jit(solution)/shard_map/ppermute | solution.py:75
  30.2 9.8 %collective-permute-start.10 = (bf16[256,512]{1,0:T(8,128)(2,1)S(1)}, bf16[256,512]{1,0:T(8,128)(2,1)S(1)}, u32[]{:S(2)}, u32[]{:S(2)}) collective-permute-start(bf16[256,512]{1,0:T(8,128)(2,1)S(1)} %collective-permute-done.3.refs_6_.refs_10_), channel_id=1, source_target_pairs={{0,8},{4,12},{8,0},{12,4},{16,24},{20,28},{24,16},{28,20},{1,9},{5... | collective-permute-start | bytes 786440 | tf_op jit(solution)/shard_map/ppermute | solution.py:75
  30.7 11.6 %collective-permute-start.12 = (bf16[256,512]{1,0:T(8,128)(2,1)S(1)}, bf16[256,512]{1,0:T(8,128)(2,1)S(1)}, u32[]{:S(2)}, u32[]{:S(2)}) collective-permute-start(bf16[256,512]{1,0:T(8,128)(2,1)S(1)} %collective-permute-done.11.refs_13_.refs_17_), channel_id=1, source_target_pairs={{0,8},{4,12},{8,0},{12,4},{16,24},{20,28},{24,16},{28,20},{1,9},{5... | collective-permute-start | bytes 786440 | tf_op jit(solution)/shard_map/ppermute | solution.py:75
  34.7 9.6 %collective-permute-start.16 = (bf16[256,512]{1,0:T(8,128)(2,1)S(1)}, bf16[256,512]{1,0:T(8,128)(2,1)S(1)}, u32[]{:S(2)}, u32[]{:S(2)}) collective-permute-start(bf16[256,512]{1,0:T(8,128)(2,1)S(1)} %collective-permute-done.6.refs_7_.refs_11_), channel_id=1, source_target_pairs={{0,16},{4,20},{8,24},{12,28},{16,0},{20,4},{24,8},{28,12},{1,17},{... | collective-permute-start | bytes 786440 | tf_op jit(solution)/shard_map/ppermute | solution.py:75
  36.2 18.7 %collective-permute-start.5 = (bf16[2,128,512]{2,1,0:T(8,128)(2,1)S(1)}, bf16[2,128,512]{2,1,0:T(8,128)(2,1)S(1)}, u32[]{:S(2)}, u32[]{:S(2)}) collective-permute-start(bf16[2,128,512]{2,1,0:T(8,128)(2,1)S(1)} %get-tuple-element.45), channel_id=1, source_target_pairs={{0,2},{1,3},{2,0},{3,1},{4,6},{5,7},{6,4},{7,5},{8,10},{9,11},{10,... | collective-permute-start | bytes 786440 | tf_op jit(solution)/shard_map/ppermute | solution.py:75
  37.2 17.8 %collective-permute-start.7 = (bf16[2,128,512]{2,1,0:T(8,128)(2,1)S(1)}, bf16[2,128,512]{2,1,0:T(8,128)(2,1)S(1)}, u32[]{:S(2)}, u32[]{:S(2)}) collective-permute-start(bf16[2,128,512]{2,1,0:T(8,128)(2,1)S(1)} %get-tuple-element.48), channel_id=1, source_target_pairs={{0,3},{1,2},{2,1},{3,0},{4,7},{5,6},{6,5},{7,4},{8,11},{9,10},{10,... | collective-permute-start | bytes 786440 | tf_op jit(solution)/shard_map/ppermute | solution.py:75
  42.3 12.7 %collective-permute-start.13 = (bf16[256,512]{1,0:T(8,128)(2,1)S(1)}, bf16[256,512]{1,0:T(8,128)(2,1)S(1)}, u32[]{:S(2)}, u32[]{:S(2)}) collective-permute-start(bf16[256,512]{1,0:T(8,128)(2,1)S(1)} %collective-permute-done.6.refs_7_.refs_11_), channel_id=1, source_target_pairs={{0,8},{4,12},{8,0},{12,4},{16,24},{20,28},{24,16},{28,20},{1,9},{5... | collective-permute-start | bytes 786440 | tf_op jit(solution)/shard_map/ppermute | solution.py:75
  42.6 12.4 %collective-permute-start.17 = (bf16[256,512]{1,0:T(8,128)(2,1)S(1)}, bf16[256,512]{1,0:T(8,128)(2,1)S(1)}, u32[]{:S(2)}, u32[]{:S(2)}) collective-permute-start(bf16[256,512]{1,0:T(8,128)(2,1)S(1)} %collective-permute-done.10.refs_10_.refs_14_), channel_id=1, source_target_pairs={{0,16},{4,20},{8,24},{12,28},{16,0},{20,4},{24,8},{28,12},{1,17},{... | collective-permute-start | bytes 786440 | tf_op jit(solution)/shard_map/ppermute | solution.py:75
  44.3 10.7 %collective-permute-start.18 = (bf16[256,512]{1,0:T(8,128)(2,1)S(1)}, bf16[256,512]{1,0:T(8,128)(2,1)S(1)}, u32[]{:S(2)}, u32[]{:S(2)}) collective-permute-start(bf16[256,512]{1,0:T(8,128)(2,1)S(1)} %collective-permute-done.16.refs_15_.refs_19_), channel_id=1, source_target_pairs={{0,8},{4,12},{8,0},{12,4},{16,24},{20,28},{24,16},{28,20},{1,9},{5... | collective-permute-start | bytes 786440 | tf_op jit(solution)/shard_map/ppermute | solution.py:75
  59.1 11.4 %collective-permute-start.20 = (f32[32,1024]{1,0:T(8,128)S(1)}, f32[32,1024]{1,0:T(8,128)S(1)}, u32[]{:S(2)}, u32[]{:S(2)}) collective-permute-start(f32[32,1024]{1,0:T(8,128)S(1)} %get-tuple-element.59), channel_id=1, source_target_pairs={{0,1},{1,0},{2,3},{3,2},{4,5},{5,4},{6,7},{7,6},{8,9},{9,8},{10,11... | collective-permute-start | bytes 393224 | tf_op jit(solution)/shard_map/ppermute | solution.py:75
  65.2 12.9 %collective-permute-start.21 = (f32[32,1024]{1,0:T(8,128)S(1)}, f32[32,1024]{1,0:T(8,128)S(1)}, u32[]{:S(2)}, u32[]{:S(2)}) collective-permute-start(f32[32,1024]{1,0:T(8,128)S(1)} %get-tuple-element.60), channel_id=1, source_target_pairs={{0,2},{1,3},{2,0},{3,1},{4,6},{5,7},{6,4},{7,5},{8,10},{9,11},{10,... | collective-permute-start | bytes 393224 | tf_op jit(solution)/shard_map/ppermute | solution.py:75
  65.6 12.5 %collective-permute-start.22 = (f32[32,1024]{1,0:T(8,128)S(1)}, f32[32,1024]{1,0:T(8,128)S(1)}, u32[]{:S(2)}, u32[]{:S(2)}) collective-permute-start(f32[32,1024]{1,0:T(8,128)S(1)} %get-tuple-element.61), channel_id=1, source_target_pairs={{0,3},{1,2},{2,1},{3,0},{4,7},{5,6},{6,5},{7,4},{8,11},{9,10},{10,... | collective-permute-start | bytes 393224 | tf_op jit(solution)/shard_map/ppermute | solution.py:75
  82.3 7.2 %collective-permute-start.26 = (f32[32,1024]{1,0:T(8,128)S(1)}, f32[32,1024]{1,0:T(8,128)S(1)}, u32[]{:S(2)}, u32[]{:S(2)}) collective-permute-start(f32[32,1024]{1,0:T(8,128)S(1)} %add_add_fusion.refs_0_), channel_id=1, source_target_pairs={{0,2},{1,3},{2,0},{3,1},{4,6},{5,7},{6,4},{7,5},{8,10},{9,11},{10,... | collective-permute-start | bytes 393224 | tf_op jit(solution)/shard_map/ppermute | solution.py:75
  89.5 7.3 %collective-permute-start.31 = (f32[2,32,1024]{2,1,0:T(8,128)S(1)}, f32[2,32,1024]{2,1,0:T(8,128)S(1)}, u32[]{:S(2)}, u32[]{:S(2)}) collective-permute-start(f32[2,32,1024]{2,1,0:T(8,128)S(1)} %pad_maximum_fusion.refs_1_), channel_id=1, source_target_pairs={{0,8},{4,12},{8,0},{12,4},{16,24},{20,28},{24,16},{28,20},{1,9},{5... | collective-permute-start | bytes 786440 | tf_op jit(solution)/shard_map/ppermute | solution.py:75
  90.9 12.6 %collective-permute-start.33 = (f32[2,32,1024]{2,1,0:T(8,128)S(1)}, f32[2,32,1024]{2,1,0:T(8,128)S(1)}, u32[]{:S(2)}, u32[]{:S(2)}) collective-permute-start(f32[2,32,1024]{2,1,0:T(8,128)S(1)} %pad_maximum_fusion.refs_1_), channel_id=1, source_target_pairs={{0,16},{4,20},{8,24},{12,28},{16,0},{20,4},{24,8},{28,12},{1,17},{... | collective-permute-start | bytes 786440 | tf_op jit(solution)/shard_map/ppermute | solution.py:75
  96.8 10.6 %collective-permute-start.36 = (f32[2,32,1024]{2,1,0:T(8,128)S(1)}, f32[2,32,1024]{2,1,0:T(8,128)S(1)}, u32[]{:S(2)}, u32[]{:S(2)}) collective-permute-start(f32[2,32,1024]{2,1,0:T(8,128)S(1)} %collective-permute-done.31.refs_4_), channel_id=1, source_target_pairs={{0,16},{4,20},{8,24},{12,28},{16,0},{20,4},{24,8},{28,12},{1,17},{... | collective-permute-start | bytes 786440 | tf_op jit(solution)/shard_map/ppermute | solution.py:75
  97.9 15.0 %collective-permute-start.29 = (f32[2,32,1024]{2,1,0:T(8,128)S(1)}, f32[2,32,1024]{2,1,0:T(8,128)S(1)}, u32[]{:S(2)}, u32[]{:S(2)}) collective-permute-start(f32[2,32,1024]{2,1,0:T(8,128)S(1)} %pad_maximum_fusion.refs_1_), channel_id=1, source_target_pairs={{0,4},{4,0},{8,12},{12,8},{16,20},{20,16},{24,28},{28,24},{1,5},{5... | collective-permute-start | bytes 786440 | tf_op jit(solution)/shard_map/ppermute | solution.py:75
  103.5 9.4 %collective-permute-start.28 = (f32[32,1024]{1,0:T(8,128)S(1)}, f32[32,1024]{1,0:T(8,128)S(1)}, u32[]{:S(2)}, u32[]{:S(2)}) collective-permute-start(f32[32,1024]{1,0:T(8,128)S(1)} %add_add_fusion.refs_0_), channel_id=1, source_target_pairs={{0,4},{4,0},{8,12},{12,8},{16,20},{20,16},{24,28},{28,24},{1,5},{5... | collective-permute-start | bytes 393224 | tf_op jit(solution)/shard_map/ppermute | solution.py:75
  104.2 8.7 %collective-permute-start.30 = (f32[32,1024]{1,0:T(8,128)S(1)}, f32[32,1024]{1,0:T(8,128)S(1)}, u32[]{:S(2)}, u32[]{:S(2)}) collective-permute-start(f32[32,1024]{1,0:T(8,128)S(1)} %collective-permute-done.27.refs_2_), channel_id=1, source_target_pairs={{0,4},{4,0},{8,12},{12,8},{16,20},{20,16},{24,28},{28,24},{1,5},{5... | collective-permute-start | bytes 393224 | tf_op jit(solution)/shard_map/ppermute | solution.py:75
  116.0 13.7 %collective-permute-start.41 = (bf16[2,4,32,512]{3,2,1,0:T(8,128)(2,1)S(1)}, bf16[2,4,32,512]{3,2,1,0:T(8,128)(2,1)S(1)}, u32[]{:S(2)}, u32[]{:S(2)}) collective-permute-start(bf16[2,4,32,512]{3,2,1,0:T(8,128)(2,1)S(1)} %get-tuple-element.64), channel_id=1, source_target_pairs={{0,1},{1,0},{2,3},{3,2},{4,5},{5,4},{6,7},{7,6},{8,9},{9,8},{10,11... | collective-permute-start | bytes 786440 | tf_op jit(solution)/shard_map/ppermute | solution.py:75
  117.0 21.6 %collective-permute-start.42 = (bf16[2,4,32,512]{3,2,1,0:T(8,128)(2,1)S(1)}, bf16[2,4,32,512]{3,2,1,0:T(8,128)(2,1)S(1)}, u32[]{:S(2)}, u32[]{:S(2)}) collective-permute-start(bf16[2,4,32,512]{3,2,1,0:T(8,128)(2,1)S(1)} %get-tuple-element.65), channel_id=1, source_target_pairs={{0,2},{1,3},{2,0},{3,1},{4,6},{5,7},{6,4},{7,5},{8,10},{9,11},{10,... | collective-permute-start | bytes 786440 | tf_op jit(solution)/shard_map/ppermute | solution.py:75
  120.3 18.4 %collective-permute-start.43 = (bf16[2,4,32,512]{3,2,1,0:T(8,128)(2,1)S(1)}, bf16[2,4,32,512]{3,2,1,0:T(8,128)(2,1)S(1)}, u32[]{:S(2)}, u32[]{:S(2)}) collective-permute-start(bf16[2,4,32,512]{3,2,1,0:T(8,128)(2,1)S(1)} %get-tuple-element.66), channel_id=1, source_target_pairs={{0,3},{1,2},{2,1},{3,0},{4,7},{5,6},{6,5},{7,4},{8,11},{9,10},{10,... | collective-permute-start | bytes 786440 | tf_op jit(solution)/shard_map/ppermute | solution.py:75
  120.4 19.4 %collective-permute-start.44 = (bf16[2,4,32,512]{3,2,1,0:T(8,128)(2,1)S(1)}, bf16[2,4,32,512]{3,2,1,0:T(8,128)(2,1)S(1)}, u32[]{:S(2)}, u32[]{:S(2)}) collective-permute-start(bf16[2,4,32,512]{3,2,1,0:T(8,128)(2,1)S(1)} %get-tuple-element.63.refs_0_), channel_id=1, source_target_pairs={{0,4},{4,0},{8,12},{12,8},{16,20},{20,16},{24,28},{28,24},{1,5},{5... | collective-permute-start | bytes 786440 | tf_op jit(solution)/shard_map/ppermute | solution.py:75
  129.7 10.1 %collective-permute-start.45 = (bf16[2,4,32,512]{3,2,1,0:T(8,128)(2,1)S(1)}, bf16[2,4,32,512]{3,2,1,0:T(8,128)(2,1)S(1)}, u32[]{:S(2)}, u32[]{:S(2)}) collective-permute-start(bf16[2,4,32,512]{3,2,1,0:T(8,128)(2,1)S(1)} %collective-permute-done.41.refs_1_), channel_id=1, source_target_pairs={{0,4},{4,0},{8,12},{12,8},{16,20},{20,16},{24,28},{28,24},{1,5},{5... | collective-permute-start | bytes 786440 | tf_op jit(solution)/shard_map/ppermute | solution.py:75
  (18 other events, 69.5 us)

commit v6 on v5

--- a/solution.py
+++ b/solution.py
@@ -371,7 +371,8 @@
     x_2, y_2 = swap_x(after(data_2, x_1)), swap_y(after(data_2, y_1, across_0))
     noise_2 = swap(after(dealt_noise[1], data_2), "col", 2)
     across_2 = swap_y(x_2)
-    x_3, y_3 = swap_x(after(data_3, across_1, x_2, noise_1)), swap_y(after(data_3, y_2, noise_1))
+    x_3 = swap_x(after(data_3, across_1, x_2, noise_1, noise_2))
+    y_3 = swap_y(after(data_3, y_2, noise_1, noise_2))
     noise_3 = swap(after(dealt_noise[2], data_3, noise_1), "col", 3)
     across_3 = swap_x(y_3)
     noise_pieces = [noise_0, noise_1, noise_2, noise_3]
@@ -386,8 +387,8 @@
     tile = functools.reduce(jnp.add, parts)
     tile_1, tile_2 = swap(tile, "col", 1), swap(tile, "col", 2)
     tile_3 = swap(tile_2, "col", 1)
-    x_tile, y_tile = swap_x(tile), swap_y(tile)
-    pair = jnp.stack([after(tile_1, x_tile, y_tile), tile_2])
+    x_tile, y_tile = swap_x(after(tile, tile_1)), swap_y(after(tile, tile_1))
+    pair = jnp.stack([tile_1, after(tile_2, x_tile)])
     x_pair, y_pair = swap_x(pair), swap_y(pair)
     x_last, y_last = swap_x(tile_3), swap_y(tile_3)
     tiles = [

time: 144 us -> 147 us (1.021)
  waiting for transfers between devices: 77.3 us -> 84.1 us
  starting transfers between devices: 52.9 us -> 49 us
    ppermute x48, waiting for transfers between devices: 77.3 us -> 84.1 us  [swap(): return lax.ppermute(array, axis, [(i, i ^ step) for i in range(count)])]
    ppermute x48, starting transfers between devices: 52.9 us -> 49 us  [swap(): return lax.ppermute(array, axis, [(i, i ^ step) for i in range(count)])]
  transfers between devices with their start and end apart: 48 -> 48, of which waited for: 26 -> 28; matrix products, arithmetic and copies ran while one was open for 0% -> 0% of each run, Pallas kernels for 2% -> 2%
where the time goes in v6:
time: 147 us; the launch traced here: 145 us
  waiting for transfers between devices  84.1 us (57%)
  starting transfers between devices  49 us (33%)
  Pallas kernels  8.24 us (6%)
  local copies, waits for them, and re-layouts  2.44 us (2%)
    ppermute x48, waiting for transfers between devices, swap(): return lax.ppermute(array, axis, [(i, i ^ step) for i in range(count)])  84.1 us
    ppermute x48, starting transfers between devices, swap(): return lax.ppermute(array, axis, [(i, i ^ step) for i in range(count)])  49 us
    pallas_call x10, Pallas kernels, kernel_call(): pl.pallas_call(kernel, in_specs=[VMEM] * len(operands), out_specs=[VMEM]...  8.24 us
  transfers between devices with their start and end apart: 48, of which 28 were waited for; matrix products, arithmetic and copies ran while one was open for 0% of the time, Pallas kernels for 2%

profile of v6, /device:TPU:0, one launch (start us, length us, event | category | flops | bytes accessed | tf_op | source)
XLA Modules:
  0.0 144.5 jit_solution(423667437459291677)
XLA Ops:
  3.2 3.0 %collective-permute-start.1 = (bf16[256,512]{1,0:T(8,128)(2,1)S(1)}, bf16[256,512]{1,0:T(8,128)(2,1)S(1)}, u32[]{:S(2)}, u32[]{:S(2)}) collective-permute-start(bf16[256,512]{1,0:T(8,128)(2,1)S(1)} %get-tuple-element.39.refs_4_.refs_8_), channel_id=1, source_target_pairs={{0,8},{4,12},{8,0},{12,4},{16,24},{20,28},{24,16},{28,20},{1,9},{5... | collective-permute-start | bytes 786440 | tf_op jit(solution)/shard_map/ppermute | solution.py:75
  7.7 1.6 %collective-permute-start.8 = (bf16[256,512]{1,0:T(8,128)(2,1)S(1)}, bf16[256,512]{1,0:T(8,128)(2,1)S(1)}, u32[]{:S(2)}, u32[]{:S(2)}) collective-permute-start(bf16[256,512]{1,0:T(8,128)(2,1)S(1)} %get-tuple-element.50), channel_id=1, source_target_pairs={{0,1},{1,0},{2,3},{3,2},{4,5},{5,4},{6,7},{7,6},{8,9},{9,8},{10,11... | collective-permute-start | bytes 786440 | tf_op jit(solution)/shard_map/ppermute | solution.py:75
  9.3 2.6 %collective-permute-start.3 = (bf16[256,512]{1,0:T(8,128)(2,1)S(1)}, bf16[256,512]{1,0:T(8,128)(2,1)S(1)}, u32[]{:S(2)}, u32[]{:S(2)}) collective-permute-start(bf16[256,512]{1,0:T(8,128)(2,1)S(1)} %get-tuple-element.43), channel_id=1, source_target_pairs={{0,2},{1,3},{2,0},{3,1},{4,6},{5,7},{6,4},{7,5},{8,10},{9,11},{10,... | collective-permute-start | bytes 786440 | tf_op jit(solution)/shard_map/ppermute | solution.py:75
  14.0 1.6 %collective-permute-start.14 = (bf16[256,512]{1,0:T(8,128)(2,1)S(1)}, bf16[256,512]{1,0:T(8,128)(2,1)S(1)}, u32[]{:S(2)}, u32[]{:S(2)}) collective-permute-start(bf16[256,512]{1,0:T(8,128)(2,1)S(1)} %collective-permute-done.1.refs_8_.refs_12_), channel_id=1, source_target_pairs={{0,16},{4,20},{8,24},{12,28},{16,0},{20,4},{24,8},{28,12},{1,17},{... | collective-permute-start | bytes 786440 | tf_op jit(solution)/shard_map/ppermute | solution.py:75
  15.6 5.1 %collective-permute-done.8.refs_5_.refs_9_ = bf16[256,512]{1,0:T(8,128)(2,1)S(1)} collective-permute-done((bf16[256,512]{1,0:T(8,128)(2,1)S(1)}, bf16[256,512]{1,0:T(8,128)(2,1)S(1)}, u32[]{:S(2)}, u32[]{:S(2)}) %collective-permute-start.8) | collective-permute-done | bytes 262176 | tf_op jit(solution)/shard_map/ppermute | solution.py:75
  21.2 2.5 %collective-permute-start.6 = (bf16[256,512]{1,0:T(8,128)(2,1)S(1)}, bf16[256,512]{1,0:T(8,128)(2,1)S(1)}, u32[]{:S(2)}, u32[]{:S(2)}) collective-permute-start(bf16[256,512]{1,0:T(8,128)(2,1)S(1)} %get-tuple-element.48), channel_id=1, source_target_pairs={{0,3},{1,2},{2,1},{3,0},{4,7},{5,6},{6,5},{7,4},{8,11},{9,10},{10,... | collective-permute-start | bytes 786440 | tf_op jit(solution)/shard_map/ppermute | solution.py:75
  24.2 3.1 %collective-permute-start.5 = (bf16[2,128,512]{2,1,0:T(8,128)(2,1)S(1)}, bf16[2,128,512]{2,1,0:T(8,128)(2,1)S(1)}, u32[]{:S(2)}, u32[]{:S(2)}) collective-permute-start(bf16[2,128,512]{2,1,0:T(8,128)(2,1)S(1)} %get-tuple-element.46), channel_id=1, source_target_pairs={{0,2},{1,3},{2,0},{3,1},{4,6},{5,7},{6,4},{7,5},{8,10},{9,11},{10,... | collective-permute-start | bytes 786440 | tf_op jit(solution)/shard_map/ppermute | solution.py:75
  28.1 2.1 %collective-permute-done.9.refs_9_.refs_13_ = bf16[256,512]{1,0:T(8,128)(2,1)S(1)} collective-permute-done((bf16[256,512]{1,0:T(8,128)(2,1)S(1)}, bf16[256,512]{1,0:T(8,128)(2,1)S(1)}, u32[]{:S(2)}, u32[]{:S(2)}) %collective-permute-start.9) | collective-permute-done | bytes 262176 | tf_op jit(solution)/shard_map/ppermute | solution.py:75
  30.7 1.5 %collective-permute-done.6.refs_7_.refs_11_ = bf16[256,512]{1,0:T(8,128)(2,1)S(1)} collective-permute-done((bf16[256,512]{1,0:T(8,128)(2,1)S(1)}, bf16[256,512]{1,0:T(8,128)(2,1)S(1)}, u32[]{:S(2)}, u32[]{:S(2)}) %collective-permute-start.6) | collective-permute-done | bytes 262176 | tf_op jit(solution)/shard_map/ppermute | solution.py:75
  32.6 3.4 %collective-permute-done.4.refs_1_ = bf16[2,128,512]{2,1,0:T(8,128)(2,1)S(1)} collective-permute-done((bf16[2,128,512]{2,1,0:T(8,128)(2,1)S(1)}, bf16[2,128,512]{2,1,0:T(8,128)(2,1)S(1)}, u32[]{:S(2)}, u32[]{:S(2)}) %collective-permute-start.4) | collective-permute-done | bytes 262176 | tf_op jit(solution)/shard_map/ppermute | solution.py:75
  36.0 9.5 %collective-permute-done.5.refs_2_ = bf16[2,128,512]{2,1,0:T(8,128)(2,1)S(1)} collective-permute-done((bf16[2,128,512]{2,1,0:T(8,128)(2,1)S(1)}, bf16[2,128,512]{2,1,0:T(8,128)(2,1)S(1)}, u32[]{:S(2)}, u32[]{:S(2)}) %collective-permute-start.5) | collective-permute-done | bytes 262176 | tf_op jit(solution)/shard_map/ppermute | solution.py:75
  46.0 2.5 %collective-permute-start.7 = (bf16[2,128,512]{2,1,0:T(8,128)(2,1)S(1)}, bf16[2,128,512]{2,1,0:T(8,128)(2,1)S(1)}, u32[]{:S(2)}, u32[]{:S(2)}) collective-permute-start(bf16[2,128,512]{2,1,0:T(8,128)(2,1)S(1)} %get-tuple-element.49), channel_id=1, source_target_pairs={{0,3},{1,2},{2,1},{3,0},{4,7},{5,6},{6,5},{7,4},{8,11},{9,10},{10,... | collective-permute-start | bytes 786440 | tf_op jit(solution)/shard_map/ppermute | solution.py:75
  50.5 4.2 %collective-permute-done.16.refs_15_.refs_19_ = bf16[256,512]{1,0:T(8,128)(2,1)S(1)} collective-permute-done((bf16[256,512]{1,0:T(8,128)(2,1)S(1)}, bf16[256,512]{1,0:T(8,128)(2,1)S(1)}, u32[]{:S(2)}, u32[]{:S(2)}) %collective-permute-start.16) | collective-permute-done | bytes 262176 | tf_op jit(solution)/shard_map/ppermute | solution.py:75
  55.3 3.6 %collective-permute-done.17.refs_18_.refs_22_ = bf16[256,512]{1,0:T(8,128)(2,1)S(1)} collective-permute-done((bf16[256,512]{1,0:T(8,128)(2,1)S(1)}, bf16[256,512]{1,0:T(8,128)(2,1)S(1)}, u32[]{:S(2)}, u32[]{:S(2)}) %collective-permute-start.17) | collective-permute-done | bytes 262176 | tf_op jit(solution)/shard_map/ppermute | solution.py:75
  58.9 2.2 %collective-permute-done.18.refs_19_.refs_23_ = bf16[256,512]{1,0:T(8,128)(2,1)S(1)} collective-permute-done((bf16[256,512]{1,0:T(8,128)(2,1)S(1)}, bf16[256,512]{1,0:T(8,128)(2,1)S(1)}, u32[]{:S(2)}, u32[]{:S(2)}) %collective-permute-start.18) | collective-permute-done | bytes 262176 | tf_op jit(solution)/shard_map/ppermute | solution.py:75
  61.1 2.0 %shard_map.52 = (f32[128,1024]{1,0:T(8,128)S(1)}, f32[128,1024]{1,0:T(8,128)S(1)}) custom-call(bf16[2,128,512]{2,1,0:T(8,128)(2,1)S(1)} %get-tuple-element.41.refs_0_, bf16[2,128,512]{2,1,0:T(8,128)(2,1)S(1)} %collective-permute-done.4.refs_1_, bf16[2,128,512]{2,1,0:T(8,128)(2,1)S(1)} %collective-permute-done.5.refs_2_, ...), custom_call_target="tpu_custom_call" | custom-call | flops 1073741824 | bytes 5242880 | tf_op jit(solution)/shard_map/pallas_call | solution.py:113
  63.2 1.9 %collective-permute-done.19.other_ref = f32[128,1024]{1,0:T(8,128)S(1)} collective-permute-done((f32[128,1024]{1,0:T(8,128)S(1)}, f32[128,1024]{1,0:T(8,128)S(1)}, u32[]{:S(2)}, u32[]{:S(2)}) %collective-permute-start.19) | collective-permute-done | bytes 524320 | tf_op jit(solution)/shard_map/ppermute | solution.py:75
  65.2 3.0 %collective-permute-start.21 = (f32[32,1024]{1,0:T(8,128)S(1)}, f32[32,1024]{1,0:T(8,128)S(1)}, u32[]{:S(2)}, u32[]{:S(2)}) collective-permute-start(f32[32,1024]{1,0:T(8,128)S(1)} %get-tuple-element.61), channel_id=1, source_target_pairs={{0,2},{1,3},{2,0},{3,1},{4,6},{5,7},{6,4},{7,5},{8,10},{9,11},{10,... | collective-permute-start | bytes 393224 | tf_op jit(solution)/shard_map/ppermute | solution.py:75
  69.6 3.4 %collective-permute-done.20 = f32[32,1024]{1,0:T(8,128)S(1)} collective-permute-done((f32[32,1024]{1,0:T(8,128)S(1)}, f32[32,1024]{1,0:T(8,128)S(1)}, u32[]{:S(2)}, u32[]{:S(2)}) %collective-permute-start.20) | collective-permute-done | bytes 131104 | tf_op jit(solution)/shard_map/ppermute | solution.py:75
  73.1 5.2 %collective-permute-done.21 = f32[32,1024]{1,0:T(8,128)S(1)} collective-permute-done((f32[32,1024]{1,0:T(8,128)S(1)}, f32[32,1024]{1,0:T(8,128)S(1)}, u32[]{:S(2)}, u32[]{:S(2)}) %collective-permute-start.21) | collective-permute-done | bytes 131104 | tf_op jit(solution)/shard_map/ppermute | solution.py:75
  78.3 2.6 %collective-permute-start.23 = (f32[32,1024]{1,0:T(8,128)S(1)}, f32[32,1024]{1,0:T(8,128)S(1)}, u32[]{:S(2)}, u32[]{:S(2)}) collective-permute-start(f32[32,1024]{1,0:T(8,128)S(1)} %add_add_fusion.refs_0_), channel_id=1, source_target_pairs={{0,1},{1,0},{2,3},{3,2},{4,5},{5,4},{6,7},{7,6},{8,9},{9,8},{10,11... | collective-permute-start | bytes 393224 | tf_op jit(solution)/shard_map/ppermute | solution.py:75
  82.0 3.2 %collective-permute-done.23 = f32[32,1024]{1,0:T(8,128)S(1)} collective-permute-done((f32[32,1024]{1,0:T(8,128)S(1)}, f32[32,1024]{1,0:T(8,128)S(1)}, u32[]{:S(2)}, u32[]{:S(2)}) %collective-permute-start.23) | collective-permute-done | bytes 131104 | tf_op jit(solution)/shard_map/ppermute | solution.py:75
  85.7 3.4 %collective-permute-done.24 = f32[32,1024]{1,0:T(8,128)S(1)} collective-permute-done((f32[32,1024]{1,0:T(8,128)S(1)}, f32[32,1024]{1,0:T(8,128)S(1)}, u32[]{:S(2)}, u32[]{:S(2)}) %collective-permute-start.24) | collective-permute-done | bytes 131104 | tf_op jit(solution)/shard_map/ppermute | solution.py:75
  89.1 2.1 %collective-permute-done.25.refs_3_ = f32[32,1024]{1,0:T(8,128)S(1)} collective-permute-done((f32[32,1024]{1,0:T(8,128)S(1)}, f32[32,1024]{1,0:T(8,128)S(1)}, u32[]{:S(2)}, u32[]{:S(2)}) %collective-permute-start.25) | collective-permute-done | bytes 131104 | tf_op jit(solution)/shard_map/ppermute | solution.py:75
  92.0 2.9 %collective-permute-start.26 = (f32[32,1024]{1,0:T(8,128)S(1)}, f32[32,1024]{1,0:T(8,128)S(1)}, u32[]{:S(2)}, u32[]{:S(2)}) collective-permute-start(f32[32,1024]{1,0:T(8,128)S(1)} %collective-permute-done.24), channel_id=1, source_target_pairs={{0,1},{1,0},{2,3},{3,2},{4,5},{5,4},{6,7},{7,6},{8,9},{9,8},{10,11... | collective-permute-start | bytes 393224 | tf_op jit(solution)/shard_map/ppermute | solution.py:75
  95.8 2.5 %collective-permute-done.32.refs_6_ = f32[32,1024]{1,0:T(8,128)S(1)} collective-permute-done((f32[32,1024]{1,0:T(8,128)S(1)}, f32[32,1024]{1,0:T(8,128)S(1)}, u32[]{:S(2)}, u32[]{:S(2)}) %collective-permute-start.32) | collective-permute-done | bytes 131104 | tf_op jit(solution)/shard_map/ppermute | solution.py:75
  100.1 1.7 %collective-permute-start.36 = (f32[2,32,1024]{2,1,0:T(8,128)S(1)}, f32[2,32,1024]{2,1,0:T(8,128)S(1)}, u32[]{:S(2)}, u32[]{:S(2)}) collective-permute-start(f32[2,32,1024]{2,1,0:T(8,128)S(1)} %collective-permute-done.30.refs_4_), channel_id=1, source_target_pairs={{0,16},{4,20},{8,24},{12,28},{16,0},{20,4},{24,8},{28,12},{1,17},{... | collective-permute-start | bytes 786440 | tf_op jit(solution)/shard_map/ppermute | solution.py:75
  107.7 2.0 %collective-permute-done.37.refs_11_ = f32[32,1024]{1,0:T(8,128)S(1)} collective-permute-done((f32[32,1024]{1,0:T(8,128)S(1)}, f32[32,1024]{1,0:T(8,128)S(1)}, u32[]{:S(2)}, u32[]{:S(2)}) %collective-permute-start.37) | collective-permute-done | bytes 131104 | tf_op jit(solution)/shard_map/ppermute | solution.py:75
  116.2 2.2 %shard_map.57 = (bf16[2,4,32,512]{3,2,1,0:T(8,128)(2,1)S(1)}, bf16[2,4,32,512]{3,2,1,0:T(8,128)(2,1)S(1)}, bf16[2,4,32,512]{3,2,1,0:T(8,128)(2,1)S(1)}, bf16[2,4...) custom-call(f32[32,1024]{1,0:T(8,128)S(1)} %add_add_fusion.refs_0_, ...), custom_call_target="tpu_custom_call" | custom-call | flops 1073741824 | bytes 5259264 | tf_op jit(solution)/shard_map/pallas_call | solution.py:113
  118.3 1.9 %collective-permute-start.41 = (bf16[2,4,32,512]{3,2,1,0:T(8,128)(2,1)S(1)}, bf16[2,4,32,512]{3,2,1,0:T(8,128)(2,1)S(1)}, u32[]{:S(2)}, u32[]{:S(2)}) collective-permute-start(bf16[2,4,32,512]{3,2,1,0:T(8,128)(2,1)S(1)} %get-tuple-element.66), channel_id=1, source_target_pairs={{0,1},{1,0},{2,3},{3,2},{4,5},{5,4},{6,7},{7,6},{8,9},{9,8},{10,11... | collective-permute-start | bytes 786440 | tf_op jit(solution)/shard_map/ppermute | solution.py:75
  122.8 9.2 %collective-permute-done.41.refs_1_ = bf16[2,4,32,512]{3,2,1,0:T(8,128)(2,1)S(1)} collective-permute-done((bf16[2,4,32,512]{3,2,1,0:T(8,128)(2,1)S(1)}, bf16[2,4,32,512]{3,2,1,0:T(8,128)(2,1)S(1)}, u32[]{:S(2)}, u32[]{:S(2)}) %collective-permute-start.41) | collective-permute-done | bytes 262176 | tf_op jit(solution)/shard_map/ppermute | solution.py:75
  131.9 9.7 %collective-permute-done.42.refs_2_ = bf16[2,4,32,512]{3,2,1,0:T(8,128)(2,1)S(1)} collective-permute-done((bf16[2,4,32,512]{3,2,1,0:T(8,128)(2,1)S(1)}, bf16[2,4,32,512]{3,2,1,0:T(8,128)(2,1)S(1)}, u32[]{:S(2)}, u32[]{:S(2)}) %collective-permute-start.42) | collective-permute-done | bytes 262176 | tf_op jit(solution)/shard_map/ppermute | solution.py:75
  (81 shorter events, 36.4 us)
Async XLA Ops:
  1.9 12.0 %collective-permute-start = (bf16[128,2048]{1,0:T(8,128)(2,1)S(1)}, bf16[128,2048]{1,0:T(8,128)(2,1)S(1)}, u32[]{:S(2)}, u32[]{:S(2)}) collective-permute-start(bf16[128,2048]{1,0:T(8,128)(2,1)S(1)} %get-tuple-element.38), channel_id=1, source_target_pairs={{0,4},{4,0},{8,12},{12,8},{16,20},{20,16},{24,28},{28,24},{1,5},{5... | collective-permute-start | bytes 1572872 | tf_op jit(solution)/shard_map/ppermute | solution.py:75
  3.2 9.3 %collective-permute-start.1 = (bf16[256,512]{1,0:T(8,128)(2,1)S(1)}, bf16[256,512]{1,0:T(8,128)(2,1)S(1)}, u32[]{:S(2)}, u32[]{:S(2)}) collective-permute-start(bf16[256,512]{1,0:T(8,128)(2,1)S(1)} %get-tuple-element.39.refs_4_.refs_8_), channel_id=1, source_target_pairs={{0,8},{4,12},{8,0},{12,4},{16,24},{20,28},{24,16},{28,20},{1,9},{5... | collective-permute-start | bytes 786440 | tf_op jit(solution)/shard_map/ppermute | solution.py:75
  6.2 7.8 %collective-permute-start.2 = (bf16[256,512]{1,0:T(8,128)(2,1)S(1)}, bf16[256,512]{1,0:T(8,128)(2,1)S(1)}, u32[]{:S(2)}, u32[]{:S(2)}) collective-permute-start(bf16[256,512]{1,0:T(8,128)(2,1)S(1)} %get-tuple-element.39.refs_4_.refs_8_), channel_id=1, source_target_pairs={{0,16},{4,20},{8,24},{12,28},{16,0},{20,4},{24,8},{28,12},{1,17},{... | collective-permute-start | bytes 786440 | tf_op jit(solution)/shard_map/ppermute | solution.py:75
  7.7 13.0 %collective-permute-start.8 = (bf16[256,512]{1,0:T(8,128)(2,1)S(1)}, bf16[256,512]{1,0:T(8,128)(2,1)S(1)}, u32[]{:S(2)}, u32[]{:S(2)}) collective-permute-start(bf16[256,512]{1,0:T(8,128)(2,1)S(1)} %get-tuple-element.50), channel_id=1, source_target_pairs={{0,1},{1,0},{2,3},{3,2},{4,5},{5,4},{6,7},{7,6},{8,9},{9,8},{10,11... | collective-permute-start | bytes 786440 | tf_op jit(solution)/shard_map/ppermute | solution.py:75
  9.3 14.9 %collective-permute-start.3 = (bf16[256,512]{1,0:T(8,128)(2,1)S(1)}, bf16[256,512]{1,0:T(8,128)(2,1)S(1)}, u32[]{:S(2)}, u32[]{:S(2)}) collective-permute-start(bf16[256,512]{1,0:T(8,128)(2,1)S(1)} %get-tuple-element.43), channel_id=1, source_target_pairs={{0,2},{1,3},{2,0},{3,1},{4,6},{5,7},{6,4},{7,5},{8,10},{9,11},{10,... | collective-permute-start | bytes 786440 | tf_op jit(solution)/shard_map/ppermute | solution.py:75
  14.0 10.2 %collective-permute-start.14 = (bf16[256,512]{1,0:T(8,128)(2,1)S(1)}, bf16[256,512]{1,0:T(8,128)(2,1)S(1)}, u32[]{:S(2)}, u32[]{:S(2)}) collective-permute-start(bf16[256,512]{1,0:T(8,128)(2,1)S(1)} %collective-permute-done.1.refs_8_.refs_12_), channel_id=1, source_target_pairs={{0,16},{4,20},{8,24},{12,28},{16,0},{20,4},{24,8},{28,12},{1,17},{... | collective-permute-start | bytes 786440 | tf_op jit(solution)/shard_map/ppermute | solution.py:75
  21.2 11.1 %collective-permute-start.6 = (bf16[256,512]{1,0:T(8,128)(2,1)S(1)}, bf16[256,512]{1,0:T(8,128)(2,1)S(1)}, u32[]{:S(2)}, u32[]{:S(2)}) collective-permute-start(bf16[256,512]{1,0:T(8,128)(2,1)S(1)} %get-tuple-element.48), channel_id=1, source_target_pairs={{0,3},{1,2},{2,1},{3,0},{4,7},{5,6},{6,5},{7,4},{8,11},{9,10},{10,... | collective-permute-start | bytes 786440 | tf_op jit(solution)/shard_map/ppermute | solution.py:75
  24.2 11.8 %collective-permute-start.4 = (bf16[2,128,512]{2,1,0:T(8,128)(2,1)S(1)}, bf16[2,128,512]{2,1,0:T(8,128)(2,1)S(1)}, u32[]{:S(2)}, u32[]{:S(2)}) collective-permute-start(bf16[2,128,512]{2,1,0:T(8,128)(2,1)S(1)} %get-tuple-element.44), channel_id=1, source_target_pairs={{0,1},{1,0},{2,3},{3,2},{4,5},{5,4},{6,7},{7,6},{8,9},{9,8},{10,11... | collective-permute-start | bytes 786440 | tf_op jit(solution)/shard_map/ppermute | solution.py:75
  24.2 21.3 %collective-permute-start.5 = (bf16[2,128,512]{2,1,0:T(8,128)(2,1)S(1)}, bf16[2,128,512]{2,1,0:T(8,128)(2,1)S(1)}, u32[]{:S(2)}, u32[]{:S(2)}) collective-permute-start(bf16[2,128,512]{2,1,0:T(8,128)(2,1)S(1)} %get-tuple-element.46), channel_id=1, source_target_pairs={{0,2},{1,3},{2,0},{3,1},{4,6},{5,7},{6,4},{7,5},{8,10},{9,11},{10,... | collective-permute-start | bytes 786440 | tf_op jit(solution)/shard_map/ppermute | solution.py:75
  27.4 18.2 %collective-permute-start.15 = (bf16[256,512]{1,0:T(8,128)(2,1)S(1)}, bf16[256,512]{1,0:T(8,128)(2,1)S(1)}, u32[]{:S(2)}, u32[]{:S(2)}) collective-permute-start(bf16[256,512]{1,0:T(8,128)(2,1)S(1)} %collective-permute-done.3.refs_6_.refs_10_), channel_id=1, source_target_pairs={{0,16},{4,20},{8,24},{12,28},{16,0},{20,4},{24,8},{28,12},{1,17},{... | collective-permute-start | bytes 786440 | tf_op jit(solution)/shard_map/ppermute | solution.py:75
  30.2 18.3 %collective-permute-start.10 = (bf16[256,512]{1,0:T(8,128)(2,1)S(1)}, bf16[256,512]{1,0:T(8,128)(2,1)S(1)}, u32[]{:S(2)}, u32[]{:S(2)}) collective-permute-start(bf16[256,512]{1,0:T(8,128)(2,1)S(1)} %collective-permute-done.3.refs_6_.refs_10_), channel_id=1, source_target_pairs={{0,8},{4,12},{8,0},{12,4},{16,24},{20,28},{24,16},{28,20},{1,9},{5... | collective-permute-start | bytes 786440 | tf_op jit(solution)/shard_map/ppermute | solution.py:75
  32.3 16.2 %collective-permute-start.12 = (bf16[256,512]{1,0:T(8,128)(2,1)S(1)}, bf16[256,512]{1,0:T(8,128)(2,1)S(1)}, u32[]{:S(2)}, u32[]{:S(2)}) collective-permute-start(bf16[256,512]{1,0:T(8,128)(2,1)S(1)} %collective-permute-done.11.refs_13_.refs_17_), channel_id=1, source_target_pairs={{0,8},{4,12},{8,0},{12,4},{16,24},{20,28},{24,16},{28,20},{1,9},{5... | collective-permute-start | bytes 786440 | tf_op jit(solution)/shard_map/ppermute | solution.py:75
  45.5 9.2 %collective-permute-start.16 = (bf16[256,512]{1,0:T(8,128)(2,1)S(1)}, bf16[256,512]{1,0:T(8,128)(2,1)S(1)}, u32[]{:S(2)}, u32[]{:S(2)}) collective-permute-start(bf16[256,512]{1,0:T(8,128)(2,1)S(1)} %collective-permute-done.6.refs_7_.refs_11_), channel_id=1, source_target_pairs={{0,16},{4,20},{8,24},{12,28},{16,0},{20,4},{24,8},{28,12},{1,17},{... | collective-permute-start | bytes 786440 | tf_op jit(solution)/shard_map/ppermute | solution.py:75
  46.0 9.3 %collective-permute-start.7 = (bf16[2,128,512]{2,1,0:T(8,128)(2,1)S(1)}, bf16[2,128,512]{2,1,0:T(8,128)(2,1)S(1)}, u32[]{:S(2)}, u32[]{:S(2)}) collective-permute-start(bf16[2,128,512]{2,1,0:T(8,128)(2,1)S(1)} %get-tuple-element.49), channel_id=1, source_target_pairs={{0,3},{1,2},{2,1},{3,0},{4,7},{5,6},{6,5},{7,4},{8,11},{9,10},{10,... | collective-permute-start | bytes 786440 | tf_op jit(solution)/shard_map/ppermute | solution.py:75
  49.0 9.9 %collective-permute-start.17 = (bf16[256,512]{1,0:T(8,128)(2,1)S(1)}, bf16[256,512]{1,0:T(8,128)(2,1)S(1)}, u32[]{:S(2)}, u32[]{:S(2)}) collective-permute-start(bf16[256,512]{1,0:T(8,128)(2,1)S(1)} %collective-permute-done.10.refs_10_.refs_14_), channel_id=1, source_target_pairs={{0,16},{4,20},{8,24},{12,28},{16,0},{20,4},{24,8},{28,12},{1,17},{... | collective-permute-start | bytes 786440 | tf_op jit(solution)/shard_map/ppermute | solution.py:75
  65.2 7.9 %collective-permute-start.20 = (f32[32,1024]{1,0:T(8,128)S(1)}, f32[32,1024]{1,0:T(8,128)S(1)}, u32[]{:S(2)}, u32[]{:S(2)}) collective-permute-start(f32[32,1024]{1,0:T(8,128)S(1)} %get-tuple-element.60), channel_id=1, source_target_pairs={{0,1},{1,0},{2,3},{3,2},{4,5},{5,4},{6,7},{7,6},{8,9},{9,8},{10,11... | collective-permute-start | bytes 393224 | tf_op jit(solution)/shard_map/ppermute | solution.py:75
  65.2 13.0 %collective-permute-start.21 = (f32[32,1024]{1,0:T(8,128)S(1)}, f32[32,1024]{1,0:T(8,128)S(1)}, u32[]{:S(2)}, u32[]{:S(2)}) collective-permute-start(f32[32,1024]{1,0:T(8,128)S(1)} %get-tuple-element.61), channel_id=1, source_target_pairs={{0,2},{1,3},{2,0},{3,1},{4,6},{5,7},{6,4},{7,5},{8,10},{9,11},{10,... | collective-permute-start | bytes 393224 | tf_op jit(solution)/shard_map/ppermute | solution.py:75
  68.3 10.0 %collective-permute-start.22 = (f32[32,1024]{1,0:T(8,128)S(1)}, f32[32,1024]{1,0:T(8,128)S(1)}, u32[]{:S(2)}, u32[]{:S(2)}) collective-permute-start(f32[32,1024]{1,0:T(8,128)S(1)} %get-tuple-element.62), channel_id=1, source_target_pairs={{0,3},{1,2},{2,1},{3,0},{4,7},{5,6},{6,5},{7,4},{8,11},{9,10},{10,... | collective-permute-start | bytes 393224 | tf_op jit(solution)/shard_map/ppermute | solution.py:75
  78.3 6.9 %collective-permute-start.23 = (f32[32,1024]{1,0:T(8,128)S(1)}, f32[32,1024]{1,0:T(8,128)S(1)}, u32[]{:S(2)}, u32[]{:S(2)}) collective-permute-start(f32[32,1024]{1,0:T(8,128)S(1)} %add_add_fusion.refs_0_), channel_id=1, source_target_pairs={{0,1},{1,0},{2,3},{3,2},{4,5},{5,4},{6,7},{7,6},{8,9},{9,8},{10,11... | collective-permute-start | bytes 393224 | tf_op jit(solution)/shard_map/ppermute | solution.py:75
  80.9 8.2 %collective-permute-start.24 = (f32[32,1024]{1,0:T(8,128)S(1)}, f32[32,1024]{1,0:T(8,128)S(1)}, u32[]{:S(2)}, u32[]{:S(2)}) collective-permute-start(f32[32,1024]{1,0:T(8,128)S(1)} %add_add_fusion.refs_0_), channel_id=1, source_target_pairs={{0,2},{1,3},{2,0},{3,1},{4,6},{5,7},{6,4},{7,5},{8,10},{9,11},{10,... | collective-permute-start | bytes 393224 | tf_op jit(solution)/shard_map/ppermute | solution.py:75
  91.2 8.8 %collective-permute-start.30 = (f32[2,32,1024]{2,1,0:T(8,128)S(1)}, f32[2,32,1024]{2,1,0:T(8,128)S(1)}, u32[]{:S(2)}, u32[]{:S(2)}) collective-permute-start(f32[2,32,1024]{2,1,0:T(8,128)S(1)} %pad_maximum_fusion.refs_1_), channel_id=1, source_target_pairs={{0,8},{4,12},{8,0},{12,4},{16,24},{20,28},{24,16},{28,20},{1,9},{5... | collective-permute-start | bytes 786440 | tf_op jit(solution)/shard_map/ppermute | solution.py:75
  92.0 7.8 %collective-permute-start.26 = (f32[32,1024]{1,0:T(8,128)S(1)}, f32[32,1024]{1,0:T(8,128)S(1)}, u32[]{:S(2)}, u32[]{:S(2)}) collective-permute-start(f32[32,1024]{1,0:T(8,128)S(1)} %collective-permute-done.24), channel_id=1, source_target_pairs={{0,1},{1,0},{2,3},{3,2},{4,5},{5,4},{6,7},{7,6},{8,9},{9,8},{10,11... | collective-permute-start | bytes 393224 | tf_op jit(solution)/shard_map/ppermute | solution.py:75
  94.9 12.3 %collective-permute-start.33 = (f32[2,32,1024]{2,1,0:T(8,128)S(1)}, f32[2,32,1024]{2,1,0:T(8,128)S(1)}, u32[]{:S(2)}, u32[]{:S(2)}) collective-permute-start(f32[2,32,1024]{2,1,0:T(8,128)S(1)} %pad_maximum_fusion.refs_1_), channel_id=1, source_target_pairs={{0,16},{4,20},{8,24},{12,28},{16,0},{20,4},{24,8},{28,12},{1,17},{... | collective-permute-start | bytes 786440 | tf_op jit(solution)/shard_map/ppermute | solution.py:75
  100.1 9.6 %collective-permute-start.36 = (f32[2,32,1024]{2,1,0:T(8,128)S(1)}, f32[2,32,1024]{2,1,0:T(8,128)S(1)}, u32[]{:S(2)}, u32[]{:S(2)}) collective-permute-start(f32[2,32,1024]{2,1,0:T(8,128)S(1)} %collective-permute-done.30.refs_4_), channel_id=1, source_target_pairs={{0,16},{4,20},{8,24},{12,28},{16,0},{20,4},{24,8},{28,12},{1,17},{... | collective-permute-start | bytes 786440 | tf_op jit(solution)/shard_map/ppermute | solution.py:75
  103.2 11.9 %collective-permute-start.28 = (f32[2,32,1024]{2,1,0:T(8,128)S(1)}, f32[2,32,1024]{2,1,0:T(8,128)S(1)}, u32[]{:S(2)}, u32[]{:S(2)}) collective-permute-start(f32[2,32,1024]{2,1,0:T(8,128)S(1)} %pad_maximum_fusion.refs_1_), channel_id=1, source_target_pairs={{0,4},{4,0},{8,12},{12,8},{16,20},{20,16},{24,28},{28,24},{1,5},{5... | collective-permute-start | bytes 786440 | tf_op jit(solution)/shard_map/ppermute | solution.py:75
  107.2 8.0 %collective-permute-start.27 = (f32[32,1024]{1,0:T(8,128)S(1)}, f32[32,1024]{1,0:T(8,128)S(1)}, u32[]{:S(2)}, u32[]{:S(2)}) collective-permute-start(f32[32,1024]{1,0:T(8,128)S(1)} %add_add_fusion.refs_0_), channel_id=1, source_target_pairs={{0,4},{4,0},{8,12},{12,8},{16,20},{20,16},{24,28},{28,24},{1,5},{5... | collective-permute-start | bytes 393224 | tf_op jit(solution)/shard_map/ppermute | solution.py:75
  107.2 8.0 %collective-permute-start.29 = (f32[32,1024]{1,0:T(8,128)S(1)}, f32[32,1024]{1,0:T(8,128)S(1)}, u32[]{:S(2)}, u32[]{:S(2)}) collective-permute-start(f32[32,1024]{1,0:T(8,128)S(1)} %collective-permute-done.26.refs_2_), channel_id=1, source_target_pairs={{0,4},{4,0},{8,12},{12,8},{16,20},{20,16},{24,28},{28,24},{1,5},{5... | collective-permute-start | bytes 393224 | tf_op jit(solution)/shard_map/ppermute | solution.py:75
  118.3 13.6 %collective-permute-start.41 = (bf16[2,4,32,512]{3,2,1,0:T(8,128)(2,1)S(1)}, bf16[2,4,32,512]{3,2,1,0:T(8,128)(2,1)S(1)}, u32[]{:S(2)}, u32[]{:S(2)}) collective-permute-start(bf16[2,4,32,512]{3,2,1,0:T(8,128)(2,1)S(1)} %get-tuple-element.66), channel_id=1, source_target_pairs={{0,1},{1,0},{2,3},{3,2},{4,5},{5,4},{6,7},{7,6},{8,9},{9,8},{10,11... | collective-permute-start | bytes 786440 | tf_op jit(solution)/shard_map/ppermute | solution.py:75
  120.3 21.3 %collective-permute-start.42 = (bf16[2,4,32,512]{3,2,1,0:T(8,128)(2,1)S(1)}, bf16[2,4,32,512]{3,2,1,0:T(8,128)(2,1)S(1)}, u32[]{:S(2)}, u32[]{:S(2)}) collective-permute-start(bf16[2,4,32,512]{3,2,1,0:T(8,128)(2,1)S(1)} %get-tuple-element.67), channel_id=1, source_target_pairs={{0,2},{1,3},{2,0},{3,1},{4,6},{5,7},{6,4},{7,5},{8,10},{9,11},{10,... | collective-permute-start | bytes 786440 | tf_op jit(solution)/shard_map/ppermute | solution.py:75
  121.8 19.8 %collective-permute-start.43 = (bf16[2,4,32,512]{3,2,1,0:T(8,128)(2,1)S(1)}, bf16[2,4,32,512]{3,2,1,0:T(8,128)(2,1)S(1)}, u32[]{:S(2)}, u32[]{:S(2)}) collective-permute-start(bf16[2,4,32,512]{3,2,1,0:T(8,128)(2,1)S(1)} %get-tuple-element.68), channel_id=1, source_target_pairs={{0,3},{1,2},{2,1},{3,0},{4,7},{5,6},{6,5},{7,4},{8,11},{9,10},{10,... | collective-permute-start | bytes 786440 | tf_op jit(solution)/shard_map/ppermute | solution.py:75
  122.7 20.0 %collective-permute-start.44 = (bf16[2,4,32,512]{3,2,1,0:T(8,128)(2,1)S(1)}, bf16[2,4,32,512]{3,2,1,0:T(8,128)(2,1)S(1)}, u32[]{:S(2)}, u32[]{:S(2)}) collective-permute-start(bf16[2,4,32,512]{3,2,1,0:T(8,128)(2,1)S(1)} %get-tuple-element.65.refs_0_), channel_id=1, source_target_pairs={{0,4},{4,0},{8,12},{12,8},{16,20},{20,16},{24,28},{28,24},{1,5},{5... | collective-permute-start | bytes 786440 | tf_op jit(solution)/shard_map/ppermute | solution.py:75
  131.9 10.8 %collective-permute-start.45 = (bf16[2,4,32,512]{3,2,1,0:T(8,128)(2,1)S(1)}, bf16[2,4,32,512]{3,2,1,0:T(8,128)(2,1)S(1)}, u32[]{:S(2)}, u32[]{:S(2)}) collective-permute-start(bf16[2,4,32,512]{3,2,1,0:T(8,128)(2,1)S(1)} %collective-permute-done.41.refs_1_), channel_id=1, source_target_pairs={{0,4},{4,0},{8,12},{12,8},{16,20},{20,16},{24,28},{28,24},{1,5},{5... | collective-permute-start | bytes 786440 | tf_op jit(solution)/shard_map/ppermute | solution.py:75
  (18 other events, 70.7 us)

commit v7 on v5

--- a/solution.py
+++ b/solution.py
@@ -92,7 +92,9 @@
 
 
 def col_exchange(pieces):
-    return [pieces[0]] + [swap(piece, "col", d) for d, piece in enumerate(pieces) if d]
+    count = len(pieces)
+    moved = [swap(pieces[d], "col", d) for d in reversed(range(1, count))]
+    return [pieces[0]] + moved[::-1]
 
 
 def chip_gather(pieces):
@@ -226,7 +228,7 @@
         if len(ref.shape) == 2:
             parts.append(ref[:, lanes])
         else:
-            parts += [ref[i, :, lanes] for i in range(ref.shape[0])]
+            parts += [ref[i, :, lanes] for i in reversed(range(ref.shape[0]))]
     return jnp.concatenate(parts)
 
 
@@ -341,7 +343,7 @@
     row, col = place()
     _, n_chip, _, part = pieces[0].shape
     for i, piece in enumerate(pieces):
-        other, d = divmod(i, n_col)
+        other, d = i // n_col, n_col - 1 - i % n_col
         for k in range(n_chip):
             out_ref[:, block((row ^ other ^ (2 * k)) * n_col + (col ^ d), part)] = piece[other, k]
 
@@ -383,11 +385,11 @@
     ]
     own_part, other_part = partial_cost(noise_pieces, latents)
     parts = col_exchange(core_sum(own_part, swap_core(other_part), n_col))
-    tile = functools.reduce(jnp.add, parts)
-    tile_1, tile_2 = swap(tile, "col", 1), swap(tile, "col", 2)
+    tile = functools.reduce(jnp.add, parts[::-1])
+    tile_2, tile_1 = swap(tile, "col", 2), swap(tile, "col", 1)
     tile_3 = swap(tile_2, "col", 1)
     x_tile, y_tile = swap_x(tile), swap_y(tile)
-    pair = jnp.stack([after(tile_1, x_tile, y_tile), tile_2])
+    pair = jnp.stack([after(tile_2, y_tile), after(tile_1, x_tile)])
     x_pair, y_pair = swap_x(pair), swap_y(pair)
     x_last, y_last = swap_x(tile_3), swap_y(tile_3)
     tiles = [
@@ -403,6 +405,7 @@
         stats = iteration(tiles, stats, log_noise)
     *products, noise_pot, data_pot = make_targets(tiles[0], other_tiles, stats, latents, n_col, log_noise)
     products = col_exchange(products)
+    products = products[::-1]
     targets = join(products + [swap_core(piece) for piece in products], n_col)
     return (targets, noise_pot.reshape((own,)), data_pot.reshape((own_data,)))
 

time: 144 us -> 141 us (0.979); the launches traced: 142 us -> 141 us
  transfers between devices with their start and end apart: 48 -> 48, of which waited for: 26 -> 25; matrix products, arithmetic and copies ran while one was open for 0% -> 0% of each run, Pallas kernels for 2% -> 2%
where the time goes in v7:
time: 141 us
  waiting for transfers between devices  77.8 us (55%)
  starting transfers between devices  52 us (37%)
  Pallas kernels  8.26 us (6%)
  local copies, waits for them, and re-layouts  2.44 us (2%)
    ppermute x48, waiting for transfers between devices, swap(): return lax.ppermute(array, axis, [(i, i ^ step) for i in range(count)])  77.8 us
    ppermute x48, starting transfers between devices, swap(): return lax.ppermute(array, axis, [(i, i ^ step) for i in range(count)])  52 us
    pallas_call x10, Pallas kernels, kernel_call(): pl.pallas_call(kernel, in_specs=[VMEM] * len(operands), out_specs=[VMEM]...  8.26 us
  transfers between devices with their start and end apart: 48, of which 25 were waited for; matrix products, arithmetic and copies ran while one was open for 0% of the time, Pallas kernels for 2%

profile of v7, /device:TPU:0, one launch (start us, length us, event | category | flops | bytes accessed | tf_op | source)
XLA Modules:
  0.0 141.3 jit_solution(8277588693976849062)
XLA Ops:
  3.2 3.0 %collective-permute-start.1 = (bf16[256,512]{1,0:T(8,128)(2,1)S(1)}, bf16[256,512]{1,0:T(8,128)(2,1)S(1)}, u32[]{:S(2)}, u32[]{:S(2)}) collective-permute-start(bf16[256,512]{1,0:T(8,128)(2,1)S(1)} %get-tuple-element.39.refs_4_.refs_8_), channel_id=1, source_target_pairs={{0,8},{4,12},{8,0},{12,4},{16,24},{20,28},{24,16},{28,20},{1,9},{5... | collective-permute-start | bytes 786440 | tf_op jit(solution)/shard_map/ppermute | solution.py:75
  6.2 1.5 %collective-permute-start.2 = (bf16[256,512]{1,0:T(8,128)(2,1)S(1)}, bf16[256,512]{1,0:T(8,128)(2,1)S(1)}, u32[]{:S(2)}, u32[]{:S(2)}) collective-permute-start(bf16[256,512]{1,0:T(8,128)(2,1)S(1)} %get-tuple-element.39.refs_4_.refs_8_), channel_id=1, source_target_pairs={{0,16},{4,20},{8,24},{12,28},{16,0},{20,4},{24,8},{28,12},{1,17},{... | collective-permute-start | bytes 786440 | tf_op jit(solution)/shard_map/ppermute | solution.py:75
  7.7 1.6 %collective-permute-start.8 = (bf16[256,512]{1,0:T(8,128)(2,1)S(1)}, bf16[256,512]{1,0:T(8,128)(2,1)S(1)}, u32[]{:S(2)}, u32[]{:S(2)}) collective-permute-start(bf16[256,512]{1,0:T(8,128)(2,1)S(1)} %get-tuple-element.50), channel_id=1, source_target_pairs={{0,1},{1,0},{2,3},{3,2},{4,5},{5,4},{6,7},{7,6},{8,9},{9,8},{10,11... | collective-permute-start | bytes 786440 | tf_op jit(solution)/shard_map/ppermute | solution.py:75
  9.3 2.6 %collective-permute-start.3 = (bf16[256,512]{1,0:T(8,128)(2,1)S(1)}, bf16[256,512]{1,0:T(8,128)(2,1)S(1)}, u32[]{:S(2)}, u32[]{:S(2)}) collective-permute-start(bf16[256,512]{1,0:T(8,128)(2,1)S(1)} %get-tuple-element.43), channel_id=1, source_target_pairs={{0,2},{1,3},{2,0},{3,1},{4,6},{5,7},{6,4},{7,5},{8,10},{9,11},{10,... | collective-permute-start | bytes 786440 | tf_op jit(solution)/shard_map/ppermute | solution.py:75
  14.0 1.6 %collective-permute-start.14 = (bf16[256,512]{1,0:T(8,128)(2,1)S(1)}, bf16[256,512]{1,0:T(8,128)(2,1)S(1)}, u32[]{:S(2)}, u32[]{:S(2)}) collective-permute-start(bf16[256,512]{1,0:T(8,128)(2,1)S(1)} %collective-permute-done.1.refs_8_.refs_12_), channel_id=1, source_target_pairs={{0,16},{4,20},{8,24},{12,28},{16,0},{20,4},{24,8},{28,12},{1,17},{... | collective-permute-start | bytes 786440 | tf_op jit(solution)/shard_map/ppermute | solution.py:75
  15.6 5.1 %collective-permute-done.8.refs_5_.refs_9_ = bf16[256,512]{1,0:T(8,128)(2,1)S(1)} collective-permute-done((bf16[256,512]{1,0:T(8,128)(2,1)S(1)}, bf16[256,512]{1,0:T(8,128)(2,1)S(1)}, u32[]{:S(2)}, u32[]{:S(2)}) %collective-permute-start.8) | collective-permute-done | bytes 262176 | tf_op jit(solution)/shard_map/ppermute | solution.py:75
  21.2 2.5 %collective-permute-start.6 = (bf16[256,512]{1,0:T(8,128)(2,1)S(1)}, bf16[256,512]{1,0:T(8,128)(2,1)S(1)}, u32[]{:S(2)}, u32[]{:S(2)}) collective-permute-start(bf16[256,512]{1,0:T(8,128)(2,1)S(1)} %get-tuple-element.48), channel_id=1, source_target_pairs={{0,3},{1,2},{2,1},{3,0},{4,7},{5,6},{6,5},{7,4},{8,11},{9,10},{10,... | collective-permute-start | bytes 786440 | tf_op jit(solution)/shard_map/ppermute | solution.py:75
  24.2 3.1 %collective-permute-done.11.refs_13_.refs_17_ = bf16[256,512]{1,0:T(8,128)(2,1)S(1)} collective-permute-done((bf16[256,512]{1,0:T(8,128)(2,1)S(1)}, bf16[256,512]{1,0:T(8,128)(2,1)S(1)}, u32[]{:S(2)}, u32[]{:S(2)}) %collective-permute-start.11) | collective-permute-done | bytes 262176 | tf_op jit(solution)/shard_map/ppermute | solution.py:75
  28.1 2.1 %collective-permute-done.9.refs_9_.refs_13_ = bf16[256,512]{1,0:T(8,128)(2,1)S(1)} collective-permute-done((bf16[256,512]{1,0:T(8,128)(2,1)S(1)}, bf16[256,512]{1,0:T(8,128)(2,1)S(1)}, u32[]{:S(2)}, u32[]{:S(2)}) %collective-permute-start.9) | collective-permute-done | bytes 262176 | tf_op jit(solution)/shard_map/ppermute | solution.py:75
  30.7 1.5 %collective-permute-start.12 = (bf16[256,512]{1,0:T(8,128)(2,1)S(1)}, bf16[256,512]{1,0:T(8,128)(2,1)S(1)}, u32[]{:S(2)}, u32[]{:S(2)}) collective-permute-start(bf16[256,512]{1,0:T(8,128)(2,1)S(1)} %collective-permute-done.11.refs_13_.refs_17_), channel_id=1, source_target_pairs={{0,8},{4,12},{8,0},{12,4},{16,24},{20,28},{24,16},{28,20},{1,9},{5... | collective-permute-start | bytes 786440 | tf_op jit(solution)/shard_map/ppermute | solution.py:75
  32.2 2.5 %collective-permute-done.4.refs_1_ = bf16[2,128,512]{2,1,0:T(8,128)(2,1)S(1)} collective-permute-done((bf16[2,128,512]{2,1,0:T(8,128)(2,1)S(1)}, bf16[2,128,512]{2,1,0:T(8,128)(2,1)S(1)}, u32[]{:S(2)}, u32[]{:S(2)}) %collective-permute-start.4) | collective-permute-done | bytes 262176 | tf_op jit(solution)/shard_map/ppermute | solution.py:75
  34.7 1.5 %collective-permute-start.16 = (bf16[256,512]{1,0:T(8,128)(2,1)S(1)}, bf16[256,512]{1,0:T(8,128)(2,1)S(1)}, u32[]{:S(2)}, u32[]{:S(2)}) collective-permute-start(bf16[256,512]{1,0:T(8,128)(2,1)S(1)} %collective-permute-done.6.refs_7_.refs_11_), channel_id=1, source_target_pairs={{0,16},{4,20},{8,24},{12,28},{16,0},{20,4},{24,8},{28,12},{1,17},{... | collective-permute-start | bytes 786440 | tf_op jit(solution)/shard_map/ppermute | solution.py:75
  37.2 2.8 %collective-permute-start.7 = (bf16[2,128,512]{2,1,0:T(8,128)(2,1)S(1)}, bf16[2,128,512]{2,1,0:T(8,128)(2,1)S(1)}, u32[]{:S(2)}, u32[]{:S(2)}) collective-permute-start(bf16[2,128,512]{2,1,0:T(8,128)(2,1)S(1)} %get-tuple-element.49), channel_id=1, source_target_pairs={{0,3},{1,2},{2,1},{3,0},{4,7},{5,6},{6,5},{7,4},{8,11},{9,10},{10,... | collective-permute-start | bytes 786440 | tf_op jit(solution)/shard_map/ppermute | solution.py:75
  40.0 2.3 %collective-permute-done.12.refs_17_.refs_21_ = bf16[256,512]{1,0:T(8,128)(2,1)S(1)} collective-permute-done((bf16[256,512]{1,0:T(8,128)(2,1)S(1)}, bf16[256,512]{1,0:T(8,128)(2,1)S(1)}, u32[]{:S(2)}, u32[]{:S(2)}) %collective-permute-start.12) | collective-permute-done | bytes 262176 | tf_op jit(solution)/shard_map/ppermute | solution.py:75
  42.6 1.8 %collective-permute-start.17 = (bf16[256,512]{1,0:T(8,128)(2,1)S(1)}, bf16[256,512]{1,0:T(8,128)(2,1)S(1)}, u32[]{:S(2)}, u32[]{:S(2)}) collective-permute-start(bf16[256,512]{1,0:T(8,128)(2,1)S(1)} %collective-permute-done.10.refs_10_.refs_14_), channel_id=1, source_target_pairs={{0,16},{4,20},{8,24},{12,28},{16,0},{20,4},{24,8},{28,12},{1,17},{... | collective-permute-start | bytes 786440 | tf_op jit(solution)/shard_map/ppermute | solution.py:75
  44.3 1.5 %collective-permute-start.18 = (bf16[256,512]{1,0:T(8,128)(2,1)S(1)}, bf16[256,512]{1,0:T(8,128)(2,1)S(1)}, u32[]{:S(2)}, u32[]{:S(2)}) collective-permute-start(bf16[256,512]{1,0:T(8,128)(2,1)S(1)} %collective-permute-done.16.refs_15_.refs_19_), channel_id=1, source_target_pairs={{0,8},{4,12},{8,0},{12,4},{16,24},{20,28},{24,16},{28,20},{1,9},{5... | collective-permute-start | bytes 786440 | tf_op jit(solution)/shard_map/ppermute | solution.py:75
  45.8 9.1 %collective-permute-done.5.refs_2_ = bf16[2,128,512]{2,1,0:T(8,128)(2,1)S(1)} collective-permute-done((bf16[2,128,512]{2,1,0:T(8,128)(2,1)S(1)}, bf16[2,128,512]{2,1,0:T(8,128)(2,1)S(1)}, u32[]{:S(2)}, u32[]{:S(2)}) %collective-permute-start.5) | collective-permute-done | bytes 262176 | tf_op jit(solution)/shard_map/ppermute | solution.py:75
  55.0 2.0 %shard_map.52 = (f32[128,1024]{1,0:T(8,128)S(1)}, f32[128,1024]{1,0:T(8,128)S(1)}) custom-call(bf16[2,128,512]{2,1,0:T(8,128)(2,1)S(1)} %get-tuple-element.41.refs_0_, bf16[2,128,512]{2,1,0:T(8,128)(2,1)S(1)} %collective-permute-done.4.refs_1_, bf16[2,128,512]{2,1,0:T(8,128)(2,1)S(1)} %collective-permute-done.5.refs_2_, ...), custom_call_target="tpu_custom_call" | custom-call | flops 1073741824 | bytes 5242880 | tf_op jit(solution)/shard_map/pallas_call | solution.py:115
  57.1 1.9 %collective-permute-done.19.other_ref = f32[128,1024]{1,0:T(8,128)S(1)} collective-permute-done((f32[128,1024]{1,0:T(8,128)S(1)}, f32[128,1024]{1,0:T(8,128)S(1)}, u32[]{:S(2)}, u32[]{:S(2)}) %collective-permute-start.19) | collective-permute-done | bytes 524320 | tf_op jit(solution)/shard_map/ppermute | solution.py:75
  59.1 1.8 %collective-permute-start.20 = (f32[32,1024]{1,0:T(8,128)S(1)}, f32[32,1024]{1,0:T(8,128)S(1)}, u32[]{:S(2)}, u32[]{:S(2)}) collective-permute-start(f32[32,1024]{1,0:T(8,128)S(1)} %get-tuple-element.59), channel_id=1, source_target_pairs={{0,3},{1,2},{2,1},{3,0},{4,7},{5,6},{6,5},{7,4},{8,11},{9,10},{10,... | collective-permute-start | bytes 393224 | tf_op jit(solution)/shard_map/ppermute | solution.py:75
  60.9 5.8 %collective-permute-start.21 = (f32[32,1024]{1,0:T(8,128)S(1)}, f32[32,1024]{1,0:T(8,128)S(1)}, u32[]{:S(2)}, u32[]{:S(2)}) collective-permute-start(f32[32,1024]{1,0:T(8,128)S(1)} %get-tuple-element.60), channel_id=1, source_target_pairs={{0,2},{1,3},{2,0},{3,1},{4,6},{5,7},{6,4},{7,5},{8,10},{9,11},{10,... | collective-permute-start | bytes 393224 | tf_op jit(solution)/shard_map/ppermute | solution.py:75
  66.7 9.1 %collective-permute-done.21 = f32[32,1024]{1,0:T(8,128)S(1)} collective-permute-done((f32[32,1024]{1,0:T(8,128)S(1)}, f32[32,1024]{1,0:T(8,128)S(1)}, u32[]{:S(2)}, u32[]{:S(2)}) %collective-permute-start.21) | collective-permute-done | bytes 131104 | tf_op jit(solution)/shard_map/ppermute | solution.py:75
  77.1 2.3 %collective-permute-start.25 = (f32[32,1024]{1,0:T(8,128)S(1)}, f32[32,1024]{1,0:T(8,128)S(1)}, u32[]{:S(2)}, u32[]{:S(2)}) collective-permute-start(f32[32,1024]{1,0:T(8,128)S(1)} %add_add_fusion.refs_0_), channel_id=1, source_target_pairs={{0,1},{1,0},{2,3},{3,2},{4,5},{5,4},{6,7},{7,6},{8,9},{9,8},{10,11... | collective-permute-start | bytes 393224 | tf_op jit(solution)/shard_map/ppermute | solution.py:75
  80.6 2.9 %collective-permute-done.23 = f32[32,1024]{1,0:T(8,128)S(1)} collective-permute-done((f32[32,1024]{1,0:T(8,128)S(1)}, f32[32,1024]{1,0:T(8,128)S(1)}, u32[]{:S(2)}, u32[]{:S(2)}) %collective-permute-start.23) | collective-permute-done | bytes 131104 | tf_op jit(solution)/shard_map/ppermute | solution.py:75
  88.0 3.0 %collective-permute-done.27.refs_2_ = f32[32,1024]{1,0:T(8,128)S(1)} collective-permute-done((f32[32,1024]{1,0:T(8,128)S(1)}, f32[32,1024]{1,0:T(8,128)S(1)}, u32[]{:S(2)}, u32[]{:S(2)}) %collective-permute-start.27) | collective-permute-done | bytes 131104 | tf_op jit(solution)/shard_map/ppermute | solution.py:75
  94.6 1.6 %collective-permute-start.32 = (f32[32,1024]{1,0:T(8,128)S(1)}, f32[32,1024]{1,0:T(8,128)S(1)}, u32[]{:S(2)}, u32[]{:S(2)}) collective-permute-start(f32[32,1024]{1,0:T(8,128)S(1)} %collective-permute-done.27.refs_2_), channel_id=1, source_target_pairs={{0,8},{4,12},{8,0},{12,4},{16,24},{20,28},{24,16},{28,20},{1,9},{5... | collective-permute-start | bytes 393224 | tf_op jit(solution)/shard_map/ppermute | solution.py:75
  98.4 2.6 %collective-permute-done.32.refs_5_ = f32[32,1024]{1,0:T(8,128)S(1)} collective-permute-done((f32[32,1024]{1,0:T(8,128)S(1)}, f32[32,1024]{1,0:T(8,128)S(1)}, u32[]{:S(2)}, u32[]{:S(2)}) %collective-permute-start.32) | collective-permute-done | bytes 131104 | tf_op jit(solution)/shard_map/ppermute | solution.py:75
  101.0 2.1 %collective-permute-done.37.refs_11_ = f32[32,1024]{1,0:T(8,128)S(1)} collective-permute-done((f32[32,1024]{1,0:T(8,128)S(1)}, f32[32,1024]{1,0:T(8,128)S(1)}, u32[]{:S(2)}, u32[]{:S(2)}) %collective-permute-start.37) | collective-permute-done | bytes 131104 | tf_op jit(solution)/shard_map/ppermute | solution.py:75
  109.6 2.2 %shard_map.57 = (bf16[2,4,32,512]{3,2,1,0:T(8,128)(2,1)S(1)}, bf16[2,4,32,512]{3,2,1,0:T(8,128)(2,1)S(1)}, bf16[2,4,32,512]{3,2,1,0:T(8,128)(2,1)S(1)}, bf16[2,4...) custom-call(f32[32,1024]{1,0:T(8,128)S(1)} %add_add_fusion.refs_0_, ...), custom_call_target="tpu_custom_call" | custom-call | flops 1073741824 | bytes 5259264 | tf_op jit(solution)/shard_map/pallas_call | solution.py:115
  111.7 2.0 %collective-permute-start.41 = (bf16[2,4,32,512]{3,2,1,0:T(8,128)(2,1)S(1)}, bf16[2,4,32,512]{3,2,1,0:T(8,128)(2,1)S(1)}, u32[]{:S(2)}, u32[]{:S(2)}) collective-permute-start(bf16[2,4,32,512]{3,2,1,0:T(8,128)(2,1)S(1)} %get-tuple-element.65), channel_id=1, source_target_pairs={{0,3},{1,2},{2,1},{3,0},{4,7},{5,6},{6,5},{7,4},{8,11},{9,10},{10,... | collective-permute-start | bytes 786440 | tf_op jit(solution)/shard_map/ppermute | solution.py:75
  116.1 6.7 %collective-permute-done.41.refs_0_ = bf16[2,4,32,512]{3,2,1,0:T(8,128)(2,1)S(1)} collective-permute-done((bf16[2,4,32,512]{3,2,1,0:T(8,128)(2,1)S(1)}, bf16[2,4,32,512]{3,2,1,0:T(8,128)(2,1)S(1)}, u32[]{:S(2)}, u32[]{:S(2)}) %collective-permute-start.41) | collective-permute-done | bytes 262176 | tf_op jit(solution)/shard_map/ppermute | solution.py:75
  122.8 15.5 %collective-permute-done.42.refs_1_ = bf16[2,4,32,512]{3,2,1,0:T(8,128)(2,1)S(1)} collective-permute-done((bf16[2,4,32,512]{3,2,1,0:T(8,128)(2,1)S(1)}, bf16[2,4,32,512]{3,2,1,0:T(8,128)(2,1)S(1)}, u32[]{:S(2)}, u32[]{:S(2)}) %collective-permute-start.42) | collective-permute-done | bytes 262176 | tf_op jit(solution)/shard_map/ppermute | solution.py:75
  (81 shorter events, 32.9 us)
Async XLA Ops:
  1.9 12.0 %collective-permute-start = (bf16[128,2048]{1,0:T(8,128)(2,1)S(1)}, bf16[128,2048]{1,0:T(8,128)(2,1)S(1)}, u32[]{:S(2)}, u32[]{:S(2)}) collective-permute-start(bf16[128,2048]{1,0:T(8,128)(2,1)S(1)} %get-tuple-element.38), channel_id=1, source_target_pairs={{0,4},{4,0},{8,12},{12,8},{16,20},{20,16},{24,28},{28,24},{1,5},{5... | collective-permute-start | bytes 1572872 | tf_op jit(solution)/shard_map/ppermute | solution.py:75
  3.2 9.3 %collective-permute-start.1 = (bf16[256,512]{1,0:T(8,128)(2,1)S(1)}, bf16[256,512]{1,0:T(8,128)(2,1)S(1)}, u32[]{:S(2)}, u32[]{:S(2)}) collective-permute-start(bf16[256,512]{1,0:T(8,128)(2,1)S(1)} %get-tuple-element.39.refs_4_.refs_8_), channel_id=1, source_target_pairs={{0,8},{4,12},{8,0},{12,4},{16,24},{20,28},{24,16},{28,20},{1,9},{5... | collective-permute-start | bytes 786440 | tf_op jit(solution)/shard_map/ppermute | solution.py:75
  6.2 7.8 %collective-permute-start.2 = (bf16[256,512]{1,0:T(8,128)(2,1)S(1)}, bf16[256,512]{1,0:T(8,128)(2,1)S(1)}, u32[]{:S(2)}, u32[]{:S(2)}) collective-permute-start(bf16[256,512]{1,0:T(8,128)(2,1)S(1)} %get-tuple-element.39.refs_4_.refs_8_), channel_id=1, source_target_pairs={{0,16},{4,20},{8,24},{12,28},{16,0},{20,4},{24,8},{28,12},{1,17},{... | collective-permute-start | bytes 786440 | tf_op jit(solution)/shard_map/ppermute | solution.py:75
  7.7 13.0 %collective-permute-start.8 = (bf16[256,512]{1,0:T(8,128)(2,1)S(1)}, bf16[256,512]{1,0:T(8,128)(2,1)S(1)}, u32[]{:S(2)}, u32[]{:S(2)}) collective-permute-start(bf16[256,512]{1,0:T(8,128)(2,1)S(1)} %get-tuple-element.50), channel_id=1, source_target_pairs={{0,1},{1,0},{2,3},{3,2},{4,5},{5,4},{6,7},{7,6},{8,9},{9,8},{10,11... | collective-permute-start | bytes 786440 | tf_op jit(solution)/shard_map/ppermute | solution.py:75
  9.3 14.9 %collective-permute-start.3 = (bf16[256,512]{1,0:T(8,128)(2,1)S(1)}, bf16[256,512]{1,0:T(8,128)(2,1)S(1)}, u32[]{:S(2)}, u32[]{:S(2)}) collective-permute-start(bf16[256,512]{1,0:T(8,128)(2,1)S(1)} %get-tuple-element.43), channel_id=1, source_target_pairs={{0,2},{1,3},{2,0},{3,1},{4,6},{5,7},{6,4},{7,5},{8,10},{9,11},{10,... | collective-permute-start | bytes 786440 | tf_op jit(solution)/shard_map/ppermute | solution.py:75
  14.0 10.2 %collective-permute-start.14 = (bf16[256,512]{1,0:T(8,128)(2,1)S(1)}, bf16[256,512]{1,0:T(8,128)(2,1)S(1)}, u32[]{:S(2)}, u32[]{:S(2)}) collective-permute-start(bf16[256,512]{1,0:T(8,128)(2,1)S(1)} %collective-permute-done.1.refs_8_.refs_12_), channel_id=1, source_target_pairs={{0,16},{4,20},{8,24},{12,28},{16,0},{20,4},{24,8},{28,12},{1,17},{... | collective-permute-start | bytes 786440 | tf_op jit(solution)/shard_map/ppermute | solution.py:75
  21.2 11.0 %collective-permute-start.6 = (bf16[256,512]{1,0:T(8,128)(2,1)S(1)}, bf16[256,512]{1,0:T(8,128)(2,1)S(1)}, u32[]{:S(2)}, u32[]{:S(2)}) collective-permute-start(bf16[256,512]{1,0:T(8,128)(2,1)S(1)} %get-tuple-element.48), channel_id=1, source_target_pairs={{0,3},{1,2},{2,1},{3,0},{4,7},{5,6},{6,5},{7,4},{8,11},{9,10},{10,... | collective-permute-start | bytes 786440 | tf_op jit(solution)/shard_map/ppermute | solution.py:75
  24.2 10.5 %collective-permute-start.4 = (bf16[2,128,512]{2,1,0:T(8,128)(2,1)S(1)}, bf16[2,128,512]{2,1,0:T(8,128)(2,1)S(1)}, u32[]{:S(2)}, u32[]{:S(2)}) collective-permute-start(bf16[2,128,512]{2,1,0:T(8,128)(2,1)S(1)} %get-tuple-element.44), channel_id=1, source_target_pairs={{0,1},{1,0},{2,3},{3,2},{4,5},{5,4},{6,7},{7,6},{8,9},{9,8},{10,11... | collective-permute-start | bytes 786440 | tf_op jit(solution)/shard_map/ppermute | solution.py:75
  30.2 9.8 %collective-permute-start.10 = (bf16[256,512]{1,0:T(8,128)(2,1)S(1)}, bf16[256,512]{1,0:T(8,128)(2,1)S(1)}, u32[]{:S(2)}, u32[]{:S(2)}) collective-permute-start(bf16[256,512]{1,0:T(8,128)(2,1)S(1)} %collective-permute-done.3.refs_6_.refs_10_), channel_id=1, source_target_pairs={{0,8},{4,12},{8,0},{12,4},{16,24},{20,28},{24,16},{28,20},{1,9},{5... | collective-permute-start | bytes 786440 | tf_op jit(solution)/shard_map/ppermute | solution.py:75
  30.7 11.6 %collective-permute-start.12 = (bf16[256,512]{1,0:T(8,128)(2,1)S(1)}, bf16[256,512]{1,0:T(8,128)(2,1)S(1)}, u32[]{:S(2)}, u32[]{:S(2)}) collective-permute-start(bf16[256,512]{1,0:T(8,128)(2,1)S(1)} %collective-permute-done.11.refs_13_.refs_17_), channel_id=1, source_target_pairs={{0,8},{4,12},{8,0},{12,4},{16,24},{20,28},{24,16},{28,20},{1,9},{5... | collective-permute-start | bytes 786440 | tf_op jit(solution)/shard_map/ppermute | solution.py:75
  34.7 9.6 %collective-permute-start.16 = (bf16[256,512]{1,0:T(8,128)(2,1)S(1)}, bf16[256,512]{1,0:T(8,128)(2,1)S(1)}, u32[]{:S(2)}, u32[]{:S(2)}) collective-permute-start(bf16[256,512]{1,0:T(8,128)(2,1)S(1)} %collective-permute-done.6.refs_7_.refs_11_), channel_id=1, source_target_pairs={{0,16},{4,20},{8,24},{12,28},{16,0},{20,4},{24,8},{28,12},{1,17},{... | collective-permute-start | bytes 786440 | tf_op jit(solution)/shard_map/ppermute | solution.py:75
  36.2 18.7 %collective-permute-start.5 = (bf16[2,128,512]{2,1,0:T(8,128)(2,1)S(1)}, bf16[2,128,512]{2,1,0:T(8,128)(2,1)S(1)}, u32[]{:S(2)}, u32[]{:S(2)}) collective-permute-start(bf16[2,128,512]{2,1,0:T(8,128)(2,1)S(1)} %get-tuple-element.46), channel_id=1, source_target_pairs={{0,2},{1,3},{2,0},{3,1},{4,6},{5,7},{6,4},{7,5},{8,10},{9,11},{10,... | collective-permute-start | bytes 786440 | tf_op jit(solution)/shard_map/ppermute | solution.py:75
  37.2 17.8 %collective-permute-start.7 = (bf16[2,128,512]{2,1,0:T(8,128)(2,1)S(1)}, bf16[2,128,512]{2,1,0:T(8,128)(2,1)S(1)}, u32[]{:S(2)}, u32[]{:S(2)}) collective-permute-start(bf16[2,128,512]{2,1,0:T(8,128)(2,1)S(1)} %get-tuple-element.49), channel_id=1, source_target_pairs={{0,3},{1,2},{2,1},{3,0},{4,7},{5,6},{6,5},{7,4},{8,11},{9,10},{10,... | collective-permute-start | bytes 786440 | tf_op jit(solution)/shard_map/ppermute | solution.py:75
  42.3 12.7 %collective-permute-start.13 = (bf16[256,512]{1,0:T(8,128)(2,1)S(1)}, bf16[256,512]{1,0:T(8,128)(2,1)S(1)}, u32[]{:S(2)}, u32[]{:S(2)}) collective-permute-start(bf16[256,512]{1,0:T(8,128)(2,1)S(1)} %collective-permute-done.6.refs_7_.refs_11_), channel_id=1, source_target_pairs={{0,8},{4,12},{8,0},{12,4},{16,24},{20,28},{24,16},{28,20},{1,9},{5... | collective-permute-start | bytes 786440 | tf_op jit(solution)/shard_map/ppermute | solution.py:75
  42.6 12.4 %collective-permute-start.17 = (bf16[256,512]{1,0:T(8,128)(2,1)S(1)}, bf16[256,512]{1,0:T(8,128)(2,1)S(1)}, u32[]{:S(2)}, u32[]{:S(2)}) collective-permute-start(bf16[256,512]{1,0:T(8,128)(2,1)S(1)} %collective-permute-done.10.refs_10_.refs_14_), channel_id=1, source_target_pairs={{0,16},{4,20},{8,24},{12,28},{16,0},{20,4},{24,8},{28,12},{1,17},{... | collective-permute-start | bytes 786440 | tf_op jit(solution)/shard_map/ppermute | solution.py:75
  44.3 10.7 %collective-permute-start.18 = (bf16[256,512]{1,0:T(8,128)(2,1)S(1)}, bf16[256,512]{1,0:T(8,128)(2,1)S(1)}, u32[]{:S(2)}, u32[]{:S(2)}) collective-permute-start(bf16[256,512]{1,0:T(8,128)(2,1)S(1)} %collective-permute-done.16.refs_15_.refs_19_), channel_id=1, source_target_pairs={{0,8},{4,12},{8,0},{12,4},{16,24},{20,28},{24,16},{28,20},{1,9},{5... | collective-permute-start | bytes 786440 | tf_op jit(solution)/shard_map/ppermute | solution.py:75
  59.1 7.6 %collective-permute-start.20 = (f32[32,1024]{1,0:T(8,128)S(1)}, f32[32,1024]{1,0:T(8,128)S(1)}, u32[]{:S(2)}, u32[]{:S(2)}) collective-permute-start(f32[32,1024]{1,0:T(8,128)S(1)} %get-tuple-element.59), channel_id=1, source_target_pairs={{0,3},{1,2},{2,1},{3,0},{4,7},{5,6},{6,5},{7,4},{8,11},{9,10},{10,... | collective-permute-start | bytes 393224 | tf_op jit(solution)/shard_map/ppermute | solution.py:75
  60.9 14.9 %collective-permute-start.21 = (f32[32,1024]{1,0:T(8,128)S(1)}, f32[32,1024]{1,0:T(8,128)S(1)}, u32[]{:S(2)}, u32[]{:S(2)}) collective-permute-start(f32[32,1024]{1,0:T(8,128)S(1)} %get-tuple-element.60), channel_id=1, source_target_pairs={{0,2},{1,3},{2,0},{3,1},{4,6},{5,7},{6,4},{7,5},{8,10},{9,11},{10,... | collective-permute-start | bytes 393224 | tf_op jit(solution)/shard_map/ppermute | solution.py:75
  66.7 9.1 %collective-permute-start.22 = (f32[32,1024]{1,0:T(8,128)S(1)}, f32[32,1024]{1,0:T(8,128)S(1)}, u32[]{:S(2)}, u32[]{:S(2)}) collective-permute-start(f32[32,1024]{1,0:T(8,128)S(1)} %get-tuple-element.61), channel_id=1, source_target_pairs={{0,1},{1,0},{2,3},{3,2},{4,5},{5,4},{6,7},{7,6},{8,9},{9,8},{10,11... | collective-permute-start | bytes 393224 | tf_op jit(solution)/shard_map/ppermute | solution.py:75
  75.8 7.7 %collective-permute-start.23 = (f32[32,1024]{1,0:T(8,128)S(1)}, f32[32,1024]{1,0:T(8,128)S(1)}, u32[]{:S(2)}, u32[]{:S(2)}) collective-permute-start(f32[32,1024]{1,0:T(8,128)S(1)} %add_add_fusion.refs_0_), channel_id=1, source_target_pairs={{0,2},{1,3},{2,0},{3,1},{4,6},{5,7},{6,4},{7,5},{8,10},{9,11},{10,... | collective-permute-start | bytes 393224 | tf_op jit(solution)/shard_map/ppermute | solution.py:75
  75.9 7.6 %collective-permute-start.24 = (f32[32,1024]{1,0:T(8,128)S(1)}, f32[32,1024]{1,0:T(8,128)S(1)}, u32[]{:S(2)}, u32[]{:S(2)}) collective-permute-start(f32[32,1024]{1,0:T(8,128)S(1)} %add_add_fusion.refs_0_), channel_id=1, source_target_pairs={{0,16},{4,20},{8,24},{12,28},{16,0},{20,4},{24,8},{28,12},{1,17},{... | collective-permute-start | bytes 393224 | tf_op jit(solution)/shard_map/ppermute | solution.py:75
  77.1 7.8 %collective-permute-start.25 = (f32[32,1024]{1,0:T(8,128)S(1)}, f32[32,1024]{1,0:T(8,128)S(1)}, u32[]{:S(2)}, u32[]{:S(2)}) collective-permute-start(f32[32,1024]{1,0:T(8,128)S(1)} %add_add_fusion.refs_0_), channel_id=1, source_target_pairs={{0,1},{1,0},{2,3},{3,2},{4,5},{5,4},{6,7},{7,6},{8,9},{9,8},{10,11... | collective-permute-start | bytes 393224 | tf_op jit(solution)/shard_map/ppermute | solution.py:75
  84.9 8.3 %collective-permute-start.31 = (f32[2,32,1024]{2,1,0:T(8,128)S(1)}, f32[2,32,1024]{2,1,0:T(8,128)S(1)}, u32[]{:S(2)}, u32[]{:S(2)}) collective-permute-start(f32[2,32,1024]{2,1,0:T(8,128)S(1)} %pad_maximum_fusion.refs_1_), channel_id=1, source_target_pairs={{0,8},{4,12},{8,0},{12,4},{16,24},{20,28},{24,16},{28,20},{1,9},{5... | collective-permute-start | bytes 786440 | tf_op jit(solution)/shard_map/ppermute | solution.py:75
  86.0 12.4 %collective-permute-start.33 = (f32[2,32,1024]{2,1,0:T(8,128)S(1)}, f32[2,32,1024]{2,1,0:T(8,128)S(1)}, u32[]{:S(2)}, u32[]{:S(2)}) collective-permute-start(f32[2,32,1024]{2,1,0:T(8,128)S(1)} %pad_maximum_fusion.refs_1_), channel_id=1, source_target_pairs={{0,16},{4,20},{8,24},{12,28},{16,0},{20,4},{24,8},{28,12},{1,17},{... | collective-permute-start | bytes 786440 | tf_op jit(solution)/shard_map/ppermute | solution.py:75
  93.2 9.9 %collective-permute-start.36 = (f32[2,32,1024]{2,1,0:T(8,128)S(1)}, f32[2,32,1024]{2,1,0:T(8,128)S(1)}, u32[]{:S(2)}, u32[]{:S(2)}) collective-permute-start(f32[2,32,1024]{2,1,0:T(8,128)S(1)} %collective-permute-done.31.refs_4_), channel_id=1, source_target_pairs={{0,16},{4,20},{8,24},{12,28},{16,0},{20,4},{24,8},{28,12},{1,17},{... | collective-permute-start | bytes 786440 | tf_op jit(solution)/shard_map/ppermute | solution.py:75
  94.4 14.2 %collective-permute-start.29 = (f32[2,32,1024]{2,1,0:T(8,128)S(1)}, f32[2,32,1024]{2,1,0:T(8,128)S(1)}, u32[]{:S(2)}, u32[]{:S(2)}) collective-permute-start(f32[2,32,1024]{2,1,0:T(8,128)S(1)} %pad_maximum_fusion.refs_1_), channel_id=1, source_target_pairs={{0,4},{4,0},{8,12},{12,8},{16,20},{20,16},{24,28},{28,24},{1,5},{5... | collective-permute-start | bytes 786440 | tf_op jit(solution)/shard_map/ppermute | solution.py:75
  98.4 10.2 %collective-permute-start.28 = (f32[32,1024]{1,0:T(8,128)S(1)}, f32[32,1024]{1,0:T(8,128)S(1)}, u32[]{:S(2)}, u32[]{:S(2)}) collective-permute-start(f32[32,1024]{1,0:T(8,128)S(1)} %add_add_fusion.refs_0_), channel_id=1, source_target_pairs={{0,4},{4,0},{8,12},{12,8},{16,20},{20,16},{24,28},{28,24},{1,5},{5... | collective-permute-start | bytes 393224 | tf_op jit(solution)/shard_map/ppermute | solution.py:75
  111.7 11.1 %collective-permute-start.41 = (bf16[2,4,32,512]{3,2,1,0:T(8,128)(2,1)S(1)}, bf16[2,4,32,512]{3,2,1,0:T(8,128)(2,1)S(1)}, u32[]{:S(2)}, u32[]{:S(2)}) collective-permute-start(bf16[2,4,32,512]{3,2,1,0:T(8,128)(2,1)S(1)} %get-tuple-element.65), channel_id=1, source_target_pairs={{0,3},{1,2},{2,1},{3,0},{4,7},{5,6},{6,5},{7,4},{8,11},{9,10},{10,... | collective-permute-start | bytes 786440 | tf_op jit(solution)/shard_map/ppermute | solution.py:75
  113.7 24.6 %collective-permute-start.42 = (bf16[2,4,32,512]{3,2,1,0:T(8,128)(2,1)S(1)}, bf16[2,4,32,512]{3,2,1,0:T(8,128)(2,1)S(1)}, u32[]{:S(2)}, u32[]{:S(2)}) collective-permute-start(bf16[2,4,32,512]{3,2,1,0:T(8,128)(2,1)S(1)} %get-tuple-element.66), channel_id=1, source_target_pairs={{0,2},{1,3},{2,0},{3,1},{4,6},{5,7},{6,4},{7,5},{8,10},{9,11},{10,... | collective-permute-start | bytes 786440 | tf_op jit(solution)/shard_map/ppermute | solution.py:75
  115.1 23.2 %collective-permute-start.43 = (bf16[2,4,32,512]{3,2,1,0:T(8,128)(2,1)S(1)}, bf16[2,4,32,512]{3,2,1,0:T(8,128)(2,1)S(1)}, u32[]{:S(2)}, u32[]{:S(2)}) collective-permute-start(bf16[2,4,32,512]{3,2,1,0:T(8,128)(2,1)S(1)} %get-tuple-element.67), channel_id=1, source_target_pairs={{0,1},{1,0},{2,3},{3,2},{4,5},{5,4},{6,7},{7,6},{8,9},{9,8},{10,11... | collective-permute-start | bytes 786440 | tf_op jit(solution)/shard_map/ppermute | solution.py:75
  116.1 23.3 %collective-permute-start.47 = (bf16[2,4,32,512]{3,2,1,0:T(8,128)(2,1)S(1)}, bf16[2,4,32,512]{3,2,1,0:T(8,128)(2,1)S(1)}, u32[]{:S(2)}, u32[]{:S(2)}) collective-permute-start(bf16[2,4,32,512]{3,2,1,0:T(8,128)(2,1)S(1)} %get-tuple-element.68.refs_3_), channel_id=1, source_target_pairs={{0,4},{4,0},{8,12},{12,8},{16,20},{20,16},{24,28},{28,24},{1,5},{5... | collective-permute-start | bytes 786440 | tf_op jit(solution)/shard_map/ppermute | solution.py:75
  122.8 16.6 %collective-permute-start.44 = (bf16[2,4,32,512]{3,2,1,0:T(8,128)(2,1)S(1)}, bf16[2,4,32,512]{3,2,1,0:T(8,128)(2,1)S(1)}, u32[]{:S(2)}, u32[]{:S(2)}) collective-permute-start(bf16[2,4,32,512]{3,2,1,0:T(8,128)(2,1)S(1)} %collective-permute-done.41.refs_0_), channel_id=1, source_target_pairs={{0,4},{4,0},{8,12},{12,8},{16,20},{20,16},{24,28},{28,24},{1,5},{5... | collective-permute-start | bytes 786440 | tf_op jit(solution)/shard_map/ppermute | solution.py:75
  (18 other events, 76.0 us)

commit v8 on v7

--- a/solution.py
+++ b/solution.py
@@ -396,7 +396,7 @@
         [tile, pair, tile_3],
         [x_tile, x_pair, x_last],
         [y_tile, y_pair, y_last],
-        [swap_x(y_tile), swap_y(x_pair), swap_x(y_last)],
+        [swap_y(x_tile), swap_x(y_pair), swap_y(x_last)],
     ]
     other_tiles = [swap_core(piece) for piece in tiles[0]]
     log_noise = math.log2(own * lax.axis_size("row"))

time: 141 us -> 141 us (level)
  transfers between devices with their start and end apart: 48 -> 48, of which waited for: 25 -> 24; matrix products, arithmetic and copies ran while one was open for 0% -> 0% of each run, Pallas kernels for 2% -> 2%
where the time goes in v8:
time: 141 us
  waiting for transfers between devices  78 us (55%)
  starting transfers between devices  51.8 us (37%)
  Pallas kernels  8.26 us (6%)
  local copies, waits for them, and re-layouts  2.44 us (2%)
    ppermute x48, waiting for transfers between devices, swap(): return lax.ppermute(array, axis, [(i, i ^ step) for i in range(count)])  78 us
    ppermute x48, starting transfers between devices, swap(): return lax.ppermute(array, axis, [(i, i ^ step) for i in range(count)])  51.8 us
    pallas_call x10, Pallas kernels, kernel_call(): pl.pallas_call(kernel, in_specs=[VMEM] * len(operands), out_specs=[VMEM]...  8.26 us
  transfers between devices with their start and end apart: 48, of which 24 were waited for; matrix products, arithmetic and copies ran while one was open for 0% of the time, Pallas kernels for 2%

profile of v8, /device:TPU:0, one launch (start us, length us, event | category | flops | bytes accessed | tf_op | source)
XLA Modules:
  0.0 141.2 jit_solution(14056722233317969260)
XLA Ops:
  3.2 3.0 %collective-permute-start.1 = (bf16[256,512]{1,0:T(8,128)(2,1)S(1)}, bf16[256,512]{1,0:T(8,128)(2,1)S(1)}, u32[]{:S(2)}, u32[]{:S(2)}) collective-permute-start(bf16[256,512]{1,0:T(8,128)(2,1)S(1)} %get-tuple-element.39.refs_4_.refs_8_), channel_id=1, source_target_pairs={{0,8},{4,12},{8,0},{12,4},{16,24},{20,28},{24,16},{28,20},{1,9},{5... | collective-permute-start | bytes 786440 | tf_op jit(solution)/shard_map/ppermute | solution.py:75
  6.2 1.5 %collective-permute-start.2 = (bf16[256,512]{1,0:T(8,128)(2,1)S(1)}, bf16[256,512]{1,0:T(8,128)(2,1)S(1)}, u32[]{:S(2)}, u32[]{:S(2)}) collective-permute-start(bf16[256,512]{1,0:T(8,128)(2,1)S(1)} %get-tuple-element.39.refs_4_.refs_8_), channel_id=1, source_target_pairs={{0,16},{4,20},{8,24},{12,28},{16,0},{20,4},{24,8},{28,12},{1,17},{... | collective-permute-start | bytes 786440 | tf_op jit(solution)/shard_map/ppermute | solution.py:75
  7.7 1.6 %collective-permute-start.8 = (bf16[256,512]{1,0:T(8,128)(2,1)S(1)}, bf16[256,512]{1,0:T(8,128)(2,1)S(1)}, u32[]{:S(2)}, u32[]{:S(2)}) collective-permute-start(bf16[256,512]{1,0:T(8,128)(2,1)S(1)} %get-tuple-element.50), channel_id=1, source_target_pairs={{0,1},{1,0},{2,3},{3,2},{4,5},{5,4},{6,7},{7,6},{8,9},{9,8},{10,11... | collective-permute-start | bytes 786440 | tf_op jit(solution)/shard_map/ppermute | solution.py:75
  9.3 2.6 %collective-permute-start.3 = (bf16[256,512]{1,0:T(8,128)(2,1)S(1)}, bf16[256,512]{1,0:T(8,128)(2,1)S(1)}, u32[]{:S(2)}, u32[]{:S(2)}) collective-permute-start(bf16[256,512]{1,0:T(8,128)(2,1)S(1)} %get-tuple-element.43), channel_id=1, source_target_pairs={{0,2},{1,3},{2,0},{3,1},{4,6},{5,7},{6,4},{7,5},{8,10},{9,11},{10,... | collective-permute-start | bytes 786440 | tf_op jit(solution)/shard_map/ppermute | solution.py:75
  14.0 1.6 %collective-permute-start.14 = (bf16[256,512]{1,0:T(8,128)(2,1)S(1)}, bf16[256,512]{1,0:T(8,128)(2,1)S(1)}, u32[]{:S(2)}, u32[]{:S(2)}) collective-permute-start(bf16[256,512]{1,0:T(8,128)(2,1)S(1)} %collective-permute-done.1.refs_8_.refs_12_), channel_id=1, source_target_pairs={{0,16},{4,20},{8,24},{12,28},{16,0},{20,4},{24,8},{28,12},{1,17},{... | collective-permute-start | bytes 786440 | tf_op jit(solution)/shard_map/ppermute | solution.py:75
  15.6 5.1 %collective-permute-done.8.refs_5_.refs_9_ = bf16[256,512]{1,0:T(8,128)(2,1)S(1)} collective-permute-done((bf16[256,512]{1,0:T(8,128)(2,1)S(1)}, bf16[256,512]{1,0:T(8,128)(2,1)S(1)}, u32[]{:S(2)}, u32[]{:S(2)}) %collective-permute-start.8) | collective-permute-done | bytes 262176 | tf_op jit(solution)/shard_map/ppermute | solution.py:75
  21.2 2.5 %collective-permute-start.6 = (bf16[256,512]{1,0:T(8,128)(2,1)S(1)}, bf16[256,512]{1,0:T(8,128)(2,1)S(1)}, u32[]{:S(2)}, u32[]{:S(2)}) collective-permute-start(bf16[256,512]{1,0:T(8,128)(2,1)S(1)} %get-tuple-element.48), channel_id=1, source_target_pairs={{0,3},{1,2},{2,1},{3,0},{4,7},{5,6},{6,5},{7,4},{8,11},{9,10},{10,... | collective-permute-start | bytes 786440 | tf_op jit(solution)/shard_map/ppermute | solution.py:75
  24.2 3.1 %collective-permute-done.11.refs_13_.refs_17_ = bf16[256,512]{1,0:T(8,128)(2,1)S(1)} collective-permute-done((bf16[256,512]{1,0:T(8,128)(2,1)S(1)}, bf16[256,512]{1,0:T(8,128)(2,1)S(1)}, u32[]{:S(2)}, u32[]{:S(2)}) %collective-permute-start.11) | collective-permute-done | bytes 262176 | tf_op jit(solution)/shard_map/ppermute | solution.py:75
  28.1 2.1 %collective-permute-done.9.refs_9_.refs_13_ = bf16[256,512]{1,0:T(8,128)(2,1)S(1)} collective-permute-done((bf16[256,512]{1,0:T(8,128)(2,1)S(1)}, bf16[256,512]{1,0:T(8,128)(2,1)S(1)}, u32[]{:S(2)}, u32[]{:S(2)}) %collective-permute-start.9) | collective-permute-done | bytes 262176 | tf_op jit(solution)/shard_map/ppermute | solution.py:75
  32.2 2.5 %collective-permute-done.4.refs_1_ = bf16[2,128,512]{2,1,0:T(8,128)(2,1)S(1)} collective-permute-done((bf16[2,128,512]{2,1,0:T(8,128)(2,1)S(1)}, bf16[2,128,512]{2,1,0:T(8,128)(2,1)S(1)}, u32[]{:S(2)}, u32[]{:S(2)}) %collective-permute-start.4) | collective-permute-done | bytes 262176 | tf_op jit(solution)/shard_map/ppermute | solution.py:75
  34.7 1.5 %collective-permute-start.16 = (bf16[256,512]{1,0:T(8,128)(2,1)S(1)}, bf16[256,512]{1,0:T(8,128)(2,1)S(1)}, u32[]{:S(2)}, u32[]{:S(2)}) collective-permute-start(bf16[256,512]{1,0:T(8,128)(2,1)S(1)} %collective-permute-done.6.refs_7_.refs_11_), channel_id=1, source_target_pairs={{0,16},{4,20},{8,24},{12,28},{16,0},{20,4},{24,8},{28,12},{1,17},{... | collective-permute-start | bytes 786440 | tf_op jit(solution)/shard_map/ppermute | solution.py:75
  37.2 2.8 %collective-permute-start.7 = (bf16[2,128,512]{2,1,0:T(8,128)(2,1)S(1)}, bf16[2,128,512]{2,1,0:T(8,128)(2,1)S(1)}, u32[]{:S(2)}, u32[]{:S(2)}) collective-permute-start(bf16[2,128,512]{2,1,0:T(8,128)(2,1)S(1)} %get-tuple-element.49), channel_id=1, source_target_pairs={{0,3},{1,2},{2,1},{3,0},{4,7},{5,6},{6,5},{7,4},{8,11},{9,10},{10,... | collective-permute-start | bytes 786440 | tf_op jit(solution)/shard_map/ppermute | solution.py:75
  40.0 2.3 %collective-permute-done.12.refs_17_.refs_21_ = bf16[256,512]{1,0:T(8,128)(2,1)S(1)} collective-permute-done((bf16[256,512]{1,0:T(8,128)(2,1)S(1)}, bf16[256,512]{1,0:T(8,128)(2,1)S(1)}, u32[]{:S(2)}, u32[]{:S(2)}) %collective-permute-start.12) | collective-permute-done | bytes 262176 | tf_op jit(solution)/shard_map/ppermute | solution.py:75
  42.6 1.8 %collective-permute-start.17 = (bf16[256,512]{1,0:T(8,128)(2,1)S(1)}, bf16[256,512]{1,0:T(8,128)(2,1)S(1)}, u32[]{:S(2)}, u32[]{:S(2)}) collective-permute-start(bf16[256,512]{1,0:T(8,128)(2,1)S(1)} %collective-permute-done.10.refs_10_.refs_14_), channel_id=1, source_target_pairs={{0,16},{4,20},{8,24},{12,28},{16,0},{20,4},{24,8},{28,12},{1,17},{... | collective-permute-start | bytes 786440 | tf_op jit(solution)/shard_map/ppermute | solution.py:75
  45.8 9.1 %collective-permute-done.5.refs_2_ = bf16[2,128,512]{2,1,0:T(8,128)(2,1)S(1)} collective-permute-done((bf16[2,128,512]{2,1,0:T(8,128)(2,1)S(1)}, bf16[2,128,512]{2,1,0:T(8,128)(2,1)S(1)}, u32[]{:S(2)}, u32[]{:S(2)}) %collective-permute-start.5) | collective-permute-done | bytes 262176 | tf_op jit(solution)/shard_map/ppermute | solution.py:75
  55.0 2.0 %shard_map.52 = (f32[128,1024]{1,0:T(8,128)S(1)}, f32[128,1024]{1,0:T(8,128)S(1)}) custom-call(bf16[2,128,512]{2,1,0:T(8,128)(2,1)S(1)} %get-tuple-element.41.refs_0_, bf16[2,128,512]{2,1,0:T(8,128)(2,1)S(1)} %collective-permute-done.4.refs_1_, bf16[2,128,512]{2,1,0:T(8,128)(2,1)S(1)} %collective-permute-done.5.refs_2_, ...), custom_call_target="tpu_custom_call" | custom-call | flops 1073741824 | bytes 5242880 | tf_op jit(solution)/shard_map/pallas_call | solution.py:115
  57.1 1.9 %collective-permute-done.19.other_ref = f32[128,1024]{1,0:T(8,128)S(1)} collective-permute-done((f32[128,1024]{1,0:T(8,128)S(1)}, f32[128,1024]{1,0:T(8,128)S(1)}, u32[]{:S(2)}, u32[]{:S(2)}) %collective-permute-start.19) | collective-permute-done | bytes 524320 | tf_op jit(solution)/shard_map/ppermute | solution.py:75
  59.1 1.8 %collective-permute-start.20 = (f32[32,1024]{1,0:T(8,128)S(1)}, f32[32,1024]{1,0:T(8,128)S(1)}, u32[]{:S(2)}, u32[]{:S(2)}) collective-permute-start(f32[32,1024]{1,0:T(8,128)S(1)} %get-tuple-element.59), channel_id=1, source_target_pairs={{0,3},{1,2},{2,1},{3,0},{4,7},{5,6},{6,5},{7,4},{8,11},{9,10},{10,... | collective-permute-start | bytes 393224 | tf_op jit(solution)/shard_map/ppermute | solution.py:75
  60.9 5.8 %collective-permute-start.21 = (f32[32,1024]{1,0:T(8,128)S(1)}, f32[32,1024]{1,0:T(8,128)S(1)}, u32[]{:S(2)}, u32[]{:S(2)}) collective-permute-start(f32[32,1024]{1,0:T(8,128)S(1)} %get-tuple-element.60), channel_id=1, source_target_pairs={{0,2},{1,3},{2,0},{3,1},{4,6},{5,7},{6,4},{7,5},{8,10},{9,11},{10,... | collective-permute-start | bytes 393224 | tf_op jit(solution)/shard_map/ppermute | solution.py:75
  66.7 9.1 %collective-permute-done.21 = f32[32,1024]{1,0:T(8,128)S(1)} collective-permute-done((f32[32,1024]{1,0:T(8,128)S(1)}, f32[32,1024]{1,0:T(8,128)S(1)}, u32[]{:S(2)}, u32[]{:S(2)}) %collective-permute-start.21) | collective-permute-done | bytes 131104 | tf_op jit(solution)/shard_map/ppermute | solution.py:75
  77.1 2.3 %collective-permute-start.25 = (f32[32,1024]{1,0:T(8,128)S(1)}, f32[32,1024]{1,0:T(8,128)S(1)}, u32[]{:S(2)}, u32[]{:S(2)}) collective-permute-start(f32[32,1024]{1,0:T(8,128)S(1)} %add_add_fusion.refs_0_), channel_id=1, source_target_pairs={{0,1},{1,0},{2,3},{3,2},{4,5},{5,4},{6,7},{7,6},{8,9},{9,8},{10,11... | collective-permute-start | bytes 393224 | tf_op jit(solution)/shard_map/ppermute | solution.py:75
  80.6 2.9 %collective-permute-done.23 = f32[32,1024]{1,0:T(8,128)S(1)} collective-permute-done((f32[32,1024]{1,0:T(8,128)S(1)}, f32[32,1024]{1,0:T(8,128)S(1)}, u32[]{:S(2)}, u32[]{:S(2)}) %collective-permute-start.23) | collective-permute-done | bytes 131104 | tf_op jit(solution)/shard_map/ppermute | solution.py:75
  88.1 2.9 %collective-permute-done.27.refs_2_ = f32[32,1024]{1,0:T(8,128)S(1)} collective-permute-done((f32[32,1024]{1,0:T(8,128)S(1)}, f32[32,1024]{1,0:T(8,128)S(1)}, u32[]{:S(2)}, u32[]{:S(2)}) %collective-permute-start.27) | collective-permute-done | bytes 131104 | tf_op jit(solution)/shard_map/ppermute | solution.py:75
  93.2 1.6 %collective-permute-start.36 = (f32[2,32,1024]{2,1,0:T(8,128)S(1)}, f32[2,32,1024]{2,1,0:T(8,128)S(1)}, u32[]{:S(2)}, u32[]{:S(2)}) collective-permute-start(f32[2,32,1024]{2,1,0:T(8,128)S(1)} %collective-permute-done.33.refs_7_), channel_id=1, source_target_pairs={{0,8},{4,12},{8,0},{12,4},{16,24},{20,28},{24,16},{28,20},{1,9},{5... | collective-permute-start | bytes 786440 | tf_op jit(solution)/shard_map/ppermute | solution.py:75
  95.8 1.6 %collective-permute-done.32.refs_5_ = f32[32,1024]{1,0:T(8,128)S(1)} collective-permute-done((f32[32,1024]{1,0:T(8,128)S(1)}, f32[32,1024]{1,0:T(8,128)S(1)}, u32[]{:S(2)}, u32[]{:S(2)}) %collective-permute-start.32) | collective-permute-done | bytes 131104 | tf_op jit(solution)/shard_map/ppermute | solution.py:75
  98.4 2.8 %collective-permute-done.34.refs_8_ = f32[32,1024]{1,0:T(8,128)S(1)} collective-permute-done((f32[32,1024]{1,0:T(8,128)S(1)}, f32[32,1024]{1,0:T(8,128)S(1)}, u32[]{:S(2)}, u32[]{:S(2)}) %collective-permute-start.34) | collective-permute-done | bytes 131104 | tf_op jit(solution)/shard_map/ppermute | solution.py:75
  101.2 2.4 %collective-permute-done.37.refs_11_ = f32[32,1024]{1,0:T(8,128)S(1)} collective-permute-done((f32[32,1024]{1,0:T(8,128)S(1)}, f32[32,1024]{1,0:T(8,128)S(1)}, u32[]{:S(2)}, u32[]{:S(2)}) %collective-permute-start.37) | collective-permute-done | bytes 131104 | tf_op jit(solution)/shard_map/ppermute | solution.py:75
  110.1 2.2 %shard_map.57 = (bf16[2,4,32,512]{3,2,1,0:T(8,128)(2,1)S(1)}, bf16[2,4,32,512]{3,2,1,0:T(8,128)(2,1)S(1)}, bf16[2,4,32,512]{3,2,1,0:T(8,128)(2,1)S(1)}, bf16[2,4...) custom-call(f32[32,1024]{1,0:T(8,128)S(1)} %add_add_fusion.refs_0_, ...), custom_call_target="tpu_custom_call" | custom-call | flops 1073741824 | bytes 5259264 | tf_op jit(solution)/shard_map/pallas_call | solution.py:115
  112.2 1.6 %collective-permute-start.41 = (bf16[2,4,32,512]{3,2,1,0:T(8,128)(2,1)S(1)}, bf16[2,4,32,512]{3,2,1,0:T(8,128)(2,1)S(1)}, u32[]{:S(2)}, u32[]{:S(2)}) collective-permute-start(bf16[2,4,32,512]{3,2,1,0:T(8,128)(2,1)S(1)} %get-tuple-element.65), channel_id=1, source_target_pairs={{0,3},{1,2},{2,1},{3,0},{4,7},{5,6},{6,5},{7,4},{8,11},{9,10},{10,... | collective-permute-start | bytes 786440 | tf_op jit(solution)/shard_map/ppermute | solution.py:75
  115.1 1.5 %collective-permute-start.43 = (bf16[2,4,32,512]{3,2,1,0:T(8,128)(2,1)S(1)}, bf16[2,4,32,512]{3,2,1,0:T(8,128)(2,1)S(1)}, u32[]{:S(2)}, u32[]{:S(2)}) collective-permute-start(bf16[2,4,32,512]{3,2,1,0:T(8,128)(2,1)S(1)} %get-tuple-element.67), channel_id=1, source_target_pairs={{0,1},{1,0},{2,3},{3,2},{4,5},{5,4},{6,7},{7,6},{8,9},{9,8},{10,11... | collective-permute-start | bytes 786440 | tf_op jit(solution)/shard_map/ppermute | solution.py:75
  116.6 6.7 %collective-permute-done.41.refs_0_ = bf16[2,4,32,512]{3,2,1,0:T(8,128)(2,1)S(1)} collective-permute-done((bf16[2,4,32,512]{3,2,1,0:T(8,128)(2,1)S(1)}, bf16[2,4,32,512]{3,2,1,0:T(8,128)(2,1)S(1)}, u32[]{:S(2)}, u32[]{:S(2)}) %collective-permute-start.41) | collective-permute-done | bytes 262176 | tf_op jit(solution)/shard_map/ppermute | solution.py:75
  123.3 15.0 %collective-permute-done.42.refs_1_ = bf16[2,4,32,512]{3,2,1,0:T(8,128)(2,1)S(1)} collective-permute-done((bf16[2,4,32,512]{3,2,1,0:T(8,128)(2,1)S(1)}, bf16[2,4,32,512]{3,2,1,0:T(8,128)(2,1)S(1)}, u32[]{:S(2)}, u32[]{:S(2)}) %collective-permute-start.42) | collective-permute-done | bytes 262176 | tf_op jit(solution)/shard_map/ppermute | solution.py:75
  (81 shorter events, 33.1 us)
Async XLA Ops:
  1.9 12.0 %collective-permute-start = (bf16[128,2048]{1,0:T(8,128)(2,1)S(1)}, bf16[128,2048]{1,0:T(8,128)(2,1)S(1)}, u32[]{:S(2)}, u32[]{:S(2)}) collective-permute-start(bf16[128,2048]{1,0:T(8,128)(2,1)S(1)} %get-tuple-element.38), channel_id=1, source_target_pairs={{0,4},{4,0},{8,12},{12,8},{16,20},{20,16},{24,28},{28,24},{1,5},{5... | collective-permute-start | bytes 1572872 | tf_op jit(solution)/shard_map/ppermute | solution.py:75
  3.2 9.3 %collective-permute-start.1 = (bf16[256,512]{1,0:T(8,128)(2,1)S(1)}, bf16[256,512]{1,0:T(8,128)(2,1)S(1)}, u32[]{:S(2)}, u32[]{:S(2)}) collective-permute-start(bf16[256,512]{1,0:T(8,128)(2,1)S(1)} %get-tuple-element.39.refs_4_.refs_8_), channel_id=1, source_target_pairs={{0,8},{4,12},{8,0},{12,4},{16,24},{20,28},{24,16},{28,20},{1,9},{5... | collective-permute-start | bytes 786440 | tf_op jit(solution)/shard_map/ppermute | solution.py:75
  6.2 7.8 %collective-permute-start.2 = (bf16[256,512]{1,0:T(8,128)(2,1)S(1)}, bf16[256,512]{1,0:T(8,128)(2,1)S(1)}, u32[]{:S(2)}, u32[]{:S(2)}) collective-permute-start(bf16[256,512]{1,0:T(8,128)(2,1)S(1)} %get-tuple-element.39.refs_4_.refs_8_), channel_id=1, source_target_pairs={{0,16},{4,20},{8,24},{12,28},{16,0},{20,4},{24,8},{28,12},{1,17},{... | collective-permute-start | bytes 786440 | tf_op jit(solution)/shard_map/ppermute | solution.py:75
  7.7 13.0 %collective-permute-start.8 = (bf16[256,512]{1,0:T(8,128)(2,1)S(1)}, bf16[256,512]{1,0:T(8,128)(2,1)S(1)}, u32[]{:S(2)}, u32[]{:S(2)}) collective-permute-start(bf16[256,512]{1,0:T(8,128)(2,1)S(1)} %get-tuple-element.50), channel_id=1, source_target_pairs={{0,1},{1,0},{2,3},{3,2},{4,5},{5,4},{6,7},{7,6},{8,9},{9,8},{10,11... | collective-permute-start | bytes 786440 | tf_op jit(solution)/shard_map/ppermute | solution.py:75
  9.3 14.9 %collective-permute-start.3 = (bf16[256,512]{1,0:T(8,128)(2,1)S(1)}, bf16[256,512]{1,0:T(8,128)(2,1)S(1)}, u32[]{:S(2)}, u32[]{:S(2)}) collective-permute-start(bf16[256,512]{1,0:T(8,128)(2,1)S(1)} %get-tuple-element.43), channel_id=1, source_target_pairs={{0,2},{1,3},{2,0},{3,1},{4,6},{5,7},{6,4},{7,5},{8,10},{9,11},{10,... | collective-permute-start | bytes 786440 | tf_op jit(solution)/shard_map/ppermute | solution.py:75
  14.0 10.2 %collective-permute-start.14 = (bf16[256,512]{1,0:T(8,128)(2,1)S(1)}, bf16[256,512]{1,0:T(8,128)(2,1)S(1)}, u32[]{:S(2)}, u32[]{:S(2)}) collective-permute-start(bf16[256,512]{1,0:T(8,128)(2,1)S(1)} %collective-permute-done.1.refs_8_.refs_12_), channel_id=1, source_target_pairs={{0,16},{4,20},{8,24},{12,28},{16,0},{20,4},{24,8},{28,12},{1,17},{... | collective-permute-start | bytes 786440 | tf_op jit(solution)/shard_map/ppermute | solution.py:75
  21.2 11.0 %collective-permute-start.6 = (bf16[256,512]{1,0:T(8,128)(2,1)S(1)}, bf16[256,512]{1,0:T(8,128)(2,1)S(1)}, u32[]{:S(2)}, u32[]{:S(2)}) collective-permute-start(bf16[256,512]{1,0:T(8,128)(2,1)S(1)} %get-tuple-element.48), channel_id=1, source_target_pairs={{0,3},{1,2},{2,1},{3,0},{4,7},{5,6},{6,5},{7,4},{8,11},{9,10},{10,... | collective-permute-start | bytes 786440 | tf_op jit(solution)/shard_map/ppermute | solution.py:75
  24.2 10.5 %collective-permute-start.4 = (bf16[2,128,512]{2,1,0:T(8,128)(2,1)S(1)}, bf16[2,128,512]{2,1,0:T(8,128)(2,1)S(1)}, u32[]{:S(2)}, u32[]{:S(2)}) collective-permute-start(bf16[2,128,512]{2,1,0:T(8,128)(2,1)S(1)} %get-tuple-element.44), channel_id=1, source_target_pairs={{0,1},{1,0},{2,3},{3,2},{4,5},{5,4},{6,7},{7,6},{8,9},{9,8},{10,11... | collective-permute-start | bytes 786440 | tf_op jit(solution)/shard_map/ppermute | solution.py:75
  30.2 9.8 %collective-permute-start.10 = (bf16[256,512]{1,0:T(8,128)(2,1)S(1)}, bf16[256,512]{1,0:T(8,128)(2,1)S(1)}, u32[]{:S(2)}, u32[]{:S(2)}) collective-permute-start(bf16[256,512]{1,0:T(8,128)(2,1)S(1)} %collective-permute-done.3.refs_6_.refs_10_), channel_id=1, source_target_pairs={{0,8},{4,12},{8,0},{12,4},{16,24},{20,28},{24,16},{28,20},{1,9},{5... | collective-permute-start | bytes 786440 | tf_op jit(solution)/shard_map/ppermute | solution.py:75
  30.7 11.6 %collective-permute-start.12 = (bf16[256,512]{1,0:T(8,128)(2,1)S(1)}, bf16[256,512]{1,0:T(8,128)(2,1)S(1)}, u32[]{:S(2)}, u32[]{:S(2)}) collective-permute-start(bf16[256,512]{1,0:T(8,128)(2,1)S(1)} %collective-permute-done.11.refs_13_.refs_17_), channel_id=1, source_target_pairs={{0,8},{4,12},{8,0},{12,4},{16,24},{20,28},{24,16},{28,20},{1,9},{5... | collective-permute-start | bytes 786440 | tf_op jit(solution)/shard_map/ppermute | solution.py:75
  34.7 9.6 %collective-permute-start.16 = (bf16[256,512]{1,0:T(8,128)(2,1)S(1)}, bf16[256,512]{1,0:T(8,128)(2,1)S(1)}, u32[]{:S(2)}, u32[]{:S(2)}) collective-permute-start(bf16[256,512]{1,0:T(8,128)(2,1)S(1)} %collective-permute-done.6.refs_7_.refs_11_), channel_id=1, source_target_pairs={{0,16},{4,20},{8,24},{12,28},{16,0},{20,4},{24,8},{28,12},{1,17},{... | collective-permute-start | bytes 786440 | tf_op jit(solution)/shard_map/ppermute | solution.py:75
  36.2 18.7 %collective-permute-start.5 = (bf16[2,128,512]{2,1,0:T(8,128)(2,1)S(1)}, bf16[2,128,512]{2,1,0:T(8,128)(2,1)S(1)}, u32[]{:S(2)}, u32[]{:S(2)}) collective-permute-start(bf16[2,128,512]{2,1,0:T(8,128)(2,1)S(1)} %get-tuple-element.46), channel_id=1, source_target_pairs={{0,2},{1,3},{2,0},{3,1},{4,6},{5,7},{6,4},{7,5},{8,10},{9,11},{10,... | collective-permute-start | bytes 786440 | tf_op jit(solution)/shard_map/ppermute | solution.py:75
  37.2 17.8 %collective-permute-start.7 = (bf16[2,128,512]{2,1,0:T(8,128)(2,1)S(1)}, bf16[2,128,512]{2,1,0:T(8,128)(2,1)S(1)}, u32[]{:S(2)}, u32[]{:S(2)}) collective-permute-start(bf16[2,128,512]{2,1,0:T(8,128)(2,1)S(1)} %get-tuple-element.49), channel_id=1, source_target_pairs={{0,3},{1,2},{2,1},{3,0},{4,7},{5,6},{6,5},{7,4},{8,11},{9,10},{10,... | collective-permute-start | bytes 786440 | tf_op jit(solution)/shard_map/ppermute | solution.py:75
  42.3 12.7 %collective-permute-start.13 = (bf16[256,512]{1,0:T(8,128)(2,1)S(1)}, bf16[256,512]{1,0:T(8,128)(2,1)S(1)}, u32[]{:S(2)}, u32[]{:S(2)}) collective-permute-start(bf16[256,512]{1,0:T(8,128)(2,1)S(1)} %collective-permute-done.6.refs_7_.refs_11_), channel_id=1, source_target_pairs={{0,8},{4,12},{8,0},{12,4},{16,24},{20,28},{24,16},{28,20},{1,9},{5... | collective-permute-start | bytes 786440 | tf_op jit(solution)/shard_map/ppermute | solution.py:75
  42.6 12.4 %collective-permute-start.17 = (bf16[256,512]{1,0:T(8,128)(2,1)S(1)}, bf16[256,512]{1,0:T(8,128)(2,1)S(1)}, u32[]{:S(2)}, u32[]{:S(2)}) collective-permute-start(bf16[256,512]{1,0:T(8,128)(2,1)S(1)} %collective-permute-done.10.refs_10_.refs_14_), channel_id=1, source_target_pairs={{0,16},{4,20},{8,24},{12,28},{16,0},{20,4},{24,8},{28,12},{1,17},{... | collective-permute-start | bytes 786440 | tf_op jit(solution)/shard_map/ppermute | solution.py:75
  44.3 10.7 %collective-permute-start.18 = (bf16[256,512]{1,0:T(8,128)(2,1)S(1)}, bf16[256,512]{1,0:T(8,128)(2,1)S(1)}, u32[]{:S(2)}, u32[]{:S(2)}) collective-permute-start(bf16[256,512]{1,0:T(8,128)(2,1)S(1)} %collective-permute-done.16.refs_15_.refs_19_), channel_id=1, source_target_pairs={{0,8},{4,12},{8,0},{12,4},{16,24},{20,28},{24,16},{28,20},{1,9},{5... | collective-permute-start | bytes 786440 | tf_op jit(solution)/shard_map/ppermute | solution.py:75
  60.9 14.9 %collective-permute-start.21 = (f32[32,1024]{1,0:T(8,128)S(1)}, f32[32,1024]{1,0:T(8,128)S(1)}, u32[]{:S(2)}, u32[]{:S(2)}) collective-permute-start(f32[32,1024]{1,0:T(8,128)S(1)} %get-tuple-element.60), channel_id=1, source_target_pairs={{0,2},{1,3},{2,0},{3,1},{4,6},{5,7},{6,4},{7,5},{8,10},{9,11},{10,... | collective-permute-start | bytes 393224 | tf_op jit(solution)/shard_map/ppermute | solution.py:75
  66.7 9.1 %collective-permute-start.22 = (f32[32,1024]{1,0:T(8,128)S(1)}, f32[32,1024]{1,0:T(8,128)S(1)}, u32[]{:S(2)}, u32[]{:S(2)}) collective-permute-start(f32[32,1024]{1,0:T(8,128)S(1)} %get-tuple-element.61), channel_id=1, source_target_pairs={{0,1},{1,0},{2,3},{3,2},{4,5},{5,4},{6,7},{7,6},{8,9},{9,8},{10,11... | collective-permute-start | bytes 393224 | tf_op jit(solution)/shard_map/ppermute | solution.py:75
  75.8 7.7 %collective-permute-start.23 = (f32[32,1024]{1,0:T(8,128)S(1)}, f32[32,1024]{1,0:T(8,128)S(1)}, u32[]{:S(2)}, u32[]{:S(2)}) collective-permute-start(f32[32,1024]{1,0:T(8,128)S(1)} %add_add_fusion.refs_0_), channel_id=1, source_target_pairs={{0,2},{1,3},{2,0},{3,1},{4,6},{5,7},{6,4},{7,5},{8,10},{9,11},{10,... | collective-permute-start | bytes 393224 | tf_op jit(solution)/shard_map/ppermute | solution.py:75
  75.9 7.6 %collective-permute-start.24 = (f32[32,1024]{1,0:T(8,128)S(1)}, f32[32,1024]{1,0:T(8,128)S(1)}, u32[]{:S(2)}, u32[]{:S(2)}) collective-permute-start(f32[32,1024]{1,0:T(8,128)S(1)} %add_add_fusion.refs_0_), channel_id=1, source_target_pairs={{0,16},{4,20},{8,24},{12,28},{16,0},{20,4},{24,8},{28,12},{1,17},{... | collective-permute-start | bytes 393224 | tf_op jit(solution)/shard_map/ppermute | solution.py:75
  77.1 7.8 %collective-permute-start.25 = (f32[32,1024]{1,0:T(8,128)S(1)}, f32[32,1024]{1,0:T(8,128)S(1)}, u32[]{:S(2)}, u32[]{:S(2)}) collective-permute-start(f32[32,1024]{1,0:T(8,128)S(1)} %add_add_fusion.refs_0_), channel_id=1, source_target_pairs={{0,1},{1,0},{2,3},{3,2},{4,5},{5,4},{6,7},{7,6},{8,9},{9,8},{10,11... | collective-permute-start | bytes 393224 | tf_op jit(solution)/shard_map/ppermute | solution.py:75
  84.9 8.3 %collective-permute-start.33 = (f32[2,32,1024]{2,1,0:T(8,128)S(1)}, f32[2,32,1024]{2,1,0:T(8,128)S(1)}, u32[]{:S(2)}, u32[]{:S(2)}) collective-permute-start(f32[2,32,1024]{2,1,0:T(8,128)S(1)} %pad_maximum_fusion.refs_1_), channel_id=1, source_target_pairs={{0,16},{4,20},{8,24},{12,28},{16,0},{20,4},{24,8},{28,12},{1,17},{... | collective-permute-start | bytes 786440 | tf_op jit(solution)/shard_map/ppermute | solution.py:75
  86.0 12.4 %collective-permute-start.31 = (f32[2,32,1024]{2,1,0:T(8,128)S(1)}, f32[2,32,1024]{2,1,0:T(8,128)S(1)}, u32[]{:S(2)}, u32[]{:S(2)}) collective-permute-start(f32[2,32,1024]{2,1,0:T(8,128)S(1)} %pad_maximum_fusion.refs_1_), channel_id=1, source_target_pairs={{0,8},{4,12},{8,0},{12,4},{16,24},{20,28},{24,16},{28,20},{1,9},{5... | collective-permute-start | bytes 786440 | tf_op jit(solution)/shard_map/ppermute | solution.py:75
  93.2 10.4 %collective-permute-start.36 = (f32[2,32,1024]{2,1,0:T(8,128)S(1)}, f32[2,32,1024]{2,1,0:T(8,128)S(1)}, u32[]{:S(2)}, u32[]{:S(2)}) collective-permute-start(f32[2,32,1024]{2,1,0:T(8,128)S(1)} %collective-permute-done.33.refs_7_), channel_id=1, source_target_pairs={{0,8},{4,12},{8,0},{12,4},{16,24},{20,28},{24,16},{28,20},{1,9},{5... | collective-permute-start | bytes 786440 | tf_op jit(solution)/shard_map/ppermute | solution.py:75
  94.9 14.2 %collective-permute-start.29 = (f32[2,32,1024]{2,1,0:T(8,128)S(1)}, f32[2,32,1024]{2,1,0:T(8,128)S(1)}, u32[]{:S(2)}, u32[]{:S(2)}) collective-permute-start(f32[2,32,1024]{2,1,0:T(8,128)S(1)} %pad_maximum_fusion.refs_1_), channel_id=1, source_target_pairs={{0,4},{4,0},{8,12},{12,8},{16,20},{20,16},{24,28},{28,24},{1,5},{5... | collective-permute-start | bytes 786440 | tf_op jit(solution)/shard_map/ppermute | solution.py:75
  98.4 10.7 %collective-permute-start.28 = (f32[32,1024]{1,0:T(8,128)S(1)}, f32[32,1024]{1,0:T(8,128)S(1)}, u32[]{:S(2)}, u32[]{:S(2)}) collective-permute-start(f32[32,1024]{1,0:T(8,128)S(1)} %add_add_fusion.refs_0_), channel_id=1, source_target_pairs={{0,4},{4,0},{8,12},{12,8},{16,20},{20,16},{24,28},{28,24},{1,5},{5... | collective-permute-start | bytes 393224 | tf_op jit(solution)/shard_map/ppermute | solution.py:75
  101.2 7.9 %collective-permute-start.30 = (f32[32,1024]{1,0:T(8,128)S(1)}, f32[32,1024]{1,0:T(8,128)S(1)}, u32[]{:S(2)}, u32[]{:S(2)}) collective-permute-start(f32[32,1024]{1,0:T(8,128)S(1)} %collective-permute-done.27.refs_2_), channel_id=1, source_target_pairs={{0,4},{4,0},{8,12},{12,8},{16,20},{20,16},{24,28},{28,24},{1,5},{5... | collective-permute-start | bytes 393224 | tf_op jit(solution)/shard_map/ppermute | solution.py:75
  112.2 11.1 %collective-permute-start.41 = (bf16[2,4,32,512]{3,2,1,0:T(8,128)(2,1)S(1)}, bf16[2,4,32,512]{3,2,1,0:T(8,128)(2,1)S(1)}, u32[]{:S(2)}, u32[]{:S(2)}) collective-permute-start(bf16[2,4,32,512]{3,2,1,0:T(8,128)(2,1)S(1)} %get-tuple-element.65), channel_id=1, source_target_pairs={{0,3},{1,2},{2,1},{3,0},{4,7},{5,6},{6,5},{7,4},{8,11},{9,10},{10,... | collective-permute-start | bytes 786440 | tf_op jit(solution)/shard_map/ppermute | solution.py:75
  113.9 24.4 %collective-permute-start.42 = (bf16[2,4,32,512]{3,2,1,0:T(8,128)(2,1)S(1)}, bf16[2,4,32,512]{3,2,1,0:T(8,128)(2,1)S(1)}, u32[]{:S(2)}, u32[]{:S(2)}) collective-permute-start(bf16[2,4,32,512]{3,2,1,0:T(8,128)(2,1)S(1)} %get-tuple-element.66), channel_id=1, source_target_pairs={{0,2},{1,3},{2,0},{3,1},{4,6},{5,7},{6,4},{7,5},{8,10},{9,11},{10,... | collective-permute-start | bytes 786440 | tf_op jit(solution)/shard_map/ppermute | solution.py:75
  115.1 23.2 %collective-permute-start.43 = (bf16[2,4,32,512]{3,2,1,0:T(8,128)(2,1)S(1)}, bf16[2,4,32,512]{3,2,1,0:T(8,128)(2,1)S(1)}, u32[]{:S(2)}, u32[]{:S(2)}) collective-permute-start(bf16[2,4,32,512]{3,2,1,0:T(8,128)(2,1)S(1)} %get-tuple-element.67), channel_id=1, source_target_pairs={{0,1},{1,0},{2,3},{3,2},{4,5},{5,4},{6,7},{7,6},{8,9},{9,8},{10,11... | collective-permute-start | bytes 786440 | tf_op jit(solution)/shard_map/ppermute | solution.py:75
  116.6 22.8 %collective-permute-start.47 = (bf16[2,4,32,512]{3,2,1,0:T(8,128)(2,1)S(1)}, bf16[2,4,32,512]{3,2,1,0:T(8,128)(2,1)S(1)}, u32[]{:S(2)}, u32[]{:S(2)}) collective-permute-start(bf16[2,4,32,512]{3,2,1,0:T(8,128)(2,1)S(1)} %get-tuple-element.68.refs_3_), channel_id=1, source_target_pairs={{0,4},{4,0},{8,12},{12,8},{16,20},{20,16},{24,28},{28,24},{1,5},{5... | collective-permute-start | bytes 786440 | tf_op jit(solution)/shard_map/ppermute | solution.py:75
  123.3 16.1 %collective-permute-start.44 = (bf16[2,4,32,512]{3,2,1,0:T(8,128)(2,1)S(1)}, bf16[2,4,32,512]{3,2,1,0:T(8,128)(2,1)S(1)}, u32[]{:S(2)}, u32[]{:S(2)}) collective-permute-start(bf16[2,4,32,512]{3,2,1,0:T(8,128)(2,1)S(1)} %collective-permute-done.41.refs_0_), channel_id=1, source_target_pairs={{0,4},{4,0},{8,12},{12,8},{16,20},{20,16},{24,28},{28,24},{1,5},{5... | collective-permute-start | bytes 786440 | tf_op jit(solution)/shard_map/ppermute | solution.py:75
  (18 other events, 76.7 us)

commit v9 on v8

--- a/solution.py
+++ b/solution.py
@@ -280,7 +280,7 @@
         *operands,
         flops=16 * sum(piece.size for piece in operands),
     )
-    return own, swap_core(own)
+    return own, swap_y(own)
 
 
 def target_kernel(n_col, n_chip, log_noise, *refs):
@@ -388,17 +388,11 @@
     tile = functools.reduce(jnp.add, parts[::-1])
     tile_2, tile_1 = swap(tile, "col", 2), swap(tile, "col", 1)
     tile_3 = swap(tile_2, "col", 1)
-    x_tile, y_tile = swap_x(tile), swap_y(tile)
-    pair = jnp.stack([after(tile_2, y_tile), after(tile_1, x_tile)])
-    x_pair, y_pair = swap_x(pair), swap_y(pair)
-    x_last, y_last = swap_x(tile_3), swap_y(tile_3)
-    tiles = [
-        [tile, pair, tile_3],
-        [x_tile, x_pair, x_last],
-        [y_tile, y_pair, y_last],
-        [swap_y(x_tile), swap_x(y_pair), swap_y(x_last)],
-    ]
+    x_tile = swap_x(tile)
+    pair = jnp.stack([after(tile_2, x_tile), tile_1])
+    tiles = [[tile, pair, tile_3], [x_tile, swap_x(pair), swap_x(tile_3)]]
     other_tiles = [swap_core(piece) for piece in tiles[0]]
+    tiles += [other_tiles, [swap_core(piece) for piece in tiles[1]]]
     log_noise = math.log2(own * lax.axis_size("row"))
     stats = ()
     for _ in range(ITERS):

time: 141 us -> 139 us (0.986)
  starting transfers between devices: 51.8 us -> 46.1 us
  waiting for transfers between devices: 78 us -> 81.4 us
    ppermute x48 -> x45, starting transfers between devices: 51.8 us -> 46.1 us  [swap(): return lax.ppermute(array, axis, [(i, i ^ step) for i in range(count)])]
    ppermute x48 -> x45, waiting for transfers between devices: 78 us -> 81.4 us  [swap(): return lax.ppermute(array, axis, [(i, i ^ step) for i in range(count)])]
  transfers between devices with their start and end apart: 48 -> 45, of which waited for: 24 -> 27; matrix products, arithmetic and copies ran while one was open for 0% -> 0% of each run, Pallas kernels for 2% -> 0%
where the time goes in v9:
time: 139 us
  waiting for transfers between devices  81.4 us (59%)
  starting transfers between devices  46.1 us (33%)
  Pallas kernels  8.26 us (6%)
  local copies, waits for them, and re-layouts  2.44 us (2%)
    ppermute x45, waiting for transfers between devices, swap(): return lax.ppermute(array, axis, [(i, i ^ step) for i in range(count)])  81.4 us
    ppermute x45, starting transfers between devices, swap(): return lax.ppermute(array, axis, [(i, i ^ step) for i in range(count)])  46.1 us
    pallas_call x10, Pallas kernels, kernel_call(): pl.pallas_call(kernel, in_specs=[VMEM] * len(operands), out_specs=[VMEM]...  8.26 us
  transfers between devices with their start and end apart: 45, of which 27 were waited for; matrix products, arithmetic and copies ran while one was open for 0% of the time, Pallas kernels for 0%

profile of v9, /device:TPU:0, one launch (start us, length us, event | category | flops | bytes accessed | tf_op | source)
XLA Modules:
  0.0 139.0 jit_solution(1614701813485222387)
XLA Ops:
  3.2 3.0 %collective-permute-start.2 = (bf16[256,512]{1,0:T(8,128)(2,1)S(1)}, bf16[256,512]{1,0:T(8,128)(2,1)S(1)}, u32[]{:S(2)}, u32[]{:S(2)}) collective-permute-start(bf16[256,512]{1,0:T(8,128)(2,1)S(1)} %get-tuple-element.38.refs_4_.refs_8_), channel_id=1, source_target_pairs={{0,16},{4,20},{8,24},{12,28},{16,0},{20,4},{24,8},{28,12},{1,17},{... | collective-permute-start | bytes 786440 | tf_op jit(solution)/shard_map/ppermute | solution.py:75
  7.7 1.6 %collective-permute-start.8 = (bf16[256,512]{1,0:T(8,128)(2,1)S(1)}, bf16[256,512]{1,0:T(8,128)(2,1)S(1)}, u32[]{:S(2)}, u32[]{:S(2)}) collective-permute-start(bf16[256,512]{1,0:T(8,128)(2,1)S(1)} %get-tuple-element.49), channel_id=1, source_target_pairs={{0,1},{1,0},{2,3},{3,2},{4,5},{5,4},{6,7},{7,6},{8,9},{9,8},{10,11... | collective-permute-start | bytes 786440 | tf_op jit(solution)/shard_map/ppermute | solution.py:75
  9.3 2.6 %collective-permute-start.3 = (bf16[256,512]{1,0:T(8,128)(2,1)S(1)}, bf16[256,512]{1,0:T(8,128)(2,1)S(1)}, u32[]{:S(2)}, u32[]{:S(2)}) collective-permute-start(bf16[256,512]{1,0:T(8,128)(2,1)S(1)} %get-tuple-element.42), channel_id=1, source_target_pairs={{0,2},{1,3},{2,0},{3,1},{4,6},{5,7},{6,4},{7,5},{8,10},{9,11},{10,... | collective-permute-start | bytes 786440 | tf_op jit(solution)/shard_map/ppermute | solution.py:75
  14.0 6.6 %collective-permute-done.8.refs_5_.refs_9_ = bf16[256,512]{1,0:T(8,128)(2,1)S(1)} collective-permute-done((bf16[256,512]{1,0:T(8,128)(2,1)S(1)}, bf16[256,512]{1,0:T(8,128)(2,1)S(1)}, u32[]{:S(2)}, u32[]{:S(2)}) %collective-permute-start.8) | collective-permute-done | bytes 262176 | tf_op jit(solution)/shard_map/ppermute | solution.py:75
  22.7 2.5 %collective-permute-start.6 = (bf16[256,512]{1,0:T(8,128)(2,1)S(1)}, bf16[256,512]{1,0:T(8,128)(2,1)S(1)}, u32[]{:S(2)}, u32[]{:S(2)}) collective-permute-start(bf16[256,512]{1,0:T(8,128)(2,1)S(1)} %get-tuple-element.47), channel_id=1, source_target_pairs={{0,3},{1,2},{2,1},{3,0},{4,7},{5,6},{6,5},{7,4},{8,11},{9,10},{10,... | collective-permute-start | bytes 786440 | tf_op jit(solution)/shard_map/ppermute | solution.py:75
  25.7 4.1 %collective-permute-done.11.refs_13_.refs_17_ = bf16[256,512]{1,0:T(8,128)(2,1)S(1)} collective-permute-done((bf16[256,512]{1,0:T(8,128)(2,1)S(1)}, bf16[256,512]{1,0:T(8,128)(2,1)S(1)}, u32[]{:S(2)}, u32[]{:S(2)}) %collective-permute-start.11) | collective-permute-done | bytes 262176 | tf_op jit(solution)/shard_map/ppermute | solution.py:75
  29.8 3.0 %collective-permute-done.14.refs_16_.refs_20_ = bf16[256,512]{1,0:T(8,128)(2,1)S(1)} collective-permute-done((bf16[256,512]{1,0:T(8,128)(2,1)S(1)}, bf16[256,512]{1,0:T(8,128)(2,1)S(1)}, u32[]{:S(2)}, u32[]{:S(2)}) %collective-permute-start.14) | collective-permute-done | bytes 262176 | tf_op jit(solution)/shard_map/ppermute | solution.py:75
  36.0 4.1 %collective-permute-done.15.refs_14_.refs_18_ = bf16[256,512]{1,0:T(8,128)(2,1)S(1)} collective-permute-done((bf16[256,512]{1,0:T(8,128)(2,1)S(1)}, bf16[256,512]{1,0:T(8,128)(2,1)S(1)}, u32[]{:S(2)}, u32[]{:S(2)}) %collective-permute-start.15) | collective-permute-done | bytes 262176 | tf_op jit(solution)/shard_map/ppermute | solution.py:75
  41.4 1.9 %collective-permute-start.7 = (bf16[2,128,512]{2,1,0:T(8,128)(2,1)S(1)}, bf16[2,128,512]{2,1,0:T(8,128)(2,1)S(1)}, u32[]{:S(2)}, u32[]{:S(2)}) collective-permute-start(bf16[2,128,512]{2,1,0:T(8,128)(2,1)S(1)} %get-tuple-element.48), channel_id=1, source_target_pairs={{0,3},{1,2},{2,1},{3,0},{4,7},{5,6},{6,5},{7,4},{8,11},{9,10},{10,... | collective-permute-start | bytes 786440 | tf_op jit(solution)/shard_map/ppermute | solution.py:75
  43.3 1.9 %collective-permute-done.12.refs_17_.refs_21_ = bf16[256,512]{1,0:T(8,128)(2,1)S(1)} collective-permute-done((bf16[256,512]{1,0:T(8,128)(2,1)S(1)}, bf16[256,512]{1,0:T(8,128)(2,1)S(1)}, u32[]{:S(2)}, u32[]{:S(2)}) %collective-permute-start.12) | collective-permute-done | bytes 262176 | tf_op jit(solution)/shard_map/ppermute | solution.py:75
  47.4 1.7 %collective-permute-done.16.refs_15_.refs_19_ = bf16[256,512]{1,0:T(8,128)(2,1)S(1)} collective-permute-done((bf16[256,512]{1,0:T(8,128)(2,1)S(1)}, bf16[256,512]{1,0:T(8,128)(2,1)S(1)}, u32[]{:S(2)}, u32[]{:S(2)}) %collective-permute-start.16) | collective-permute-done | bytes 262176 | tf_op jit(solution)/shard_map/ppermute | solution.py:75
  49.7 7.4 %collective-permute-done.5.refs_2_ = bf16[2,128,512]{2,1,0:T(8,128)(2,1)S(1)} collective-permute-done((bf16[2,128,512]{2,1,0:T(8,128)(2,1)S(1)}, bf16[2,128,512]{2,1,0:T(8,128)(2,1)S(1)}, u32[]{:S(2)}, u32[]{:S(2)}) %collective-permute-start.5) | collective-permute-done | bytes 262176 | tf_op jit(solution)/shard_map/ppermute | solution.py:75
  57.2 2.0 %shard_map.52 = (f32[128,1024]{1,0:T(8,128)S(1)}, f32[128,1024]{1,0:T(8,128)S(1)}) custom-call(bf16[2,128,512]{2,1,0:T(8,128)(2,1)S(1)} %get-tuple-element.40.refs_0_, bf16[2,128,512]{2,1,0:T(8,128)(2,1)S(1)} %collective-permute-done.4.refs_1_, bf16[2,128,512]{2,1,0:T(8,128)(2,1)S(1)} %collective-permute-done.5.refs_2_, ...), custom_call_target="tpu_custom_call" | custom-call | flops 1073741824 | bytes 5242880 | tf_op jit(solution)/shard_map/pallas_call | solution.py:115
  59.3 1.9 %collective-permute-done.19.other_ref = f32[128,1024]{1,0:T(8,128)S(1)} collective-permute-done((f32[128,1024]{1,0:T(8,128)S(1)}, f32[128,1024]{1,0:T(8,128)S(1)}, u32[]{:S(2)}, u32[]{:S(2)}) %collective-permute-start.19) | collective-permute-done | bytes 524320 | tf_op jit(solution)/shard_map/ppermute | solution.py:75
  61.2 2.0 %collective-permute-start.20 = (f32[32,1024]{1,0:T(8,128)S(1)}, f32[32,1024]{1,0:T(8,128)S(1)}, u32[]{:S(2)}, u32[]{:S(2)}) collective-permute-start(f32[32,1024]{1,0:T(8,128)S(1)} %get-tuple-element.58), channel_id=1, source_target_pairs={{0,3},{1,2},{2,1},{3,0},{4,7},{5,6},{6,5},{7,4},{8,11},{9,10},{10,... | collective-permute-start | bytes 393224 | tf_op jit(solution)/shard_map/ppermute | solution.py:75
  63.3 4.6 %collective-permute-start.21 = (f32[32,1024]{1,0:T(8,128)S(1)}, f32[32,1024]{1,0:T(8,128)S(1)}, u32[]{:S(2)}, u32[]{:S(2)}) collective-permute-start(f32[32,1024]{1,0:T(8,128)S(1)} %get-tuple-element.59), channel_id=1, source_target_pairs={{0,2},{1,3},{2,0},{3,1},{4,6},{5,7},{6,4},{7,5},{8,10},{9,11},{10,... | collective-permute-start | bytes 393224 | tf_op jit(solution)/shard_map/ppermute | solution.py:75
  68.6 8.4 %collective-permute-done.21 = f32[32,1024]{1,0:T(8,128)S(1)} collective-permute-done((f32[32,1024]{1,0:T(8,128)S(1)}, f32[32,1024]{1,0:T(8,128)S(1)}, u32[]{:S(2)}, u32[]{:S(2)}) %collective-permute-start.21) | collective-permute-done | bytes 131104 | tf_op jit(solution)/shard_map/ppermute | solution.py:75
  78.2 2.6 %collective-permute-start.25 = (f32[32,1024]{1,0:T(8,128)S(1)}, f32[32,1024]{1,0:T(8,128)S(1)}, u32[]{:S(2)}, u32[]{:S(2)}) collective-permute-start(f32[32,1024]{1,0:T(8,128)S(1)} %add_add_fusion.refs_0_), channel_id=1, source_target_pairs={{0,1},{1,0},{2,3},{3,2},{4,5},{5,4},{6,7},{7,6},{8,9},{9,8},{10,11... | collective-permute-start | bytes 393224 | tf_op jit(solution)/shard_map/ppermute | solution.py:75
  82.1 3.6 %collective-permute-done.23 = f32[32,1024]{1,0:T(8,128)S(1)} collective-permute-done((f32[32,1024]{1,0:T(8,128)S(1)}, f32[32,1024]{1,0:T(8,128)S(1)}, u32[]{:S(2)}, u32[]{:S(2)}) %collective-permute-start.23) | collective-permute-done | bytes 131104 | tf_op jit(solution)/shard_map/ppermute | solution.py:75
  88.0 4.5 %collective-permute-done.26.refs_2_ = f32[32,1024]{1,0:T(8,128)S(1)} collective-permute-done((f32[32,1024]{1,0:T(8,128)S(1)}, f32[32,1024]{1,0:T(8,128)S(1)}, u32[]{:S(2)}, u32[]{:S(2)}) %collective-permute-start.26) | collective-permute-done | bytes 131104 | tf_op jit(solution)/shard_map/ppermute | solution.py:75
  94.5 3.0 %collective-permute-done.31.refs_5_ = f32[32,1024]{1,0:T(8,128)S(1)} collective-permute-done((f32[32,1024]{1,0:T(8,128)S(1)}, f32[32,1024]{1,0:T(8,128)S(1)}, u32[]{:S(2)}, u32[]{:S(2)}) %collective-permute-start.31) | collective-permute-done | bytes 131104 | tf_op jit(solution)/shard_map/ppermute | solution.py:75
  99.7 1.6 %collective-permute-start.35 = (f32[2,1024]{1,0:T(2,128)S(1)}, f32[2,1024]{1,0:T(2,128)S(1)}, u32[]{:S(2)}, u32[]{:S(2)}) collective-permute-start(f32[2,1024]{1,0:T(2,128)S(1)} %shard_map.54.refs_12_), channel_id=1, source_target_pairs={{0,16},{4,20},{8,24},{12,28},{16,0},{20,4},{24,8},{28,12},{1,17},{... | collective-permute-start | bytes 24584 | tf_op jit(solution)/shard_map/ppermute | solution.py:75
  101.3 2.1 %collective-permute-done.35.refs_13_ = f32[2,1024]{1,0:T(2,128)S(1)} collective-permute-done((f32[2,1024]{1,0:T(2,128)S(1)}, f32[2,1024]{1,0:T(2,128)S(1)}, u32[]{:S(2)}, u32[]{:S(2)}) %collective-permute-start.35) | collective-permute-done | bytes 8224 | tf_op jit(solution)/shard_map/ppermute | solution.py:75
  104.4 1.6 %collective-permute-start.36 = (f32[2,1024]{1,0:T(2,128)S(1)}, f32[2,1024]{1,0:T(2,128)S(1)}, u32[]{:S(2)}, u32[]{:S(2)}) collective-permute-start(f32[2,1024]{1,0:T(2,128)S(1)} %shard_map.55.refs_12_), channel_id=1, source_target_pairs={{0,16},{4,20},{8,24},{12,28},{16,0},{20,4},{24,8},{28,12},{1,17},{... | collective-permute-start | bytes 24584 | tf_op jit(solution)/shard_map/ppermute | solution.py:75
  105.9 2.1 %collective-permute-done.36.refs_13_ = f32[2,1024]{1,0:T(2,128)S(1)} collective-permute-done((f32[2,1024]{1,0:T(2,128)S(1)}, f32[2,1024]{1,0:T(2,128)S(1)}, u32[]{:S(2)}, u32[]{:S(2)}) %collective-permute-start.36) | collective-permute-done | bytes 8224 | tf_op jit(solution)/shard_map/ppermute | solution.py:75
  109.0 1.6 %collective-permute-start.37 = (f32[2,1024]{1,0:T(2,128)S(1)}, f32[2,1024]{1,0:T(2,128)S(1)}, u32[]{:S(2)}, u32[]{:S(2)}) collective-permute-start(f32[2,1024]{1,0:T(2,128)S(1)} %shard_map.56.refs_6_), channel_id=1, source_target_pairs={{0,16},{4,20},{8,24},{12,28},{16,0},{20,4},{24,8},{28,12},{1,17},{... | collective-permute-start | bytes 24584 | tf_op jit(solution)/shard_map/ppermute | solution.py:75
  110.6 2.1 %collective-permute-done.37.refs_7_ = f32[2,1024]{1,0:T(2,128)S(1)} collective-permute-done((f32[2,1024]{1,0:T(2,128)S(1)}, f32[2,1024]{1,0:T(2,128)S(1)}, u32[]{:S(2)}, u32[]{:S(2)}) %collective-permute-start.37) | collective-permute-done | bytes 8224 | tf_op jit(solution)/shard_map/ppermute | solution.py:75
  112.7 2.2 %shard_map.57 = (bf16[2,4,32,512]{3,2,1,0:T(8,128)(2,1)S(1)}, bf16[2,4,32,512]{3,2,1,0:T(8,128)(2,1)S(1)}, bf16[2,4,32,512]{3,2,1,0:T(8,128)(2,1)S(1)}, bf16[2,4...) custom-call(f32[32,1024]{1,0:T(8,128)S(1)} %add_add_fusion.refs_0_, ...), custom_call_target="tpu_custom_call" | custom-call | flops 1073741824 | bytes 5259264 | tf_op jit(solution)/shard_map/pallas_call | solution.py:115
  114.9 1.8 %collective-permute-start.38 = (bf16[2,4,32,512]{3,2,1,0:T(8,128)(2,1)S(1)}, bf16[2,4,32,512]{3,2,1,0:T(8,128)(2,1)S(1)}, u32[]{:S(2)}, u32[]{:S(2)}) collective-permute-start(bf16[2,4,32,512]{3,2,1,0:T(8,128)(2,1)S(1)} %get-tuple-element.63), channel_id=1, source_target_pairs={{0,3},{1,2},{2,1},{3,0},{4,7},{5,6},{6,5},{7,4},{8,11},{9,10},{10,... | collective-permute-start | bytes 786440 | tf_op jit(solution)/shard_map/ppermute | solution.py:75
  116.6 2.6 %collective-permute-start.40 = (bf16[2,4,32,512]{3,2,1,0:T(8,128)(2,1)S(1)}, bf16[2,4,32,512]{3,2,1,0:T(8,128)(2,1)S(1)}, u32[]{:S(2)}, u32[]{:S(2)}) collective-permute-start(bf16[2,4,32,512]{3,2,1,0:T(8,128)(2,1)S(1)} %get-tuple-element.65), channel_id=1, source_target_pairs={{0,1},{1,0},{2,3},{3,2},{4,5},{5,4},{6,7},{7,6},{8,9},{9,8},{10,11... | collective-permute-start | bytes 786440 | tf_op jit(solution)/shard_map/ppermute | solution.py:75
  119.3 6.7 %collective-permute-done.38.refs_0_ = bf16[2,4,32,512]{3,2,1,0:T(8,128)(2,1)S(1)} collective-permute-done((bf16[2,4,32,512]{3,2,1,0:T(8,128)(2,1)S(1)}, bf16[2,4,32,512]{3,2,1,0:T(8,128)(2,1)S(1)}, u32[]{:S(2)}, u32[]{:S(2)}) %collective-permute-start.38) | collective-permute-done | bytes 262176 | tf_op jit(solution)/shard_map/ppermute | solution.py:75
  125.9 10.1 %collective-permute-done.39.refs_1_ = bf16[2,4,32,512]{3,2,1,0:T(8,128)(2,1)S(1)} collective-permute-done((bf16[2,4,32,512]{3,2,1,0:T(8,128)(2,1)S(1)}, bf16[2,4,32,512]{3,2,1,0:T(8,128)(2,1)S(1)}, u32[]{:S(2)}, u32[]{:S(2)}) %collective-permute-start.39) | collective-permute-done | bytes 262176 | tf_op jit(solution)/shard_map/ppermute | solution.py:75
  (75 shorter events, 30.7 us)
Async XLA Ops:
  1.9 12.0 %collective-permute-start = (bf16[128,2048]{1,0:T(8,128)(2,1)S(1)}, bf16[128,2048]{1,0:T(8,128)(2,1)S(1)}, u32[]{:S(2)}, u32[]{:S(2)}) collective-permute-start(bf16[128,2048]{1,0:T(8,128)(2,1)S(1)} %get-tuple-element.37), channel_id=1, source_target_pairs={{0,4},{4,0},{8,12},{12,8},{16,20},{20,16},{24,28},{28,24},{1,5},{5... | collective-permute-start | bytes 1572872 | tf_op jit(solution)/shard_map/ppermute | solution.py:75
  3.2 9.3 %collective-permute-start.2 = (bf16[256,512]{1,0:T(8,128)(2,1)S(1)}, bf16[256,512]{1,0:T(8,128)(2,1)S(1)}, u32[]{:S(2)}, u32[]{:S(2)}) collective-permute-start(bf16[256,512]{1,0:T(8,128)(2,1)S(1)} %get-tuple-element.38.refs_4_.refs_8_), channel_id=1, source_target_pairs={{0,16},{4,20},{8,24},{12,28},{16,0},{20,4},{24,8},{28,12},{1,17},{... | collective-permute-start | bytes 786440 | tf_op jit(solution)/shard_map/ppermute | solution.py:75
  6.2 7.8 %collective-permute-start.1 = (bf16[256,512]{1,0:T(8,128)(2,1)S(1)}, bf16[256,512]{1,0:T(8,128)(2,1)S(1)}, u32[]{:S(2)}, u32[]{:S(2)}) collective-permute-start(bf16[256,512]{1,0:T(8,128)(2,1)S(1)} %get-tuple-element.38.refs_4_.refs_8_), channel_id=1, source_target_pairs={{0,8},{4,12},{8,0},{12,4},{16,24},{20,28},{24,16},{28,20},{1,9},{5... | collective-permute-start | bytes 786440 | tf_op jit(solution)/shard_map/ppermute | solution.py:75
  7.7 13.0 %collective-permute-start.8 = (bf16[256,512]{1,0:T(8,128)(2,1)S(1)}, bf16[256,512]{1,0:T(8,128)(2,1)S(1)}, u32[]{:S(2)}, u32[]{:S(2)}) collective-permute-start(bf16[256,512]{1,0:T(8,128)(2,1)S(1)} %get-tuple-element.49), channel_id=1, source_target_pairs={{0,1},{1,0},{2,3},{3,2},{4,5},{5,4},{6,7},{7,6},{8,9},{9,8},{10,11... | collective-permute-start | bytes 786440 | tf_op jit(solution)/shard_map/ppermute | solution.py:75
  9.3 16.5 %collective-permute-start.3 = (bf16[256,512]{1,0:T(8,128)(2,1)S(1)}, bf16[256,512]{1,0:T(8,128)(2,1)S(1)}, u32[]{:S(2)}, u32[]{:S(2)}) collective-permute-start(bf16[256,512]{1,0:T(8,128)(2,1)S(1)} %get-tuple-element.42), channel_id=1, source_target_pairs={{0,2},{1,3},{2,0},{3,1},{4,6},{5,7},{6,4},{7,5},{8,10},{9,11},{10,... | collective-permute-start | bytes 786440 | tf_op jit(solution)/shard_map/ppermute | solution.py:75
  20.7 9.1 %collective-permute-start.11 = (bf16[256,512]{1,0:T(8,128)(2,1)S(1)}, bf16[256,512]{1,0:T(8,128)(2,1)S(1)}, u32[]{:S(2)}, u32[]{:S(2)}) collective-permute-start(bf16[256,512]{1,0:T(8,128)(2,1)S(1)} %collective-permute-done.8.refs_5_.refs_9_), channel_id=1, source_target_pairs={{0,16},{4,20},{8,24},{12,28},{16,0},{20,4},{24,8},{28,12},{1,17},{... | collective-permute-start | bytes 786440 | tf_op jit(solution)/shard_map/ppermute | solution.py:75
  21.2 11.6 %collective-permute-start.14 = (bf16[256,512]{1,0:T(8,128)(2,1)S(1)}, bf16[256,512]{1,0:T(8,128)(2,1)S(1)}, u32[]{:S(2)}, u32[]{:S(2)}) collective-permute-start(bf16[256,512]{1,0:T(8,128)(2,1)S(1)} %collective-permute-done.1.refs_8_.refs_12_), channel_id=1, source_target_pairs={{0,16},{4,20},{8,24},{12,28},{16,0},{20,4},{24,8},{28,12},{1,17},{... | collective-permute-start | bytes 786440 | tf_op jit(solution)/shard_map/ppermute | solution.py:75
  22.7 12.6 %collective-permute-start.6 = (bf16[256,512]{1,0:T(8,128)(2,1)S(1)}, bf16[256,512]{1,0:T(8,128)(2,1)S(1)}, u32[]{:S(2)}, u32[]{:S(2)}) collective-permute-start(bf16[256,512]{1,0:T(8,128)(2,1)S(1)} %get-tuple-element.47), channel_id=1, source_target_pairs={{0,3},{1,2},{2,1},{3,0},{4,7},{5,6},{6,5},{7,4},{8,11},{9,10},{10,... | collective-permute-start | bytes 786440 | tf_op jit(solution)/shard_map/ppermute | solution.py:75
  25.2 8.1 %collective-permute-start.9 = (bf16[256,512]{1,0:T(8,128)(2,1)S(1)}, bf16[256,512]{1,0:T(8,128)(2,1)S(1)}, u32[]{:S(2)}, u32[]{:S(2)}) collective-permute-start(bf16[256,512]{1,0:T(8,128)(2,1)S(1)} %collective-permute-done.8.refs_5_.refs_9_), channel_id=1, source_target_pairs={{0,8},{4,12},{8,0},{12,4},{16,24},{20,28},{24,16},{28,20},{1,9},{5... | collective-permute-start | bytes 786440 | tf_op jit(solution)/shard_map/ppermute | solution.py:75
  25.7 10.2 %collective-permute-start.4 = (bf16[2,128,512]{2,1,0:T(8,128)(2,1)S(1)}, bf16[2,128,512]{2,1,0:T(8,128)(2,1)S(1)}, u32[]{:S(2)}, u32[]{:S(2)}) collective-permute-start(bf16[2,128,512]{2,1,0:T(8,128)(2,1)S(1)} %get-tuple-element.43), channel_id=1, source_target_pairs={{0,1},{1,0},{2,3},{3,2},{4,5},{5,4},{6,7},{7,6},{8,9},{9,8},{10,11... | collective-permute-start | bytes 786440 | tf_op jit(solution)/shard_map/ppermute | solution.py:75
  32.8 7.3 %collective-permute-start.15 = (bf16[256,512]{1,0:T(8,128)(2,1)S(1)}, bf16[256,512]{1,0:T(8,128)(2,1)S(1)}, u32[]{:S(2)}, u32[]{:S(2)}) collective-permute-start(bf16[256,512]{1,0:T(8,128)(2,1)S(1)} %collective-permute-done.3.refs_6_.refs_10_), channel_id=1, source_target_pairs={{0,16},{4,20},{8,24},{12,28},{16,0},{20,4},{24,8},{28,12},{1,17},{... | collective-permute-start | bytes 786440 | tf_op jit(solution)/shard_map/ppermute | solution.py:75
  33.3 11.9 %collective-permute-start.10 = (bf16[256,512]{1,0:T(8,128)(2,1)S(1)}, bf16[256,512]{1,0:T(8,128)(2,1)S(1)}, u32[]{:S(2)}, u32[]{:S(2)}) collective-permute-start(bf16[256,512]{1,0:T(8,128)(2,1)S(1)} %collective-permute-done.3.refs_6_.refs_10_), channel_id=1, source_target_pairs={{0,8},{4,12},{8,0},{12,4},{16,24},{20,28},{24,16},{28,20},{1,9},{5... | collective-permute-start | bytes 786440 | tf_op jit(solution)/shard_map/ppermute | solution.py:75
  33.9 11.3 %collective-permute-start.12 = (bf16[256,512]{1,0:T(8,128)(2,1)S(1)}, bf16[256,512]{1,0:T(8,128)(2,1)S(1)}, u32[]{:S(2)}, u32[]{:S(2)}) collective-permute-start(bf16[256,512]{1,0:T(8,128)(2,1)S(1)} %collective-permute-done.11.refs_13_.refs_17_), channel_id=1, source_target_pairs={{0,8},{4,12},{8,0},{12,4},{16,24},{20,28},{24,16},{28,20},{1,9},{5... | collective-permute-start | bytes 786440 | tf_op jit(solution)/shard_map/ppermute | solution.py:75
  40.1 9.0 %collective-permute-start.16 = (bf16[256,512]{1,0:T(8,128)(2,1)S(1)}, bf16[256,512]{1,0:T(8,128)(2,1)S(1)}, u32[]{:S(2)}, u32[]{:S(2)}) collective-permute-start(bf16[256,512]{1,0:T(8,128)(2,1)S(1)} %collective-permute-done.6.refs_7_.refs_11_), channel_id=1, source_target_pairs={{0,16},{4,20},{8,24},{12,28},{16,0},{20,4},{24,8},{28,12},{1,17},{... | collective-permute-start | bytes 786440 | tf_op jit(solution)/shard_map/ppermute | solution.py:75
  40.6 16.5 %collective-permute-start.5 = (bf16[2,128,512]{2,1,0:T(8,128)(2,1)S(1)}, bf16[2,128,512]{2,1,0:T(8,128)(2,1)S(1)}, u32[]{:S(2)}, u32[]{:S(2)}) collective-permute-start(bf16[2,128,512]{2,1,0:T(8,128)(2,1)S(1)} %get-tuple-element.45), channel_id=1, source_target_pairs={{0,2},{1,3},{2,0},{3,1},{4,6},{5,7},{6,4},{7,5},{8,10},{9,11},{10,... | collective-permute-start | bytes 786440 | tf_op jit(solution)/shard_map/ppermute | solution.py:75
  41.4 15.8 %collective-permute-start.7 = (bf16[2,128,512]{2,1,0:T(8,128)(2,1)S(1)}, bf16[2,128,512]{2,1,0:T(8,128)(2,1)S(1)}, u32[]{:S(2)}, u32[]{:S(2)}) collective-permute-start(bf16[2,128,512]{2,1,0:T(8,128)(2,1)S(1)} %get-tuple-element.48), channel_id=1, source_target_pairs={{0,3},{1,2},{2,1},{3,0},{4,7},{5,6},{6,5},{7,4},{8,11},{9,10},{10,... | collective-permute-start | bytes 786440 | tf_op jit(solution)/shard_map/ppermute | solution.py:75
  45.2 11.9 %collective-permute-start.13 = (bf16[256,512]{1,0:T(8,128)(2,1)S(1)}, bf16[256,512]{1,0:T(8,128)(2,1)S(1)}, u32[]{:S(2)}, u32[]{:S(2)}) collective-permute-start(bf16[256,512]{1,0:T(8,128)(2,1)S(1)} %collective-permute-done.6.refs_7_.refs_11_), channel_id=1, source_target_pairs={{0,8},{4,12},{8,0},{12,4},{16,24},{20,28},{24,16},{28,20},{1,9},{5... | collective-permute-start | bytes 786440 | tf_op jit(solution)/shard_map/ppermute | solution.py:75
  46.0 11.1 %collective-permute-start.17 = (bf16[256,512]{1,0:T(8,128)(2,1)S(1)}, bf16[256,512]{1,0:T(8,128)(2,1)S(1)}, u32[]{:S(2)}, u32[]{:S(2)}) collective-permute-start(bf16[256,512]{1,0:T(8,128)(2,1)S(1)} %collective-permute-done.10.refs_10_.refs_14_), channel_id=1, source_target_pairs={{0,16},{4,20},{8,24},{12,28},{16,0},{20,4},{24,8},{28,12},{1,17},{... | collective-permute-start | bytes 786440 | tf_op jit(solution)/shard_map/ppermute | solution.py:75
  49.1 8.1 %collective-permute-start.18 = (bf16[256,512]{1,0:T(8,128)(2,1)S(1)}, bf16[256,512]{1,0:T(8,128)(2,1)S(1)}, u32[]{:S(2)}, u32[]{:S(2)}) collective-permute-start(bf16[256,512]{1,0:T(8,128)(2,1)S(1)} %collective-permute-done.16.refs_15_.refs_19_), channel_id=1, source_target_pairs={{0,8},{4,12},{8,0},{12,4},{16,24},{20,28},{24,16},{28,20},{1,9},{5... | collective-permute-start | bytes 786440 | tf_op jit(solution)/shard_map/ppermute | solution.py:75
  61.2 7.4 %collective-permute-start.20 = (f32[32,1024]{1,0:T(8,128)S(1)}, f32[32,1024]{1,0:T(8,128)S(1)}, u32[]{:S(2)}, u32[]{:S(2)}) collective-permute-start(f32[32,1024]{1,0:T(8,128)S(1)} %get-tuple-element.58), channel_id=1, source_target_pairs={{0,3},{1,2},{2,1},{3,0},{4,7},{5,6},{6,5},{7,4},{8,11},{9,10},{10,... | collective-permute-start | bytes 393224 | tf_op jit(solution)/shard_map/ppermute | solution.py:75
  63.3 13.8 %collective-permute-start.21 = (f32[32,1024]{1,0:T(8,128)S(1)}, f32[32,1024]{1,0:T(8,128)S(1)}, u32[]{:S(2)}, u32[]{:S(2)}) collective-permute-start(f32[32,1024]{1,0:T(8,128)S(1)} %get-tuple-element.59), channel_id=1, source_target_pairs={{0,2},{1,3},{2,0},{3,1},{4,6},{5,7},{6,4},{7,5},{8,10},{9,11},{10,... | collective-permute-start | bytes 393224 | tf_op jit(solution)/shard_map/ppermute | solution.py:75
  67.9 9.2 %collective-permute-start.22 = (f32[32,1024]{1,0:T(8,128)S(1)}, f32[32,1024]{1,0:T(8,128)S(1)}, u32[]{:S(2)}, u32[]{:S(2)}) collective-permute-start(f32[32,1024]{1,0:T(8,128)S(1)} %get-tuple-element.60), channel_id=1, source_target_pairs={{0,1},{1,0},{2,3},{3,2},{4,5},{5,4},{6,7},{7,6},{8,9},{9,8},{10,11... | collective-permute-start | bytes 393224 | tf_op jit(solution)/shard_map/ppermute | solution.py:75
  78.2 7.6 %collective-permute-start.23 = (f32[32,1024]{1,0:T(8,128)S(1)}, f32[32,1024]{1,0:T(8,128)S(1)}, u32[]{:S(2)}, u32[]{:S(2)}) collective-permute-start(f32[32,1024]{1,0:T(8,128)S(1)} %add_add_fusion.refs_0_), channel_id=1, source_target_pairs={{0,2},{1,3},{2,0},{3,1},{4,6},{5,7},{6,4},{7,5},{8,10},{9,11},{10,... | collective-permute-start | bytes 393224 | tf_op jit(solution)/shard_map/ppermute | solution.py:75
  78.2 7.9 %collective-permute-start.25 = (f32[32,1024]{1,0:T(8,128)S(1)}, f32[32,1024]{1,0:T(8,128)S(1)}, u32[]{:S(2)}, u32[]{:S(2)}) collective-permute-start(f32[32,1024]{1,0:T(8,128)S(1)} %add_add_fusion.refs_0_), channel_id=1, source_target_pairs={{0,1},{1,0},{2,3},{3,2},{4,5},{5,4},{6,7},{7,6},{8,9},{9,8},{10,11... | collective-permute-start | bytes 393224 | tf_op jit(solution)/shard_map/ppermute | solution.py:75
  86.0 7.9 %collective-permute-start.30 = (f32[2,32,1024]{2,1,0:T(8,128)S(1)}, f32[2,32,1024]{2,1,0:T(8,128)S(1)}, u32[]{:S(2)}, u32[]{:S(2)}) collective-permute-start(f32[2,32,1024]{2,1,0:T(8,128)S(1)} %pad_maximum_fusion.refs_1_), channel_id=1, source_target_pairs={{0,8},{4,12},{8,0},{12,4},{16,24},{20,28},{24,16},{28,20},{1,9},{5... | collective-permute-start | bytes 786440 | tf_op jit(solution)/shard_map/ppermute | solution.py:75
  87.5 6.9 %collective-permute-start.27 = (f32[32,1024]{1,0:T(8,128)S(1)}, f32[32,1024]{1,0:T(8,128)S(1)}, u32[]{:S(2)}, u32[]{:S(2)}) collective-permute-start(f32[32,1024]{1,0:T(8,128)S(1)} %add_add_fusion.refs_0_), channel_id=1, source_target_pairs={{0,4},{4,0},{8,12},{12,8},{16,20},{20,16},{24,28},{28,24},{1,5},{5... | collective-permute-start | bytes 393224 | tf_op jit(solution)/shard_map/ppermute | solution.py:75
  87.5 9.9 %collective-permute-start.28 = (f32[2,32,1024]{2,1,0:T(8,128)S(1)}, f32[2,32,1024]{2,1,0:T(8,128)S(1)}, u32[]{:S(2)}, u32[]{:S(2)}) collective-permute-start(f32[2,32,1024]{2,1,0:T(8,128)S(1)} %pad_maximum_fusion.refs_1_), channel_id=1, source_target_pairs={{0,4},{4,0},{8,12},{12,8},{16,20},{20,16},{24,28},{28,24},{1,5},{5... | collective-permute-start | bytes 786440 | tf_op jit(solution)/shard_map/ppermute | solution.py:75
  114.9 11.0 %collective-permute-start.38 = (bf16[2,4,32,512]{3,2,1,0:T(8,128)(2,1)S(1)}, bf16[2,4,32,512]{3,2,1,0:T(8,128)(2,1)S(1)}, u32[]{:S(2)}, u32[]{:S(2)}) collective-permute-start(bf16[2,4,32,512]{3,2,1,0:T(8,128)(2,1)S(1)} %get-tuple-element.63), channel_id=1, source_target_pairs={{0,3},{1,2},{2,1},{3,0},{4,7},{5,6},{6,5},{7,4},{8,11},{9,10},{10,... | collective-permute-start | bytes 786440 | tf_op jit(solution)/shard_map/ppermute | solution.py:75
  116.6 19.4 %collective-permute-start.39 = (bf16[2,4,32,512]{3,2,1,0:T(8,128)(2,1)S(1)}, bf16[2,4,32,512]{3,2,1,0:T(8,128)(2,1)S(1)}, u32[]{:S(2)}, u32[]{:S(2)}) collective-permute-start(bf16[2,4,32,512]{3,2,1,0:T(8,128)(2,1)S(1)} %get-tuple-element.64), channel_id=1, source_target_pairs={{0,2},{1,3},{2,0},{3,1},{4,6},{5,7},{6,4},{7,5},{8,10},{9,11},{10,... | collective-permute-start | bytes 786440 | tf_op jit(solution)/shard_map/ppermute | solution.py:75
  116.6 19.4 %collective-permute-start.40 = (bf16[2,4,32,512]{3,2,1,0:T(8,128)(2,1)S(1)}, bf16[2,4,32,512]{3,2,1,0:T(8,128)(2,1)S(1)}, u32[]{:S(2)}, u32[]{:S(2)}) collective-permute-start(bf16[2,4,32,512]{3,2,1,0:T(8,128)(2,1)S(1)} %get-tuple-element.65), channel_id=1, source_target_pairs={{0,1},{1,0},{2,3},{3,2},{4,5},{5,4},{6,7},{7,6},{8,9},{9,8},{10,11... | collective-permute-start | bytes 786440 | tf_op jit(solution)/shard_map/ppermute | solution.py:75
  119.3 17.9 %collective-permute-start.44 = (bf16[2,4,32,512]{3,2,1,0:T(8,128)(2,1)S(1)}, bf16[2,4,32,512]{3,2,1,0:T(8,128)(2,1)S(1)}, u32[]{:S(2)}, u32[]{:S(2)}) collective-permute-start(bf16[2,4,32,512]{3,2,1,0:T(8,128)(2,1)S(1)} %get-tuple-element.66.refs_3_), channel_id=1, source_target_pairs={{0,4},{4,0},{8,12},{12,8},{16,20},{20,16},{24,28},{28,24},{1,5},{5... | collective-permute-start | bytes 786440 | tf_op jit(solution)/shard_map/ppermute | solution.py:75
  125.9 11.2 %collective-permute-start.41 = (bf16[2,4,32,512]{3,2,1,0:T(8,128)(2,1)S(1)}, bf16[2,4,32,512]{3,2,1,0:T(8,128)(2,1)S(1)}, u32[]{:S(2)}, u32[]{:S(2)}) collective-permute-start(bf16[2,4,32,512]{3,2,1,0:T(8,128)(2,1)S(1)} %collective-permute-done.38.refs_0_), channel_id=1, source_target_pairs={{0,4},{4,0},{8,12},{12,8},{16,20},{20,16},{24,28},{28,24},{1,5},{5... | collective-permute-start | bytes 786440 | tf_op jit(solution)/shard_map/ppermute | solution.py:75
  (15 other events, 46.7 us)

commit v10 on v9

--- a/solution.py
+++ b/solution.py
@@ -223,12 +223,7 @@
 
 def rows_of(refs, b):
     lanes = slice(b * WIDTH, (b + 1) * WIDTH)
-    parts = []
-    for ref in refs:
-        if len(ref.shape) == 2:
-            parts.append(ref[:, lanes])
-        else:
-            parts += [ref[i, :, lanes] for i in reversed(range(ref.shape[0]))]
+    parts = [ref[i, :, lanes] for ref in refs for i in (1, 0)]
     return jnp.concatenate(parts)
 
 
@@ -258,8 +253,8 @@
 def iteration_kernel(n_groups, log_noise, *refs):
     *refs, out_ref = refs
     wide = out_ref.shape[1]
-    chips = [refs[i : i + 3] for i in range(0, 3 * n_groups, 3)]
-    g = data_potentials(refs[3 * n_groups :], wide)
+    chips = [refs[i : i + 2] for i in range(0, 2 * n_groups, 2)]
+    g = data_potentials(refs[2 * n_groups :], wide)
     potentials = [row_update(chip, g, log_noise) for chip in chips]
     for b in range(len(g)):
         scores = [f - rows_of(chip, b) for f, chip in zip(potentials, chips)]
@@ -270,7 +265,7 @@
 
 
 def iteration(tiles, stats, log_noise):
-    wide = tiles[0][0].shape[1]
+    wide = tiles[0][0].shape[2]
     operands = [piece for group in tiles for piece in group] + list(stats)
     (own,) = kernel_call(
         functools.partial(iteration_kernel, len(tiles), log_noise),
@@ -284,8 +279,8 @@
 
 
 def target_kernel(n_col, n_chip, log_noise, *refs):
-    tiles, stats, latent_refs = refs[:6], refs[6:8], refs[8 : 8 + n_chip * n_col]
-    refs = refs[8 + n_chip * n_col :]
+    tiles, stats, latent_refs = refs[:4], refs[4:6], refs[6 : 6 + n_chip * n_col]
+    refs = refs[6 + n_chip * n_col :]
     target_refs, refs = refs[:n_col], refs[n_col:]
     noise_pot_ref, data_pot_ref, pots, weights = refs
     _, col = place()
@@ -321,7 +316,7 @@
 
 def make_targets(own_tiles, other_tiles, stats, latents, n_col, log_noise):
     n_chip = len(latents)
-    share, wide = own_tiles[0].shape
+    _, share, wide = own_tiles[0].shape
     own = n_col * share
     part = latents[0][0].shape[1]
     return kernel_call(
@@ -386,11 +381,11 @@
     own_part, other_part = partial_cost(noise_pieces, latents)
     parts = col_exchange(core_sum(own_part, swap_core(other_part), n_col))
     tile = functools.reduce(jnp.add, parts[::-1])
-    tile_2, tile_1 = swap(tile, "col", 2), swap(tile, "col", 1)
-    tile_3 = swap(tile_2, "col", 1)
-    x_tile = swap_x(tile)
-    pair = jnp.stack([after(tile_2, x_tile), tile_1])
-    tiles = [[tile, pair, tile_3], [x_tile, swap_x(pair), swap_x(tile_3)]]
+    tile_3, tile_2, tile_1 = [swap(tile, "col", d) for d in (3, 2, 1)]
+    near = jnp.stack([tile_1, tile])
+    x_near = swap_x(near)
+    far = jnp.stack([after(tile_3, x_near), tile_2])
+    tiles = [[near, far], [x_near, swap_x(far)]]
     other_tiles = [swap_core(piece) for piece in tiles[0]]
     tiles += [other_tiles, [swap_core(piece) for piece in tiles[1]]]
     log_noise = math.log2(own * lax.axis_size("row"))

time: 139 us -> 144 us (1.036)
  waiting for transfers between devices: 81.4 us -> 88 us
  starting transfers between devices: 46.1 us -> 43.8 us
    ppermute x45 -> x42, waiting for transfers between devices: 81.4 us -> 88 us  [swap(): return lax.ppermute(array, axis, [(i, i ^ step) for i in range(count)])]
    ppermute x45 -> x42, starting transfers between devices: 46.1 us -> 43.8 us  [swap(): return lax.ppermute(array, axis, [(i, i ^ step) for i in range(count)])]
  transfers between devices with their start and end apart: 45 -> 42, of which waited for: 27 -> 25; matrix products, arithmetic and copies ran while one was open for 0% -> 0% of each run, Pallas kernels for 0% -> 0%
where the time goes in v10:
time: 144 us; the launch traced here: 143 us
  waiting for transfers between devices  88 us (61%)
  starting transfers between devices  43.8 us (30%)
  Pallas kernels  8.26 us (6%)
  local copies, waits for them, and re-layouts  2.44 us (2%)
    ppermute x42, waiting for transfers between devices, swap(): return lax.ppermute(array, axis, [(i, i ^ step) for i in range(count)])  88 us
    ppermute x42, starting transfers between devices, swap(): return lax.ppermute(array, axis, [(i, i ^ step) for i in range(count)])  43.8 us
    pallas_call x10, Pallas kernels, kernel_call(): pl.pallas_call(kernel, in_specs=[VMEM] * len(operands), out_specs=[VMEM]...  8.26 us
  transfers between devices with their start and end apart: 42, of which 25 were waited for; matrix products, arithmetic and copies ran while one was open for 0% of the time, Pallas kernels for 0%

profile of v10, /device:TPU:0, one launch (start us, length us, event | category | flops | bytes accessed | tf_op | source)
XLA Modules:
  0.0 143.3 jit_solution(16848797937842048594)
XLA Ops:
  3.2 3.0 %collective-permute-start.2 = (bf16[256,512]{1,0:T(8,128)(2,1)S(1)}, bf16[256,512]{1,0:T(8,128)(2,1)S(1)}, u32[]{:S(2)}, u32[]{:S(2)}) collective-permute-start(bf16[256,512]{1,0:T(8,128)(2,1)S(1)} %get-tuple-element.38.refs_4_.refs_6_), channel_id=1, source_target_pairs={{0,16},{4,20},{8,24},{12,28},{16,0},{20,4},{24,8},{28,12},{1,17},{... | collective-permute-start | bytes 786440 | tf_op jit(solution)/shard_map/ppermute | solution.py:75
  7.7 1.6 %collective-permute-start.8 = (bf16[256,512]{1,0:T(8,128)(2,1)S(1)}, bf16[256,512]{1,0:T(8,128)(2,1)S(1)}, u32[]{:S(2)}, u32[]{:S(2)}) collective-permute-start(bf16[256,512]{1,0:T(8,128)(2,1)S(1)} %get-tuple-element.49), channel_id=1, source_target_pairs={{0,1},{1,0},{2,3},{3,2},{4,5},{5,4},{6,7},{7,6},{8,9},{9,8},{10,11... | collective-permute-start | bytes 786440 | tf_op jit(solution)/shard_map/ppermute | solution.py:75
  9.3 2.6 %collective-permute-start.3 = (bf16[256,512]{1,0:T(8,128)(2,1)S(1)}, bf16[256,512]{1,0:T(8,128)(2,1)S(1)}, u32[]{:S(2)}, u32[]{:S(2)}) collective-permute-start(bf16[256,512]{1,0:T(8,128)(2,1)S(1)} %get-tuple-element.42), channel_id=1, source_target_pairs={{0,2},{1,3},{2,0},{3,1},{4,6},{5,7},{6,4},{7,5},{8,10},{9,11},{10,... | collective-permute-start | bytes 786440 | tf_op jit(solution)/shard_map/ppermute | solution.py:75
  14.0 6.6 %collective-permute-done.8.refs_5_.refs_7_ = bf16[256,512]{1,0:T(8,128)(2,1)S(1)} collective-permute-done((bf16[256,512]{1,0:T(8,128)(2,1)S(1)}, bf16[256,512]{1,0:T(8,128)(2,1)S(1)}, u32[]{:S(2)}, u32[]{:S(2)}) %collective-permute-start.8) | collective-permute-done | bytes 262176 | tf_op jit(solution)/shard_map/ppermute | solution.py:75
  21.2 1.5 %collective-permute-start.14 = (bf16[256,512]{1,0:T(8,128)(2,1)S(1)}, bf16[256,512]{1,0:T(8,128)(2,1)S(1)}, u32[]{:S(2)}, u32[]{:S(2)}) collective-permute-start(bf16[256,512]{1,0:T(8,128)(2,1)S(1)} %collective-permute-done.1.refs_8_.refs_10_), channel_id=1, source_target_pairs={{0,16},{4,20},{8,24},{12,28},{16,0},{20,4},{24,8},{28,12},{1,17},{... | collective-permute-start | bytes 786440 | tf_op jit(solution)/shard_map/ppermute | solution.py:75
  22.7 2.5 %collective-permute-start.6 = (bf16[256,512]{1,0:T(8,128)(2,1)S(1)}, bf16[256,512]{1,0:T(8,128)(2,1)S(1)}, u32[]{:S(2)}, u32[]{:S(2)}) collective-permute-start(bf16[256,512]{1,0:T(8,128)(2,1)S(1)} %get-tuple-element.47), channel_id=1, source_target_pairs={{0,3},{1,2},{2,1},{3,0},{4,7},{5,6},{6,5},{7,4},{8,11},{9,10},{10,... | collective-permute-start | bytes 786440 | tf_op jit(solution)/shard_map/ppermute | solution.py:75
  25.7 4.1 %collective-permute-done.11.refs_13_.refs_15_ = bf16[256,512]{1,0:T(8,128)(2,1)S(1)} collective-permute-done((bf16[256,512]{1,0:T(8,128)(2,1)S(1)}, bf16[256,512]{1,0:T(8,128)(2,1)S(1)}, u32[]{:S(2)}, u32[]{:S(2)}) %collective-permute-start.11) | collective-permute-done | bytes 262176 | tf_op jit(solution)/shard_map/ppermute | solution.py:75
  29.8 3.0 %collective-permute-done.14.refs_16_.refs_18_ = bf16[256,512]{1,0:T(8,128)(2,1)S(1)} collective-permute-done((bf16[256,512]{1,0:T(8,128)(2,1)S(1)}, bf16[256,512]{1,0:T(8,128)(2,1)S(1)}, u32[]{:S(2)}, u32[]{:S(2)}) %collective-permute-start.14) | collective-permute-done | bytes 262176 | tf_op jit(solution)/shard_map/ppermute | solution.py:75
  36.0 4.1 %collective-permute-done.15.refs_14_.refs_16_ = bf16[256,512]{1,0:T(8,128)(2,1)S(1)} collective-permute-done((bf16[256,512]{1,0:T(8,128)(2,1)S(1)}, bf16[256,512]{1,0:T(8,128)(2,1)S(1)}, u32[]{:S(2)}, u32[]{:S(2)}) %collective-permute-start.15) | collective-permute-done | bytes 262176 | tf_op jit(solution)/shard_map/ppermute | solution.py:75
  41.4 1.9 %collective-permute-start.7 = (bf16[2,128,512]{2,1,0:T(8,128)(2,1)S(1)}, bf16[2,128,512]{2,1,0:T(8,128)(2,1)S(1)}, u32[]{:S(2)}, u32[]{:S(2)}) collective-permute-start(bf16[2,128,512]{2,1,0:T(8,128)(2,1)S(1)} %get-tuple-element.48), channel_id=1, source_target_pairs={{0,3},{1,2},{2,1},{3,0},{4,7},{5,6},{6,5},{7,4},{8,11},{9,10},{10,... | collective-permute-start | bytes 786440 | tf_op jit(solution)/shard_map/ppermute | solution.py:75
  43.3 1.9 %collective-permute-done.12.refs_17_.refs_19_ = bf16[256,512]{1,0:T(8,128)(2,1)S(1)} collective-permute-done((bf16[256,512]{1,0:T(8,128)(2,1)S(1)}, bf16[256,512]{1,0:T(8,128)(2,1)S(1)}, u32[]{:S(2)}, u32[]{:S(2)}) %collective-permute-start.12) | collective-permute-done | bytes 262176 | tf_op jit(solution)/shard_map/ppermute | solution.py:75
  47.4 1.7 %collective-permute-done.16.refs_15_.refs_17_ = bf16[256,512]{1,0:T(8,128)(2,1)S(1)} collective-permute-done((bf16[256,512]{1,0:T(8,128)(2,1)S(1)}, bf16[256,512]{1,0:T(8,128)(2,1)S(1)}, u32[]{:S(2)}, u32[]{:S(2)}) %collective-permute-start.16) | collective-permute-done | bytes 262176 | tf_op jit(solution)/shard_map/ppermute | solution.py:75
  49.7 7.4 %collective-permute-done.5.refs_2_ = bf16[2,128,512]{2,1,0:T(8,128)(2,1)S(1)} collective-permute-done((bf16[2,128,512]{2,1,0:T(8,128)(2,1)S(1)}, bf16[2,128,512]{2,1,0:T(8,128)(2,1)S(1)}, u32[]{:S(2)}, u32[]{:S(2)}) %collective-permute-start.5) | collective-permute-done | bytes 262176 | tf_op jit(solution)/shard_map/ppermute | solution.py:75
  57.2 2.0 %shard_map.52 = (f32[128,1024]{1,0:T(8,128)S(1)}, f32[128,1024]{1,0:T(8,128)S(1)}) custom-call(bf16[2,128,512]{2,1,0:T(8,128)(2,1)S(1)} %get-tuple-element.40.refs_0_, bf16[2,128,512]{2,1,0:T(8,128)(2,1)S(1)} %collective-permute-done.4.refs_1_, bf16[2,128,512]{2,1,0:T(8,128)(2,1)S(1)} %collective-permute-done.5.refs_2_, ...), custom_call_target="tpu_custom_call" | custom-call | flops 1073741824 | bytes 5242880 | tf_op jit(solution)/shard_map/pallas_call | solution.py:115
  59.3 1.9 %collective-permute-done.19.other_ref = f32[128,1024]{1,0:T(8,128)S(1)} collective-permute-done((f32[128,1024]{1,0:T(8,128)S(1)}, f32[128,1024]{1,0:T(8,128)S(1)}, u32[]{:S(2)}, u32[]{:S(2)}) %collective-permute-start.19) | collective-permute-done | bytes 524320 | tf_op jit(solution)/shard_map/ppermute | solution.py:75
  61.2 2.0 %collective-permute-start.20 = (f32[32,1024]{1,0:T(8,128)S(1)}, f32[32,1024]{1,0:T(8,128)S(1)}, u32[]{:S(2)}, u32[]{:S(2)}) collective-permute-start(f32[32,1024]{1,0:T(8,128)S(1)} %get-tuple-element.58), channel_id=1, source_target_pairs={{0,3},{1,2},{2,1},{3,0},{4,7},{5,6},{6,5},{7,4},{8,11},{9,10},{10,... | collective-permute-start | bytes 393224 | tf_op jit(solution)/shard_map/ppermute | solution.py:75
  63.3 4.6 %collective-permute-start.21 = (f32[32,1024]{1,0:T(8,128)S(1)}, f32[32,1024]{1,0:T(8,128)S(1)}, u32[]{:S(2)}, u32[]{:S(2)}) collective-permute-start(f32[32,1024]{1,0:T(8,128)S(1)} %get-tuple-element.59), channel_id=1, source_target_pairs={{0,2},{1,3},{2,0},{3,1},{4,6},{5,7},{6,4},{7,5},{8,10},{9,11},{10,... | collective-permute-start | bytes 393224 | tf_op jit(solution)/shard_map/ppermute | solution.py:75
  68.6 8.4 %collective-permute-done.21 = f32[32,1024]{1,0:T(8,128)S(1)} collective-permute-done((f32[32,1024]{1,0:T(8,128)S(1)}, f32[32,1024]{1,0:T(8,128)S(1)}, u32[]{:S(2)}, u32[]{:S(2)}) %collective-permute-start.21) | collective-permute-done | bytes 131104 | tf_op jit(solution)/shard_map/ppermute | solution.py:75
  77.2 5.0 %collective-permute-done.23 = f32[32,1024]{1,0:T(8,128)S(1)} collective-permute-done((f32[32,1024]{1,0:T(8,128)S(1)}, f32[32,1024]{1,0:T(8,128)S(1)}, u32[]{:S(2)}, u32[]{:S(2)}) %collective-permute-start.23) | collective-permute-done | bytes 131104 | tf_op jit(solution)/shard_map/ppermute | solution.py:75
  83.2 2.0 %collective-permute-start.24 = (f32[32,1024]{1,0:T(8,128)S(1)}, f32[32,1024]{1,0:T(8,128)S(1)}, u32[]{:S(2)}, u32[]{:S(2)}) collective-permute-start(f32[32,1024]{1,0:T(8,128)S(1)} %add_add_fusion), channel_id=1, source_target_pairs={{0,3},{1,2},{2,1},{3,0},{4,7},{5,6},{6,5},{7,4},{8,11},{9,10},{10,... | collective-permute-start | bytes 393224 | tf_op jit(solution)/shard_map/ppermute | solution.py:75
  85.2 4.8 %collective-permute-done.24 = f32[32,1024]{1,0:T(8,128)S(1)} collective-permute-done((f32[32,1024]{1,0:T(8,128)S(1)}, f32[32,1024]{1,0:T(8,128)S(1)}, u32[]{:S(2)}, u32[]{:S(2)}) %collective-permute-start.24) | collective-permute-done | bytes 131104 | tf_op jit(solution)/shard_map/ppermute | solution.py:75
  90.0 5.3 %collective-permute-done.26 = f32[32,1024]{1,0:T(8,128)S(1)} collective-permute-done((f32[32,1024]{1,0:T(8,128)S(1)}, f32[32,1024]{1,0:T(8,128)S(1)}, u32[]{:S(2)}, u32[]{:S(2)}) %collective-permute-start.26) | collective-permute-done | bytes 131104 | tf_op jit(solution)/shard_map/ppermute | solution.py:75
  97.0 5.0 %collective-permute-done.29.refs_3_ = f32[2,32,1024]{2,1,0:T(8,128)S(1)} collective-permute-done((f32[2,32,1024]{2,1,0:T(8,128)S(1)}, f32[2,32,1024]{2,1,0:T(8,128)S(1)}, u32[]{:S(2)}, u32[]{:S(2)}) %collective-permute-start.29) | collective-permute-done | bytes 262176 | tf_op jit(solution)/shard_map/ppermute | solution.py:75
  102.1 1.5 %collective-permute-done.31.refs_7_ = f32[2,32,1024]{2,1,0:T(8,128)S(1)} collective-permute-done((f32[2,32,1024]{2,1,0:T(8,128)S(1)}, f32[2,32,1024]{2,1,0:T(8,128)S(1)}, u32[]{:S(2)}, u32[]{:S(2)}) %collective-permute-start.31) | collective-permute-done | bytes 262176 | tf_op jit(solution)/shard_map/ppermute | solution.py:75
  106.0 2.2 %collective-permute-done.32.refs_9_ = f32[2,1024]{1,0:T(2,128)S(1)} collective-permute-done((f32[2,1024]{1,0:T(2,128)S(1)}, f32[2,1024]{1,0:T(2,128)S(1)}, u32[]{:S(2)}, u32[]{:S(2)}) %collective-permute-start.32) | collective-permute-done | bytes 8224 | tf_op jit(solution)/shard_map/ppermute | solution.py:75
  110.6 2.2 %collective-permute-done.33.refs_9_ = f32[2,1024]{1,0:T(2,128)S(1)} collective-permute-done((f32[2,1024]{1,0:T(2,128)S(1)}, f32[2,1024]{1,0:T(2,128)S(1)}, u32[]{:S(2)}, u32[]{:S(2)}) %collective-permute-start.33) | collective-permute-done | bytes 8224 | tf_op jit(solution)/shard_map/ppermute | solution.py:75
  115.2 2.2 %collective-permute-done.34.refs_5_ = f32[2,1024]{1,0:T(2,128)S(1)} collective-permute-done((f32[2,1024]{1,0:T(2,128)S(1)}, f32[2,1024]{1,0:T(2,128)S(1)}, u32[]{:S(2)}, u32[]{:S(2)}) %collective-permute-start.34) | collective-permute-done | bytes 8224 | tf_op jit(solution)/shard_map/ppermute | solution.py:75
  117.5 2.2 %shard_map.57 = (bf16[2,4,32,512]{3,2,1,0:T(8,128)(2,1)S(1)}, bf16[2,4,32,512]{3,2,1,0:T(8,128)(2,1)S(1)}, bf16[2,4,32,512]{3,2,1,0:T(8,128)(2,1)S(1)}, bf16[2,4...) custom-call(f32[2,32,1024]{2,1,0:T(8,128)S(1)} %pad_maximum_fusion.refs_0_, ...), custom_call_target="tpu_custom_call" | custom-call | flops 1073741824 | bytes 5259264 | tf_op jit(solution)/shard_map/pallas_call | solution.py:115
  119.6 2.0 %collective-permute-start.35 = (bf16[2,4,32,512]{3,2,1,0:T(8,128)(2,1)S(1)}, bf16[2,4,32,512]{3,2,1,0:T(8,128)(2,1)S(1)}, u32[]{:S(2)}, u32[]{:S(2)}) collective-permute-start(bf16[2,4,32,512]{3,2,1,0:T(8,128)(2,1)S(1)} %get-tuple-element.63), channel_id=1, source_target_pairs={{0,3},{1,2},{2,1},{3,0},{4,7},{5,6},{6,5},{7,4},{8,11},{9,10},{10,... | collective-permute-start | bytes 786440 | tf_op jit(solution)/shard_map/ppermute | solution.py:75
  121.6 2.4 %collective-permute-start.37 = (bf16[2,4,32,512]{3,2,1,0:T(8,128)(2,1)S(1)}, bf16[2,4,32,512]{3,2,1,0:T(8,128)(2,1)S(1)}, u32[]{:S(2)}, u32[]{:S(2)}) collective-permute-start(bf16[2,4,32,512]{3,2,1,0:T(8,128)(2,1)S(1)} %get-tuple-element.65), channel_id=1, source_target_pairs={{0,1},{1,0},{2,3},{3,2},{4,5},{5,4},{6,7},{7,6},{8,9},{9,8},{10,11... | collective-permute-start | bytes 786440 | tf_op jit(solution)/shard_map/ppermute | solution.py:75
  124.0 6.6 %collective-permute-done.35.refs_0_ = bf16[2,4,32,512]{3,2,1,0:T(8,128)(2,1)S(1)} collective-permute-done((bf16[2,4,32,512]{3,2,1,0:T(8,128)(2,1)S(1)}, bf16[2,4,32,512]{3,2,1,0:T(8,128)(2,1)S(1)}, u32[]{:S(2)}, u32[]{:S(2)}) %collective-permute-start.35) | collective-permute-done | bytes 262176 | tf_op jit(solution)/shard_map/ppermute | solution.py:75
  130.7 9.7 %collective-permute-done.36.refs_1_ = bf16[2,4,32,512]{3,2,1,0:T(8,128)(2,1)S(1)} collective-permute-done((bf16[2,4,32,512]{3,2,1,0:T(8,128)(2,1)S(1)}, bf16[2,4,32,512]{3,2,1,0:T(8,128)(2,1)S(1)}, u32[]{:S(2)}, u32[]{:S(2)}) %collective-permute-start.36) | collective-permute-done | bytes 262176 | tf_op jit(solution)/shard_map/ppermute | solution.py:75
  (70 shorter events, 28.5 us)
Async XLA Ops:
  1.9 12.0 %collective-permute-start = (bf16[128,2048]{1,0:T(8,128)(2,1)S(1)}, bf16[128,2048]{1,0:T(8,128)(2,1)S(1)}, u32[]{:S(2)}, u32[]{:S(2)}) collective-permute-start(bf16[128,2048]{1,0:T(8,128)(2,1)S(1)} %get-tuple-element.37), channel_id=1, source_target_pairs={{0,4},{4,0},{8,12},{12,8},{16,20},{20,16},{24,28},{28,24},{1,5},{5... | collective-permute-start | bytes 1572872 | tf_op jit(solution)/shard_map/ppermute | solution.py:75
  3.2 9.3 %collective-permute-start.2 = (bf16[256,512]{1,0:T(8,128)(2,1)S(1)}, bf16[256,512]{1,0:T(8,128)(2,1)S(1)}, u32[]{:S(2)}, u32[]{:S(2)}) collective-permute-start(bf16[256,512]{1,0:T(8,128)(2,1)S(1)} %get-tuple-element.38.refs_4_.refs_6_), channel_id=1, source_target_pairs={{0,16},{4,20},{8,24},{12,28},{16,0},{20,4},{24,8},{28,12},{1,17},{... | collective-permute-start | bytes 786440 | tf_op jit(solution)/shard_map/ppermute | solution.py:75
  6.2 7.8 %collective-permute-start.1 = (bf16[256,512]{1,0:T(8,128)(2,1)S(1)}, bf16[256,512]{1,0:T(8,128)(2,1)S(1)}, u32[]{:S(2)}, u32[]{:S(2)}) collective-permute-start(bf16[256,512]{1,0:T(8,128)(2,1)S(1)} %get-tuple-element.38.refs_4_.refs_6_), channel_id=1, source_target_pairs={{0,8},{4,12},{8,0},{12,4},{16,24},{20,28},{24,16},{28,20},{1,9},{5... | collective-permute-start | bytes 786440 | tf_op jit(solution)/shard_map/ppermute | solution.py:75
  7.7 13.0 %collective-permute-start.8 = (bf16[256,512]{1,0:T(8,128)(2,1)S(1)}, bf16[256,512]{1,0:T(8,128)(2,1)S(1)}, u32[]{:S(2)}, u32[]{:S(2)}) collective-permute-start(bf16[256,512]{1,0:T(8,128)(2,1)S(1)} %get-tuple-element.49), channel_id=1, source_target_pairs={{0,1},{1,0},{2,3},{3,2},{4,5},{5,4},{6,7},{7,6},{8,9},{9,8},{10,11... | collective-permute-start | bytes 786440 | tf_op jit(solution)/shard_map/ppermute | solution.py:75
  9.3 16.5 %collective-permute-start.3 = (bf16[256,512]{1,0:T(8,128)(2,1)S(1)}, bf16[256,512]{1,0:T(8,128)(2,1)S(1)}, u32[]{:S(2)}, u32[]{:S(2)}) collective-permute-start(bf16[256,512]{1,0:T(8,128)(2,1)S(1)} %get-tuple-element.42), channel_id=1, source_target_pairs={{0,2},{1,3},{2,0},{3,1},{4,6},{5,7},{6,4},{7,5},{8,10},{9,11},{10,... | collective-permute-start | bytes 786440 | tf_op jit(solution)/shard_map/ppermute | solution.py:75
  20.7 9.1 %collective-permute-start.11 = (bf16[256,512]{1,0:T(8,128)(2,1)S(1)}, bf16[256,512]{1,0:T(8,128)(2,1)S(1)}, u32[]{:S(2)}, u32[]{:S(2)}) collective-permute-start(bf16[256,512]{1,0:T(8,128)(2,1)S(1)} %collective-permute-done.8.refs_5_.refs_7_), channel_id=1, source_target_pairs={{0,16},{4,20},{8,24},{12,28},{16,0},{20,4},{24,8},{28,12},{1,17},{... | collective-permute-start | bytes 786440 | tf_op jit(solution)/shard_map/ppermute | solution.py:75
  21.2 11.6 %collective-permute-start.14 = (bf16[256,512]{1,0:T(8,128)(2,1)S(1)}, bf16[256,512]{1,0:T(8,128)(2,1)S(1)}, u32[]{:S(2)}, u32[]{:S(2)}) collective-permute-start(bf16[256,512]{1,0:T(8,128)(2,1)S(1)} %collective-permute-done.1.refs_8_.refs_10_), channel_id=1, source_target_pairs={{0,16},{4,20},{8,24},{12,28},{16,0},{20,4},{24,8},{28,12},{1,17},{... | collective-permute-start | bytes 786440 | tf_op jit(solution)/shard_map/ppermute | solution.py:75
  22.7 12.6 %collective-permute-start.6 = (bf16[256,512]{1,0:T(8,128)(2,1)S(1)}, bf16[256,512]{1,0:T(8,128)(2,1)S(1)}, u32[]{:S(2)}, u32[]{:S(2)}) collective-permute-start(bf16[256,512]{1,0:T(8,128)(2,1)S(1)} %get-tuple-element.47), channel_id=1, source_target_pairs={{0,3},{1,2},{2,1},{3,0},{4,7},{5,6},{6,5},{7,4},{8,11},{9,10},{10,... | collective-permute-start | bytes 786440 | tf_op jit(solution)/shard_map/ppermute | solution.py:75
  25.2 8.1 %collective-permute-start.9 = (bf16[256,512]{1,0:T(8,128)(2,1)S(1)}, bf16[256,512]{1,0:T(8,128)(2,1)S(1)}, u32[]{:S(2)}, u32[]{:S(2)}) collective-permute-start(bf16[256,512]{1,0:T(8,128)(2,1)S(1)} %collective-permute-done.8.refs_5_.refs_7_), channel_id=1, source_target_pairs={{0,8},{4,12},{8,0},{12,4},{16,24},{20,28},{24,16},{28,20},{1,9},{5... | collective-permute-start | bytes 786440 | tf_op jit(solution)/shard_map/ppermute | solution.py:75
  25.7 10.2 %collective-permute-start.4 = (bf16[2,128,512]{2,1,0:T(8,128)(2,1)S(1)}, bf16[2,128,512]{2,1,0:T(8,128)(2,1)S(1)}, u32[]{:S(2)}, u32[]{:S(2)}) collective-permute-start(bf16[2,128,512]{2,1,0:T(8,128)(2,1)S(1)} %get-tuple-element.43), channel_id=1, source_target_pairs={{0,1},{1,0},{2,3},{3,2},{4,5},{5,4},{6,7},{7,6},{8,9},{9,8},{10,11... | collective-permute-start | bytes 786440 | tf_op jit(solution)/shard_map/ppermute | solution.py:75
  32.8 7.3 %collective-permute-start.15 = (bf16[256,512]{1,0:T(8,128)(2,1)S(1)}, bf16[256,512]{1,0:T(8,128)(2,1)S(1)}, u32[]{:S(2)}, u32[]{:S(2)}) collective-permute-start(bf16[256,512]{1,0:T(8,128)(2,1)S(1)} %collective-permute-done.3.refs_6_.refs_8_), channel_id=1, source_target_pairs={{0,16},{4,20},{8,24},{12,28},{16,0},{20,4},{24,8},{28,12},{1,17},{... | collective-permute-start | bytes 786440 | tf_op jit(solution)/shard_map/ppermute | solution.py:75
  33.3 11.9 %collective-permute-start.10 = (bf16[256,512]{1,0:T(8,128)(2,1)S(1)}, bf16[256,512]{1,0:T(8,128)(2,1)S(1)}, u32[]{:S(2)}, u32[]{:S(2)}) collective-permute-start(bf16[256,512]{1,0:T(8,128)(2,1)S(1)} %collective-permute-done.3.refs_6_.refs_8_), channel_id=1, source_target_pairs={{0,8},{4,12},{8,0},{12,4},{16,24},{20,28},{24,16},{28,20},{1,9},{5... | collective-permute-start | bytes 786440 | tf_op jit(solution)/shard_map/ppermute | solution.py:75
  33.9 11.3 %collective-permute-start.12 = (bf16[256,512]{1,0:T(8,128)(2,1)S(1)}, bf16[256,512]{1,0:T(8,128)(2,1)S(1)}, u32[]{:S(2)}, u32[]{:S(2)}) collective-permute-start(bf16[256,512]{1,0:T(8,128)(2,1)S(1)} %collective-permute-done.11.refs_13_.refs_15_), channel_id=1, source_target_pairs={{0,8},{4,12},{8,0},{12,4},{16,24},{20,28},{24,16},{28,20},{1,9},{5... | collective-permute-start | bytes 786440 | tf_op jit(solution)/shard_map/ppermute | solution.py:75
  40.1 9.0 %collective-permute-start.16 = (bf16[256,512]{1,0:T(8,128)(2,1)S(1)}, bf16[256,512]{1,0:T(8,128)(2,1)S(1)}, u32[]{:S(2)}, u32[]{:S(2)}) collective-permute-start(bf16[256,512]{1,0:T(8,128)(2,1)S(1)} %collective-permute-done.6.refs_7_.refs_9_), channel_id=1, source_target_pairs={{0,16},{4,20},{8,24},{12,28},{16,0},{20,4},{24,8},{28,12},{1,17},{... | collective-permute-start | bytes 786440 | tf_op jit(solution)/shard_map/ppermute | solution.py:75
  40.6 16.5 %collective-permute-start.5 = (bf16[2,128,512]{2,1,0:T(8,128)(2,1)S(1)}, bf16[2,128,512]{2,1,0:T(8,128)(2,1)S(1)}, u32[]{:S(2)}, u32[]{:S(2)}) collective-permute-start(bf16[2,128,512]{2,1,0:T(8,128)(2,1)S(1)} %get-tuple-element.45), channel_id=1, source_target_pairs={{0,2},{1,3},{2,0},{3,1},{4,6},{5,7},{6,4},{7,5},{8,10},{9,11},{10,... | collective-permute-start | bytes 786440 | tf_op jit(solution)/shard_map/ppermute | solution.py:75
  41.4 15.8 %collective-permute-start.7 = (bf16[2,128,512]{2,1,0:T(8,128)(2,1)S(1)}, bf16[2,128,512]{2,1,0:T(8,128)(2,1)S(1)}, u32[]{:S(2)}, u32[]{:S(2)}) collective-permute-start(bf16[2,128,512]{2,1,0:T(8,128)(2,1)S(1)} %get-tuple-element.48), channel_id=1, source_target_pairs={{0,3},{1,2},{2,1},{3,0},{4,7},{5,6},{6,5},{7,4},{8,11},{9,10},{10,... | collective-permute-start | bytes 786440 | tf_op jit(solution)/shard_map/ppermute | solution.py:75
  45.2 11.9 %collective-permute-start.13 = (bf16[256,512]{1,0:T(8,128)(2,1)S(1)}, bf16[256,512]{1,0:T(8,128)(2,1)S(1)}, u32[]{:S(2)}, u32[]{:S(2)}) collective-permute-start(bf16[256,512]{1,0:T(8,128)(2,1)S(1)} %collective-permute-done.6.refs_7_.refs_9_), channel_id=1, source_target_pairs={{0,8},{4,12},{8,0},{12,4},{16,24},{20,28},{24,16},{28,20},{1,9},{5... | collective-permute-start | bytes 786440 | tf_op jit(solution)/shard_map/ppermute | solution.py:75
  46.0 11.1 %collective-permute-start.17 = (bf16[256,512]{1,0:T(8,128)(2,1)S(1)}, bf16[256,512]{1,0:T(8,128)(2,1)S(1)}, u32[]{:S(2)}, u32[]{:S(2)}) collective-permute-start(bf16[256,512]{1,0:T(8,128)(2,1)S(1)} %collective-permute-done.10.refs_10_.refs_12_), channel_id=1, source_target_pairs={{0,16},{4,20},{8,24},{12,28},{16,0},{20,4},{24,8},{28,12},{1,17},{... | collective-permute-start | bytes 786440 | tf_op jit(solution)/shard_map/ppermute | solution.py:75
  49.1 8.1 %collective-permute-start.18 = (bf16[256,512]{1,0:T(8,128)(2,1)S(1)}, bf16[256,512]{1,0:T(8,128)(2,1)S(1)}, u32[]{:S(2)}, u32[]{:S(2)}) collective-permute-start(bf16[256,512]{1,0:T(8,128)(2,1)S(1)} %collective-permute-done.16.refs_15_.refs_17_), channel_id=1, source_target_pairs={{0,8},{4,12},{8,0},{12,4},{16,24},{20,28},{24,16},{28,20},{1,9},{5... | collective-permute-start | bytes 786440 | tf_op jit(solution)/shard_map/ppermute | solution.py:75
  61.2 7.4 %collective-permute-start.20 = (f32[32,1024]{1,0:T(8,128)S(1)}, f32[32,1024]{1,0:T(8,128)S(1)}, u32[]{:S(2)}, u32[]{:S(2)}) collective-permute-start(f32[32,1024]{1,0:T(8,128)S(1)} %get-tuple-element.58), channel_id=1, source_target_pairs={{0,3},{1,2},{2,1},{3,0},{4,7},{5,6},{6,5},{7,4},{8,11},{9,10},{10,... | collective-permute-start | bytes 393224 | tf_op jit(solution)/shard_map/ppermute | solution.py:75
  63.3 13.8 %collective-permute-start.21 = (f32[32,1024]{1,0:T(8,128)S(1)}, f32[32,1024]{1,0:T(8,128)S(1)}, u32[]{:S(2)}, u32[]{:S(2)}) collective-permute-start(f32[32,1024]{1,0:T(8,128)S(1)} %get-tuple-element.59), channel_id=1, source_target_pairs={{0,2},{1,3},{2,0},{3,1},{4,6},{5,7},{6,4},{7,5},{8,10},{9,11},{10,... | collective-permute-start | bytes 393224 | tf_op jit(solution)/shard_map/ppermute | solution.py:75
  67.9 9.2 %collective-permute-start.22 = (f32[32,1024]{1,0:T(8,128)S(1)}, f32[32,1024]{1,0:T(8,128)S(1)}, u32[]{:S(2)}, u32[]{:S(2)}) collective-permute-start(f32[32,1024]{1,0:T(8,128)S(1)} %get-tuple-element.60), channel_id=1, source_target_pairs={{0,1},{1,0},{2,3},{3,2},{4,5},{5,4},{6,7},{7,6},{8,9},{9,8},{10,11... | collective-permute-start | bytes 393224 | tf_op jit(solution)/shard_map/ppermute | solution.py:75
  82.2 7.8 %collective-permute-start.25 = (f32[2,32,1024]{2,1,0:T(8,128)S(1)}, f32[2,32,1024]{2,1,0:T(8,128)S(1)}, u32[]{:S(2)}, u32[]{:S(2)}) collective-permute-start(f32[2,32,1024]{2,1,0:T(8,128)S(1)} %pad_maximum_fusion.refs_0_), channel_id=1, source_target_pairs={{0,8},{4,12},{8,0},{12,4},{16,24},{20,28},{24,16},{28,20},{1,9},{5... | collective-permute-start | bytes 786440 | tf_op jit(solution)/shard_map/ppermute | solution.py:75
  83.2 6.8 %collective-permute-start.24 = (f32[32,1024]{1,0:T(8,128)S(1)}, f32[32,1024]{1,0:T(8,128)S(1)}, u32[]{:S(2)}, u32[]{:S(2)}) collective-permute-start(f32[32,1024]{1,0:T(8,128)S(1)} %add_add_fusion), channel_id=1, source_target_pairs={{0,3},{1,2},{2,1},{3,0},{4,7},{5,6},{6,5},{7,4},{8,11},{9,10},{10,... | collective-permute-start | bytes 393224 | tf_op jit(solution)/shard_map/ppermute | solution.py:75
  85.2 10.1 %collective-permute-start.26 = (f32[32,1024]{1,0:T(8,128)S(1)}, f32[32,1024]{1,0:T(8,128)S(1)}, u32[]{:S(2)}, u32[]{:S(2)}) collective-permute-start(f32[32,1024]{1,0:T(8,128)S(1)} %add_add_fusion), channel_id=1, source_target_pairs={{0,2},{1,3},{2,0},{3,1},{4,6},{5,7},{6,4},{7,5},{8,10},{9,11},{10,... | collective-permute-start | bytes 393224 | tf_op jit(solution)/shard_map/ppermute | solution.py:75
  95.3 6.7 %collective-permute-start.29 = (f32[2,32,1024]{2,1,0:T(8,128)S(1)}, f32[2,32,1024]{2,1,0:T(8,128)S(1)}, u32[]{:S(2)}, u32[]{:S(2)}) collective-permute-start(f32[2,32,1024]{2,1,0:T(8,128)S(1)} %pad_maximum_fusion.1.refs_1_), channel_id=1, source_target_pairs={{0,8},{4,12},{8,0},{12,4},{16,24},{20,28},{24,16},{28,20},{1,9},{5... | collective-permute-start | bytes 786440 | tf_op jit(solution)/shard_map/ppermute | solution.py:75
  96.5 5.6 %collective-permute-start.27 = (f32[2,32,1024]{2,1,0:T(8,128)S(1)}, f32[2,32,1024]{2,1,0:T(8,128)S(1)}, u32[]{:S(2)}, u32[]{:S(2)}) collective-permute-start(f32[2,32,1024]{2,1,0:T(8,128)S(1)} %pad_maximum_fusion.refs_0_), channel_id=1, source_target_pairs={{0,4},{4,0},{8,12},{12,8},{16,20},{20,16},{24,28},{28,24},{1,5},{5... | collective-permute-start | bytes 786440 | tf_op jit(solution)/shard_map/ppermute | solution.py:75
  119.6 11.0 %collective-permute-start.35 = (bf16[2,4,32,512]{3,2,1,0:T(8,128)(2,1)S(1)}, bf16[2,4,32,512]{3,2,1,0:T(8,128)(2,1)S(1)}, u32[]{:S(2)}, u32[]{:S(2)}) collective-permute-start(bf16[2,4,32,512]{3,2,1,0:T(8,128)(2,1)S(1)} %get-tuple-element.63), channel_id=1, source_target_pairs={{0,3},{1,2},{2,1},{3,0},{4,7},{5,6},{6,5},{7,4},{8,11},{9,10},{10,... | collective-permute-start | bytes 786440 | tf_op jit(solution)/shard_map/ppermute | solution.py:75
  121.6 18.8 %collective-permute-start.36 = (bf16[2,4,32,512]{3,2,1,0:T(8,128)(2,1)S(1)}, bf16[2,4,32,512]{3,2,1,0:T(8,128)(2,1)S(1)}, u32[]{:S(2)}, u32[]{:S(2)}) collective-permute-start(bf16[2,4,32,512]{3,2,1,0:T(8,128)(2,1)S(1)} %get-tuple-element.64), channel_id=1, source_target_pairs={{0,2},{1,3},{2,0},{3,1},{4,6},{5,7},{6,4},{7,5},{8,10},{9,11},{10,... | collective-permute-start | bytes 786440 | tf_op jit(solution)/shard_map/ppermute | solution.py:75
  121.6 18.8 %collective-permute-start.37 = (bf16[2,4,32,512]{3,2,1,0:T(8,128)(2,1)S(1)}, bf16[2,4,32,512]{3,2,1,0:T(8,128)(2,1)S(1)}, u32[]{:S(2)}, u32[]{:S(2)}) collective-permute-start(bf16[2,4,32,512]{3,2,1,0:T(8,128)(2,1)S(1)} %get-tuple-element.65), channel_id=1, source_target_pairs={{0,1},{1,0},{2,3},{3,2},{4,5},{5,4},{6,7},{7,6},{8,9},{9,8},{10,11... | collective-permute-start | bytes 786440 | tf_op jit(solution)/shard_map/ppermute | solution.py:75
  124.0 17.5 %collective-permute-start.41 = (bf16[2,4,32,512]{3,2,1,0:T(8,128)(2,1)S(1)}, bf16[2,4,32,512]{3,2,1,0:T(8,128)(2,1)S(1)}, u32[]{:S(2)}, u32[]{:S(2)}) collective-permute-start(bf16[2,4,32,512]{3,2,1,0:T(8,128)(2,1)S(1)} %get-tuple-element.66.refs_3_), channel_id=1, source_target_pairs={{0,4},{4,0},{8,12},{12,8},{16,20},{20,16},{24,28},{28,24},{1,5},{5... | collective-permute-start | bytes 786440 | tf_op jit(solution)/shard_map/ppermute | solution.py:75
  130.7 10.8 %collective-permute-start.38 = (bf16[2,4,32,512]{3,2,1,0:T(8,128)(2,1)S(1)}, bf16[2,4,32,512]{3,2,1,0:T(8,128)(2,1)S(1)}, u32[]{:S(2)}, u32[]{:S(2)}) collective-permute-start(bf16[2,4,32,512]{3,2,1,0:T(8,128)(2,1)S(1)} %collective-permute-done.35.refs_0_), channel_id=1, source_target_pairs={{0,4},{4,0},{8,12},{12,8},{16,20},{20,16},{24,28},{28,24},{1,5},{5... | collective-permute-start | bytes 786440 | tf_op jit(solution)/shard_map/ppermute | solution.py:75
  (12 other events, 36.2 us)

commit v11 on v9

--- a/solution.py
+++ b/solution.py
@@ -258,8 +258,8 @@
 def iteration_kernel(n_groups, log_noise, *refs):
     *refs, out_ref = refs
     wide = out_ref.shape[1]
-    chips = [refs[i : i + 3] for i in range(0, 3 * n_groups, 3)]
-    g = data_potentials(refs[3 * n_groups :], wide)
+    chips = [refs[i : i + 2] for i in range(0, 2 * n_groups, 2)]
+    g = data_potentials(refs[2 * n_groups :], wide)
     potentials = [row_update(chip, g, log_noise) for chip in chips]
     for b in range(len(g)):
         scores = [f - rows_of(chip, b) for f, chip in zip(potentials, chips)]
@@ -284,8 +284,8 @@
 
 
 def target_kernel(n_col, n_chip, log_noise, *refs):
-    tiles, stats, latent_refs = refs[:6], refs[6:8], refs[8 : 8 + n_chip * n_col]
-    refs = refs[8 + n_chip * n_col :]
+    tiles, stats, latent_refs = refs[:4], refs[4:6], refs[6 : 6 + n_chip * n_col]
+    refs = refs[6 + n_chip * n_col :]
     target_refs, refs = refs[:n_col], refs[n_col:]
     noise_pot_ref, data_pot_ref, pots, weights = refs
     _, col = place()
@@ -386,11 +386,10 @@
     own_part, other_part = partial_cost(noise_pieces, latents)
     parts = col_exchange(core_sum(own_part, swap_core(other_part), n_col))
     tile = functools.reduce(jnp.add, parts[::-1])
-    tile_2, tile_1 = swap(tile, "col", 2), swap(tile, "col", 1)
-    tile_3 = swap(tile_2, "col", 1)
+    tile_3, tile_2, tile_1 = [swap(tile, "col", d) for d in (3, 2, 1)]
     x_tile = swap_x(tile)
-    pair = jnp.stack([after(tile_2, x_tile), tile_1])
-    tiles = [[tile, pair, tile_3], [x_tile, swap_x(pair), swap_x(tile_3)]]
+    others = jnp.stack([after(tile_3, x_tile), tile_2, tile_1])
+    tiles = [[tile, others], [x_tile, swap_x(others)]]
     other_tiles = [swap_core(piece) for piece in tiles[0]]
     tiles += [other_tiles, [swap_core(piece) for piece in tiles[1]]]
     log_noise = math.log2(own * lax.axis_size("row"))

time: 139 us -> 143 us (1.029)
  waiting for transfers between devices: 81.4 us -> 86.7 us
  starting transfers between devices: 46.1 us -> 44.6 us
    ppermute x45 -> x42, waiting for transfers between devices: 81.4 us -> 86.7 us  [swap(): return lax.ppermute(array, axis, [(i, i ^ step) for i in range(count)])]
    ppermute x45 -> x42, starting transfers between devices: 46.1 us -> 44.6 us  [swap(): return lax.ppermute(array, axis, [(i, i ^ step) for i in range(count)])]
  transfers between devices with their start and end apart: 45 -> 42, of which waited for: 27 -> 25; matrix products, arithmetic and copies ran while one was open for 0% -> 0% of each run, Pallas kernels for 0% -> 0%
where the time goes in v11:
time: 143 us
  waiting for transfers between devices  86.7 us (61%)
  starting transfers between devices  44.6 us (31%)
  Pallas kernels  8.28 us (6%)
  local copies, waits for them, and re-layouts  2.44 us (2%)
    ppermute x42, waiting for transfers between devices, swap(): return lax.ppermute(array, axis, [(i, i ^ step) for i in range(count)])  86.7 us
    ppermute x42, starting transfers between devices, swap(): return lax.ppermute(array, axis, [(i, i ^ step) for i in range(count)])  44.6 us
    pallas_call x10, Pallas kernels, kernel_call(): pl.pallas_call(kernel, in_specs=[VMEM] * len(operands), out_specs=[VMEM]...  8.28 us
  transfers between devices with their start and end apart: 42, of which 25 were waited for; matrix products, arithmetic and copies ran while one was open for 0% of the time, Pallas kernels for 0%

profile of v11, /device:TPU:0, one launch (start us, length us, event | category | flops | bytes accessed | tf_op | source)
XLA Modules:
  0.0 142.8 jit_solution(8039052167045060058)
XLA Ops:
  3.2 3.0 %collective-permute-start.2 = (bf16[256,512]{1,0:T(8,128)(2,1)S(1)}, bf16[256,512]{1,0:T(8,128)(2,1)S(1)}, u32[]{:S(2)}, u32[]{:S(2)}) collective-permute-start(bf16[256,512]{1,0:T(8,128)(2,1)S(1)} %get-tuple-element.38.refs_4_.refs_6_), channel_id=1, source_target_pairs={{0,16},{4,20},{8,24},{12,28},{16,0},{20,4},{24,8},{28,12},{1,17},{... | collective-permute-start | bytes 786440 | tf_op jit(solution)/shard_map/ppermute | solution.py:75
  7.7 1.6 %collective-permute-start.8 = (bf16[256,512]{1,0:T(8,128)(2,1)S(1)}, bf16[256,512]{1,0:T(8,128)(2,1)S(1)}, u32[]{:S(2)}, u32[]{:S(2)}) collective-permute-start(bf16[256,512]{1,0:T(8,128)(2,1)S(1)} %get-tuple-element.49), channel_id=1, source_target_pairs={{0,1},{1,0},{2,3},{3,2},{4,5},{5,4},{6,7},{7,6},{8,9},{9,8},{10,11... | collective-permute-start | bytes 786440 | tf_op jit(solution)/shard_map/ppermute | solution.py:75
  9.3 2.6 %collective-permute-start.3 = (bf16[256,512]{1,0:T(8,128)(2,1)S(1)}, bf16[256,512]{1,0:T(8,128)(2,1)S(1)}, u32[]{:S(2)}, u32[]{:S(2)}) collective-permute-start(bf16[256,512]{1,0:T(8,128)(2,1)S(1)} %get-tuple-element.42), channel_id=1, source_target_pairs={{0,2},{1,3},{2,0},{3,1},{4,6},{5,7},{6,4},{7,5},{8,10},{9,11},{10,... | collective-permute-start | bytes 786440 | tf_op jit(solution)/shard_map/ppermute | solution.py:75
  14.0 6.6 %collective-permute-done.8.refs_5_.refs_7_ = bf16[256,512]{1,0:T(8,128)(2,1)S(1)} collective-permute-done((bf16[256,512]{1,0:T(8,128)(2,1)S(1)}, bf16[256,512]{1,0:T(8,128)(2,1)S(1)}, u32[]{:S(2)}, u32[]{:S(2)}) %collective-permute-start.8) | collective-permute-done | bytes 262176 | tf_op jit(solution)/shard_map/ppermute | solution.py:75
  21.2 1.5 %collective-permute-start.14 = (bf16[256,512]{1,0:T(8,128)(2,1)S(1)}, bf16[256,512]{1,0:T(8,128)(2,1)S(1)}, u32[]{:S(2)}, u32[]{:S(2)}) collective-permute-start(bf16[256,512]{1,0:T(8,128)(2,1)S(1)} %collective-permute-done.1.refs_8_.refs_10_), channel_id=1, source_target_pairs={{0,16},{4,20},{8,24},{12,28},{16,0},{20,4},{24,8},{28,12},{1,17},{... | collective-permute-start | bytes 786440 | tf_op jit(solution)/shard_map/ppermute | solution.py:75
  22.7 2.5 %collective-permute-start.6 = (bf16[256,512]{1,0:T(8,128)(2,1)S(1)}, bf16[256,512]{1,0:T(8,128)(2,1)S(1)}, u32[]{:S(2)}, u32[]{:S(2)}) collective-permute-start(bf16[256,512]{1,0:T(8,128)(2,1)S(1)} %get-tuple-element.47), channel_id=1, source_target_pairs={{0,3},{1,2},{2,1},{3,0},{4,7},{5,6},{6,5},{7,4},{8,11},{9,10},{10,... | collective-permute-start | bytes 786440 | tf_op jit(solution)/shard_map/ppermute | solution.py:75
  25.7 4.1 %collective-permute-done.11.refs_13_.refs_15_ = bf16[256,512]{1,0:T(8,128)(2,1)S(1)} collective-permute-done((bf16[256,512]{1,0:T(8,128)(2,1)S(1)}, bf16[256,512]{1,0:T(8,128)(2,1)S(1)}, u32[]{:S(2)}, u32[]{:S(2)}) %collective-permute-start.11) | collective-permute-done | bytes 262176 | tf_op jit(solution)/shard_map/ppermute | solution.py:75
  29.8 3.0 %collective-permute-done.14.refs_16_.refs_18_ = bf16[256,512]{1,0:T(8,128)(2,1)S(1)} collective-permute-done((bf16[256,512]{1,0:T(8,128)(2,1)S(1)}, bf16[256,512]{1,0:T(8,128)(2,1)S(1)}, u32[]{:S(2)}, u32[]{:S(2)}) %collective-permute-start.14) | collective-permute-done | bytes 262176 | tf_op jit(solution)/shard_map/ppermute | solution.py:75
  36.0 4.1 %collective-permute-done.15.refs_14_.refs_16_ = bf16[256,512]{1,0:T(8,128)(2,1)S(1)} collective-permute-done((bf16[256,512]{1,0:T(8,128)(2,1)S(1)}, bf16[256,512]{1,0:T(8,128)(2,1)S(1)}, u32[]{:S(2)}, u32[]{:S(2)}) %collective-permute-start.15) | collective-permute-done | bytes 262176 | tf_op jit(solution)/shard_map/ppermute | solution.py:75
  41.4 1.9 %collective-permute-start.7 = (bf16[2,128,512]{2,1,0:T(8,128)(2,1)S(1)}, bf16[2,128,512]{2,1,0:T(8,128)(2,1)S(1)}, u32[]{:S(2)}, u32[]{:S(2)}) collective-permute-start(bf16[2,128,512]{2,1,0:T(8,128)(2,1)S(1)} %get-tuple-element.48), channel_id=1, source_target_pairs={{0,3},{1,2},{2,1},{3,0},{4,7},{5,6},{6,5},{7,4},{8,11},{9,10},{10,... | collective-permute-start | bytes 786440 | tf_op jit(solution)/shard_map/ppermute | solution.py:75
  43.3 1.9 %collective-permute-done.12.refs_17_.refs_19_ = bf16[256,512]{1,0:T(8,128)(2,1)S(1)} collective-permute-done((bf16[256,512]{1,0:T(8,128)(2,1)S(1)}, bf16[256,512]{1,0:T(8,128)(2,1)S(1)}, u32[]{:S(2)}, u32[]{:S(2)}) %collective-permute-start.12) | collective-permute-done | bytes 262176 | tf_op jit(solution)/shard_map/ppermute | solution.py:75
  47.4 1.7 %collective-permute-done.16.refs_15_.refs_17_ = bf16[256,512]{1,0:T(8,128)(2,1)S(1)} collective-permute-done((bf16[256,512]{1,0:T(8,128)(2,1)S(1)}, bf16[256,512]{1,0:T(8,128)(2,1)S(1)}, u32[]{:S(2)}, u32[]{:S(2)}) %collective-permute-start.16) | collective-permute-done | bytes 262176 | tf_op jit(solution)/shard_map/ppermute | solution.py:75
  49.7 7.4 %collective-permute-done.5.refs_2_ = bf16[2,128,512]{2,1,0:T(8,128)(2,1)S(1)} collective-permute-done((bf16[2,128,512]{2,1,0:T(8,128)(2,1)S(1)}, bf16[2,128,512]{2,1,0:T(8,128)(2,1)S(1)}, u32[]{:S(2)}, u32[]{:S(2)}) %collective-permute-start.5) | collective-permute-done | bytes 262176 | tf_op jit(solution)/shard_map/ppermute | solution.py:75
  57.2 2.0 %shard_map.52 = (f32[128,1024]{1,0:T(8,128)S(1)}, f32[128,1024]{1,0:T(8,128)S(1)}) custom-call(bf16[2,128,512]{2,1,0:T(8,128)(2,1)S(1)} %get-tuple-element.40.refs_0_, bf16[2,128,512]{2,1,0:T(8,128)(2,1)S(1)} %collective-permute-done.4.refs_1_, bf16[2,128,512]{2,1,0:T(8,128)(2,1)S(1)} %collective-permute-done.5.refs_2_, ...), custom_call_target="tpu_custom_call" | custom-call | flops 1073741824 | bytes 5242880 | tf_op jit(solution)/shard_map/pallas_call | solution.py:115
  59.3 1.9 %collective-permute-done.19.other_ref = f32[128,1024]{1,0:T(8,128)S(1)} collective-permute-done((f32[128,1024]{1,0:T(8,128)S(1)}, f32[128,1024]{1,0:T(8,128)S(1)}, u32[]{:S(2)}, u32[]{:S(2)}) %collective-permute-start.19) | collective-permute-done | bytes 524320 | tf_op jit(solution)/shard_map/ppermute | solution.py:75
  61.2 2.0 %collective-permute-start.20 = (f32[32,1024]{1,0:T(8,128)S(1)}, f32[32,1024]{1,0:T(8,128)S(1)}, u32[]{:S(2)}, u32[]{:S(2)}) collective-permute-start(f32[32,1024]{1,0:T(8,128)S(1)} %get-tuple-element.58), channel_id=1, source_target_pairs={{0,3},{1,2},{2,1},{3,0},{4,7},{5,6},{6,5},{7,4},{8,11},{9,10},{10,... | collective-permute-start | bytes 393224 | tf_op jit(solution)/shard_map/ppermute | solution.py:75
  63.3 4.6 %collective-permute-start.21 = (f32[32,1024]{1,0:T(8,128)S(1)}, f32[32,1024]{1,0:T(8,128)S(1)}, u32[]{:S(2)}, u32[]{:S(2)}) collective-permute-start(f32[32,1024]{1,0:T(8,128)S(1)} %get-tuple-element.59), channel_id=1, source_target_pairs={{0,2},{1,3},{2,0},{3,1},{4,6},{5,7},{6,4},{7,5},{8,10},{9,11},{10,... | collective-permute-start | bytes 393224 | tf_op jit(solution)/shard_map/ppermute | solution.py:75
  68.6 8.4 %collective-permute-done.21 = f32[32,1024]{1,0:T(8,128)S(1)} collective-permute-done((f32[32,1024]{1,0:T(8,128)S(1)}, f32[32,1024]{1,0:T(8,128)S(1)}, u32[]{:S(2)}, u32[]{:S(2)}) %collective-permute-start.21) | collective-permute-done | bytes 131104 | tf_op jit(solution)/shard_map/ppermute | solution.py:75
  78.2 2.0 %collective-permute-start.23 = (f32[32,1024]{1,0:T(8,128)S(1)}, f32[32,1024]{1,0:T(8,128)S(1)}, u32[]{:S(2)}, u32[]{:S(2)}) collective-permute-start(f32[32,1024]{1,0:T(8,128)S(1)} %add_add_fusion.refs_0_), channel_id=1, source_target_pairs={{0,3},{1,2},{2,1},{3,0},{4,7},{5,6},{6,5},{7,4},{8,11},{9,10},{10,... | collective-permute-start | bytes 393224 | tf_op jit(solution)/shard_map/ppermute | solution.py:75
  80.2 2.4 %collective-permute-start.25 = (f32[32,1024]{1,0:T(8,128)S(1)}, f32[32,1024]{1,0:T(8,128)S(1)}, u32[]{:S(2)}, u32[]{:S(2)}) collective-permute-start(f32[32,1024]{1,0:T(8,128)S(1)} %add_add_fusion.refs_0_), channel_id=1, source_target_pairs={{0,2},{1,3},{2,0},{3,1},{4,6},{5,7},{6,4},{7,5},{8,10},{9,11},{10,... | collective-permute-start | bytes 393224 | tf_op jit(solution)/shard_map/ppermute | solution.py:75
  82.6 3.9 %collective-permute-done.23 = f32[32,1024]{1,0:T(8,128)S(1)} collective-permute-done((f32[32,1024]{1,0:T(8,128)S(1)}, f32[32,1024]{1,0:T(8,128)S(1)}, u32[]{:S(2)}, u32[]{:S(2)}) %collective-permute-start.23) | collective-permute-done | bytes 131104 | tf_op jit(solution)/shard_map/ppermute | solution.py:75
  86.5 3.4 %collective-permute-done.26 = f32[32,1024]{1,0:T(8,128)S(1)} collective-permute-done((f32[32,1024]{1,0:T(8,128)S(1)}, f32[32,1024]{1,0:T(8,128)S(1)}, u32[]{:S(2)}, u32[]{:S(2)}) %collective-permute-start.26) | collective-permute-done | bytes 131104 | tf_op jit(solution)/shard_map/ppermute | solution.py:75
  90.0 1.8 %collective-permute-start.29 = (f32[3,32,1024]{2,1,0:T(8,128)S(1)}, f32[3,32,1024]{2,1,0:T(8,128)S(1)}, u32[]{:S(2)}, u32[]{:S(2)}) collective-permute-start(f32[3,32,1024]{2,1,0:T(8,128)S(1)} %pad_maximum_fusion.refs_1_), channel_id=1, source_target_pairs={{0,8},{4,12},{8,0},{12,4},{16,24},{20,28},{24,16},{28,20},{1,9},{5... | collective-permute-start | bytes 1179656 | tf_op jit(solution)/shard_map/ppermute | solution.py:75
  91.8 9.1 %collective-permute-done.29.refs_3_ = f32[3,32,1024]{2,1,0:T(8,128)S(1)} collective-permute-done((f32[3,32,1024]{2,1,0:T(8,128)S(1)}, f32[3,32,1024]{2,1,0:T(8,128)S(1)}, u32[]{:S(2)}, u32[]{:S(2)}) %collective-permute-start.29) | collective-permute-done | bytes 393248 | tf_op jit(solution)/shard_map/ppermute | solution.py:75
  104.6 3.0 %collective-permute-done.32.refs_9_ = f32[2,1024]{1,0:T(2,128)S(1)} collective-permute-done((f32[2,1024]{1,0:T(2,128)S(1)}, f32[2,1024]{1,0:T(2,128)S(1)}, u32[]{:S(2)}, u32[]{:S(2)}) %collective-permute-start.32) | collective-permute-done | bytes 8224 | tf_op jit(solution)/shard_map/ppermute | solution.py:75
  109.3 3.0 %collective-permute-done.33.refs_9_ = f32[2,1024]{1,0:T(2,128)S(1)} collective-permute-done((f32[2,1024]{1,0:T(2,128)S(1)}, f32[2,1024]{1,0:T(2,128)S(1)}, u32[]{:S(2)}, u32[]{:S(2)}) %collective-permute-start.33) | collective-permute-done | bytes 8224 | tf_op jit(solution)/shard_map/ppermute | solution.py:75
  113.9 3.0 %collective-permute-done.34.refs_5_ = f32[2,1024]{1,0:T(2,128)S(1)} collective-permute-done((f32[2,1024]{1,0:T(2,128)S(1)}, f32[2,1024]{1,0:T(2,128)S(1)}, u32[]{:S(2)}, u32[]{:S(2)}) %collective-permute-start.34) | collective-permute-done | bytes 8224 | tf_op jit(solution)/shard_map/ppermute | solution.py:75
  116.9 2.2 %shard_map.57 = (bf16[2,4,32,512]{3,2,1,0:T(8,128)(2,1)S(1)}, bf16[2,4,32,512]{3,2,1,0:T(8,128)(2,1)S(1)}, bf16[2,4,32,512]{3,2,1,0:T(8,128)(2,1)S(1)}, bf16[2,4...) custom-call(f32[32,1024]{1,0:T(8,128)S(1)} %add_add_fusion.refs_0_, ...), custom_call_target="tpu_custom_call" | custom-call | flops 1073741824 | bytes 5259264 | tf_op jit(solution)/shard_map/pallas_call | solution.py:115
  119.1 1.7 %collective-permute-start.35 = (bf16[2,4,32,512]{3,2,1,0:T(8,128)(2,1)S(1)}, bf16[2,4,32,512]{3,2,1,0:T(8,128)(2,1)S(1)}, u32[]{:S(2)}, u32[]{:S(2)}) collective-permute-start(bf16[2,4,32,512]{3,2,1,0:T(8,128)(2,1)S(1)} %get-tuple-element.63), channel_id=1, source_target_pairs={{0,3},{1,2},{2,1},{3,0},{4,7},{5,6},{6,5},{7,4},{8,11},{9,10},{10,... | collective-permute-start | bytes 786440 | tf_op jit(solution)/shard_map/ppermute | solution.py:75
  120.7 2.7 %collective-permute-start.37 = (bf16[2,4,32,512]{3,2,1,0:T(8,128)(2,1)S(1)}, bf16[2,4,32,512]{3,2,1,0:T(8,128)(2,1)S(1)}, u32[]{:S(2)}, u32[]{:S(2)}) collective-permute-start(bf16[2,4,32,512]{3,2,1,0:T(8,128)(2,1)S(1)} %get-tuple-element.65), channel_id=1, source_target_pairs={{0,1},{1,0},{2,3},{3,2},{4,5},{5,4},{6,7},{7,6},{8,9},{9,8},{10,11... | collective-permute-start | bytes 786440 | tf_op jit(solution)/shard_map/ppermute | solution.py:75
  123.4 6.6 %collective-permute-done.35.refs_0_ = bf16[2,4,32,512]{3,2,1,0:T(8,128)(2,1)S(1)} collective-permute-done((bf16[2,4,32,512]{3,2,1,0:T(8,128)(2,1)S(1)}, bf16[2,4,32,512]{3,2,1,0:T(8,128)(2,1)S(1)}, u32[]{:S(2)}, u32[]{:S(2)}) %collective-permute-start.35) | collective-permute-done | bytes 262176 | tf_op jit(solution)/shard_map/ppermute | solution.py:75
  130.1 9.7 %collective-permute-done.36.refs_1_ = bf16[2,4,32,512]{3,2,1,0:T(8,128)(2,1)S(1)} collective-permute-done((bf16[2,4,32,512]{3,2,1,0:T(8,128)(2,1)S(1)}, bf16[2,4,32,512]{3,2,1,0:T(8,128)(2,1)S(1)}, u32[]{:S(2)}, u32[]{:S(2)}) %collective-permute-start.36) | collective-permute-done | bytes 262176 | tf_op jit(solution)/shard_map/ppermute | solution.py:75
  (69 shorter events, 26.6 us)
Async XLA Ops:
  1.9 12.0 %collective-permute-start = (bf16[128,2048]{1,0:T(8,128)(2,1)S(1)}, bf16[128,2048]{1,0:T(8,128)(2,1)S(1)}, u32[]{:S(2)}, u32[]{:S(2)}) collective-permute-start(bf16[128,2048]{1,0:T(8,128)(2,1)S(1)} %get-tuple-element.37), channel_id=1, source_target_pairs={{0,4},{4,0},{8,12},{12,8},{16,20},{20,16},{24,28},{28,24},{1,5},{5... | collective-permute-start | bytes 1572872 | tf_op jit(solution)/shard_map/ppermute | solution.py:75
  3.2 9.3 %collective-permute-start.2 = (bf16[256,512]{1,0:T(8,128)(2,1)S(1)}, bf16[256,512]{1,0:T(8,128)(2,1)S(1)}, u32[]{:S(2)}, u32[]{:S(2)}) collective-permute-start(bf16[256,512]{1,0:T(8,128)(2,1)S(1)} %get-tuple-element.38.refs_4_.refs_6_), channel_id=1, source_target_pairs={{0,16},{4,20},{8,24},{12,28},{16,0},{20,4},{24,8},{28,12},{1,17},{... | collective-permute-start | bytes 786440 | tf_op jit(solution)/shard_map/ppermute | solution.py:75
  6.2 7.8 %collective-permute-start.1 = (bf16[256,512]{1,0:T(8,128)(2,1)S(1)}, bf16[256,512]{1,0:T(8,128)(2,1)S(1)}, u32[]{:S(2)}, u32[]{:S(2)}) collective-permute-start(bf16[256,512]{1,0:T(8,128)(2,1)S(1)} %get-tuple-element.38.refs_4_.refs_6_), channel_id=1, source_target_pairs={{0,8},{4,12},{8,0},{12,4},{16,24},{20,28},{24,16},{28,20},{1,9},{5... | collective-permute-start | bytes 786440 | tf_op jit(solution)/shard_map/ppermute | solution.py:75
  7.7 13.0 %collective-permute-start.8 = (bf16[256,512]{1,0:T(8,128)(2,1)S(1)}, bf16[256,512]{1,0:T(8,128)(2,1)S(1)}, u32[]{:S(2)}, u32[]{:S(2)}) collective-permute-start(bf16[256,512]{1,0:T(8,128)(2,1)S(1)} %get-tuple-element.49), channel_id=1, source_target_pairs={{0,1},{1,0},{2,3},{3,2},{4,5},{5,4},{6,7},{7,6},{8,9},{9,8},{10,11... | collective-permute-start | bytes 786440 | tf_op jit(solution)/shard_map/ppermute | solution.py:75
  9.3 16.5 %collective-permute-start.3 = (bf16[256,512]{1,0:T(8,128)(2,1)S(1)}, bf16[256,512]{1,0:T(8,128)(2,1)S(1)}, u32[]{:S(2)}, u32[]{:S(2)}) collective-permute-start(bf16[256,512]{1,0:T(8,128)(2,1)S(1)} %get-tuple-element.42), channel_id=1, source_target_pairs={{0,2},{1,3},{2,0},{3,1},{4,6},{5,7},{6,4},{7,5},{8,10},{9,11},{10,... | collective-permute-start | bytes 786440 | tf_op jit(solution)/shard_map/ppermute | solution.py:75
  20.7 9.1 %collective-permute-start.11 = (bf16[256,512]{1,0:T(8,128)(2,1)S(1)}, bf16[256,512]{1,0:T(8,128)(2,1)S(1)}, u32[]{:S(2)}, u32[]{:S(2)}) collective-permute-start(bf16[256,512]{1,0:T(8,128)(2,1)S(1)} %collective-permute-done.8.refs_5_.refs_7_), channel_id=1, source_target_pairs={{0,16},{4,20},{8,24},{12,28},{16,0},{20,4},{24,8},{28,12},{1,17},{... | collective-permute-start | bytes 786440 | tf_op jit(solution)/shard_map/ppermute | solution.py:75
  21.2 11.6 %collective-permute-start.14 = (bf16[256,512]{1,0:T(8,128)(2,1)S(1)}, bf16[256,512]{1,0:T(8,128)(2,1)S(1)}, u32[]{:S(2)}, u32[]{:S(2)}) collective-permute-start(bf16[256,512]{1,0:T(8,128)(2,1)S(1)} %collective-permute-done.1.refs_8_.refs_10_), channel_id=1, source_target_pairs={{0,16},{4,20},{8,24},{12,28},{16,0},{20,4},{24,8},{28,12},{1,17},{... | collective-permute-start | bytes 786440 | tf_op jit(solution)/shard_map/ppermute | solution.py:75
  22.7 12.6 %collective-permute-start.6 = (bf16[256,512]{1,0:T(8,128)(2,1)S(1)}, bf16[256,512]{1,0:T(8,128)(2,1)S(1)}, u32[]{:S(2)}, u32[]{:S(2)}) collective-permute-start(bf16[256,512]{1,0:T(8,128)(2,1)S(1)} %get-tuple-element.47), channel_id=1, source_target_pairs={{0,3},{1,2},{2,1},{3,0},{4,7},{5,6},{6,5},{7,4},{8,11},{9,10},{10,... | collective-permute-start | bytes 786440 | tf_op jit(solution)/shard_map/ppermute | solution.py:75
  25.2 8.1 %collective-permute-start.9 = (bf16[256,512]{1,0:T(8,128)(2,1)S(1)}, bf16[256,512]{1,0:T(8,128)(2,1)S(1)}, u32[]{:S(2)}, u32[]{:S(2)}) collective-permute-start(bf16[256,512]{1,0:T(8,128)(2,1)S(1)} %collective-permute-done.8.refs_5_.refs_7_), channel_id=1, source_target_pairs={{0,8},{4,12},{8,0},{12,4},{16,24},{20,28},{24,16},{28,20},{1,9},{5... | collective-permute-start | bytes 786440 | tf_op jit(solution)/shard_map/ppermute | solution.py:75
  25.7 10.2 %collective-permute-start.4 = (bf16[2,128,512]{2,1,0:T(8,128)(2,1)S(1)}, bf16[2,128,512]{2,1,0:T(8,128)(2,1)S(1)}, u32[]{:S(2)}, u32[]{:S(2)}) collective-permute-start(bf16[2,128,512]{2,1,0:T(8,128)(2,1)S(1)} %get-tuple-element.43), channel_id=1, source_target_pairs={{0,1},{1,0},{2,3},{3,2},{4,5},{5,4},{6,7},{7,6},{8,9},{9,8},{10,11... | collective-permute-start | bytes 786440 | tf_op jit(solution)/shard_map/ppermute | solution.py:75
  32.8 7.3 %collective-permute-start.15 = (bf16[256,512]{1,0:T(8,128)(2,1)S(1)}, bf16[256,512]{1,0:T(8,128)(2,1)S(1)}, u32[]{:S(2)}, u32[]{:S(2)}) collective-permute-start(bf16[256,512]{1,0:T(8,128)(2,1)S(1)} %collective-permute-done.3.refs_6_.refs_8_), channel_id=1, source_target_pairs={{0,16},{4,20},{8,24},{12,28},{16,0},{20,4},{24,8},{28,12},{1,17},{... | collective-permute-start | bytes 786440 | tf_op jit(solution)/shard_map/ppermute | solution.py:75
  33.3 11.9 %collective-permute-start.10 = (bf16[256,512]{1,0:T(8,128)(2,1)S(1)}, bf16[256,512]{1,0:T(8,128)(2,1)S(1)}, u32[]{:S(2)}, u32[]{:S(2)}) collective-permute-start(bf16[256,512]{1,0:T(8,128)(2,1)S(1)} %collective-permute-done.3.refs_6_.refs_8_), channel_id=1, source_target_pairs={{0,8},{4,12},{8,0},{12,4},{16,24},{20,28},{24,16},{28,20},{1,9},{5... | collective-permute-start | bytes 786440 | tf_op jit(solution)/shard_map/ppermute | solution.py:75
  33.9 11.3 %collective-permute-start.12 = (bf16[256,512]{1,0:T(8,128)(2,1)S(1)}, bf16[256,512]{1,0:T(8,128)(2,1)S(1)}, u32[]{:S(2)}, u32[]{:S(2)}) collective-permute-start(bf16[256,512]{1,0:T(8,128)(2,1)S(1)} %collective-permute-done.11.refs_13_.refs_15_), channel_id=1, source_target_pairs={{0,8},{4,12},{8,0},{12,4},{16,24},{20,28},{24,16},{28,20},{1,9},{5... | collective-permute-start | bytes 786440 | tf_op jit(solution)/shard_map/ppermute | solution.py:75
  40.1 9.0 %collective-permute-start.16 = (bf16[256,512]{1,0:T(8,128)(2,1)S(1)}, bf16[256,512]{1,0:T(8,128)(2,1)S(1)}, u32[]{:S(2)}, u32[]{:S(2)}) collective-permute-start(bf16[256,512]{1,0:T(8,128)(2,1)S(1)} %collective-permute-done.6.refs_7_.refs_9_), channel_id=1, source_target_pairs={{0,16},{4,20},{8,24},{12,28},{16,0},{20,4},{24,8},{28,12},{1,17},{... | collective-permute-start | bytes 786440 | tf_op jit(solution)/shard_map/ppermute | solution.py:75
  40.6 16.5 %collective-permute-start.5 = (bf16[2,128,512]{2,1,0:T(8,128)(2,1)S(1)}, bf16[2,128,512]{2,1,0:T(8,128)(2,1)S(1)}, u32[]{:S(2)}, u32[]{:S(2)}) collective-permute-start(bf16[2,128,512]{2,1,0:T(8,128)(2,1)S(1)} %get-tuple-element.45), channel_id=1, source_target_pairs={{0,2},{1,3},{2,0},{3,1},{4,6},{5,7},{6,4},{7,5},{8,10},{9,11},{10,... | collective-permute-start | bytes 786440 | tf_op jit(solution)/shard_map/ppermute | solution.py:75
  41.4 15.8 %collective-permute-start.7 = (bf16[2,128,512]{2,1,0:T(8,128)(2,1)S(1)}, bf16[2,128,512]{2,1,0:T(8,128)(2,1)S(1)}, u32[]{:S(2)}, u32[]{:S(2)}) collective-permute-start(bf16[2,128,512]{2,1,0:T(8,128)(2,1)S(1)} %get-tuple-element.48), channel_id=1, source_target_pairs={{0,3},{1,2},{2,1},{3,0},{4,7},{5,6},{6,5},{7,4},{8,11},{9,10},{10,... | collective-permute-start | bytes 786440 | tf_op jit(solution)/shard_map/ppermute | solution.py:75
  45.2 11.9 %collective-permute-start.13 = (bf16[256,512]{1,0:T(8,128)(2,1)S(1)}, bf16[256,512]{1,0:T(8,128)(2,1)S(1)}, u32[]{:S(2)}, u32[]{:S(2)}) collective-permute-start(bf16[256,512]{1,0:T(8,128)(2,1)S(1)} %collective-permute-done.6.refs_7_.refs_9_), channel_id=1, source_target_pairs={{0,8},{4,12},{8,0},{12,4},{16,24},{20,28},{24,16},{28,20},{1,9},{5... | collective-permute-start | bytes 786440 | tf_op jit(solution)/shard_map/ppermute | solution.py:75
  46.0 11.1 %collective-permute-start.17 = (bf16[256,512]{1,0:T(8,128)(2,1)S(1)}, bf16[256,512]{1,0:T(8,128)(2,1)S(1)}, u32[]{:S(2)}, u32[]{:S(2)}) collective-permute-start(bf16[256,512]{1,0:T(8,128)(2,1)S(1)} %collective-permute-done.10.refs_10_.refs_12_), channel_id=1, source_target_pairs={{0,16},{4,20},{8,24},{12,28},{16,0},{20,4},{24,8},{28,12},{1,17},{... | collective-permute-start | bytes 786440 | tf_op jit(solution)/shard_map/ppermute | solution.py:75
  49.1 8.1 %collective-permute-start.18 = (bf16[256,512]{1,0:T(8,128)(2,1)S(1)}, bf16[256,512]{1,0:T(8,128)(2,1)S(1)}, u32[]{:S(2)}, u32[]{:S(2)}) collective-permute-start(bf16[256,512]{1,0:T(8,128)(2,1)S(1)} %collective-permute-done.16.refs_15_.refs_17_), channel_id=1, source_target_pairs={{0,8},{4,12},{8,0},{12,4},{16,24},{20,28},{24,16},{28,20},{1,9},{5... | collective-permute-start | bytes 786440 | tf_op jit(solution)/shard_map/ppermute | solution.py:75
  61.2 7.4 %collective-permute-start.20 = (f32[32,1024]{1,0:T(8,128)S(1)}, f32[32,1024]{1,0:T(8,128)S(1)}, u32[]{:S(2)}, u32[]{:S(2)}) collective-permute-start(f32[32,1024]{1,0:T(8,128)S(1)} %get-tuple-element.58), channel_id=1, source_target_pairs={{0,3},{1,2},{2,1},{3,0},{4,7},{5,6},{6,5},{7,4},{8,11},{9,10},{10,... | collective-permute-start | bytes 393224 | tf_op jit(solution)/shard_map/ppermute | solution.py:75
  63.3 13.8 %collective-permute-start.21 = (f32[32,1024]{1,0:T(8,128)S(1)}, f32[32,1024]{1,0:T(8,128)S(1)}, u32[]{:S(2)}, u32[]{:S(2)}) collective-permute-start(f32[32,1024]{1,0:T(8,128)S(1)} %get-tuple-element.59), channel_id=1, source_target_pairs={{0,2},{1,3},{2,0},{3,1},{4,6},{5,7},{6,4},{7,5},{8,10},{9,11},{10,... | collective-permute-start | bytes 393224 | tf_op jit(solution)/shard_map/ppermute | solution.py:75
  67.9 9.2 %collective-permute-start.22 = (f32[32,1024]{1,0:T(8,128)S(1)}, f32[32,1024]{1,0:T(8,128)S(1)}, u32[]{:S(2)}, u32[]{:S(2)}) collective-permute-start(f32[32,1024]{1,0:T(8,128)S(1)} %get-tuple-element.60), channel_id=1, source_target_pairs={{0,1},{1,0},{2,3},{3,2},{4,5},{5,4},{6,7},{7,6},{8,9},{9,8},{10,11... | collective-permute-start | bytes 393224 | tf_op jit(solution)/shard_map/ppermute | solution.py:75
  78.2 8.3 %collective-permute-start.23 = (f32[32,1024]{1,0:T(8,128)S(1)}, f32[32,1024]{1,0:T(8,128)S(1)}, u32[]{:S(2)}, u32[]{:S(2)}) collective-permute-start(f32[32,1024]{1,0:T(8,128)S(1)} %add_add_fusion.refs_0_), channel_id=1, source_target_pairs={{0,3},{1,2},{2,1},{3,0},{4,7},{5,6},{6,5},{7,4},{8,11},{9,10},{10,... | collective-permute-start | bytes 393224 | tf_op jit(solution)/shard_map/ppermute | solution.py:75
  80.2 9.8 %collective-permute-start.26 = (f32[32,1024]{1,0:T(8,128)S(1)}, f32[32,1024]{1,0:T(8,128)S(1)}, u32[]{:S(2)}, u32[]{:S(2)}) collective-permute-start(f32[32,1024]{1,0:T(8,128)S(1)} %add_add_fusion.refs_0_), channel_id=1, source_target_pairs={{0,1},{1,0},{2,3},{3,2},{4,5},{5,4},{6,7},{7,6},{8,9},{9,8},{10,11... | collective-permute-start | bytes 393224 | tf_op jit(solution)/shard_map/ppermute | solution.py:75
  80.2 9.8 %collective-permute-start.25 = (f32[32,1024]{1,0:T(8,128)S(1)}, f32[32,1024]{1,0:T(8,128)S(1)}, u32[]{:S(2)}, u32[]{:S(2)}) collective-permute-start(f32[32,1024]{1,0:T(8,128)S(1)} %add_add_fusion.refs_0_), channel_id=1, source_target_pairs={{0,2},{1,3},{2,0},{3,1},{4,6},{5,7},{6,4},{7,5},{8,10},{9,11},{10,... | collective-permute-start | bytes 393224 | tf_op jit(solution)/shard_map/ppermute | solution.py:75
  90.0 10.9 %collective-permute-start.29 = (f32[3,32,1024]{2,1,0:T(8,128)S(1)}, f32[3,32,1024]{2,1,0:T(8,128)S(1)}, u32[]{:S(2)}, u32[]{:S(2)}) collective-permute-start(f32[3,32,1024]{2,1,0:T(8,128)S(1)} %pad_maximum_fusion.refs_1_), channel_id=1, source_target_pairs={{0,8},{4,12},{8,0},{12,4},{16,24},{20,28},{24,16},{28,20},{1,9},{5... | collective-permute-start | bytes 1179656 | tf_op jit(solution)/shard_map/ppermute | solution.py:75
  91.8 11.2 %collective-permute-start.28 = (f32[3,32,1024]{2,1,0:T(8,128)S(1)}, f32[3,32,1024]{2,1,0:T(8,128)S(1)}, u32[]{:S(2)}, u32[]{:S(2)}) collective-permute-start(f32[3,32,1024]{2,1,0:T(8,128)S(1)} %pad_maximum_fusion.refs_1_), channel_id=1, source_target_pairs={{0,4},{4,0},{8,12},{12,8},{16,20},{20,16},{24,28},{28,24},{1,5},{5... | collective-permute-start | bytes 1179656 | tf_op jit(solution)/shard_map/ppermute | solution.py:75
  119.1 11.0 %collective-permute-start.35 = (bf16[2,4,32,512]{3,2,1,0:T(8,128)(2,1)S(1)}, bf16[2,4,32,512]{3,2,1,0:T(8,128)(2,1)S(1)}, u32[]{:S(2)}, u32[]{:S(2)}) collective-permute-start(bf16[2,4,32,512]{3,2,1,0:T(8,128)(2,1)S(1)} %get-tuple-element.63), channel_id=1, source_target_pairs={{0,3},{1,2},{2,1},{3,0},{4,7},{5,6},{6,5},{7,4},{8,11},{9,10},{10,... | collective-permute-start | bytes 786440 | tf_op jit(solution)/shard_map/ppermute | solution.py:75
  120.7 19.1 %collective-permute-start.36 = (bf16[2,4,32,512]{3,2,1,0:T(8,128)(2,1)S(1)}, bf16[2,4,32,512]{3,2,1,0:T(8,128)(2,1)S(1)}, u32[]{:S(2)}, u32[]{:S(2)}) collective-permute-start(bf16[2,4,32,512]{3,2,1,0:T(8,128)(2,1)S(1)} %get-tuple-element.64), channel_id=1, source_target_pairs={{0,2},{1,3},{2,0},{3,1},{4,6},{5,7},{6,4},{7,5},{8,10},{9,11},{10,... | collective-permute-start | bytes 786440 | tf_op jit(solution)/shard_map/ppermute | solution.py:75
  120.7 19.1 %collective-permute-start.37 = (bf16[2,4,32,512]{3,2,1,0:T(8,128)(2,1)S(1)}, bf16[2,4,32,512]{3,2,1,0:T(8,128)(2,1)S(1)}, u32[]{:S(2)}, u32[]{:S(2)}) collective-permute-start(bf16[2,4,32,512]{3,2,1,0:T(8,128)(2,1)S(1)} %get-tuple-element.65), channel_id=1, source_target_pairs={{0,1},{1,0},{2,3},{3,2},{4,5},{5,4},{6,7},{7,6},{8,9},{9,8},{10,11... | collective-permute-start | bytes 786440 | tf_op jit(solution)/shard_map/ppermute | solution.py:75
  123.4 17.5 %collective-permute-start.41 = (bf16[2,4,32,512]{3,2,1,0:T(8,128)(2,1)S(1)}, bf16[2,4,32,512]{3,2,1,0:T(8,128)(2,1)S(1)}, u32[]{:S(2)}, u32[]{:S(2)}) collective-permute-start(bf16[2,4,32,512]{3,2,1,0:T(8,128)(2,1)S(1)} %get-tuple-element.66.refs_3_), channel_id=1, source_target_pairs={{0,4},{4,0},{8,12},{12,8},{16,20},{20,16},{24,28},{28,24},{1,5},{5... | collective-permute-start | bytes 786440 | tf_op jit(solution)/shard_map/ppermute | solution.py:75
  130.1 10.9 %collective-permute-start.38 = (bf16[2,4,32,512]{3,2,1,0:T(8,128)(2,1)S(1)}, bf16[2,4,32,512]{3,2,1,0:T(8,128)(2,1)S(1)}, u32[]{:S(2)}, u32[]{:S(2)}) collective-permute-start(bf16[2,4,32,512]{3,2,1,0:T(8,128)(2,1)S(1)} %collective-permute-done.35.refs_0_), channel_id=1, source_target_pairs={{0,4},{4,0},{8,12},{12,8},{16,20},{20,16},{24,28},{28,24},{1,5},{5... | collective-permute-start | bytes 786440 | tf_op jit(solution)/shard_map/ppermute | solution.py:75
  (12 other events, 30.1 us)

commit v12 on v9

--- a/solution.py
+++ b/solution.py
@@ -389,7 +389,7 @@
     tile_2, tile_1 = swap(tile, "col", 2), swap(tile, "col", 1)
     tile_3 = swap(tile_2, "col", 1)
     x_tile = swap_x(tile)
-    pair = jnp.stack([after(tile_2, x_tile), tile_1])
+    pair = after(jnp.stack([tile_2, tile_1]), x_tile)
     tiles = [[tile, pair, tile_3], [x_tile, swap_x(pair), swap_x(tile_3)]]
     other_tiles = [swap_core(piece) for piece in tiles[0]]
     tiles += [other_tiles, [swap_core(piece) for piece in tiles[1]]]

time: 139 us -> 138 us (level)
  transfers between devices with their start and end apart: 45 -> 45, of which waited for: 27 -> 26; matrix products, arithmetic and copies ran while one was open for 0% -> 0% of each run, Pallas kernels for 0% -> 0%
where the time goes in v12:
time: 138 us
  waiting for transfers between devices  82 us (59%)
  starting transfers between devices  44.8 us (32%)
  Pallas kernels  8.26 us (6%)
  local copies, waits for them, and re-layouts  2.44 us (2%)
    ppermute x45, waiting for transfers between devices, swap(): return lax.ppermute(array, axis, [(i, i ^ step) for i in range(count)])  82 us
    ppermute x45, starting transfers between devices, swap(): return lax.ppermute(array, axis, [(i, i ^ step) for i in range(count)])  44.8 us
    pallas_call x10, Pallas kernels, kernel_call(): pl.pallas_call(kernel, in_specs=[VMEM] * len(operands), out_specs=[VMEM]...  8.26 us
  transfers between devices with their start and end apart: 45, of which 26 were waited for; matrix products, arithmetic and copies ran while one was open for 0% of the time, Pallas kernels for 0%

profile of v12, /device:TPU:0, one launch (start us, length us, event | category | flops | bytes accessed | tf_op | source)
XLA Modules:
  0.0 138.3 jit_solution(8034614780682806493)
XLA Ops:
  3.2 3.0 %collective-permute-start.2 = (bf16[256,512]{1,0:T(8,128)(2,1)S(1)}, bf16[256,512]{1,0:T(8,128)(2,1)S(1)}, u32[]{:S(2)}, u32[]{:S(2)}) collective-permute-start(bf16[256,512]{1,0:T(8,128)(2,1)S(1)} %get-tuple-element.38.refs_4_.refs_8_), channel_id=1, source_target_pairs={{0,16},{4,20},{8,24},{12,28},{16,0},{20,4},{24,8},{28,12},{1,17},{... | collective-permute-start | bytes 786440 | tf_op jit(solution)/shard_map/ppermute | solution.py:75
  6.2 1.5 %collective-permute-start.1 = (bf16[256,512]{1,0:T(8,128)(2,1)S(1)}, bf16[256,512]{1,0:T(8,128)(2,1)S(1)}, u32[]{:S(2)}, u32[]{:S(2)}) collective-permute-start(bf16[256,512]{1,0:T(8,128)(2,1)S(1)} %get-tuple-element.38.refs_4_.refs_8_), channel_id=1, source_target_pairs={{0,8},{4,12},{8,0},{12,4},{16,24},{20,28},{24,16},{28,20},{1,9},{5... | collective-permute-start | bytes 786440 | tf_op jit(solution)/shard_map/ppermute | solution.py:75
  7.7 1.6 %collective-permute-start.8 = (bf16[256,512]{1,0:T(8,128)(2,1)S(1)}, bf16[256,512]{1,0:T(8,128)(2,1)S(1)}, u32[]{:S(2)}, u32[]{:S(2)}) collective-permute-start(bf16[256,512]{1,0:T(8,128)(2,1)S(1)} %get-tuple-element.49), channel_id=1, source_target_pairs={{0,1},{1,0},{2,3},{3,2},{4,5},{5,4},{6,7},{7,6},{8,9},{9,8},{10,11... | collective-permute-start | bytes 786440 | tf_op jit(solution)/shard_map/ppermute | solution.py:75
  9.3 2.6 %collective-permute-start.3 = (bf16[256,512]{1,0:T(8,128)(2,1)S(1)}, bf16[256,512]{1,0:T(8,128)(2,1)S(1)}, u32[]{:S(2)}, u32[]{:S(2)}) collective-permute-start(bf16[256,512]{1,0:T(8,128)(2,1)S(1)} %get-tuple-element.42), channel_id=1, source_target_pairs={{0,2},{1,3},{2,0},{3,1},{4,6},{5,7},{6,4},{7,5},{8,10},{9,11},{10,... | collective-permute-start | bytes 786440 | tf_op jit(solution)/shard_map/ppermute | solution.py:75
  12.5 1.5 %collective-permute-done.1.refs_8_.refs_12_ = bf16[256,512]{1,0:T(8,128)(2,1)S(1)} collective-permute-done((bf16[256,512]{1,0:T(8,128)(2,1)S(1)}, bf16[256,512]{1,0:T(8,128)(2,1)S(1)}, u32[]{:S(2)}, u32[]{:S(2)}) %collective-permute-start.1) | collective-permute-done | bytes 262176 | tf_op jit(solution)/shard_map/ppermute | solution.py:75
  14.0 6.6 %collective-permute-done.8.refs_5_.refs_9_ = bf16[256,512]{1,0:T(8,128)(2,1)S(1)} collective-permute-done((bf16[256,512]{1,0:T(8,128)(2,1)S(1)}, bf16[256,512]{1,0:T(8,128)(2,1)S(1)}, u32[]{:S(2)}, u32[]{:S(2)}) %collective-permute-start.8) | collective-permute-done | bytes 262176 | tf_op jit(solution)/shard_map/ppermute | solution.py:75
  21.2 1.5 %collective-permute-start.14 = (bf16[256,512]{1,0:T(8,128)(2,1)S(1)}, bf16[256,512]{1,0:T(8,128)(2,1)S(1)}, u32[]{:S(2)}, u32[]{:S(2)}) collective-permute-start(bf16[256,512]{1,0:T(8,128)(2,1)S(1)} %collective-permute-done.1.refs_8_.refs_12_), channel_id=1, source_target_pairs={{0,16},{4,20},{8,24},{12,28},{16,0},{20,4},{24,8},{28,12},{1,17},{... | collective-permute-start | bytes 786440 | tf_op jit(solution)/shard_map/ppermute | solution.py:75
  22.7 2.5 %collective-permute-start.6 = (bf16[256,512]{1,0:T(8,128)(2,1)S(1)}, bf16[256,512]{1,0:T(8,128)(2,1)S(1)}, u32[]{:S(2)}, u32[]{:S(2)}) collective-permute-start(bf16[256,512]{1,0:T(8,128)(2,1)S(1)} %get-tuple-element.47), channel_id=1, source_target_pairs={{0,3},{1,2},{2,1},{3,0},{4,7},{5,6},{6,5},{7,4},{8,11},{9,10},{10,... | collective-permute-start | bytes 786440 | tf_op jit(solution)/shard_map/ppermute | solution.py:75
  25.7 4.1 %collective-permute-done.11.refs_13_.refs_17_ = bf16[256,512]{1,0:T(8,128)(2,1)S(1)} collective-permute-done((bf16[256,512]{1,0:T(8,128)(2,1)S(1)}, bf16[256,512]{1,0:T(8,128)(2,1)S(1)}, u32[]{:S(2)}, u32[]{:S(2)}) %collective-permute-start.11) | collective-permute-done | bytes 262176 | tf_op jit(solution)/shard_map/ppermute | solution.py:75
  29.8 3.0 %collective-permute-done.14.refs_16_.refs_20_ = bf16[256,512]{1,0:T(8,128)(2,1)S(1)} collective-permute-done((bf16[256,512]{1,0:T(8,128)(2,1)S(1)}, bf16[256,512]{1,0:T(8,128)(2,1)S(1)}, u32[]{:S(2)}, u32[]{:S(2)}) %collective-permute-start.14) | collective-permute-done | bytes 262176 | tf_op jit(solution)/shard_map/ppermute | solution.py:75
  36.0 4.1 %collective-permute-done.15.refs_14_.refs_18_ = bf16[256,512]{1,0:T(8,128)(2,1)S(1)} collective-permute-done((bf16[256,512]{1,0:T(8,128)(2,1)S(1)}, bf16[256,512]{1,0:T(8,128)(2,1)S(1)}, u32[]{:S(2)}, u32[]{:S(2)}) %collective-permute-start.15) | collective-permute-done | bytes 262176 | tf_op jit(solution)/shard_map/ppermute | solution.py:75
  41.4 1.9 %collective-permute-start.7 = (bf16[2,128,512]{2,1,0:T(8,128)(2,1)S(1)}, bf16[2,128,512]{2,1,0:T(8,128)(2,1)S(1)}, u32[]{:S(2)}, u32[]{:S(2)}) collective-permute-start(bf16[2,128,512]{2,1,0:T(8,128)(2,1)S(1)} %get-tuple-element.48), channel_id=1, source_target_pairs={{0,3},{1,2},{2,1},{3,0},{4,7},{5,6},{6,5},{7,4},{8,11},{9,10},{10,... | collective-permute-start | bytes 786440 | tf_op jit(solution)/shard_map/ppermute | solution.py:75
  43.3 1.9 %collective-permute-done.12.refs_17_.refs_21_ = bf16[256,512]{1,0:T(8,128)(2,1)S(1)} collective-permute-done((bf16[256,512]{1,0:T(8,128)(2,1)S(1)}, bf16[256,512]{1,0:T(8,128)(2,1)S(1)}, u32[]{:S(2)}, u32[]{:S(2)}) %collective-permute-start.12) | collective-permute-done | bytes 262176 | tf_op jit(solution)/shard_map/ppermute | solution.py:75
  47.4 1.7 %collective-permute-done.16.refs_15_.refs_19_ = bf16[256,512]{1,0:T(8,128)(2,1)S(1)} collective-permute-done((bf16[256,512]{1,0:T(8,128)(2,1)S(1)}, bf16[256,512]{1,0:T(8,128)(2,1)S(1)}, u32[]{:S(2)}, u32[]{:S(2)}) %collective-permute-start.16) | collective-permute-done | bytes 262176 | tf_op jit(solution)/shard_map/ppermute | solution.py:75
  49.7 7.4 %collective-permute-done.5.refs_2_ = bf16[2,128,512]{2,1,0:T(8,128)(2,1)S(1)} collective-permute-done((bf16[2,128,512]{2,1,0:T(8,128)(2,1)S(1)}, bf16[2,128,512]{2,1,0:T(8,128)(2,1)S(1)}, u32[]{:S(2)}, u32[]{:S(2)}) %collective-permute-start.5) | collective-permute-done | bytes 262176 | tf_op jit(solution)/shard_map/ppermute | solution.py:75
  57.2 2.0 %shard_map.52 = (f32[128,1024]{1,0:T(8,128)S(1)}, f32[128,1024]{1,0:T(8,128)S(1)}) custom-call(bf16[2,128,512]{2,1,0:T(8,128)(2,1)S(1)} %get-tuple-element.40.refs_0_, bf16[2,128,512]{2,1,0:T(8,128)(2,1)S(1)} %collective-permute-done.4.refs_1_, bf16[2,128,512]{2,1,0:T(8,128)(2,1)S(1)} %collective-permute-done.5.refs_2_, ...), custom_call_target="tpu_custom_call" | custom-call | flops 1073741824 | bytes 5242880 | tf_op jit(solution)/shard_map/pallas_call | solution.py:115
  59.3 1.9 %collective-permute-done.19.other_ref = f32[128,1024]{1,0:T(8,128)S(1)} collective-permute-done((f32[128,1024]{1,0:T(8,128)S(1)}, f32[128,1024]{1,0:T(8,128)S(1)}, u32[]{:S(2)}, u32[]{:S(2)}) %collective-permute-start.19) | collective-permute-done | bytes 524320 | tf_op jit(solution)/shard_map/ppermute | solution.py:75
  61.2 2.0 %collective-permute-start.20 = (f32[32,1024]{1,0:T(8,128)S(1)}, f32[32,1024]{1,0:T(8,128)S(1)}, u32[]{:S(2)}, u32[]{:S(2)}) collective-permute-start(f32[32,1024]{1,0:T(8,128)S(1)} %get-tuple-element.58), channel_id=1, source_target_pairs={{0,3},{1,2},{2,1},{3,0},{4,7},{5,6},{6,5},{7,4},{8,11},{9,10},{10,... | collective-permute-start | bytes 393224 | tf_op jit(solution)/shard_map/ppermute | solution.py:75
  63.3 4.6 %collective-permute-start.21 = (f32[32,1024]{1,0:T(8,128)S(1)}, f32[32,1024]{1,0:T(8,128)S(1)}, u32[]{:S(2)}, u32[]{:S(2)}) collective-permute-start(f32[32,1024]{1,0:T(8,128)S(1)} %get-tuple-element.59), channel_id=1, source_target_pairs={{0,2},{1,3},{2,0},{3,1},{4,6},{5,7},{6,4},{7,5},{8,10},{9,11},{10,... | collective-permute-start | bytes 393224 | tf_op jit(solution)/shard_map/ppermute | solution.py:75
  68.6 8.4 %collective-permute-done.21 = f32[32,1024]{1,0:T(8,128)S(1)} collective-permute-done((f32[32,1024]{1,0:T(8,128)S(1)}, f32[32,1024]{1,0:T(8,128)S(1)}, u32[]{:S(2)}, u32[]{:S(2)}) %collective-permute-start.21) | collective-permute-done | bytes 131104 | tf_op jit(solution)/shard_map/ppermute | solution.py:75
  77.2 3.0 %collective-permute-start.23 = (f32[32,1024]{1,0:T(8,128)S(1)}, f32[32,1024]{1,0:T(8,128)S(1)}, u32[]{:S(2)}, u32[]{:S(2)}) collective-permute-start(f32[32,1024]{1,0:T(8,128)S(1)} %add_add_fusion.refs_0_), channel_id=1, source_target_pairs={{0,2},{1,3},{2,0},{3,1},{4,6},{5,7},{6,4},{7,5},{8,10},{9,11},{10,... | collective-permute-start | bytes 393224 | tf_op jit(solution)/shard_map/ppermute | solution.py:75
  80.7 3.7 %collective-permute-done.24 = f32[32,1024]{1,0:T(8,128)S(1)} collective-permute-done((f32[32,1024]{1,0:T(8,128)S(1)}, f32[32,1024]{1,0:T(8,128)S(1)}, u32[]{:S(2)}, u32[]{:S(2)}) %collective-permute-start.24) | collective-permute-done | bytes 131104 | tf_op jit(solution)/shard_map/ppermute | solution.py:75
  87.3 4.5 %collective-permute-done.26.refs_2_ = f32[32,1024]{1,0:T(8,128)S(1)} collective-permute-done((f32[32,1024]{1,0:T(8,128)S(1)}, f32[32,1024]{1,0:T(8,128)S(1)}, u32[]{:S(2)}, u32[]{:S(2)}) %collective-permute-start.26) | collective-permute-done | bytes 131104 | tf_op jit(solution)/shard_map/ppermute | solution.py:75
  94.1 2.6 %collective-permute-done.31.refs_5_ = f32[32,1024]{1,0:T(8,128)S(1)} collective-permute-done((f32[32,1024]{1,0:T(8,128)S(1)}, f32[32,1024]{1,0:T(8,128)S(1)}, u32[]{:S(2)}, u32[]{:S(2)}) %collective-permute-start.31) | collective-permute-done | bytes 131104 | tf_op jit(solution)/shard_map/ppermute | solution.py:75
  100.2 2.6 %collective-permute-done.35.refs_13_ = f32[2,1024]{1,0:T(2,128)S(1)} collective-permute-done((f32[2,1024]{1,0:T(2,128)S(1)}, f32[2,1024]{1,0:T(2,128)S(1)}, u32[]{:S(2)}, u32[]{:S(2)}) %collective-permute-start.35) | collective-permute-done | bytes 8224 | tf_op jit(solution)/shard_map/ppermute | solution.py:75
  104.8 2.6 %collective-permute-done.36.refs_13_ = f32[2,1024]{1,0:T(2,128)S(1)} collective-permute-done((f32[2,1024]{1,0:T(2,128)S(1)}, f32[2,1024]{1,0:T(2,128)S(1)}, u32[]{:S(2)}, u32[]{:S(2)}) %collective-permute-start.36) | collective-permute-done | bytes 8224 | tf_op jit(solution)/shard_map/ppermute | solution.py:75
  109.4 2.6 %collective-permute-done.37.refs_7_ = f32[2,1024]{1,0:T(2,128)S(1)} collective-permute-done((f32[2,1024]{1,0:T(2,128)S(1)}, f32[2,1024]{1,0:T(2,128)S(1)}, u32[]{:S(2)}, u32[]{:S(2)}) %collective-permute-start.37) | collective-permute-done | bytes 8224 | tf_op jit(solution)/shard_map/ppermute | solution.py:75
  112.0 2.2 %shard_map.57 = (bf16[2,4,32,512]{3,2,1,0:T(8,128)(2,1)S(1)}, bf16[2,4,32,512]{3,2,1,0:T(8,128)(2,1)S(1)}, bf16[2,4,32,512]{3,2,1,0:T(8,128)(2,1)S(1)}, bf16[2,4...) custom-call(f32[32,1024]{1,0:T(8,128)S(1)} %add_add_fusion.refs_0_, ...), custom_call_target="tpu_custom_call" | custom-call | flops 1073741824 | bytes 5259264 | tf_op jit(solution)/shard_map/pallas_call | solution.py:115
  114.1 2.0 %collective-permute-start.38 = (bf16[2,4,32,512]{3,2,1,0:T(8,128)(2,1)S(1)}, bf16[2,4,32,512]{3,2,1,0:T(8,128)(2,1)S(1)}, u32[]{:S(2)}, u32[]{:S(2)}) collective-permute-start(bf16[2,4,32,512]{3,2,1,0:T(8,128)(2,1)S(1)} %get-tuple-element.63), channel_id=1, source_target_pairs={{0,3},{1,2},{2,1},{3,0},{4,7},{5,6},{6,5},{7,4},{8,11},{9,10},{10,... | collective-permute-start | bytes 786440 | tf_op jit(solution)/shard_map/ppermute | solution.py:75
  116.1 2.4 %collective-permute-start.40 = (bf16[2,4,32,512]{3,2,1,0:T(8,128)(2,1)S(1)}, bf16[2,4,32,512]{3,2,1,0:T(8,128)(2,1)S(1)}, u32[]{:S(2)}, u32[]{:S(2)}) collective-permute-start(bf16[2,4,32,512]{3,2,1,0:T(8,128)(2,1)S(1)} %get-tuple-element.65), channel_id=1, source_target_pairs={{0,1},{1,0},{2,3},{3,2},{4,5},{5,4},{6,7},{7,6},{8,9},{9,8},{10,11... | collective-permute-start | bytes 786440 | tf_op jit(solution)/shard_map/ppermute | solution.py:75
  118.5 6.6 %collective-permute-done.38.refs_0_ = bf16[2,4,32,512]{3,2,1,0:T(8,128)(2,1)S(1)} collective-permute-done((bf16[2,4,32,512]{3,2,1,0:T(8,128)(2,1)S(1)}, bf16[2,4,32,512]{3,2,1,0:T(8,128)(2,1)S(1)}, u32[]{:S(2)}, u32[]{:S(2)}) %collective-permute-start.38) | collective-permute-done | bytes 262176 | tf_op jit(solution)/shard_map/ppermute | solution.py:75
  125.2 10.1 %collective-permute-done.39.refs_1_ = bf16[2,4,32,512]{3,2,1,0:T(8,128)(2,1)S(1)} collective-permute-done((bf16[2,4,32,512]{3,2,1,0:T(8,128)(2,1)S(1)}, bf16[2,4,32,512]{3,2,1,0:T(8,128)(2,1)S(1)}, u32[]{:S(2)}, u32[]{:S(2)}) %collective-permute-start.39) | collective-permute-done | bytes 262176 | tf_op jit(solution)/shard_map/ppermute | solution.py:75
  (75 shorter events, 28.9 us)
Async XLA Ops:
  1.9 12.0 %collective-permute-start = (bf16[128,2048]{1,0:T(8,128)(2,1)S(1)}, bf16[128,2048]{1,0:T(8,128)(2,1)S(1)}, u32[]{:S(2)}, u32[]{:S(2)}) collective-permute-start(bf16[128,2048]{1,0:T(8,128)(2,1)S(1)} %get-tuple-element.37), channel_id=1, source_target_pairs={{0,4},{4,0},{8,12},{12,8},{16,20},{20,16},{24,28},{28,24},{1,5},{5... | collective-permute-start | bytes 1572872 | tf_op jit(solution)/shard_map/ppermute | solution.py:75
  3.2 9.3 %collective-permute-start.2 = (bf16[256,512]{1,0:T(8,128)(2,1)S(1)}, bf16[256,512]{1,0:T(8,128)(2,1)S(1)}, u32[]{:S(2)}, u32[]{:S(2)}) collective-permute-start(bf16[256,512]{1,0:T(8,128)(2,1)S(1)} %get-tuple-element.38.refs_4_.refs_8_), channel_id=1, source_target_pairs={{0,16},{4,20},{8,24},{12,28},{16,0},{20,4},{24,8},{28,12},{1,17},{... | collective-permute-start | bytes 786440 | tf_op jit(solution)/shard_map/ppermute | solution.py:75
  6.2 7.8 %collective-permute-start.1 = (bf16[256,512]{1,0:T(8,128)(2,1)S(1)}, bf16[256,512]{1,0:T(8,128)(2,1)S(1)}, u32[]{:S(2)}, u32[]{:S(2)}) collective-permute-start(bf16[256,512]{1,0:T(8,128)(2,1)S(1)} %get-tuple-element.38.refs_4_.refs_8_), channel_id=1, source_target_pairs={{0,8},{4,12},{8,0},{12,4},{16,24},{20,28},{24,16},{28,20},{1,9},{5... | collective-permute-start | bytes 786440 | tf_op jit(solution)/shard_map/ppermute | solution.py:75
  7.7 13.0 %collective-permute-start.8 = (bf16[256,512]{1,0:T(8,128)(2,1)S(1)}, bf16[256,512]{1,0:T(8,128)(2,1)S(1)}, u32[]{:S(2)}, u32[]{:S(2)}) collective-permute-start(bf16[256,512]{1,0:T(8,128)(2,1)S(1)} %get-tuple-element.49), channel_id=1, source_target_pairs={{0,1},{1,0},{2,3},{3,2},{4,5},{5,4},{6,7},{7,6},{8,9},{9,8},{10,11... | collective-permute-start | bytes 786440 | tf_op jit(solution)/shard_map/ppermute | solution.py:75
  9.3 16.5 %collective-permute-start.3 = (bf16[256,512]{1,0:T(8,128)(2,1)S(1)}, bf16[256,512]{1,0:T(8,128)(2,1)S(1)}, u32[]{:S(2)}, u32[]{:S(2)}) collective-permute-start(bf16[256,512]{1,0:T(8,128)(2,1)S(1)} %get-tuple-element.42), channel_id=1, source_target_pairs={{0,2},{1,3},{2,0},{3,1},{4,6},{5,7},{6,4},{7,5},{8,10},{9,11},{10,... | collective-permute-start | bytes 786440 | tf_op jit(solution)/shard_map/ppermute | solution.py:75
  20.7 9.1 %collective-permute-start.11 = (bf16[256,512]{1,0:T(8,128)(2,1)S(1)}, bf16[256,512]{1,0:T(8,128)(2,1)S(1)}, u32[]{:S(2)}, u32[]{:S(2)}) collective-permute-start(bf16[256,512]{1,0:T(8,128)(2,1)S(1)} %collective-permute-done.8.refs_5_.refs_9_), channel_id=1, source_target_pairs={{0,16},{4,20},{8,24},{12,28},{16,0},{20,4},{24,8},{28,12},{1,17},{... | collective-permute-start | bytes 786440 | tf_op jit(solution)/shard_map/ppermute | solution.py:75
  21.2 11.6 %collective-permute-start.14 = (bf16[256,512]{1,0:T(8,128)(2,1)S(1)}, bf16[256,512]{1,0:T(8,128)(2,1)S(1)}, u32[]{:S(2)}, u32[]{:S(2)}) collective-permute-start(bf16[256,512]{1,0:T(8,128)(2,1)S(1)} %collective-permute-done.1.refs_8_.refs_12_), channel_id=1, source_target_pairs={{0,16},{4,20},{8,24},{12,28},{16,0},{20,4},{24,8},{28,12},{1,17},{... | collective-permute-start | bytes 786440 | tf_op jit(solution)/shard_map/ppermute | solution.py:75
  22.7 12.6 %collective-permute-start.6 = (bf16[256,512]{1,0:T(8,128)(2,1)S(1)}, bf16[256,512]{1,0:T(8,128)(2,1)S(1)}, u32[]{:S(2)}, u32[]{:S(2)}) collective-permute-start(bf16[256,512]{1,0:T(8,128)(2,1)S(1)} %get-tuple-element.47), channel_id=1, source_target_pairs={{0,3},{1,2},{2,1},{3,0},{4,7},{5,6},{6,5},{7,4},{8,11},{9,10},{10,... | collective-permute-start | bytes 786440 | tf_op jit(solution)/shard_map/ppermute | solution.py:75
  25.2 8.1 %collective-permute-start.9 = (bf16[256,512]{1,0:T(8,128)(2,1)S(1)}, bf16[256,512]{1,0:T(8,128)(2,1)S(1)}, u32[]{:S(2)}, u32[]{:S(2)}) collective-permute-start(bf16[256,512]{1,0:T(8,128)(2,1)S(1)} %collective-permute-done.8.refs_5_.refs_9_), channel_id=1, source_target_pairs={{0,8},{4,12},{8,0},{12,4},{16,24},{20,28},{24,16},{28,20},{1,9},{5... | collective-permute-start | bytes 786440 | tf_op jit(solution)/shard_map/ppermute | solution.py:75
  25.7 10.2 %collective-permute-start.4 = (bf16[2,128,512]{2,1,0:T(8,128)(2,1)S(1)}, bf16[2,128,512]{2,1,0:T(8,128)(2,1)S(1)}, u32[]{:S(2)}, u32[]{:S(2)}) collective-permute-start(bf16[2,128,512]{2,1,0:T(8,128)(2,1)S(1)} %get-tuple-element.43), channel_id=1, source_target_pairs={{0,1},{1,0},{2,3},{3,2},{4,5},{5,4},{6,7},{7,6},{8,9},{9,8},{10,11... | collective-permute-start | bytes 786440 | tf_op jit(solution)/shard_map/ppermute | solution.py:75
  32.8 7.3 %collective-permute-start.15 = (bf16[256,512]{1,0:T(8,128)(2,1)S(1)}, bf16[256,512]{1,0:T(8,128)(2,1)S(1)}, u32[]{:S(2)}, u32[]{:S(2)}) collective-permute-start(bf16[256,512]{1,0:T(8,128)(2,1)S(1)} %collective-permute-done.3.refs_6_.refs_10_), channel_id=1, source_target_pairs={{0,16},{4,20},{8,24},{12,28},{16,0},{20,4},{24,8},{28,12},{1,17},{... | collective-permute-start | bytes 786440 | tf_op jit(solution)/shard_map/ppermute | solution.py:75
  33.3 11.9 %collective-permute-start.10 = (bf16[256,512]{1,0:T(8,128)(2,1)S(1)}, bf16[256,512]{1,0:T(8,128)(2,1)S(1)}, u32[]{:S(2)}, u32[]{:S(2)}) collective-permute-start(bf16[256,512]{1,0:T(8,128)(2,1)S(1)} %collective-permute-done.3.refs_6_.refs_10_), channel_id=1, source_target_pairs={{0,8},{4,12},{8,0},{12,4},{16,24},{20,28},{24,16},{28,20},{1,9},{5... | collective-permute-start | bytes 786440 | tf_op jit(solution)/shard_map/ppermute | solution.py:75
  33.9 11.3 %collective-permute-start.12 = (bf16[256,512]{1,0:T(8,128)(2,1)S(1)}, bf16[256,512]{1,0:T(8,128)(2,1)S(1)}, u32[]{:S(2)}, u32[]{:S(2)}) collective-permute-start(bf16[256,512]{1,0:T(8,128)(2,1)S(1)} %collective-permute-done.11.refs_13_.refs_17_), channel_id=1, source_target_pairs={{0,8},{4,12},{8,0},{12,4},{16,24},{20,28},{24,16},{28,20},{1,9},{5... | collective-permute-start | bytes 786440 | tf_op jit(solution)/shard_map/ppermute | solution.py:75
  40.1 9.0 %collective-permute-start.16 = (bf16[256,512]{1,0:T(8,128)(2,1)S(1)}, bf16[256,512]{1,0:T(8,128)(2,1)S(1)}, u32[]{:S(2)}, u32[]{:S(2)}) collective-permute-start(bf16[256,512]{1,0:T(8,128)(2,1)S(1)} %collective-permute-done.6.refs_7_.refs_11_), channel_id=1, source_target_pairs={{0,16},{4,20},{8,24},{12,28},{16,0},{20,4},{24,8},{28,12},{1,17},{... | collective-permute-start | bytes 786440 | tf_op jit(solution)/shard_map/ppermute | solution.py:75
  40.6 16.5 %collective-permute-start.5 = (bf16[2,128,512]{2,1,0:T(8,128)(2,1)S(1)}, bf16[2,128,512]{2,1,0:T(8,128)(2,1)S(1)}, u32[]{:S(2)}, u32[]{:S(2)}) collective-permute-start(bf16[2,128,512]{2,1,0:T(8,128)(2,1)S(1)} %get-tuple-element.45), channel_id=1, source_target_pairs={{0,2},{1,3},{2,0},{3,1},{4,6},{5,7},{6,4},{7,5},{8,10},{9,11},{10,... | collective-permute-start | bytes 786440 | tf_op jit(solution)/shard_map/ppermute | solution.py:75
  41.4 15.8 %collective-permute-start.7 = (bf16[2,128,512]{2,1,0:T(8,128)(2,1)S(1)}, bf16[2,128,512]{2,1,0:T(8,128)(2,1)S(1)}, u32[]{:S(2)}, u32[]{:S(2)}) collective-permute-start(bf16[2,128,512]{2,1,0:T(8,128)(2,1)S(1)} %get-tuple-element.48), channel_id=1, source_target_pairs={{0,3},{1,2},{2,1},{3,0},{4,7},{5,6},{6,5},{7,4},{8,11},{9,10},{10,... | collective-permute-start | bytes 786440 | tf_op jit(solution)/shard_map/ppermute | solution.py:75
  45.2 11.9 %collective-permute-start.13 = (bf16[256,512]{1,0:T(8,128)(2,1)S(1)}, bf16[256,512]{1,0:T(8,128)(2,1)S(1)}, u32[]{:S(2)}, u32[]{:S(2)}) collective-permute-start(bf16[256,512]{1,0:T(8,128)(2,1)S(1)} %collective-permute-done.6.refs_7_.refs_11_), channel_id=1, source_target_pairs={{0,8},{4,12},{8,0},{12,4},{16,24},{20,28},{24,16},{28,20},{1,9},{5... | collective-permute-start | bytes 786440 | tf_op jit(solution)/shard_map/ppermute | solution.py:75
  46.0 11.1 %collective-permute-start.17 = (bf16[256,512]{1,0:T(8,128)(2,1)S(1)}, bf16[256,512]{1,0:T(8,128)(2,1)S(1)}, u32[]{:S(2)}, u32[]{:S(2)}) collective-permute-start(bf16[256,512]{1,0:T(8,128)(2,1)S(1)} %collective-permute-done.10.refs_10_.refs_14_), channel_id=1, source_target_pairs={{0,16},{4,20},{8,24},{12,28},{16,0},{20,4},{24,8},{28,12},{1,17},{... | collective-permute-start | bytes 786440 | tf_op jit(solution)/shard_map/ppermute | solution.py:75
  49.1 8.1 %collective-permute-start.18 = (bf16[256,512]{1,0:T(8,128)(2,1)S(1)}, bf16[256,512]{1,0:T(8,128)(2,1)S(1)}, u32[]{:S(2)}, u32[]{:S(2)}) collective-permute-start(bf16[256,512]{1,0:T(8,128)(2,1)S(1)} %collective-permute-done.16.refs_15_.refs_19_), channel_id=1, source_target_pairs={{0,8},{4,12},{8,0},{12,4},{16,24},{20,28},{24,16},{28,20},{1,9},{5... | collective-permute-start | bytes 786440 | tf_op jit(solution)/shard_map/ppermute | solution.py:75
  61.2 7.4 %collective-permute-start.20 = (f32[32,1024]{1,0:T(8,128)S(1)}, f32[32,1024]{1,0:T(8,128)S(1)}, u32[]{:S(2)}, u32[]{:S(2)}) collective-permute-start(f32[32,1024]{1,0:T(8,128)S(1)} %get-tuple-element.58), channel_id=1, source_target_pairs={{0,3},{1,2},{2,1},{3,0},{4,7},{5,6},{6,5},{7,4},{8,11},{9,10},{10,... | collective-permute-start | bytes 393224 | tf_op jit(solution)/shard_map/ppermute | solution.py:75
  63.3 13.8 %collective-permute-start.21 = (f32[32,1024]{1,0:T(8,128)S(1)}, f32[32,1024]{1,0:T(8,128)S(1)}, u32[]{:S(2)}, u32[]{:S(2)}) collective-permute-start(f32[32,1024]{1,0:T(8,128)S(1)} %get-tuple-element.59), channel_id=1, source_target_pairs={{0,2},{1,3},{2,0},{3,1},{4,6},{5,7},{6,4},{7,5},{8,10},{9,11},{10,... | collective-permute-start | bytes 393224 | tf_op jit(solution)/shard_map/ppermute | solution.py:75
  67.9 9.2 %collective-permute-start.22 = (f32[32,1024]{1,0:T(8,128)S(1)}, f32[32,1024]{1,0:T(8,128)S(1)}, u32[]{:S(2)}, u32[]{:S(2)}) collective-permute-start(f32[32,1024]{1,0:T(8,128)S(1)} %get-tuple-element.60), channel_id=1, source_target_pairs={{0,1},{1,0},{2,3},{3,2},{4,5},{5,4},{6,7},{7,6},{8,9},{9,8},{10,11... | collective-permute-start | bytes 393224 | tf_op jit(solution)/shard_map/ppermute | solution.py:75
  77.1 7.3 %collective-permute-start.24 = (f32[32,1024]{1,0:T(8,128)S(1)}, f32[32,1024]{1,0:T(8,128)S(1)}, u32[]{:S(2)}, u32[]{:S(2)}) collective-permute-start(f32[32,1024]{1,0:T(8,128)S(1)} %add_add_fusion.refs_0_), channel_id=1, source_target_pairs={{0,1},{1,0},{2,3},{3,2},{4,5},{5,4},{6,7},{7,6},{8,9},{9,8},{10,11... | collective-permute-start | bytes 393224 | tf_op jit(solution)/shard_map/ppermute | solution.py:75
  77.2 8.6 %collective-permute-start.23 = (f32[32,1024]{1,0:T(8,128)S(1)}, f32[32,1024]{1,0:T(8,128)S(1)}, u32[]{:S(2)}, u32[]{:S(2)}) collective-permute-start(f32[32,1024]{1,0:T(8,128)S(1)} %add_add_fusion.refs_0_), channel_id=1, source_target_pairs={{0,2},{1,3},{2,0},{3,1},{4,6},{5,7},{6,4},{7,5},{8,10},{9,11},{10,... | collective-permute-start | bytes 393224 | tf_op jit(solution)/shard_map/ppermute | solution.py:75
  85.8 7.8 %collective-permute-start.30 = (f32[2,32,1024]{2,1,0:T(8,128)S(1)}, f32[2,32,1024]{2,1,0:T(8,128)S(1)}, u32[]{:S(2)}, u32[]{:S(2)}) collective-permute-start(f32[2,32,1024]{2,1,0:T(8,128)S(1)} %pad_maximum_fusion.refs_1_), channel_id=1, source_target_pairs={{0,8},{4,12},{8,0},{12,4},{16,24},{20,28},{24,16},{28,20},{1,9},{5... | collective-permute-start | bytes 786440 | tf_op jit(solution)/shard_map/ppermute | solution.py:75
  86.8 7.3 %collective-permute-start.27 = (f32[32,1024]{1,0:T(8,128)S(1)}, f32[32,1024]{1,0:T(8,128)S(1)}, u32[]{:S(2)}, u32[]{:S(2)}) collective-permute-start(f32[32,1024]{1,0:T(8,128)S(1)} %add_add_fusion.refs_0_), channel_id=1, source_target_pairs={{0,4},{4,0},{8,12},{12,8},{16,20},{20,16},{24,28},{28,24},{1,5},{5... | collective-permute-start | bytes 393224 | tf_op jit(solution)/shard_map/ppermute | solution.py:75
  86.8 9.9 %collective-permute-start.28 = (f32[2,32,1024]{2,1,0:T(8,128)S(1)}, f32[2,32,1024]{2,1,0:T(8,128)S(1)}, u32[]{:S(2)}, u32[]{:S(2)}) collective-permute-start(f32[2,32,1024]{2,1,0:T(8,128)S(1)} %pad_maximum_fusion.refs_1_), channel_id=1, source_target_pairs={{0,4},{4,0},{8,12},{12,8},{16,20},{20,16},{24,28},{28,24},{1,5},{5... | collective-permute-start | bytes 786440 | tf_op jit(solution)/shard_map/ppermute | solution.py:75
  114.1 11.0 %collective-permute-start.38 = (bf16[2,4,32,512]{3,2,1,0:T(8,128)(2,1)S(1)}, bf16[2,4,32,512]{3,2,1,0:T(8,128)(2,1)S(1)}, u32[]{:S(2)}, u32[]{:S(2)}) collective-permute-start(bf16[2,4,32,512]{3,2,1,0:T(8,128)(2,1)S(1)} %get-tuple-element.63), channel_id=1, source_target_pairs={{0,3},{1,2},{2,1},{3,0},{4,7},{5,6},{6,5},{7,4},{8,11},{9,10},{10,... | collective-permute-start | bytes 786440 | tf_op jit(solution)/shard_map/ppermute | solution.py:75
  116.1 19.2 %collective-permute-start.39 = (bf16[2,4,32,512]{3,2,1,0:T(8,128)(2,1)S(1)}, bf16[2,4,32,512]{3,2,1,0:T(8,128)(2,1)S(1)}, u32[]{:S(2)}, u32[]{:S(2)}) collective-permute-start(bf16[2,4,32,512]{3,2,1,0:T(8,128)(2,1)S(1)} %get-tuple-element.64), channel_id=1, source_target_pairs={{0,2},{1,3},{2,0},{3,1},{4,6},{5,7},{6,4},{7,5},{8,10},{9,11},{10,... | collective-permute-start | bytes 786440 | tf_op jit(solution)/shard_map/ppermute | solution.py:75
  116.1 19.2 %collective-permute-start.40 = (bf16[2,4,32,512]{3,2,1,0:T(8,128)(2,1)S(1)}, bf16[2,4,32,512]{3,2,1,0:T(8,128)(2,1)S(1)}, u32[]{:S(2)}, u32[]{:S(2)}) collective-permute-start(bf16[2,4,32,512]{3,2,1,0:T(8,128)(2,1)S(1)} %get-tuple-element.65), channel_id=1, source_target_pairs={{0,1},{1,0},{2,3},{3,2},{4,5},{5,4},{6,7},{7,6},{8,9},{9,8},{10,11... | collective-permute-start | bytes 786440 | tf_op jit(solution)/shard_map/ppermute | solution.py:75
  118.5 17.9 %collective-permute-start.44 = (bf16[2,4,32,512]{3,2,1,0:T(8,128)(2,1)S(1)}, bf16[2,4,32,512]{3,2,1,0:T(8,128)(2,1)S(1)}, u32[]{:S(2)}, u32[]{:S(2)}) collective-permute-start(bf16[2,4,32,512]{3,2,1,0:T(8,128)(2,1)S(1)} %get-tuple-element.66.refs_3_), channel_id=1, source_target_pairs={{0,4},{4,0},{8,12},{12,8},{16,20},{20,16},{24,28},{28,24},{1,5},{5... | collective-permute-start | bytes 786440 | tf_op jit(solution)/shard_map/ppermute | solution.py:75
  125.2 11.2 %collective-permute-start.41 = (bf16[2,4,32,512]{3,2,1,0:T(8,128)(2,1)S(1)}, bf16[2,4,32,512]{3,2,1,0:T(8,128)(2,1)S(1)}, u32[]{:S(2)}, u32[]{:S(2)}) collective-permute-start(bf16[2,4,32,512]{3,2,1,0:T(8,128)(2,1)S(1)} %collective-permute-done.38.refs_0_), channel_id=1, source_target_pairs={{0,4},{4,0},{8,12},{12,8},{16,20},{20,16},{24,28},{28,24},{1,5},{5... | collective-permute-start | bytes 786440 | tf_op jit(solution)/shard_map/ppermute | solution.py:75
  (15 other events, 46.1 us)

commit v13 on v12

--- a/solution.py
+++ b/solution.py
@@ -170,7 +170,7 @@
     _, own, part = noise_refs[0].shape
     height = latent_refs[0].shape[0]
     for d in range(n_col):
-        noise_all[(row // 2) ^ col ^ d] = noise_refs[d][...].reshape(2 * own, part)
+        noise_all[(row // 2) ^ col ^ d] = noise_refs[-d % n_col][...].reshape(2 * own, part)
     noise_norm = jnp.zeros((2 * own, 1), jnp.float32)
     for k in range(n_chip):
         values = noise_all[k].astype(jnp.float32)
@@ -200,7 +200,7 @@
         [((own, width), jnp.float32)] * 2,
         [pltpu.VMEM((n_chip, 2 * own, part), jnp.bfloat16)],
         24,
-        *noise_pieces,
+        *[noise_pieces[-i] for i in range(n_col)],
         *[piece for group in latents for piece in group],
         flops=4 * own * width * n_chip * part,
     )
@@ -371,7 +371,7 @@
     noise_1 = swap(after(dealt_noise[0], data_2), "col", 1)
     across_1 = swap_x(y_1)
     x_2, y_2 = swap_x(after(data_2, x_1)), swap_y(after(data_2, y_1, across_0))
-    noise_2 = swap(after(dealt_noise[1], data_2), "col", 2)
+    noise_2 = swap(after(dealt_noise[1], data_3, noise_1), "col", 2)
     across_2 = swap_y(x_2)
     x_3, y_3 = swap_x(after(data_3, across_1, x_2, noise_1)), swap_y(after(data_3, y_2, noise_1))
     noise_3 = swap(after(dealt_noise[2], data_3, noise_1), "col", 3)

time: 138 us -> 140 us (1.014)
  waiting for transfers between devices: 82 us -> 84.4 us
    ppermute x45, waiting for transfers between devices: 82 us -> 84.4 us  [swap(): return lax.ppermute(array, axis, [(i, i ^ step) for i in range(count)])]
where the time goes in v13:
time: 140 us
  waiting for transfers between devices  84.4 us (60%)
  starting transfers between devices  43.9 us (31%)
  Pallas kernels  8.26 us (6%)
  local copies, waits for them, and re-layouts  2.44 us (2%)
    ppermute x45, waiting for transfers between devices, swap(): return lax.ppermute(array, axis, [(i, i ^ step) for i in range(count)])  84.4 us
    ppermute x45, starting transfers between devices, swap(): return lax.ppermute(array, axis, [(i, i ^ step) for i in range(count)])  43.9 us
    pallas_call x10, Pallas kernels, kernel_call(): pl.pallas_call(kernel, in_specs=[VMEM] * len(operands), out_specs=[VMEM]...  8.26 us
  transfers between devices with their start and end apart: 45, of which 26 were waited for; matrix products, arithmetic and copies ran while one was open for 0% of the time, Pallas kernels for 0%

profile of v13, /device:TPU:0, one launch (start us, length us, event | category | flops | bytes accessed | tf_op | source)
XLA Modules:
  0.0 139.8 jit_solution(6128906835273996532)
XLA Ops:
  3.2 3.0 %collective-permute-start.2 = (bf16[256,512]{1,0:T(8,128)(2,1)S(1)}, bf16[256,512]{1,0:T(8,128)(2,1)S(1)}, u32[]{:S(2)}, u32[]{:S(2)}) collective-permute-start(bf16[256,512]{1,0:T(8,128)(2,1)S(1)} %get-tuple-element.38.refs_4_.refs_8_), channel_id=1, source_target_pairs={{0,16},{4,20},{8,24},{12,28},{16,0},{20,4},{24,8},{28,12},{1,17},{... | collective-permute-start | bytes 786440 | tf_op jit(solution)/shard_map/ppermute | solution.py:75
  9.3 2.6 %collective-permute-start.4 = (bf16[256,512]{1,0:T(8,128)(2,1)S(1)}, bf16[256,512]{1,0:T(8,128)(2,1)S(1)}, u32[]{:S(2)}, u32[]{:S(2)}) collective-permute-start(bf16[256,512]{1,0:T(8,128)(2,1)S(1)} %get-tuple-element.44), channel_id=1, source_target_pairs={{0,2},{1,3},{2,0},{3,1},{4,6},{5,7},{6,4},{7,5},{8,10},{9,11},{10,... | collective-permute-start | bytes 786440 | tf_op jit(solution)/shard_map/ppermute | solution.py:75
  14.0 6.6 %collective-permute-done.8.refs_5_.refs_9_ = bf16[256,512]{1,0:T(8,128)(2,1)S(1)} collective-permute-done((bf16[256,512]{1,0:T(8,128)(2,1)S(1)}, bf16[256,512]{1,0:T(8,128)(2,1)S(1)}, u32[]{:S(2)}, u32[]{:S(2)}) %collective-permute-start.8) | collective-permute-done | bytes 262176 | tf_op jit(solution)/shard_map/ppermute | solution.py:75
  22.7 2.5 %collective-permute-start.3 = (bf16[256,512]{1,0:T(8,128)(2,1)S(1)}, bf16[256,512]{1,0:T(8,128)(2,1)S(1)}, u32[]{:S(2)}, u32[]{:S(2)}) collective-permute-start(bf16[256,512]{1,0:T(8,128)(2,1)S(1)} %get-tuple-element.42), channel_id=1, source_target_pairs={{0,3},{1,2},{2,1},{3,0},{4,7},{5,6},{6,5},{7,4},{8,11},{9,10},{10,... | collective-permute-start | bytes 786440 | tf_op jit(solution)/shard_map/ppermute | solution.py:75
  25.7 4.1 %collective-permute-done.11.refs_13_.refs_17_ = bf16[256,512]{1,0:T(8,128)(2,1)S(1)} collective-permute-done((bf16[256,512]{1,0:T(8,128)(2,1)S(1)}, bf16[256,512]{1,0:T(8,128)(2,1)S(1)}, u32[]{:S(2)}, u32[]{:S(2)}) %collective-permute-start.11) | collective-permute-done | bytes 262176 | tf_op jit(solution)/shard_map/ppermute | solution.py:75
  29.8 3.0 %collective-permute-done.14.refs_16_.refs_20_ = bf16[256,512]{1,0:T(8,128)(2,1)S(1)} collective-permute-done((bf16[256,512]{1,0:T(8,128)(2,1)S(1)}, bf16[256,512]{1,0:T(8,128)(2,1)S(1)}, u32[]{:S(2)}, u32[]{:S(2)}) %collective-permute-start.14) | collective-permute-done | bytes 262176 | tf_op jit(solution)/shard_map/ppermute | solution.py:75
  36.0 4.1 %collective-permute-done.15.refs_14_.refs_18_ = bf16[256,512]{1,0:T(8,128)(2,1)S(1)} collective-permute-done((bf16[256,512]{1,0:T(8,128)(2,1)S(1)}, bf16[256,512]{1,0:T(8,128)(2,1)S(1)}, u32[]{:S(2)}, u32[]{:S(2)}) %collective-permute-start.15) | collective-permute-done | bytes 262176 | tf_op jit(solution)/shard_map/ppermute | solution.py:75
  40.6 2.7 %collective-permute-start.6 = (bf16[2,128,512]{2,1,0:T(8,128)(2,1)S(1)}, bf16[2,128,512]{2,1,0:T(8,128)(2,1)S(1)}, u32[]{:S(2)}, u32[]{:S(2)}) collective-permute-start(bf16[2,128,512]{2,1,0:T(8,128)(2,1)S(1)} %get-tuple-element.46), channel_id=1, source_target_pairs={{0,3},{1,2},{2,1},{3,0},{4,7},{5,6},{6,5},{7,4},{8,11},{9,10},{10,... | collective-permute-start | bytes 786440 | tf_op jit(solution)/shard_map/ppermute | solution.py:75
  43.3 1.9 %collective-permute-done.12.refs_17_.refs_21_ = bf16[256,512]{1,0:T(8,128)(2,1)S(1)} collective-permute-done((bf16[256,512]{1,0:T(8,128)(2,1)S(1)}, bf16[256,512]{1,0:T(8,128)(2,1)S(1)}, u32[]{:S(2)}, u32[]{:S(2)}) %collective-permute-start.12) | collective-permute-done | bytes 262176 | tf_op jit(solution)/shard_map/ppermute | solution.py:75
  47.4 1.7 %collective-permute-done.16.refs_15_.refs_19_ = bf16[256,512]{1,0:T(8,128)(2,1)S(1)} collective-permute-done((bf16[256,512]{1,0:T(8,128)(2,1)S(1)}, bf16[256,512]{1,0:T(8,128)(2,1)S(1)}, u32[]{:S(2)}, u32[]{:S(2)}) %collective-permute-start.16) | collective-permute-done | bytes 262176 | tf_op jit(solution)/shard_map/ppermute | solution.py:75
  49.7 10.9 %collective-permute-done.7.refs_2_ = bf16[2,128,512]{2,1,0:T(8,128)(2,1)S(1)} collective-permute-done((bf16[2,128,512]{2,1,0:T(8,128)(2,1)S(1)}, bf16[2,128,512]{2,1,0:T(8,128)(2,1)S(1)}, u32[]{:S(2)}, u32[]{:S(2)}) %collective-permute-start.7) | collective-permute-done | bytes 262176 | tf_op jit(solution)/shard_map/ppermute | solution.py:75
  60.7 2.0 %shard_map.52 = (f32[128,1024]{1,0:T(8,128)S(1)}, f32[128,1024]{1,0:T(8,128)S(1)}) custom-call(bf16[2,128,512]{2,1,0:T(8,128)(2,1)S(1)} %get-tuple-element.40.refs_0_, bf16[2,128,512]{2,1,0:T(8,128)(2,1)S(1)} %collective-permute-done.6.refs_1_, bf16[2,128,512]{2,1,0:T(8,128)(2,1)S(1)} %collective-permute-done.7.refs_2_, ...), custom_call_target="tpu_custom_call" | custom-call | flops 1073741824 | bytes 5242880 | tf_op jit(solution)/shard_map/pallas_call | solution.py:115
  62.8 1.9 %collective-permute-done.19.other_ref = f32[128,1024]{1,0:T(8,128)S(1)} collective-permute-done((f32[128,1024]{1,0:T(8,128)S(1)}, f32[128,1024]{1,0:T(8,128)S(1)}, u32[]{:S(2)}, u32[]{:S(2)}) %collective-permute-start.19) | collective-permute-done | bytes 524320 | tf_op jit(solution)/shard_map/ppermute | solution.py:75
  64.8 2.7 %collective-permute-start.20 = (f32[32,1024]{1,0:T(8,128)S(1)}, f32[32,1024]{1,0:T(8,128)S(1)}, u32[]{:S(2)}, u32[]{:S(2)}) collective-permute-start(f32[32,1024]{1,0:T(8,128)S(1)} %get-tuple-element.58), channel_id=1, source_target_pairs={{0,3},{1,2},{2,1},{3,0},{4,7},{5,6},{6,5},{7,4},{8,11},{9,10},{10,... | collective-permute-start | bytes 393224 | tf_op jit(solution)/shard_map/ppermute | solution.py:75
  67.5 1.7 %collective-permute-start.22 = (f32[32,1024]{1,0:T(8,128)S(1)}, f32[32,1024]{1,0:T(8,128)S(1)}, u32[]{:S(2)}, u32[]{:S(2)}) collective-permute-start(f32[32,1024]{1,0:T(8,128)S(1)} %get-tuple-element.60), channel_id=1, source_target_pairs={{0,1},{1,0},{2,3},{3,2},{4,5},{5,4},{6,7},{7,6},{8,9},{9,8},{10,11... | collective-permute-start | bytes 393224 | tf_op jit(solution)/shard_map/ppermute | solution.py:75
  69.2 3.9 %collective-permute-done.20 = f32[32,1024]{1,0:T(8,128)S(1)} collective-permute-done((f32[32,1024]{1,0:T(8,128)S(1)}, f32[32,1024]{1,0:T(8,128)S(1)}, u32[]{:S(2)}, u32[]{:S(2)}) %collective-permute-start.20) | collective-permute-done | bytes 131104 | tf_op jit(solution)/shard_map/ppermute | solution.py:75
  73.1 5.0 %collective-permute-done.21 = f32[32,1024]{1,0:T(8,128)S(1)} collective-permute-done((f32[32,1024]{1,0:T(8,128)S(1)}, f32[32,1024]{1,0:T(8,128)S(1)}, u32[]{:S(2)}, u32[]{:S(2)}) %collective-permute-start.21) | collective-permute-done | bytes 131104 | tf_op jit(solution)/shard_map/ppermute | solution.py:75
  78.8 2.3 %collective-permute-start.23 = (f32[32,1024]{1,0:T(8,128)S(1)}, f32[32,1024]{1,0:T(8,128)S(1)}, u32[]{:S(2)}, u32[]{:S(2)}) collective-permute-start(f32[32,1024]{1,0:T(8,128)S(1)} %add_add_fusion.refs_0_), channel_id=1, source_target_pairs={{0,2},{1,3},{2,0},{3,1},{4,6},{5,7},{6,4},{7,5},{8,10},{9,11},{10,... | collective-permute-start | bytes 393224 | tf_op jit(solution)/shard_map/ppermute | solution.py:75
  81.7 4.4 %collective-permute-done.24 = f32[32,1024]{1,0:T(8,128)S(1)} collective-permute-done((f32[32,1024]{1,0:T(8,128)S(1)}, f32[32,1024]{1,0:T(8,128)S(1)}, u32[]{:S(2)}, u32[]{:S(2)}) %collective-permute-start.24) | collective-permute-done | bytes 131104 | tf_op jit(solution)/shard_map/ppermute | solution.py:75
  88.9 4.2 %collective-permute-done.26.refs_2_ = f32[32,1024]{1,0:T(8,128)S(1)} collective-permute-done((f32[32,1024]{1,0:T(8,128)S(1)}, f32[32,1024]{1,0:T(8,128)S(1)}, u32[]{:S(2)}, u32[]{:S(2)}) %collective-permute-start.26) | collective-permute-done | bytes 131104 | tf_op jit(solution)/shard_map/ppermute | solution.py:75
  95.9 2.2 %collective-permute-done.31.refs_5_ = f32[32,1024]{1,0:T(8,128)S(1)} collective-permute-done((f32[32,1024]{1,0:T(8,128)S(1)}, f32[32,1024]{1,0:T(8,128)S(1)}, u32[]{:S(2)}, u32[]{:S(2)}) %collective-permute-start.31) | collective-permute-done | bytes 131104 | tf_op jit(solution)/shard_map/ppermute | solution.py:75
  100.3 1.6 %collective-permute-start.35 = (f32[2,1024]{1,0:T(2,128)S(1)}, f32[2,1024]{1,0:T(2,128)S(1)}, u32[]{:S(2)}, u32[]{:S(2)}) collective-permute-start(f32[2,1024]{1,0:T(2,128)S(1)} %shard_map.54.refs_12_), channel_id=1, source_target_pairs={{0,16},{4,20},{8,24},{12,28},{16,0},{20,4},{24,8},{28,12},{1,17},{... | collective-permute-start | bytes 24584 | tf_op jit(solution)/shard_map/ppermute | solution.py:75
  101.9 2.1 %collective-permute-done.35.refs_13_ = f32[2,1024]{1,0:T(2,128)S(1)} collective-permute-done((f32[2,1024]{1,0:T(2,128)S(1)}, f32[2,1024]{1,0:T(2,128)S(1)}, u32[]{:S(2)}, u32[]{:S(2)}) %collective-permute-start.35) | collective-permute-done | bytes 8224 | tf_op jit(solution)/shard_map/ppermute | solution.py:75
  105.0 1.6 %collective-permute-start.36 = (f32[2,1024]{1,0:T(2,128)S(1)}, f32[2,1024]{1,0:T(2,128)S(1)}, u32[]{:S(2)}, u32[]{:S(2)}) collective-permute-start(f32[2,1024]{1,0:T(2,128)S(1)} %shard_map.55.refs_12_), channel_id=1, source_target_pairs={{0,16},{4,20},{8,24},{12,28},{16,0},{20,4},{24,8},{28,12},{1,17},{... | collective-permute-start | bytes 24584 | tf_op jit(solution)/shard_map/ppermute | solution.py:75
  106.5 2.1 %collective-permute-done.36.refs_13_ = f32[2,1024]{1,0:T(2,128)S(1)} collective-permute-done((f32[2,1024]{1,0:T(2,128)S(1)}, f32[2,1024]{1,0:T(2,128)S(1)}, u32[]{:S(2)}, u32[]{:S(2)}) %collective-permute-start.36) | collective-permute-done | bytes 8224 | tf_op jit(solution)/shard_map/ppermute | solution.py:75
  109.6 1.6 %collective-permute-start.37 = (f32[2,1024]{1,0:T(2,128)S(1)}, f32[2,1024]{1,0:T(2,128)S(1)}, u32[]{:S(2)}, u32[]{:S(2)}) collective-permute-start(f32[2,1024]{1,0:T(2,128)S(1)} %shard_map.56.refs_6_), channel_id=1, source_target_pairs={{0,16},{4,20},{8,24},{12,28},{16,0},{20,4},{24,8},{28,12},{1,17},{... | collective-permute-start | bytes 24584 | tf_op jit(solution)/shard_map/ppermute | solution.py:75
  111.2 2.1 %collective-permute-done.37.refs_7_ = f32[2,1024]{1,0:T(2,128)S(1)} collective-permute-done((f32[2,1024]{1,0:T(2,128)S(1)}, f32[2,1024]{1,0:T(2,128)S(1)}, u32[]{:S(2)}, u32[]{:S(2)}) %collective-permute-start.37) | collective-permute-done | bytes 8224 | tf_op jit(solution)/shard_map/ppermute | solution.py:75
  113.3 2.2 %shard_map.57 = (bf16[2,4,32,512]{3,2,1,0:T(8,128)(2,1)S(1)}, bf16[2,4,32,512]{3,2,1,0:T(8,128)(2,1)S(1)}, bf16[2,4,32,512]{3,2,1,0:T(8,128)(2,1)S(1)}, bf16[2,4...) custom-call(f32[32,1024]{1,0:T(8,128)S(1)} %add_add_fusion.refs_0_, ...), custom_call_target="tpu_custom_call" | custom-call | flops 1073741824 | bytes 5259264 | tf_op jit(solution)/shard_map/pallas_call | solution.py:115
  115.5 2.3 %collective-permute-start.38 = (bf16[2,4,32,512]{3,2,1,0:T(8,128)(2,1)S(1)}, bf16[2,4,32,512]{3,2,1,0:T(8,128)(2,1)S(1)}, u32[]{:S(2)}, u32[]{:S(2)}) collective-permute-start(bf16[2,4,32,512]{3,2,1,0:T(8,128)(2,1)S(1)} %get-tuple-element.63), channel_id=1, source_target_pairs={{0,3},{1,2},{2,1},{3,0},{4,7},{5,6},{6,5},{7,4},{8,11},{9,10},{10,... | collective-permute-start | bytes 786440 | tf_op jit(solution)/shard_map/ppermute | solution.py:75
  117.8 2.1 %collective-permute-start.40 = (bf16[2,4,32,512]{3,2,1,0:T(8,128)(2,1)S(1)}, bf16[2,4,32,512]{3,2,1,0:T(8,128)(2,1)S(1)}, u32[]{:S(2)}, u32[]{:S(2)}) collective-permute-start(bf16[2,4,32,512]{3,2,1,0:T(8,128)(2,1)S(1)} %get-tuple-element.65), channel_id=1, source_target_pairs={{0,1},{1,0},{2,3},{3,2},{4,5},{5,4},{6,7},{7,6},{8,9},{9,8},{10,11... | collective-permute-start | bytes 786440 | tf_op jit(solution)/shard_map/ppermute | solution.py:75
  119.8 6.6 %collective-permute-done.38.refs_0_ = bf16[2,4,32,512]{3,2,1,0:T(8,128)(2,1)S(1)} collective-permute-done((bf16[2,4,32,512]{3,2,1,0:T(8,128)(2,1)S(1)}, bf16[2,4,32,512]{3,2,1,0:T(8,128)(2,1)S(1)}, u32[]{:S(2)}, u32[]{:S(2)}) %collective-permute-start.38) | collective-permute-done | bytes 262176 | tf_op jit(solution)/shard_map/ppermute | solution.py:75
  126.5 10.4 %collective-permute-done.39.refs_1_ = bf16[2,4,32,512]{3,2,1,0:T(8,128)(2,1)S(1)} collective-permute-done((bf16[2,4,32,512]{3,2,1,0:T(8,128)(2,1)S(1)}, bf16[2,4,32,512]{3,2,1,0:T(8,128)(2,1)S(1)}, u32[]{:S(2)}, u32[]{:S(2)}) %collective-permute-start.39) | collective-permute-done | bytes 262176 | tf_op jit(solution)/shard_map/ppermute | solution.py:75
  (75 shorter events, 30.9 us)
Async XLA Ops:
  1.9 12.0 %collective-permute-start = (bf16[128,2048]{1,0:T(8,128)(2,1)S(1)}, bf16[128,2048]{1,0:T(8,128)(2,1)S(1)}, u32[]{:S(2)}, u32[]{:S(2)}) collective-permute-start(bf16[128,2048]{1,0:T(8,128)(2,1)S(1)} %get-tuple-element.37), channel_id=1, source_target_pairs={{0,4},{4,0},{8,12},{12,8},{16,20},{20,16},{24,28},{28,24},{1,5},{5... | collective-permute-start | bytes 1572872 | tf_op jit(solution)/shard_map/ppermute | solution.py:75
  3.2 9.3 %collective-permute-start.2 = (bf16[256,512]{1,0:T(8,128)(2,1)S(1)}, bf16[256,512]{1,0:T(8,128)(2,1)S(1)}, u32[]{:S(2)}, u32[]{:S(2)}) collective-permute-start(bf16[256,512]{1,0:T(8,128)(2,1)S(1)} %get-tuple-element.38.refs_4_.refs_8_), channel_id=1, source_target_pairs={{0,16},{4,20},{8,24},{12,28},{16,0},{20,4},{24,8},{28,12},{1,17},{... | collective-permute-start | bytes 786440 | tf_op jit(solution)/shard_map/ppermute | solution.py:75
  6.2 7.8 %collective-permute-start.1 = (bf16[256,512]{1,0:T(8,128)(2,1)S(1)}, bf16[256,512]{1,0:T(8,128)(2,1)S(1)}, u32[]{:S(2)}, u32[]{:S(2)}) collective-permute-start(bf16[256,512]{1,0:T(8,128)(2,1)S(1)} %get-tuple-element.38.refs_4_.refs_8_), channel_id=1, source_target_pairs={{0,8},{4,12},{8,0},{12,4},{16,24},{20,28},{24,16},{28,20},{1,9},{5... | collective-permute-start | bytes 786440 | tf_op jit(solution)/shard_map/ppermute | solution.py:75
  7.7 13.0 %collective-permute-start.8 = (bf16[256,512]{1,0:T(8,128)(2,1)S(1)}, bf16[256,512]{1,0:T(8,128)(2,1)S(1)}, u32[]{:S(2)}, u32[]{:S(2)}) collective-permute-start(bf16[256,512]{1,0:T(8,128)(2,1)S(1)} %get-tuple-element.49), channel_id=1, source_target_pairs={{0,1},{1,0},{2,3},{3,2},{4,5},{5,4},{6,7},{7,6},{8,9},{9,8},{10,11... | collective-permute-start | bytes 786440 | tf_op jit(solution)/shard_map/ppermute | solution.py:75
  9.3 16.5 %collective-permute-start.4 = (bf16[256,512]{1,0:T(8,128)(2,1)S(1)}, bf16[256,512]{1,0:T(8,128)(2,1)S(1)}, u32[]{:S(2)}, u32[]{:S(2)}) collective-permute-start(bf16[256,512]{1,0:T(8,128)(2,1)S(1)} %get-tuple-element.44), channel_id=1, source_target_pairs={{0,2},{1,3},{2,0},{3,1},{4,6},{5,7},{6,4},{7,5},{8,10},{9,11},{10,... | collective-permute-start | bytes 786440 | tf_op jit(solution)/shard_map/ppermute | solution.py:75
  20.7 9.1 %collective-permute-start.11 = (bf16[256,512]{1,0:T(8,128)(2,1)S(1)}, bf16[256,512]{1,0:T(8,128)(2,1)S(1)}, u32[]{:S(2)}, u32[]{:S(2)}) collective-permute-start(bf16[256,512]{1,0:T(8,128)(2,1)S(1)} %collective-permute-done.8.refs_5_.refs_9_), channel_id=1, source_target_pairs={{0,16},{4,20},{8,24},{12,28},{16,0},{20,4},{24,8},{28,12},{1,17},{... | collective-permute-start | bytes 786440 | tf_op jit(solution)/shard_map/ppermute | solution.py:75
  21.2 11.6 %collective-permute-start.14 = (bf16[256,512]{1,0:T(8,128)(2,1)S(1)}, bf16[256,512]{1,0:T(8,128)(2,1)S(1)}, u32[]{:S(2)}, u32[]{:S(2)}) collective-permute-start(bf16[256,512]{1,0:T(8,128)(2,1)S(1)} %collective-permute-done.1.refs_8_.refs_12_), channel_id=1, source_target_pairs={{0,16},{4,20},{8,24},{12,28},{16,0},{20,4},{24,8},{28,12},{1,17},{... | collective-permute-start | bytes 786440 | tf_op jit(solution)/shard_map/ppermute | solution.py:75
  22.7 12.6 %collective-permute-start.3 = (bf16[256,512]{1,0:T(8,128)(2,1)S(1)}, bf16[256,512]{1,0:T(8,128)(2,1)S(1)}, u32[]{:S(2)}, u32[]{:S(2)}) collective-permute-start(bf16[256,512]{1,0:T(8,128)(2,1)S(1)} %get-tuple-element.42), channel_id=1, source_target_pairs={{0,3},{1,2},{2,1},{3,0},{4,7},{5,6},{6,5},{7,4},{8,11},{9,10},{10,... | collective-permute-start | bytes 786440 | tf_op jit(solution)/shard_map/ppermute | solution.py:75
  25.2 8.1 %collective-permute-start.9 = (bf16[256,512]{1,0:T(8,128)(2,1)S(1)}, bf16[256,512]{1,0:T(8,128)(2,1)S(1)}, u32[]{:S(2)}, u32[]{:S(2)}) collective-permute-start(bf16[256,512]{1,0:T(8,128)(2,1)S(1)} %collective-permute-done.8.refs_5_.refs_9_), channel_id=1, source_target_pairs={{0,8},{4,12},{8,0},{12,4},{16,24},{20,28},{24,16},{28,20},{1,9},{5... | collective-permute-start | bytes 786440 | tf_op jit(solution)/shard_map/ppermute | solution.py:75
  25.7 10.2 %collective-permute-start.5 = (bf16[2,128,512]{2,1,0:T(8,128)(2,1)S(1)}, bf16[2,128,512]{2,1,0:T(8,128)(2,1)S(1)}, u32[]{:S(2)}, u32[]{:S(2)}) collective-permute-start(bf16[2,128,512]{2,1,0:T(8,128)(2,1)S(1)} %get-tuple-element.45), channel_id=1, source_target_pairs={{0,1},{1,0},{2,3},{3,2},{4,5},{5,4},{6,7},{7,6},{8,9},{9,8},{10,11... | collective-permute-start | bytes 786440 | tf_op jit(solution)/shard_map/ppermute | solution.py:75
  32.8 7.3 %collective-permute-start.15 = (bf16[256,512]{1,0:T(8,128)(2,1)S(1)}, bf16[256,512]{1,0:T(8,128)(2,1)S(1)}, u32[]{:S(2)}, u32[]{:S(2)}) collective-permute-start(bf16[256,512]{1,0:T(8,128)(2,1)S(1)} %collective-permute-done.4.refs_6_.refs_10_), channel_id=1, source_target_pairs={{0,16},{4,20},{8,24},{12,28},{16,0},{20,4},{24,8},{28,12},{1,17},{... | collective-permute-start | bytes 786440 | tf_op jit(solution)/shard_map/ppermute | solution.py:75
  33.3 11.9 %collective-permute-start.10 = (bf16[256,512]{1,0:T(8,128)(2,1)S(1)}, bf16[256,512]{1,0:T(8,128)(2,1)S(1)}, u32[]{:S(2)}, u32[]{:S(2)}) collective-permute-start(bf16[256,512]{1,0:T(8,128)(2,1)S(1)} %collective-permute-done.4.refs_6_.refs_10_), channel_id=1, source_target_pairs={{0,8},{4,12},{8,0},{12,4},{16,24},{20,28},{24,16},{28,20},{1,9},{5... | collective-permute-start | bytes 786440 | tf_op jit(solution)/shard_map/ppermute | solution.py:75
  33.9 11.3 %collective-permute-start.12 = (bf16[256,512]{1,0:T(8,128)(2,1)S(1)}, bf16[256,512]{1,0:T(8,128)(2,1)S(1)}, u32[]{:S(2)}, u32[]{:S(2)}) collective-permute-start(bf16[256,512]{1,0:T(8,128)(2,1)S(1)} %collective-permute-done.11.refs_13_.refs_17_), channel_id=1, source_target_pairs={{0,8},{4,12},{8,0},{12,4},{16,24},{20,28},{24,16},{28,20},{1,9},{5... | collective-permute-start | bytes 786440 | tf_op jit(solution)/shard_map/ppermute | solution.py:75
  40.1 9.0 %collective-permute-start.16 = (bf16[256,512]{1,0:T(8,128)(2,1)S(1)}, bf16[256,512]{1,0:T(8,128)(2,1)S(1)}, u32[]{:S(2)}, u32[]{:S(2)}) collective-permute-start(bf16[256,512]{1,0:T(8,128)(2,1)S(1)} %collective-permute-done.3.refs_7_.refs_11_), channel_id=1, source_target_pairs={{0,16},{4,20},{8,24},{12,28},{16,0},{20,4},{24,8},{28,12},{1,17},{... | collective-permute-start | bytes 786440 | tf_op jit(solution)/shard_map/ppermute | solution.py:75
  40.6 9.1 %collective-permute-start.6 = (bf16[2,128,512]{2,1,0:T(8,128)(2,1)S(1)}, bf16[2,128,512]{2,1,0:T(8,128)(2,1)S(1)}, u32[]{:S(2)}, u32[]{:S(2)}) collective-permute-start(bf16[2,128,512]{2,1,0:T(8,128)(2,1)S(1)} %get-tuple-element.46), channel_id=1, source_target_pairs={{0,3},{1,2},{2,1},{3,0},{4,7},{5,6},{6,5},{7,4},{8,11},{9,10},{10,... | collective-permute-start | bytes 786440 | tf_op jit(solution)/shard_map/ppermute | solution.py:75
  43.3 17.4 %collective-permute-start.7 = (bf16[2,128,512]{2,1,0:T(8,128)(2,1)S(1)}, bf16[2,128,512]{2,1,0:T(8,128)(2,1)S(1)}, u32[]{:S(2)}, u32[]{:S(2)}) collective-permute-start(bf16[2,128,512]{2,1,0:T(8,128)(2,1)S(1)} %get-tuple-element.48), channel_id=1, source_target_pairs={{0,2},{1,3},{2,0},{3,1},{4,6},{5,7},{6,4},{7,5},{8,10},{9,11},{10,... | collective-permute-start | bytes 786440 | tf_op jit(solution)/shard_map/ppermute | solution.py:75
  45.2 15.5 %collective-permute-start.13 = (bf16[256,512]{1,0:T(8,128)(2,1)S(1)}, bf16[256,512]{1,0:T(8,128)(2,1)S(1)}, u32[]{:S(2)}, u32[]{:S(2)}) collective-permute-start(bf16[256,512]{1,0:T(8,128)(2,1)S(1)} %collective-permute-done.3.refs_7_.refs_11_), channel_id=1, source_target_pairs={{0,8},{4,12},{8,0},{12,4},{16,24},{20,28},{24,16},{28,20},{1,9},{5... | collective-permute-start | bytes 786440 | tf_op jit(solution)/shard_map/ppermute | solution.py:75
  46.0 14.7 %collective-permute-start.17 = (bf16[256,512]{1,0:T(8,128)(2,1)S(1)}, bf16[256,512]{1,0:T(8,128)(2,1)S(1)}, u32[]{:S(2)}, u32[]{:S(2)}) collective-permute-start(bf16[256,512]{1,0:T(8,128)(2,1)S(1)} %collective-permute-done.10.refs_10_.refs_14_), channel_id=1, source_target_pairs={{0,16},{4,20},{8,24},{12,28},{16,0},{20,4},{24,8},{28,12},{1,17},{... | collective-permute-start | bytes 786440 | tf_op jit(solution)/shard_map/ppermute | solution.py:75
  49.1 11.6 %collective-permute-start.18 = (bf16[256,512]{1,0:T(8,128)(2,1)S(1)}, bf16[256,512]{1,0:T(8,128)(2,1)S(1)}, u32[]{:S(2)}, u32[]{:S(2)}) collective-permute-start(bf16[256,512]{1,0:T(8,128)(2,1)S(1)} %collective-permute-done.16.refs_15_.refs_19_), channel_id=1, source_target_pairs={{0,8},{4,12},{8,0},{12,4},{16,24},{20,28},{24,16},{28,20},{1,9},{5... | collective-permute-start | bytes 786440 | tf_op jit(solution)/shard_map/ppermute | solution.py:75
  64.8 8.3 %collective-permute-start.20 = (f32[32,1024]{1,0:T(8,128)S(1)}, f32[32,1024]{1,0:T(8,128)S(1)}, u32[]{:S(2)}, u32[]{:S(2)}) collective-permute-start(f32[32,1024]{1,0:T(8,128)S(1)} %get-tuple-element.58), channel_id=1, source_target_pairs={{0,3},{1,2},{2,1},{3,0},{4,7},{5,6},{6,5},{7,4},{8,11},{9,10},{10,... | collective-permute-start | bytes 393224 | tf_op jit(solution)/shard_map/ppermute | solution.py:75
  67.5 10.6 %collective-permute-start.21 = (f32[32,1024]{1,0:T(8,128)S(1)}, f32[32,1024]{1,0:T(8,128)S(1)}, u32[]{:S(2)}, u32[]{:S(2)}) collective-permute-start(f32[32,1024]{1,0:T(8,128)S(1)} %get-tuple-element.59), channel_id=1, source_target_pairs={{0,2},{1,3},{2,0},{3,1},{4,6},{5,7},{6,4},{7,5},{8,10},{9,11},{10,... | collective-permute-start | bytes 393224 | tf_op jit(solution)/shard_map/ppermute | solution.py:75
  67.5 10.6 %collective-permute-start.22 = (f32[32,1024]{1,0:T(8,128)S(1)}, f32[32,1024]{1,0:T(8,128)S(1)}, u32[]{:S(2)}, u32[]{:S(2)}) collective-permute-start(f32[32,1024]{1,0:T(8,128)S(1)} %get-tuple-element.60), channel_id=1, source_target_pairs={{0,1},{1,0},{2,3},{3,2},{4,5},{5,4},{6,7},{7,6},{8,9},{9,8},{10,11... | collective-permute-start | bytes 393224 | tf_op jit(solution)/shard_map/ppermute | solution.py:75
  78.1 8.0 %collective-permute-start.24 = (f32[32,1024]{1,0:T(8,128)S(1)}, f32[32,1024]{1,0:T(8,128)S(1)}, u32[]{:S(2)}, u32[]{:S(2)}) collective-permute-start(f32[32,1024]{1,0:T(8,128)S(1)} %add_add_fusion.refs_0_), channel_id=1, source_target_pairs={{0,1},{1,0},{2,3},{3,2},{4,5},{5,4},{6,7},{7,6},{8,9},{9,8},{10,11... | collective-permute-start | bytes 393224 | tf_op jit(solution)/shard_map/ppermute | solution.py:75
  78.8 8.7 %collective-permute-start.23 = (f32[32,1024]{1,0:T(8,128)S(1)}, f32[32,1024]{1,0:T(8,128)S(1)}, u32[]{:S(2)}, u32[]{:S(2)}) collective-permute-start(f32[32,1024]{1,0:T(8,128)S(1)} %add_add_fusion.refs_0_), channel_id=1, source_target_pairs={{0,2},{1,3},{2,0},{3,1},{4,6},{5,7},{6,4},{7,5},{8,10},{9,11},{10,... | collective-permute-start | bytes 393224 | tf_op jit(solution)/shard_map/ppermute | solution.py:75
  87.5 7.8 %collective-permute-start.30 = (f32[2,32,1024]{2,1,0:T(8,128)S(1)}, f32[2,32,1024]{2,1,0:T(8,128)S(1)}, u32[]{:S(2)}, u32[]{:S(2)}) collective-permute-start(f32[2,32,1024]{2,1,0:T(8,128)S(1)} %pad_maximum_fusion.refs_1_), channel_id=1, source_target_pairs={{0,8},{4,12},{8,0},{12,4},{16,24},{20,28},{24,16},{28,20},{1,9},{5... | collective-permute-start | bytes 786440 | tf_op jit(solution)/shard_map/ppermute | solution.py:75
  88.4 7.5 %collective-permute-start.27 = (f32[32,1024]{1,0:T(8,128)S(1)}, f32[32,1024]{1,0:T(8,128)S(1)}, u32[]{:S(2)}, u32[]{:S(2)}) collective-permute-start(f32[32,1024]{1,0:T(8,128)S(1)} %add_add_fusion.refs_0_), channel_id=1, source_target_pairs={{0,4},{4,0},{8,12},{12,8},{16,20},{20,16},{24,28},{28,24},{1,5},{5... | collective-permute-start | bytes 393224 | tf_op jit(solution)/shard_map/ppermute | solution.py:75
  88.4 9.7 %collective-permute-start.28 = (f32[2,32,1024]{2,1,0:T(8,128)S(1)}, f32[2,32,1024]{2,1,0:T(8,128)S(1)}, u32[]{:S(2)}, u32[]{:S(2)}) collective-permute-start(f32[2,32,1024]{2,1,0:T(8,128)S(1)} %pad_maximum_fusion.refs_1_), channel_id=1, source_target_pairs={{0,4},{4,0},{8,12},{12,8},{16,20},{20,16},{24,28},{28,24},{1,5},{5... | collective-permute-start | bytes 786440 | tf_op jit(solution)/shard_map/ppermute | solution.py:75
  115.5 11.0 %collective-permute-start.38 = (bf16[2,4,32,512]{3,2,1,0:T(8,128)(2,1)S(1)}, bf16[2,4,32,512]{3,2,1,0:T(8,128)(2,1)S(1)}, u32[]{:S(2)}, u32[]{:S(2)}) collective-permute-start(bf16[2,4,32,512]{3,2,1,0:T(8,128)(2,1)S(1)} %get-tuple-element.63), channel_id=1, source_target_pairs={{0,3},{1,2},{2,1},{3,0},{4,7},{5,6},{6,5},{7,4},{8,11},{9,10},{10,... | collective-permute-start | bytes 786440 | tf_op jit(solution)/shard_map/ppermute | solution.py:75
  117.8 19.1 %collective-permute-start.39 = (bf16[2,4,32,512]{3,2,1,0:T(8,128)(2,1)S(1)}, bf16[2,4,32,512]{3,2,1,0:T(8,128)(2,1)S(1)}, u32[]{:S(2)}, u32[]{:S(2)}) collective-permute-start(bf16[2,4,32,512]{3,2,1,0:T(8,128)(2,1)S(1)} %get-tuple-element.64), channel_id=1, source_target_pairs={{0,2},{1,3},{2,0},{3,1},{4,6},{5,7},{6,4},{7,5},{8,10},{9,11},{10,... | collective-permute-start | bytes 786440 | tf_op jit(solution)/shard_map/ppermute | solution.py:75
  117.8 19.1 %collective-permute-start.40 = (bf16[2,4,32,512]{3,2,1,0:T(8,128)(2,1)S(1)}, bf16[2,4,32,512]{3,2,1,0:T(8,128)(2,1)S(1)}, u32[]{:S(2)}, u32[]{:S(2)}) collective-permute-start(bf16[2,4,32,512]{3,2,1,0:T(8,128)(2,1)S(1)} %get-tuple-element.65), channel_id=1, source_target_pairs={{0,1},{1,0},{2,3},{3,2},{4,5},{5,4},{6,7},{7,6},{8,9},{9,8},{10,11... | collective-permute-start | bytes 786440 | tf_op jit(solution)/shard_map/ppermute | solution.py:75
  119.8 18.1 %collective-permute-start.44 = (bf16[2,4,32,512]{3,2,1,0:T(8,128)(2,1)S(1)}, bf16[2,4,32,512]{3,2,1,0:T(8,128)(2,1)S(1)}, u32[]{:S(2)}, u32[]{:S(2)}) collective-permute-start(bf16[2,4,32,512]{3,2,1,0:T(8,128)(2,1)S(1)} %get-tuple-element.66.refs_3_), channel_id=1, source_target_pairs={{0,4},{4,0},{8,12},{12,8},{16,20},{20,16},{24,28},{28,24},{1,5},{5... | collective-permute-start | bytes 786440 | tf_op jit(solution)/shard_map/ppermute | solution.py:75
  126.5 11.5 %collective-permute-start.41 = (bf16[2,4,32,512]{3,2,1,0:T(8,128)(2,1)S(1)}, bf16[2,4,32,512]{3,2,1,0:T(8,128)(2,1)S(1)}, u32[]{:S(2)}, u32[]{:S(2)}) collective-permute-start(bf16[2,4,32,512]{3,2,1,0:T(8,128)(2,1)S(1)} %collective-permute-done.38.refs_0_), channel_id=1, source_target_pairs={{0,4},{4,0},{8,12},{12,8},{16,20},{20,16},{24,28},{28,24},{1,5},{5... | collective-permute-start | bytes 786440 | tf_op jit(solution)/shard_map/ppermute | solution.py:75
  (15 other events, 45.6 us)

commit v14 on v12

--- a/solution.py
+++ b/solution.py
@@ -228,7 +228,7 @@
         if len(ref.shape) == 2:
             parts.append(ref[:, lanes])
         else:
-            parts += [ref[i, :, lanes] for i in reversed(range(ref.shape[0]))]
+            parts += [ref[i, :, lanes] for i in range(ref.shape[0])]
     return jnp.concatenate(parts)
 
 
@@ -389,7 +389,7 @@
     tile_2, tile_1 = swap(tile, "col", 2), swap(tile, "col", 1)
     tile_3 = swap(tile_2, "col", 1)
     x_tile = swap_x(tile)
-    pair = after(jnp.stack([tile_2, tile_1]), x_tile)
+    pair = after(jnp.stack([tile_1, tile_2]), x_tile)
     tiles = [[tile, pair, tile_3], [x_tile, swap_x(pair), swap_x(tile_3)]]
     other_tiles = [swap_core(piece) for piece in tiles[0]]
     tiles += [other_tiles, [swap_core(piece) for piece in tiles[1]]]

time: 138 us -> 138 us (level)
  waiting for transfers between devices: 82 us -> 80.4 us
    ppermute x45, waiting for transfers between devices: 82 us -> 80.4 us  [swap(): return lax.ppermute(array, axis, [(i, i ^ step) for i in range(count)])]
  transfers between devices with their start and end apart: 45 -> 45, of which waited for: 26 -> 28; matrix products, arithmetic and copies ran while one was open for 0% -> 0% of each run, Pallas kernels for 0% -> 0%
where the time goes in v14:
time: 138 us
  waiting for transfers between devices  80.4 us (58%)
  starting transfers between devices  46.1 us (33%)
  Pallas kernels  8.26 us (6%)
  local copies, waits for them, and re-layouts  2.44 us (2%)
    ppermute x45, waiting for transfers between devices, swap(): return lax.ppermute(array, axis, [(i, i ^ step) for i in range(count)])  80.4 us
    ppermute x45, starting transfers between devices, swap(): return lax.ppermute(array, axis, [(i, i ^ step) for i in range(count)])  46.1 us
    pallas_call x10, Pallas kernels, kernel_call(): pl.pallas_call(kernel, in_specs=[VMEM] * len(operands), out_specs=[VMEM]...  8.26 us
  transfers between devices with their start and end apart: 45, of which 28 were waited for; matrix products, arithmetic and copies ran while one was open for 0% of the time, Pallas kernels for 0%

profile of v14, /device:TPU:0, one launch (start us, length us, event | category | flops | bytes accessed | tf_op | source)
XLA Modules:
  0.0 137.9 jit_solution(347912128791160635)
XLA Ops:
  3.2 3.0 %collective-permute-start.2 = (bf16[256,512]{1,0:T(8,128)(2,1)S(1)}, bf16[256,512]{1,0:T(8,128)(2,1)S(1)}, u32[]{:S(2)}, u32[]{:S(2)}) collective-permute-start(bf16[256,512]{1,0:T(8,128)(2,1)S(1)} %get-tuple-element.38.refs_4_.refs_8_), channel_id=1, source_target_pairs={{0,16},{4,20},{8,24},{12,28},{16,0},{20,4},{24,8},{28,12},{1,17},{... | collective-permute-start | bytes 786440 | tf_op jit(solution)/shard_map/ppermute | solution.py:75
  7.7 1.6 %collective-permute-start.8 = (bf16[256,512]{1,0:T(8,128)(2,1)S(1)}, bf16[256,512]{1,0:T(8,128)(2,1)S(1)}, u32[]{:S(2)}, u32[]{:S(2)}) collective-permute-start(bf16[256,512]{1,0:T(8,128)(2,1)S(1)} %get-tuple-element.49), channel_id=1, source_target_pairs={{0,1},{1,0},{2,3},{3,2},{4,5},{5,4},{6,7},{7,6},{8,9},{9,8},{10,11... | collective-permute-start | bytes 786440 | tf_op jit(solution)/shard_map/ppermute | solution.py:75
  9.3 2.6 %collective-permute-start.3 = (bf16[256,512]{1,0:T(8,128)(2,1)S(1)}, bf16[256,512]{1,0:T(8,128)(2,1)S(1)}, u32[]{:S(2)}, u32[]{:S(2)}) collective-permute-start(bf16[256,512]{1,0:T(8,128)(2,1)S(1)} %get-tuple-element.42), channel_id=1, source_target_pairs={{0,2},{1,3},{2,0},{3,1},{4,6},{5,7},{6,4},{7,5},{8,10},{9,11},{10,... | collective-permute-start | bytes 786440 | tf_op jit(solution)/shard_map/ppermute | solution.py:75
  14.0 6.6 %collective-permute-done.8.refs_5_.refs_9_ = bf16[256,512]{1,0:T(8,128)(2,1)S(1)} collective-permute-done((bf16[256,512]{1,0:T(8,128)(2,1)S(1)}, bf16[256,512]{1,0:T(8,128)(2,1)S(1)}, u32[]{:S(2)}, u32[]{:S(2)}) %collective-permute-start.8) | collective-permute-done | bytes 262176 | tf_op jit(solution)/shard_map/ppermute | solution.py:75
  22.7 2.5 %collective-permute-start.6 = (bf16[256,512]{1,0:T(8,128)(2,1)S(1)}, bf16[256,512]{1,0:T(8,128)(2,1)S(1)}, u32[]{:S(2)}, u32[]{:S(2)}) collective-permute-start(bf16[256,512]{1,0:T(8,128)(2,1)S(1)} %get-tuple-element.47), channel_id=1, source_target_pairs={{0,3},{1,2},{2,1},{3,0},{4,7},{5,6},{6,5},{7,4},{8,11},{9,10},{10,... | collective-permute-start | bytes 786440 | tf_op jit(solution)/shard_map/ppermute | solution.py:75
  25.7 4.1 %collective-permute-done.11.refs_13_.refs_17_ = bf16[256,512]{1,0:T(8,128)(2,1)S(1)} collective-permute-done((bf16[256,512]{1,0:T(8,128)(2,1)S(1)}, bf16[256,512]{1,0:T(8,128)(2,1)S(1)}, u32[]{:S(2)}, u32[]{:S(2)}) %collective-permute-start.11) | collective-permute-done | bytes 262176 | tf_op jit(solution)/shard_map/ppermute | solution.py:75
  29.8 3.0 %collective-permute-done.14.refs_16_.refs_20_ = bf16[256,512]{1,0:T(8,128)(2,1)S(1)} collective-permute-done((bf16[256,512]{1,0:T(8,128)(2,1)S(1)}, bf16[256,512]{1,0:T(8,128)(2,1)S(1)}, u32[]{:S(2)}, u32[]{:S(2)}) %collective-permute-start.14) | collective-permute-done | bytes 262176 | tf_op jit(solution)/shard_map/ppermute | solution.py:75
  36.0 4.1 %collective-permute-done.15.refs_14_.refs_18_ = bf16[256,512]{1,0:T(8,128)(2,1)S(1)} collective-permute-done((bf16[256,512]{1,0:T(8,128)(2,1)S(1)}, bf16[256,512]{1,0:T(8,128)(2,1)S(1)}, u32[]{:S(2)}, u32[]{:S(2)}) %collective-permute-start.15) | collective-permute-done | bytes 262176 | tf_op jit(solution)/shard_map/ppermute | solution.py:75
  41.4 1.9 %collective-permute-start.7 = (bf16[2,128,512]{2,1,0:T(8,128)(2,1)S(1)}, bf16[2,128,512]{2,1,0:T(8,128)(2,1)S(1)}, u32[]{:S(2)}, u32[]{:S(2)}) collective-permute-start(bf16[2,128,512]{2,1,0:T(8,128)(2,1)S(1)} %get-tuple-element.48), channel_id=1, source_target_pairs={{0,3},{1,2},{2,1},{3,0},{4,7},{5,6},{6,5},{7,4},{8,11},{9,10},{10,... | collective-permute-start | bytes 786440 | tf_op jit(solution)/shard_map/ppermute | solution.py:75
  43.3 1.9 %collective-permute-done.12.refs_17_.refs_21_ = bf16[256,512]{1,0:T(8,128)(2,1)S(1)} collective-permute-done((bf16[256,512]{1,0:T(8,128)(2,1)S(1)}, bf16[256,512]{1,0:T(8,128)(2,1)S(1)}, u32[]{:S(2)}, u32[]{:S(2)}) %collective-permute-start.12) | collective-permute-done | bytes 262176 | tf_op jit(solution)/shard_map/ppermute | solution.py:75
  47.4 1.7 %collective-permute-done.16.refs_15_.refs_19_ = bf16[256,512]{1,0:T(8,128)(2,1)S(1)} collective-permute-done((bf16[256,512]{1,0:T(8,128)(2,1)S(1)}, bf16[256,512]{1,0:T(8,128)(2,1)S(1)}, u32[]{:S(2)}, u32[]{:S(2)}) %collective-permute-start.16) | collective-permute-done | bytes 262176 | tf_op jit(solution)/shard_map/ppermute | solution.py:75
  49.7 7.4 %collective-permute-done.5.refs_2_ = bf16[2,128,512]{2,1,0:T(8,128)(2,1)S(1)} collective-permute-done((bf16[2,128,512]{2,1,0:T(8,128)(2,1)S(1)}, bf16[2,128,512]{2,1,0:T(8,128)(2,1)S(1)}, u32[]{:S(2)}, u32[]{:S(2)}) %collective-permute-start.5) | collective-permute-done | bytes 262176 | tf_op jit(solution)/shard_map/ppermute | solution.py:75
  57.2 2.0 %shard_map.52 = (f32[128,1024]{1,0:T(8,128)S(1)}, f32[128,1024]{1,0:T(8,128)S(1)}) custom-call(bf16[2,128,512]{2,1,0:T(8,128)(2,1)S(1)} %get-tuple-element.40.refs_0_, bf16[2,128,512]{2,1,0:T(8,128)(2,1)S(1)} %collective-permute-done.4.refs_1_, bf16[2,128,512]{2,1,0:T(8,128)(2,1)S(1)} %collective-permute-done.5.refs_2_, ...), custom_call_target="tpu_custom_call" | custom-call | flops 1073741824 | bytes 5242880 | tf_op jit(solution)/shard_map/pallas_call | solution.py:115
  59.3 1.9 %collective-permute-done.19.other_ref = f32[128,1024]{1,0:T(8,128)S(1)} collective-permute-done((f32[128,1024]{1,0:T(8,128)S(1)}, f32[128,1024]{1,0:T(8,128)S(1)}, u32[]{:S(2)}, u32[]{:S(2)}) %collective-permute-start.19) | collective-permute-done | bytes 524320 | tf_op jit(solution)/shard_map/ppermute | solution.py:75
  61.2 2.0 %collective-permute-start.20 = (f32[32,1024]{1,0:T(8,128)S(1)}, f32[32,1024]{1,0:T(8,128)S(1)}, u32[]{:S(2)}, u32[]{:S(2)}) collective-permute-start(f32[32,1024]{1,0:T(8,128)S(1)} %get-tuple-element.58), channel_id=1, source_target_pairs={{0,3},{1,2},{2,1},{3,0},{4,7},{5,6},{6,5},{7,4},{8,11},{9,10},{10,... | collective-permute-start | bytes 393224 | tf_op jit(solution)/shard_map/ppermute | solution.py:75
  63.3 4.6 %collective-permute-start.21 = (f32[32,1024]{1,0:T(8,128)S(1)}, f32[32,1024]{1,0:T(8,128)S(1)}, u32[]{:S(2)}, u32[]{:S(2)}) collective-permute-start(f32[32,1024]{1,0:T(8,128)S(1)} %get-tuple-element.59), channel_id=1, source_target_pairs={{0,2},{1,3},{2,0},{3,1},{4,6},{5,7},{6,4},{7,5},{8,10},{9,11},{10,... | collective-permute-start | bytes 393224 | tf_op jit(solution)/shard_map/ppermute | solution.py:75
  68.6 8.4 %collective-permute-done.21 = f32[32,1024]{1,0:T(8,128)S(1)} collective-permute-done((f32[32,1024]{1,0:T(8,128)S(1)}, f32[32,1024]{1,0:T(8,128)S(1)}, u32[]{:S(2)}, u32[]{:S(2)}) %collective-permute-start.21) | collective-permute-done | bytes 131104 | tf_op jit(solution)/shard_map/ppermute | solution.py:75
  77.2 3.0 %collective-permute-start.23 = (f32[32,1024]{1,0:T(8,128)S(1)}, f32[32,1024]{1,0:T(8,128)S(1)}, u32[]{:S(2)}, u32[]{:S(2)}) collective-permute-start(f32[32,1024]{1,0:T(8,128)S(1)} %add_add_fusion.refs_0_), channel_id=1, source_target_pairs={{0,1},{1,0},{2,3},{3,2},{4,5},{5,4},{6,7},{7,6},{8,9},{9,8},{10,11... | collective-permute-start | bytes 393224 | tf_op jit(solution)/shard_map/ppermute | solution.py:75
  80.7 4.8 %collective-permute-done.24 = f32[32,1024]{1,0:T(8,128)S(1)} collective-permute-done((f32[32,1024]{1,0:T(8,128)S(1)}, f32[32,1024]{1,0:T(8,128)S(1)}, u32[]{:S(2)}, u32[]{:S(2)}) %collective-permute-start.24) | collective-permute-done | bytes 131104 | tf_op jit(solution)/shard_map/ppermute | solution.py:75
  87.0 4.5 %collective-permute-done.26.refs_2_ = f32[32,1024]{1,0:T(8,128)S(1)} collective-permute-done((f32[32,1024]{1,0:T(8,128)S(1)}, f32[32,1024]{1,0:T(8,128)S(1)}, u32[]{:S(2)}, u32[]{:S(2)}) %collective-permute-start.26) | collective-permute-done | bytes 131104 | tf_op jit(solution)/shard_map/ppermute | solution.py:75
  92.8 2.1 %collective-permute-done.30.refs_4_ = f32[2,32,1024]{2,1,0:T(8,128)S(1)} collective-permute-done((f32[2,32,1024]{2,1,0:T(8,128)S(1)}, f32[2,32,1024]{2,1,0:T(8,128)S(1)}, u32[]{:S(2)}, u32[]{:S(2)}) %collective-permute-start.30) | collective-permute-done | bytes 262176 | tf_op jit(solution)/shard_map/ppermute | solution.py:75
  98.7 1.6 %collective-permute-start.35 = (f32[2,1024]{1,0:T(2,128)S(1)}, f32[2,1024]{1,0:T(2,128)S(1)}, u32[]{:S(2)}, u32[]{:S(2)}) collective-permute-start(f32[2,1024]{1,0:T(2,128)S(1)} %shard_map.54.refs_12_), channel_id=1, source_target_pairs={{0,16},{4,20},{8,24},{12,28},{16,0},{20,4},{24,8},{28,12},{1,17},{... | collective-permute-start | bytes 24584 | tf_op jit(solution)/shard_map/ppermute | solution.py:75
  100.3 2.1 %collective-permute-done.35.refs_13_ = f32[2,1024]{1,0:T(2,128)S(1)} collective-permute-done((f32[2,1024]{1,0:T(2,128)S(1)}, f32[2,1024]{1,0:T(2,128)S(1)}, u32[]{:S(2)}, u32[]{:S(2)}) %collective-permute-start.35) | collective-permute-done | bytes 8224 | tf_op jit(solution)/shard_map/ppermute | solution.py:75
  103.4 1.6 %collective-permute-start.36 = (f32[2,1024]{1,0:T(2,128)S(1)}, f32[2,1024]{1,0:T(2,128)S(1)}, u32[]{:S(2)}, u32[]{:S(2)}) collective-permute-start(f32[2,1024]{1,0:T(2,128)S(1)} %shard_map.55.refs_12_), channel_id=1, source_target_pairs={{0,16},{4,20},{8,24},{12,28},{16,0},{20,4},{24,8},{28,12},{1,17},{... | collective-permute-start | bytes 24584 | tf_op jit(solution)/shard_map/ppermute | solution.py:75
  105.0 2.1 %collective-permute-done.36.refs_13_ = f32[2,1024]{1,0:T(2,128)S(1)} collective-permute-done((f32[2,1024]{1,0:T(2,128)S(1)}, f32[2,1024]{1,0:T(2,128)S(1)}, u32[]{:S(2)}, u32[]{:S(2)}) %collective-permute-start.36) | collective-permute-done | bytes 8224 | tf_op jit(solution)/shard_map/ppermute | solution.py:75
  108.0 1.6 %collective-permute-start.37 = (f32[2,1024]{1,0:T(2,128)S(1)}, f32[2,1024]{1,0:T(2,128)S(1)}, u32[]{:S(2)}, u32[]{:S(2)}) collective-permute-start(f32[2,1024]{1,0:T(2,128)S(1)} %shard_map.56.refs_6_), channel_id=1, source_target_pairs={{0,16},{4,20},{8,24},{12,28},{16,0},{20,4},{24,8},{28,12},{1,17},{... | collective-permute-start | bytes 24584 | tf_op jit(solution)/shard_map/ppermute | solution.py:75
  109.6 2.1 %collective-permute-done.37.refs_7_ = f32[2,1024]{1,0:T(2,128)S(1)} collective-permute-done((f32[2,1024]{1,0:T(2,128)S(1)}, f32[2,1024]{1,0:T(2,128)S(1)}, u32[]{:S(2)}, u32[]{:S(2)}) %collective-permute-start.37) | collective-permute-done | bytes 8224 | tf_op jit(solution)/shard_map/ppermute | solution.py:75
  111.7 2.2 %shard_map.57 = (bf16[2,4,32,512]{3,2,1,0:T(8,128)(2,1)S(1)}, bf16[2,4,32,512]{3,2,1,0:T(8,128)(2,1)S(1)}, bf16[2,4,32,512]{3,2,1,0:T(8,128)(2,1)S(1)}, bf16[2,4...) custom-call(f32[32,1024]{1,0:T(8,128)S(1)} %add_add_fusion.refs_0_, ...), custom_call_target="tpu_custom_call" | custom-call | flops 1073741824 | bytes 5259264 | tf_op jit(solution)/shard_map/pallas_call | solution.py:115
  113.9 1.8 %collective-permute-start.38 = (bf16[2,4,32,512]{3,2,1,0:T(8,128)(2,1)S(1)}, bf16[2,4,32,512]{3,2,1,0:T(8,128)(2,1)S(1)}, u32[]{:S(2)}, u32[]{:S(2)}) collective-permute-start(bf16[2,4,32,512]{3,2,1,0:T(8,128)(2,1)S(1)} %get-tuple-element.63), channel_id=1, source_target_pairs={{0,3},{1,2},{2,1},{3,0},{4,7},{5,6},{6,5},{7,4},{8,11},{9,10},{10,... | collective-permute-start | bytes 786440 | tf_op jit(solution)/shard_map/ppermute | solution.py:75
  115.6 2.6 %collective-permute-start.40 = (bf16[2,4,32,512]{3,2,1,0:T(8,128)(2,1)S(1)}, bf16[2,4,32,512]{3,2,1,0:T(8,128)(2,1)S(1)}, u32[]{:S(2)}, u32[]{:S(2)}) collective-permute-start(bf16[2,4,32,512]{3,2,1,0:T(8,128)(2,1)S(1)} %get-tuple-element.65), channel_id=1, source_target_pairs={{0,1},{1,0},{2,3},{3,2},{4,5},{5,4},{6,7},{7,6},{8,9},{9,8},{10,11... | collective-permute-start | bytes 786440 | tf_op jit(solution)/shard_map/ppermute | solution.py:75
  118.3 6.7 %collective-permute-done.38.refs_0_ = bf16[2,4,32,512]{3,2,1,0:T(8,128)(2,1)S(1)} collective-permute-done((bf16[2,4,32,512]{3,2,1,0:T(8,128)(2,1)S(1)}, bf16[2,4,32,512]{3,2,1,0:T(8,128)(2,1)S(1)}, u32[]{:S(2)}, u32[]{:S(2)}) %collective-permute-start.38) | collective-permute-done | bytes 262176 | tf_op jit(solution)/shard_map/ppermute | solution.py:75
  124.9 10.1 %collective-permute-done.39.refs_1_ = bf16[2,4,32,512]{3,2,1,0:T(8,128)(2,1)S(1)} collective-permute-done((bf16[2,4,32,512]{3,2,1,0:T(8,128)(2,1)S(1)}, bf16[2,4,32,512]{3,2,1,0:T(8,128)(2,1)S(1)}, u32[]{:S(2)}, u32[]{:S(2)}) %collective-permute-start.39) | collective-permute-done | bytes 262176 | tf_op jit(solution)/shard_map/ppermute | solution.py:75
  (75 shorter events, 29.0 us)
Async XLA Ops:
  1.9 12.0 %collective-permute-start = (bf16[128,2048]{1,0:T(8,128)(2,1)S(1)}, bf16[128,2048]{1,0:T(8,128)(2,1)S(1)}, u32[]{:S(2)}, u32[]{:S(2)}) collective-permute-start(bf16[128,2048]{1,0:T(8,128)(2,1)S(1)} %get-tuple-element.37), channel_id=1, source_target_pairs={{0,4},{4,0},{8,12},{12,8},{16,20},{20,16},{24,28},{28,24},{1,5},{5... | collective-permute-start | bytes 1572872 | tf_op jit(solution)/shard_map/ppermute | solution.py:75
  3.2 9.3 %collective-permute-start.2 = (bf16[256,512]{1,0:T(8,128)(2,1)S(1)}, bf16[256,512]{1,0:T(8,128)(2,1)S(1)}, u32[]{:S(2)}, u32[]{:S(2)}) collective-permute-start(bf16[256,512]{1,0:T(8,128)(2,1)S(1)} %get-tuple-element.38.refs_4_.refs_8_), channel_id=1, source_target_pairs={{0,16},{4,20},{8,24},{12,28},{16,0},{20,4},{24,8},{28,12},{1,17},{... | collective-permute-start | bytes 786440 | tf_op jit(solution)/shard_map/ppermute | solution.py:75
  6.2 7.8 %collective-permute-start.1 = (bf16[256,512]{1,0:T(8,128)(2,1)S(1)}, bf16[256,512]{1,0:T(8,128)(2,1)S(1)}, u32[]{:S(2)}, u32[]{:S(2)}) collective-permute-start(bf16[256,512]{1,0:T(8,128)(2,1)S(1)} %get-tuple-element.38.refs_4_.refs_8_), channel_id=1, source_target_pairs={{0,8},{4,12},{8,0},{12,4},{16,24},{20,28},{24,16},{28,20},{1,9},{5... | collective-permute-start | bytes 786440 | tf_op jit(solution)/shard_map/ppermute | solution.py:75
  7.7 13.0 %collective-permute-start.8 = (bf16[256,512]{1,0:T(8,128)(2,1)S(1)}, bf16[256,512]{1,0:T(8,128)(2,1)S(1)}, u32[]{:S(2)}, u32[]{:S(2)}) collective-permute-start(bf16[256,512]{1,0:T(8,128)(2,1)S(1)} %get-tuple-element.49), channel_id=1, source_target_pairs={{0,1},{1,0},{2,3},{3,2},{4,5},{5,4},{6,7},{7,6},{8,9},{9,8},{10,11... | collective-permute-start | bytes 786440 | tf_op jit(solution)/shard_map/ppermute | solution.py:75
  9.3 16.5 %collective-permute-start.3 = (bf16[256,512]{1,0:T(8,128)(2,1)S(1)}, bf16[256,512]{1,0:T(8,128)(2,1)S(1)}, u32[]{:S(2)}, u32[]{:S(2)}) collective-permute-start(bf16[256,512]{1,0:T(8,128)(2,1)S(1)} %get-tuple-element.42), channel_id=1, source_target_pairs={{0,2},{1,3},{2,0},{3,1},{4,6},{5,7},{6,4},{7,5},{8,10},{9,11},{10,... | collective-permute-start | bytes 786440 | tf_op jit(solution)/shard_map/ppermute | solution.py:75
  20.7 9.1 %collective-permute-start.11 = (bf16[256,512]{1,0:T(8,128)(2,1)S(1)}, bf16[256,512]{1,0:T(8,128)(2,1)S(1)}, u32[]{:S(2)}, u32[]{:S(2)}) collective-permute-start(bf16[256,512]{1,0:T(8,128)(2,1)S(1)} %collective-permute-done.8.refs_5_.refs_9_), channel_id=1, source_target_pairs={{0,16},{4,20},{8,24},{12,28},{16,0},{20,4},{24,8},{28,12},{1,17},{... | collective-permute-start | bytes 786440 | tf_op jit(solution)/shard_map/ppermute | solution.py:75
  21.2 11.6 %collective-permute-start.14 = (bf16[256,512]{1,0:T(8,128)(2,1)S(1)}, bf16[256,512]{1,0:T(8,128)(2,1)S(1)}, u32[]{:S(2)}, u32[]{:S(2)}) collective-permute-start(bf16[256,512]{1,0:T(8,128)(2,1)S(1)} %collective-permute-done.1.refs_8_.refs_12_), channel_id=1, source_target_pairs={{0,16},{4,20},{8,24},{12,28},{16,0},{20,4},{24,8},{28,12},{1,17},{... | collective-permute-start | bytes 786440 | tf_op jit(solution)/shard_map/ppermute | solution.py:75
  22.7 12.6 %collective-permute-start.6 = (bf16[256,512]{1,0:T(8,128)(2,1)S(1)}, bf16[256,512]{1,0:T(8,128)(2,1)S(1)}, u32[]{:S(2)}, u32[]{:S(2)}) collective-permute-start(bf16[256,512]{1,0:T(8,128)(2,1)S(1)} %get-tuple-element.47), channel_id=1, source_target_pairs={{0,3},{1,2},{2,1},{3,0},{4,7},{5,6},{6,5},{7,4},{8,11},{9,10},{10,... | collective-permute-start | bytes 786440 | tf_op jit(solution)/shard_map/ppermute | solution.py:75
  25.2 8.1 %collective-permute-start.9 = (bf16[256,512]{1,0:T(8,128)(2,1)S(1)}, bf16[256,512]{1,0:T(8,128)(2,1)S(1)}, u32[]{:S(2)}, u32[]{:S(2)}) collective-permute-start(bf16[256,512]{1,0:T(8,128)(2,1)S(1)} %collective-permute-done.8.refs_5_.refs_9_), channel_id=1, source_target_pairs={{0,8},{4,12},{8,0},{12,4},{16,24},{20,28},{24,16},{28,20},{1,9},{5... | collective-permute-start | bytes 786440 | tf_op jit(solution)/shard_map/ppermute | solution.py:75
  25.7 10.2 %collective-permute-start.4 = (bf16[2,128,512]{2,1,0:T(8,128)(2,1)S(1)}, bf16[2,128,512]{2,1,0:T(8,128)(2,1)S(1)}, u32[]{:S(2)}, u32[]{:S(2)}) collective-permute-start(bf16[2,128,512]{2,1,0:T(8,128)(2,1)S(1)} %get-tuple-element.43), channel_id=1, source_target_pairs={{0,1},{1,0},{2,3},{3,2},{4,5},{5,4},{6,7},{7,6},{8,9},{9,8},{10,11... | collective-permute-start | bytes 786440 | tf_op jit(solution)/shard_map/ppermute | solution.py:75
  32.8 7.3 %collective-permute-start.15 = (bf16[256,512]{1,0:T(8,128)(2,1)S(1)}, bf16[256,512]{1,0:T(8,128)(2,1)S(1)}, u32[]{:S(2)}, u32[]{:S(2)}) collective-permute-start(bf16[256,512]{1,0:T(8,128)(2,1)S(1)} %collective-permute-done.3.refs_6_.refs_10_), channel_id=1, source_target_pairs={{0,16},{4,20},{8,24},{12,28},{16,0},{20,4},{24,8},{28,12},{1,17},{... | collective-permute-start | bytes 786440 | tf_op jit(solution)/shard_map/ppermute | solution.py:75
  33.3 11.9 %collective-permute-start.10 = (bf16[256,512]{1,0:T(8,128)(2,1)S(1)}, bf16[256,512]{1,0:T(8,128)(2,1)S(1)}, u32[]{:S(2)}, u32[]{:S(2)}) collective-permute-start(bf16[256,512]{1,0:T(8,128)(2,1)S(1)} %collective-permute-done.3.refs_6_.refs_10_), channel_id=1, source_target_pairs={{0,8},{4,12},{8,0},{12,4},{16,24},{20,28},{24,16},{28,20},{1,9},{5... | collective-permute-start | bytes 786440 | tf_op jit(solution)/shard_map/ppermute | solution.py:75
  33.9 11.3 %collective-permute-start.12 = (bf16[256,512]{1,0:T(8,128)(2,1)S(1)}, bf16[256,512]{1,0:T(8,128)(2,1)S(1)}, u32[]{:S(2)}, u32[]{:S(2)}) collective-permute-start(bf16[256,512]{1,0:T(8,128)(2,1)S(1)} %collective-permute-done.11.refs_13_.refs_17_), channel_id=1, source_target_pairs={{0,8},{4,12},{8,0},{12,4},{16,24},{20,28},{24,16},{28,20},{1,9},{5... | collective-permute-start | bytes 786440 | tf_op jit(solution)/shard_map/ppermute | solution.py:75
  40.1 9.0 %collective-permute-start.16 = (bf16[256,512]{1,0:T(8,128)(2,1)S(1)}, bf16[256,512]{1,0:T(8,128)(2,1)S(1)}, u32[]{:S(2)}, u32[]{:S(2)}) collective-permute-start(bf16[256,512]{1,0:T(8,128)(2,1)S(1)} %collective-permute-done.6.refs_7_.refs_11_), channel_id=1, source_target_pairs={{0,16},{4,20},{8,24},{12,28},{16,0},{20,4},{24,8},{28,12},{1,17},{... | collective-permute-start | bytes 786440 | tf_op jit(solution)/shard_map/ppermute | solution.py:75
  40.6 16.5 %collective-permute-start.5 = (bf16[2,128,512]{2,1,0:T(8,128)(2,1)S(1)}, bf16[2,128,512]{2,1,0:T(8,128)(2,1)S(1)}, u32[]{:S(2)}, u32[]{:S(2)}) collective-permute-start(bf16[2,128,512]{2,1,0:T(8,128)(2,1)S(1)} %get-tuple-element.45), channel_id=1, source_target_pairs={{0,2},{1,3},{2,0},{3,1},{4,6},{5,7},{6,4},{7,5},{8,10},{9,11},{10,... | collective-permute-start | bytes 786440 | tf_op jit(solution)/shard_map/ppermute | solution.py:75
  41.4 15.8 %collective-permute-start.7 = (bf16[2,128,512]{2,1,0:T(8,128)(2,1)S(1)}, bf16[2,128,512]{2,1,0:T(8,128)(2,1)S(1)}, u32[]{:S(2)}, u32[]{:S(2)}) collective-permute-start(bf16[2,128,512]{2,1,0:T(8,128)(2,1)S(1)} %get-tuple-element.48), channel_id=1, source_target_pairs={{0,3},{1,2},{2,1},{3,0},{4,7},{5,6},{6,5},{7,4},{8,11},{9,10},{10,... | collective-permute-start | bytes 786440 | tf_op jit(solution)/shard_map/ppermute | solution.py:75
  45.2 11.9 %collective-permute-start.13 = (bf16[256,512]{1,0:T(8,128)(2,1)S(1)}, bf16[256,512]{1,0:T(8,128)(2,1)S(1)}, u32[]{:S(2)}, u32[]{:S(2)}) collective-permute-start(bf16[256,512]{1,0:T(8,128)(2,1)S(1)} %collective-permute-done.6.refs_7_.refs_11_), channel_id=1, source_target_pairs={{0,8},{4,12},{8,0},{12,4},{16,24},{20,28},{24,16},{28,20},{1,9},{5... | collective-permute-start | bytes 786440 | tf_op jit(solution)/shard_map/ppermute | solution.py:75
  46.0 11.1 %collective-permute-start.17 = (bf16[256,512]{1,0:T(8,128)(2,1)S(1)}, bf16[256,512]{1,0:T(8,128)(2,1)S(1)}, u32[]{:S(2)}, u32[]{:S(2)}) collective-permute-start(bf16[256,512]{1,0:T(8,128)(2,1)S(1)} %collective-permute-done.10.refs_10_.refs_14_), channel_id=1, source_target_pairs={{0,16},{4,20},{8,24},{12,28},{16,0},{20,4},{24,8},{28,12},{1,17},{... | collective-permute-start | bytes 786440 | tf_op jit(solution)/shard_map/ppermute | solution.py:75
  49.1 8.1 %collective-permute-start.18 = (bf16[256,512]{1,0:T(8,128)(2,1)S(1)}, bf16[256,512]{1,0:T(8,128)(2,1)S(1)}, u32[]{:S(2)}, u32[]{:S(2)}) collective-permute-start(bf16[256,512]{1,0:T(8,128)(2,1)S(1)} %collective-permute-done.16.refs_15_.refs_19_), channel_id=1, source_target_pairs={{0,8},{4,12},{8,0},{12,4},{16,24},{20,28},{24,16},{28,20},{1,9},{5... | collective-permute-start | bytes 786440 | tf_op jit(solution)/shard_map/ppermute | solution.py:75
  61.2 7.4 %collective-permute-start.20 = (f32[32,1024]{1,0:T(8,128)S(1)}, f32[32,1024]{1,0:T(8,128)S(1)}, u32[]{:S(2)}, u32[]{:S(2)}) collective-permute-start(f32[32,1024]{1,0:T(8,128)S(1)} %get-tuple-element.58), channel_id=1, source_target_pairs={{0,3},{1,2},{2,1},{3,0},{4,7},{5,6},{6,5},{7,4},{8,11},{9,10},{10,... | collective-permute-start | bytes 393224 | tf_op jit(solution)/shard_map/ppermute | solution.py:75
  63.3 13.8 %collective-permute-start.21 = (f32[32,1024]{1,0:T(8,128)S(1)}, f32[32,1024]{1,0:T(8,128)S(1)}, u32[]{:S(2)}, u32[]{:S(2)}) collective-permute-start(f32[32,1024]{1,0:T(8,128)S(1)} %get-tuple-element.59), channel_id=1, source_target_pairs={{0,2},{1,3},{2,0},{3,1},{4,6},{5,7},{6,4},{7,5},{8,10},{9,11},{10,... | collective-permute-start | bytes 393224 | tf_op jit(solution)/shard_map/ppermute | solution.py:75
  67.9 9.2 %collective-permute-start.22 = (f32[32,1024]{1,0:T(8,128)S(1)}, f32[32,1024]{1,0:T(8,128)S(1)}, u32[]{:S(2)}, u32[]{:S(2)}) collective-permute-start(f32[32,1024]{1,0:T(8,128)S(1)} %get-tuple-element.60), channel_id=1, source_target_pairs={{0,1},{1,0},{2,3},{3,2},{4,5},{5,4},{6,7},{7,6},{8,9},{9,8},{10,11... | collective-permute-start | bytes 393224 | tf_op jit(solution)/shard_map/ppermute | solution.py:75
  77.1 8.4 %collective-permute-start.24 = (f32[32,1024]{1,0:T(8,128)S(1)}, f32[32,1024]{1,0:T(8,128)S(1)}, u32[]{:S(2)}, u32[]{:S(2)}) collective-permute-start(f32[32,1024]{1,0:T(8,128)S(1)} %add_add_fusion.refs_0_), channel_id=1, source_target_pairs={{0,2},{1,3},{2,0},{3,1},{4,6},{5,7},{6,4},{7,5},{8,10},{9,11},{10,... | collective-permute-start | bytes 393224 | tf_op jit(solution)/shard_map/ppermute | solution.py:75
  77.2 8.5 %collective-permute-start.23 = (f32[32,1024]{1,0:T(8,128)S(1)}, f32[32,1024]{1,0:T(8,128)S(1)}, u32[]{:S(2)}, u32[]{:S(2)}) collective-permute-start(f32[32,1024]{1,0:T(8,128)S(1)} %add_add_fusion.refs_0_), channel_id=1, source_target_pairs={{0,1},{1,0},{2,3},{3,2},{4,5},{5,4},{6,7},{7,6},{8,9},{9,8},{10,11... | collective-permute-start | bytes 393224 | tf_op jit(solution)/shard_map/ppermute | solution.py:75
  85.7 9.2 %collective-permute-start.30 = (f32[2,32,1024]{2,1,0:T(8,128)S(1)}, f32[2,32,1024]{2,1,0:T(8,128)S(1)}, u32[]{:S(2)}, u32[]{:S(2)}) collective-permute-start(f32[2,32,1024]{2,1,0:T(8,128)S(1)} %pad_maximum_fusion.refs_1_), channel_id=1, source_target_pairs={{0,8},{4,12},{8,0},{12,4},{16,24},{20,28},{24,16},{28,20},{1,9},{5... | collective-permute-start | bytes 786440 | tf_op jit(solution)/shard_map/ppermute | solution.py:75
  86.5 8.9 %collective-permute-start.27 = (f32[32,1024]{1,0:T(8,128)S(1)}, f32[32,1024]{1,0:T(8,128)S(1)}, u32[]{:S(2)}, u32[]{:S(2)}) collective-permute-start(f32[32,1024]{1,0:T(8,128)S(1)} %add_add_fusion.refs_0_), channel_id=1, source_target_pairs={{0,4},{4,0},{8,12},{12,8},{16,20},{20,16},{24,28},{28,24},{1,5},{5... | collective-permute-start | bytes 393224 | tf_op jit(solution)/shard_map/ppermute | solution.py:75
  86.5 10.1 %collective-permute-start.28 = (f32[2,32,1024]{2,1,0:T(8,128)S(1)}, f32[2,32,1024]{2,1,0:T(8,128)S(1)}, u32[]{:S(2)}, u32[]{:S(2)}) collective-permute-start(f32[2,32,1024]{2,1,0:T(8,128)S(1)} %pad_maximum_fusion.refs_1_), channel_id=1, source_target_pairs={{0,4},{4,0},{8,12},{12,8},{16,20},{20,16},{24,28},{28,24},{1,5},{5... | collective-permute-start | bytes 786440 | tf_op jit(solution)/shard_map/ppermute | solution.py:75
  113.9 11.0 %collective-permute-start.38 = (bf16[2,4,32,512]{3,2,1,0:T(8,128)(2,1)S(1)}, bf16[2,4,32,512]{3,2,1,0:T(8,128)(2,1)S(1)}, u32[]{:S(2)}, u32[]{:S(2)}) collective-permute-start(bf16[2,4,32,512]{3,2,1,0:T(8,128)(2,1)S(1)} %get-tuple-element.63), channel_id=1, source_target_pairs={{0,3},{1,2},{2,1},{3,0},{4,7},{5,6},{6,5},{7,4},{8,11},{9,10},{10,... | collective-permute-start | bytes 786440 | tf_op jit(solution)/shard_map/ppermute | solution.py:75
  115.6 19.4 %collective-permute-start.39 = (bf16[2,4,32,512]{3,2,1,0:T(8,128)(2,1)S(1)}, bf16[2,4,32,512]{3,2,1,0:T(8,128)(2,1)S(1)}, u32[]{:S(2)}, u32[]{:S(2)}) collective-permute-start(bf16[2,4,32,512]{3,2,1,0:T(8,128)(2,1)S(1)} %get-tuple-element.64), channel_id=1, source_target_pairs={{0,2},{1,3},{2,0},{3,1},{4,6},{5,7},{6,4},{7,5},{8,10},{9,11},{10,... | collective-permute-start | bytes 786440 | tf_op jit(solution)/shard_map/ppermute | solution.py:75
  115.6 19.4 %collective-permute-start.40 = (bf16[2,4,32,512]{3,2,1,0:T(8,128)(2,1)S(1)}, bf16[2,4,32,512]{3,2,1,0:T(8,128)(2,1)S(1)}, u32[]{:S(2)}, u32[]{:S(2)}) collective-permute-start(bf16[2,4,32,512]{3,2,1,0:T(8,128)(2,1)S(1)} %get-tuple-element.65), channel_id=1, source_target_pairs={{0,1},{1,0},{2,3},{3,2},{4,5},{5,4},{6,7},{7,6},{8,9},{9,8},{10,11... | collective-permute-start | bytes 786440 | tf_op jit(solution)/shard_map/ppermute | solution.py:75
  118.3 17.8 %collective-permute-start.44 = (bf16[2,4,32,512]{3,2,1,0:T(8,128)(2,1)S(1)}, bf16[2,4,32,512]{3,2,1,0:T(8,128)(2,1)S(1)}, u32[]{:S(2)}, u32[]{:S(2)}) collective-permute-start(bf16[2,4,32,512]{3,2,1,0:T(8,128)(2,1)S(1)} %get-tuple-element.66.refs_3_), channel_id=1, source_target_pairs={{0,4},{4,0},{8,12},{12,8},{16,20},{20,16},{24,28},{28,24},{1,5},{5... | collective-permute-start | bytes 786440 | tf_op jit(solution)/shard_map/ppermute | solution.py:75
  124.9 11.2 %collective-permute-start.41 = (bf16[2,4,32,512]{3,2,1,0:T(8,128)(2,1)S(1)}, bf16[2,4,32,512]{3,2,1,0:T(8,128)(2,1)S(1)}, u32[]{:S(2)}, u32[]{:S(2)}) collective-permute-start(bf16[2,4,32,512]{3,2,1,0:T(8,128)(2,1)S(1)} %collective-permute-done.38.refs_0_), channel_id=1, source_target_pairs={{0,4},{4,0},{8,12},{12,8},{16,20},{20,16},{24,28},{28,24},{1,5},{5... | collective-permute-start | bytes 786440 | tf_op jit(solution)/shard_map/ppermute | solution.py:75
  (15 other events, 41.9 us)
